TPU v7x, 32 devices: a whole 2x2x4 slice. The times are simulated.
32 devices in a mesh: dp: 8 (over y, x, core), tensor: 4 (over z).
Axes of the slice: x: 2, y: 2, z: 4, core: 2. Of those that a mesh axis runs over, the one named last changes fastest.
Arguments:
- layer_input: bfloat16 [2, 8, 1024, 1024], P(None, 'dp', 'tensor'), may hold values from -6 to 6
- segment: int32 [2, 8, 1024], P(None, 'dp'), may hold values from 0 to 3, never falling along the last dimension, each value on 1 to 800 neighbouring positions
- d_out: bfloat16 [2, 8, 1024, 1024], P(None, 'dp', 'tensor'), may hold values from -6 to 6
- norm1_gain: bfloat16 [1024], replicated, may hold values from 0.099609375 to 1.8984375
- w_query: bfloat16 [1024, 1024], P(None, 'tensor'), may hold values from -0.1875 to 0.1875
- w_key: bfloat16 [1024, 1024], P(None, 'tensor'), may hold values from -0.1875 to 0.1875
- w_value: bfloat16 [1024, 1024], P(None, 'tensor'), may hold values from -0.1875 to 0.1875
- w_beta: bfloat16 [1024, 8], P(None, 'tensor'), may hold values from -0.1875 to 0.1875
- conv_weight: bfloat16 [3, 4, 1024], P(None, None, 'tensor'), may hold values from -2 to 2
- w_out: bfloat16 [1024, 1024], P('tensor'), may hold values from -0.25 to 0.25
- norm2_gain: bfloat16 [1024], replicated, may hold values from 0.099609375 to 1.8984375
- w_gate: bfloat16 [1024, 2816], P(None, 'tensor'), may hold values from -0.1875 to 0.1875
- w_up: bfloat16 [1024, 2816], P(None, 'tensor'), may hold values from -0.1875 to 0.1875
- w_down: bfloat16 [2816, 1024], P('tensor'), may hold values from -0.109375 to 0.109375
Outputs:
- output: bfloat16 [2, 8, 1024, 1024], P(None, 'dp', 'tensor')
- input_grad: bfloat16 [2, 8, 1024, 1024], P(None, 'dp', 'tensor')
- grad_norm1_gain: float32 [1024], P('tensor')
- grad_w_query: float32 [1024, 1024], P(None, 'tensor')
- grad_w_key: float32 [1024, 1024], P(None, 'tensor')
- grad_w_value: float32 [1024, 1024], P(None, 'tensor')
- grad_w_beta: float32 [1024, 8], P(None, 'tensor')
- grad_conv_weight: float32 [3, 4, 1024], P(None, None, 'tensor')
- grad_w_out: float32 [1024, 1024], P('tensor')
- grad_norm2_gain: float32 [1024], P('tensor')
- grad_w_gate: float32 [1024, 2816], P(None, 'tensor')
- grad_w_up: float32 [1024, 2816], P(None, 'tensor')
- grad_w_down: float32 [2816, 1024], P('tensor')
Inputs may be any that keep to these rules, and one draw needn't show every extreme that they name: `segment`: segment numbers never fall along a sequence; a document holds at most 800 tokens, and some document of each sequence holds exactly that many.
All inputs are finite; a program needn't handle non-finite values.
Results may differ from a plain program's by a relative error of at most 0.02.
Values may be sent and summed in bfloat16 or wider, within the bound.
No kernel may reach another device: no remote copies, remote signals or barrier semaphores. Data moves between devices by JAX's collectives and lax.ppermute only.
A program may use at most 256 MiB of HBM per device.

v0:
```python
import jax
import jax.numpy as jnp
from jax import lax
from jax.sharding import PartitionSpec as P

HD = 128
SPAN = 64


EPS = 1e-06


def short_conv(proj, taps, seg):
    length = proj.shape[1]
    total = jnp.zeros_like(proj)
    for offset in range(taps.shape[0]):
        moved = jnp.pad(proj, ((0, 0), (offset, 0), (0, 0)))[:, :length]
        earlier = jnp.pad(seg, ((0, 0), (offset, 0)), constant_values=-1)[:, :length]
        keep = (earlier == seg).astype(proj.dtype)
        total = total + taps[offset] * moved * keep[:, :, None]
    return total


def unit_heads(values, head):
    shaped = values.reshape(values.shape[0], values.shape[1], -1, head)
    return shaped / jnp.sqrt(jnp.sum(shaped * shaped, axis=-1, keepdims=True) + EPS)


def block_prepare(query, key, value, beta, seg, before):
    high = lax.Precision.HIGHEST
    size = query.shape[1]
    head = query.shape[3]
    same = seg[:, :, None] == seg[:, None, :]
    row_ids = lax.broadcasted_iota(jnp.int32, (size, size), 0)
    col_ids = lax.broadcasted_iota(jnp.int32, (size, size), 1)
    strict = (same & (row_ids > col_ids)[None]).astype(query.dtype)
    within = (same & (row_ids >= col_ids)[None]).astype(query.dtype)
    live = (seg == before[:, None]).astype(query.dtype)
    beta_heads = jnp.transpose(beta, (0, 2, 1))
    key_heads = jnp.transpose(key, (0, 2, 1, 3))
    query_heads = jnp.transpose(query, (0, 2, 1, 3))
    value_heads = jnp.transpose(value, (0, 2, 1, 3))
    keys_keys = jnp.einsum("ghie,ghje->ghij", key_heads, key_heads, precision=high)
    system = (
        jnp.eye(size, dtype=query.dtype) + beta_heads[:, :, :, None] * keys_keys * strict[:, None]
    )
    scaled_values = beta_heads[..., None] * value_heads
    scaled_keys = (beta_heads * live[:, None, :])[..., None] * key_heads
    solved = lax.linalg.triangular_solve(
        system,
        jnp.concatenate([scaled_values, scaled_keys], axis=-1),
        left_side=True,
        lower=True,
        unit_diagonal=True,
    )
    update_base = solved[..., :head]
    key_mix = solved[..., head:]
    scores = jnp.einsum("ghie,ghje->ghij", query_heads, key_heads, precision=high) * within[:, None]
    local_out = jnp.einsum("ghij,ghjd->ghid", scores, update_base, precision=high)
    query_eff = live[:, None, :, None] * query_heads - jnp.einsum(
        "ghij,ghje->ghie", scores, key_mix, precision=high
    )
    last = same[:, -1, :].astype(query.dtype)[:, None, :, None]
    state_add = jnp.einsum("ghjd,ghje->ghde", update_base * last, key_heads, precision=high)
    state_mix = jnp.einsum("ghjf,ghje->ghfe", key_mix * last, key_heads, precision=high)
    return (local_out, query_eff, state_add, state_mix, live[:, -1])


def block_step(state, block):
    local_out, query_eff, state_add, state_mix, live_end = block
    high = lax.Precision.HIGHEST
    mixed = local_out + jnp.einsum("ghie,ghde->ghid", query_eff, state, precision=high)
    state_next = (
        live_end[:, None, None, None] * state
        + state_add
        - jnp.einsum("ghdf,ghfe->ghde", state, state_mix, precision=high)
    )
    return (state_next, jnp.transpose(mixed, (0, 2, 1, 3)))


def delta_rule(query, key, value, beta, seg):
    batch, length, heads, head = query.shape
    blocks = length // SPAN

    def split(values):
        moved = jnp.swapaxes(values.reshape((batch, blocks, SPAN) + values.shape[2:]), 0, 1)
        return moved.reshape((blocks * batch,) + moved.shape[2:])

    def unflatten(values):
        return values.reshape((blocks, batch) + values.shape[1:])

    before = jnp.pad(seg, ((0, 0), (1, 0)), constant_values=-1)[:, :length]
    starts = jnp.swapaxes(before.reshape(batch, blocks, SPAN)[:, :, 0], 0, 1).reshape(
        blocks * batch
    )
    prepared = block_prepare(
        split(query), split(key), split(value), split(beta), split(seg), starts
    )
    state = jnp.zeros((batch, heads, head, head), query.dtype)
    _, outputs = lax.scan(block_step, state, tuple((unflatten(p) for p in prepared)))
    return jnp.swapaxes(outputs, 0, 1).reshape(batch, length, heads * head)


def mixer_core(q_proj, k_proj, v_proj, b_proj, taps, seg):
    query = unit_heads(jax.nn.silu(short_conv(q_proj, taps[0], seg)), HD)
    key = unit_heads(jax.nn.silu(short_conv(k_proj, taps[1], seg)), HD)
    value = jax.nn.silu(short_conv(v_proj, taps[2], seg)).reshape(query.shape)
    return delta_rule(query, key, value, jax.nn.sigmoid(b_proj), seg)


def norm_rows(rows, gain):
    rstd = lax.rsqrt(jnp.mean(rows * rows, axis=-1, keepdims=True) + EPS)
    unit = rows * rstd
    return (unit * gain, unit, rstd)


def norm_back(grad, unit, rstd, gain):
    scaled = grad * gain
    d_rows = rstd * (scaled - unit * jnp.mean(scaled * unit, axis=-1, keepdims=True))
    return (d_rows, jnp.sum(grad * unit, axis=0))


def project(left, right):
    return jnp.dot(left, right, preferred_element_type=jnp.float32)


def outer(left, right):
    return jnp.einsum("tc,td->cd", left, right, preferred_element_type=jnp.float32)


def back_project(left, right):
    return jnp.einsum("tc,dc->td", left, right, preferred_element_type=jnp.float32)


def shards(
    layer_input,
    segment,
    d_out,
    norm1_gain,
    w_query,
    w_key,
    w_value,
    w_beta,
    conv_weight,
    w_out,
    norm2_gain,
    w_gate,
    w_up,
    w_down,
):
    gain1 = norm1_gain.astype(jnp.float32)
    gain2 = norm2_gain.astype(jnp.float32)
    taps_f = conv_weight.astype(jnp.float32)
    micro_count = layer_input.shape[0]
    weights = (w_query, w_key, w_value, w_beta, w_out, w_gate, w_up, w_down)
    totals = [jnp.zeros(w.shape, jnp.float32) for w in weights]
    conv_total = jnp.zeros(conv_weight.shape, jnp.float32)
    gain1_total = jnp.zeros(gain1.shape, jnp.float32)
    gain2_total = jnp.zeros(gain2.shape, jnp.float32)
    results = []
    input_grads = []
    for micro_step in range(micro_count):
        rows = layer_input[micro_step, 0].astype(jnp.float32)
        seg = segment[micro_step, 0][None]
        normed1, unit1, rstd1 = norm_rows(rows, gain1)
        mixer_in = lax.all_gather(normed1.astype(jnp.bfloat16), "tensor", axis=0, tiled=True)
        q_proj = project(mixer_in, w_query)
        k_proj = project(mixer_in, w_key)
        v_proj = project(mixer_in, w_value)
        b_proj = project(mixer_in, w_beta)

        def core_local(q_part, k_part, v_part, b_part, taps_part):
            return mixer_core(q_part, k_part, v_part, b_part, taps_part, seg)

        mixed, core_back = jax.vjp(
            core_local, q_proj[None], k_proj[None], v_proj[None], b_proj[None], taps_f
        )
        mixed_low = mixed[0].astype(jnp.bfloat16)
        mid = rows + lax.psum_scatter(
            project(mixed_low, w_out).astype(jnp.bfloat16),
            "tensor",
            scatter_dimension=0,
            tiled=True,
        ).astype(jnp.float32)
        normed2, unit2, rstd2 = norm_rows(mid, gain2)
        ffn_in = lax.all_gather(normed2.astype(jnp.bfloat16), "tensor", axis=0, tiled=True)
        gate = project(ffn_in, w_gate)
        up_part = project(ffn_in, w_up)
        sigma = jax.nn.sigmoid(gate)
        hidden = (gate * sigma * up_part).astype(jnp.bfloat16)
        result = mid + lax.psum_scatter(
            project(hidden, w_down).astype(jnp.bfloat16), "tensor", scatter_dimension=0, tiled=True
        ).astype(jnp.float32)
        results.append(result.astype(jnp.bfloat16))
        out_grad = d_out[micro_step, 0]
        full_grad = lax.all_gather(out_grad, "tensor", axis=0, tiled=True)
        totals[7] = totals[7] + outer(hidden, full_grad)
        d_hidden = back_project(full_grad, w_down)
        d_gate = (d_hidden * up_part * sigma * (1.0 + gate * (1.0 - sigma))).astype(jnp.bfloat16)
        d_up = (d_hidden * gate * sigma).astype(jnp.bfloat16)
        totals[5] = totals[5] + outer(ffn_in, d_gate)
        totals[6] = totals[6] + outer(ffn_in, d_up)
        d_normed2 = lax.psum_scatter(
            (back_project(d_gate, w_gate) + back_project(d_up, w_up)).astype(jnp.bfloat16),
            "tensor",
            scatter_dimension=0,
            tiled=True,
        ).astype(jnp.float32)
        d_mid_local, gain2_part = norm_back(d_normed2, unit2, rstd2, gain2)
        gain2_total = gain2_total + gain2_part
        d_mid = out_grad.astype(jnp.float32) + d_mid_local
        mid_grad = lax.all_gather(d_mid.astype(jnp.bfloat16), "tensor", axis=0, tiled=True)
        totals[4] = totals[4] + outer(mixed_low, mid_grad)
        d_mixed = back_project(mid_grad, w_out)
        d_qf, d_kf, d_vf, d_bf, d_taps = core_back(d_mixed[None])
        d_query = d_qf[0].astype(jnp.bfloat16)
        d_key = d_kf[0].astype(jnp.bfloat16)
        d_value = d_vf[0].astype(jnp.bfloat16)
        d_beta = d_bf[0].astype(jnp.bfloat16)
        totals[0] = totals[0] + outer(mixer_in, d_query)
        totals[1] = totals[1] + outer(mixer_in, d_key)
        totals[2] = totals[2] + outer(mixer_in, d_value)
        totals[3] = totals[3] + outer(mixer_in, d_beta)
        conv_total = conv_total + d_taps
        d_normed1 = lax.psum_scatter(
            (
                back_project(d_query, w_query)
                + back_project(d_key, w_key)
                + back_project(d_value, w_value)
                + back_project(d_beta, w_beta)
            ).astype(jnp.bfloat16),
            "tensor",
            scatter_dimension=0,
            tiled=True,
        ).astype(jnp.float32)
        d_in_local, gain1_part = norm_back(d_normed1, unit1, rstd1, gain1)
        gain1_total = gain1_total + gain1_part
        input_grads.append((d_mid + d_in_local).astype(jnp.bfloat16))
    gain_parts = (
        lax.psum_scatter(gain1_total, "tensor", scatter_dimension=0, tiled=True),
        lax.psum_scatter(gain2_total, "tensor", scatter_dimension=0, tiled=True),
    )
    every_sum = (
        lax.psum(totals[0].astype(jnp.bfloat16), "dp").astype(jnp.float32),
        lax.psum(totals[1].astype(jnp.bfloat16), "dp").astype(jnp.float32),
        lax.psum(totals[2].astype(jnp.bfloat16), "dp").astype(jnp.float32),
        lax.psum(totals[3].astype(jnp.bfloat16), "dp").astype(jnp.float32),
        lax.psum(totals[4].astype(jnp.bfloat16), "dp").astype(jnp.float32),
        lax.psum(totals[5].astype(jnp.bfloat16), "dp").astype(jnp.float32),
        lax.psum(totals[6].astype(jnp.bfloat16), "dp").astype(jnp.float32),
        lax.psum(totals[7].astype(jnp.bfloat16), "dp").astype(jnp.float32),
        lax.psum(conv_total.astype(jnp.bfloat16), "dp").astype(jnp.float32),
        lax.psum(gain_parts[0].astype(jnp.bfloat16), "dp").astype(jnp.float32),
        lax.psum(gain_parts[1].astype(jnp.bfloat16), "dp").astype(jnp.float32),
    )
    output = jnp.stack(results)[:, None]
    input_grad = jnp.stack(input_grads)[:, None]
    return (
        output,
        input_grad,
        every_sum[9],
        every_sum[0],
        every_sum[1],
        every_sum[2],
        every_sum[3],
        every_sum[8],
        every_sum[4],
        every_sum[10],
        every_sum[5],
        every_sum[6],
        every_sum[7],
    )


def solution(mesh):
    in_specs = (
        P(None, "dp", "tensor", None),
        P(None, "dp", None),
        P(None, "dp", "tensor", None),
        P(),
        P(None, "tensor"),
        P(None, "tensor"),
        P(None, "tensor"),
        P(None, "tensor"),
        P(None, None, "tensor"),
        P("tensor", None),
        P(),
        P(None, "tensor"),
        P(None, "tensor"),
        P("tensor", None),
    )
    out_specs = (
        P(None, "dp", "tensor", None),
        P(None, "dp", "tensor", None),
        P("tensor"),
        P(None, "tensor"),
        P(None, "tensor"),
        P(None, "tensor"),
        P(None, "tensor"),
        P(None, None, "tensor"),
        P("tensor", None),
        P("tensor"),
        P(None, "tensor"),
        P(None, "tensor"),
        P("tensor", None),
    )
    return jax.shard_map(shards, mesh=mesh, in_specs=in_specs, out_specs=out_specs, check_vma=False)
```

profile of v0, /device:TPU:1, one launch (start us, length us, event | category | flops | bytes accessed | tf_op | source)
XLA Modules:
  0.0 1985.5 jit_solution(13902957269521412300)
XLA Ops:
  20.5 40.3 %all-gather.15.cloned.1.call-done = bf16[1024,1024]{1,0:T(8,128)(2,1)} async-done(((bf16[256,1024]{1,0:T(8,128)(2,1)}), bf16[1024,1024]{1,0:T(8,128)(2,1)}) %all-gather.15.cloned.1.call-update) | async-done | bytes 2097168 | tf_op jit(solution)/shard_map/all_gather | solution.py:166
  63.1 44.5 %all-gather.11.cloned.1.call-done = bf16[1024,1024]{1,0:T(8,128)(2,1)} async-done(((bf16[256,1024]{1,0:T(8,128)(2,1)}), bf16[1024,1024]{1,0:T(8,128)(2,1)}) %all-gather.11.cloned.1.call-update) | async-done | bytes 2097168 | tf_op jit(solution)/shard_map/all_gather | solution.py:166
  110.1 3.0 fusion.411
  118.6 2.9 reshape.1341
  131.0 3.1 fusion.414
  138.4 3.3 multiply_reduce_fusion.28
  145.6 3.2 multiply_reduce_fusion.31
  156.8 3.8 fusion.282
  164.9 158.7 %custom-call.17 = f32[16,2,1,64,64]{3,4,2,1,0:T(8,128)} custom-call(f32[16,2,1,64,64]{4,3,2,1,0:T(8,128)} %get-tuple-element.1151), custom_call_target="InvertDiagBlocksLowerTriangular" | custom-call | tf_op jit(solution)/shard_map/jvp()/triangular_solve/custom-call.1 | solution.py:49
  338.7 4.0 fusion.106
  342.7 2.8 convolution_multiply_fusion
  350.2 5.2 fusion.279
  355.4 5.2 convolution_bitcast_fusion.10
  362.7 3.1 fusion.412
  375.3 158.0 %custom-call.16 = f32[16,2,1,64,64]{3,4,2,1,0:T(8,128)S(1)} custom-call(f32[16,2,1,64,64]{4,3,2,1,0:T(8,128)} %get-tuple-element.1150), custom_call_target="InvertDiagBlocksLowerTriangular" | custom-call | tf_op jit(solution)/shard_map/jvp()/triangular_solve/custom-call.1 | solution.py:49
  549.1 5.2 fusion.303
  554.3 5.4 convolution_bitcast_fusion.11
  561.4 107.7 %while.81 = (s32[]{:T(128)}, f32[1,2,128,128]{2,3,1,0:T(8,128)S(1)}, bf16[16,1,64,2,128]{4,2,3,1,0:T(8,128)(2,1)S(1)}, f32[16,1,2,128,128]{3,4,2,1,0:T(8,128)}, ...) while((s32[]{:T(128)}, ...), condition=%wide.region_12.14_spmd.clone, body=%wide.region_11.13_spmd.clone.sunk | while | flops 75743232 | bytes 2035356 | solution.py:100
  674.3 108.0 %while.80 = (s32[]{:T(128)}, f32[1,2,128,128]{2,3,1,0:T(8,128)S(1)}, bf16[16,1,64,2,128]{4,2,3,1,0:T(8,128)(2,1)S(1)}, f32[16,1,2,128,128]{3,4,2,1,0:T(8,128)}, ...) while((s32[]{:T(128)}, ...), condition=%wide.region_4.6_spmd.clone, body=%wide.region_3.5_spmd.clone.sunk | while | flops 75743232 | bytes 2035356 | solution.py:100
  785.9 42.4 %reduce-scatter.9.cloned.1.call-done = bf16[256,1024]{1,0:T(8,128)(2,1)} async-done(((bf16[1024,1024]{1,0:T(8,128)(2,1)}), bf16[256,1024]{1,0:T(8,128)(2,1)}) %reduce-scatter.9.cloned.1.call-update) | async-done | bytes 524304 | tf_op jit(solution)/shard_map/reduce_scatter | solution.py:179
  835.9 41.7 %all-gather.17.cloned.1.call-done = bf16[1024,1024]{1,0:T(8,128)(2,1)} async-done(((bf16[256,1024]{1,0:T(8,128)(2,1)}), bf16[1024,1024]{1,0:T(8,128)(2,1)}) %all-gather.17.cloned.1.call-update) | async-done | bytes 2097168 | tf_op jit(solution)/shard_map/all_gather | solution.py:186
  877.6 5.4 fusion.442
  883.0 3.3 fusion.443
  886.3 37.4 %all-gather.25.cloned.1.call-done = bf16[1,1,1024,1024]{3,2,1,0:T(8,128)(2,1)} async-done(((bf16[1,1,256,1024]{3,2,1,0:T(8,128)(2,1)}), bf16[1,1,1024,1024]{3,2,1,0:T(8,128)(2,1)}) %all-gather.25.cloned.1.call-update) | async-done | bytes 2097168 | tf_op jit(solution)/shard_map/all_gather | solution.py:196
  923.7 6.7 multiply_convert_fusion
  932.8 3.3 add_convert_fusion.1
  936.1 34.4 %all-gather.13.cloned.1.call-done = bf16[1024,1024]{1,0:T(8,128)(2,1)} async-done(((bf16[256,1024]{1,0:T(8,128)(2,1)}), bf16[1024,1024]{1,0:T(8,128)(2,1)}) %all-gather.13.cloned.1.call-update) | async-done | bytes 2097168 | tf_op jit(solution)/shard_map/all_gather | solution.py:186
  970.5 5.4 fusion.437
  975.9 3.3 fusion.438
  979.2 37.6 %all-gather.23.cloned.1.call-done = bf16[1,1,1024,1024]{3,2,1,0:T(8,128)(2,1)} async-done(((bf16[1,1,256,1024]{3,2,1,0:T(8,128)(2,1)}), bf16[1,1,1024,1024]{3,2,1,0:T(8,128)(2,1)}) %all-gather.23.cloned.1.call-update) | async-done | bytes 2097168 | tf_op jit(solution)/shard_map/all_gather | solution.py:196
  1016.8 6.5 multiply_convert_fusion.2
  1025.7 3.2 add_convert_fusion.3
  1028.9 4.5 convolution_convert_fusion.2
  1033.5 28.0 %reduce-scatter.21.cloned.1.call-done = bf16[256,1024]{1,0:T(8,128)(2,1)} async-done(((bf16[1024,1024]{1,0:T(8,128)(2,1)}), bf16[256,1024]{1,0:T(8,128)(2,1)}) %reduce-scatter.21.cloned.1.call-update) | async-done | bytes 524304 | tf_op jit(solution)/shard_map/reduce_scatter | solution.py:203
  1061.5 46.0 %reduce-scatter.17.cloned.1.call-done = bf16[256,1024]{1,0:T(8,128)(2,1)} async-done(((bf16[1024,1024]{1,0:T(8,128)(2,1)}), bf16[256,1024]{1,0:T(8,128)(2,1)}) %reduce-scatter.17.cloned.1.call-update) | async-done | bytes 524304 | tf_op jit(solution)/shard_map/reduce_scatter | solution.py:203
  1111.4 42.2 %reduce-scatter.15.cloned.1.call-done = bf16[256,1024]{1,0:T(8,128)(2,1)} async-done(((bf16[1024,1024]{1,0:T(8,128)(2,1)}), bf16[256,1024]{1,0:T(8,128)(2,1)}) %reduce-scatter.15.cloned.1.call-update) | async-done | bytes 524304 | tf_op jit(solution)/shard_map/reduce_scatter | solution.py:191
  1153.6 3.6 fusion.409
  1178.3 3.8 fusion.449
  1186.2 2.8 add_convert_fusion.5
  1189.0 2.8 add_convert_fusion.6
  1191.8 2.8 add_convert_fusion.4
  1194.7 8.2 all-gather.21.cloned.1.call-done
  1211.1 144.9 %while.83 = (s32[]{:T(128)}, f32[1,2,128,128]{2,3,1,0:T(8,128)S(1)}, f32[16,1,2,64,128]{4,3,2,1,0:T(8,128)}, f32[16,1,2,64,128]{4,3,2,1,0:T(8,128)S(1)}, f32[16,...) while((s32[]{:T(128)}, ...), condition=%wide.region_30.34_spmd.clone, body=%wide.region_29.33_spmd.clone.sunk | while | flops 151289856 | bytes 2101943 | solution.py:100
  1356.0 6.2 fusion.160
  1380.6 4.2 fusion.112
  1411.9 191.8 %while.82 = (s32[]{:T(128)}, f32[1,2,128,128]{2,3,1,0:T(8,128)}, f32[16,1,2,64,128]{4,3,2,1,0:T(8,128)}, f32[16,1,2,64,128]{4,3,2,1,0:T(8,128)}, f32[16,1,2,128,...) while((s32[]{:T(128)}, f32[1,2,128,128]{2,3,1,0:T(8,128)}, ...), condition=%wide.region_19.21_spmd.clone, body=%wide.region_18.20_spmd.clone.sunk | while | flops 151289856 | bytes 2101943 | solution.py:100
  1603.7 3.1 fusion.317
  1612.9 4.2 fusion.151
  1627.5 4.3 fusion.124
  1631.8 3.1 fusion.308
  1656.4 3.1 broadcast_in_dim.321
  1678.3 3.1 broadcast_in_dim.316
  1687.4 3.2 broadcast_in_dim.319
  1690.6 3.0 reshape.1366
  1693.8 8.2 multiply_reduce_fusion.3
  1706.4 5.8 multiply_reduce_fusion.15
  1748.7 4.6 convolution_convert_fusion.3
  1763.6 71.5 %all-reduce.83.cloned.1.call-done = (bf16[1024,256]{1,0:T(8,128)(2,1)}, bf16[1024,256]{1,0:T(8,128)(2,1)}, bf16[1024,256]{1,0:T(8,128)(2,1)}, bf16[256,1024]{1,0...) async-done(((bf16[1024,256]{1,0:T(8,128)(2,1)}, bf16[1024,256]{1,0:T(8,128)(2,1)}, bf16[1024,256]{1,0:T(8,128)(2,1)}, ...) | async-done | bytes 6422544 | tf_op jit(solution)/shard_map/psum | solution.py:244
  1835.1 3.4 convert_element_type.463
  1846.7 34.7 %reduce-scatter.23.cloned.1.call-done = bf16[256,1024]{1,0:T(8,128)(2,1)} async-done(((bf16[1024,1024]{1,0:T(8,128)(2,1)}), bf16[256,1024]{1,0:T(8,128)(2,1)}) %reduce-scatter.23.cloned.1.call-update) | async-done | bytes 524304 | tf_op jit(solution)/shard_map/reduce_scatter | solution.py:225
  1881.4 45.4 %reduce-scatter.19.cloned.1.call-done = bf16[256,1024]{1,0:T(8,128)(2,1)} async-done(((bf16[1024,1024]{1,0:T(8,128)(2,1)}), bf16[256,1024]{1,0:T(8,128)(2,1)}) %reduce-scatter.19.cloned.1.call-update) | async-done | bytes 524304 | tf_op jit(solution)/shard_map/reduce_scatter | solution.py:225
  1929.9 9.2 all-reduce.78
  1941.6 23.4 %all-reduce.79 = (bf16[256]{0:T(256)(128)(2,1)}, bf16[1024,2]{0,1:T(2,128)(2,1)}, bf16[3,4,256]{2,1,0:T(4,128)(2,1)}, bf16[256]{0:T(256)(128)(2,1)}) all-reduce(bf16[256]{0:T(256)(128)(2,1)} %dynamic-slice.7, bf16[1024,2]{0,1:T(2,128)(2,1)S(1)} %fusion.196, ...), channel_id=1, replica_groups=mesh['dp'=8,'tensor'=4] {'dp'}, use_global_device_ids=true, to_apply=%region_41.45 | all-reduce | flops 5632 | bytes 22528 | tf_op jit(solution)/shard_map/psum | solution.py:253
  1971.3 2.9 fusion.352
  (1327 shorter events, 892.0 us)
Async XLA Ops:
  7.2 916.5 %copy-start = (bf16[704,1024]{1,0:T(8,128)(2,1)S(1)}, bf16[704,1024]{1,0:T(8,128)(2,1)}, u32[]{:S(2)}) copy-start(bf16[704,1024]{1,0:T(8,128)(2,1)} %param.41) | copy-start | bytes 4325380
  7.2 9.1 copy-start.214
  7.2 53.6 %all-gather.15.cloned.1.call-start = ((), (), s32[]{:S(2)}) async-start(), calls=%async_computation.12 | async-start | bytes 2621440 | tf_op jit(solution)/shard_map/all_gather | solution.py:166
  12.6 48.2 %copy-start.83 = (bf16[1024,256]{1,0:T(8,128)(2,1)S(1)}, bf16[1024,256]{1,0:T(8,128)(2,1)}, u32[]{:S(2)}) copy-start(bf16[1024,256]{1,0:T(8,128)(2,1)} %param.33) | copy-start | bytes 1572868
  12.6 95.0 %all-gather.11.cloned.1.call-start = ((), (), s32[]{:S(2)}) async-start(), calls=%async_computation.8 | async-start | bytes 2621440 | tf_op jit(solution)/shard_map/all_gather | solution.py:166
  13.4 772.5 %reduce-scatter.13.cloned.1.call-start = ((), (), s32[]{:S(2)}) async-start(), calls=%async_computation.13 | async-start | bytes 2621440 | tf_op jit(solution)/shard_map/reduce_scatter | solution.py:179
  17.6 92.4 %copy-start.147 = (f32[1,1024]{1,0:T(1,128)}, f32[1,1024]{1,0:T(1,128)S(1)}, u32[]{:S(2)}) copy-start(f32[1,1024]{1,0:T(1,128)S(1)} %get-tuple-element.1218) | copy-start | bytes 12292
  17.6 92.4 %copy-start.150 = (f32[1,1024]{1,0:T(1,128)}, f32[1,1024]{1,0:T(1,128)S(1)}, u32[]{:S(2)}) copy-start(f32[1,1024]{1,0:T(1,128)S(1)} %get-tuple-element.1219) | copy-start | bytes 12292
  17.6 92.4 %copy-start.153 = (f32[1,1024]{1,0:T(1,128)}, f32[1,1024]{1,0:T(1,128)S(1)}, u32[]{:S(2)}) copy-start(f32[1,1024]{1,0:T(1,128)S(1)} %get-tuple-element.1220) | copy-start | bytes 12292
  17.6 92.4 %copy-start.156 = (f32[1,1024]{1,0:T(1,128)}, f32[1,1024]{1,0:T(1,128)S(1)}, u32[]{:S(2)}) copy-start(f32[1,1024]{1,0:T(1,128)S(1)} %get-tuple-element.1203) | copy-start | bytes 12292
  63.1 46.9 %copy-start.9 = (f32[1024,256]{1,0:T(8,128)}, f32[1024,256]{1,0:T(8,128)S(1)}, u32[]{:S(2)}) copy-start(f32[1024,256]{1,0:T(8,128)S(1)} %fusion.439) | copy-start | bytes 3145732
  138.4 15.0 copy-start.20
  143.6 11.1 copy-start.179
  156.8 381.6 %copy-start.121 = (f32[16,64,2]{1,2,0:T(2,128)}, f32[16,64,2]{1,2,0:T(2,128)S(1)}, u32[]{:S(2)}) copy-start(f32[16,64,2]{1,2,0:T(2,128)S(1)} %copy.716) | copy-start | bytes 24580
  338.7 6.8 copy-start.229
  342.7 12.7 copy-start.5
  368.6 164.8 %copy-start.31 = (f32[16,64,2,128]{3,2,1,0:T(2,128)S(1)}, f32[16,64,2,128]{3,2,1,0:T(2,128)}, u32[]{:S(2)}) copy-start(f32[16,64,2,128]{3,2,1,0:T(2,128)} %reshape.1340) | copy-start | bytes 3145732
  533.3 9.1 copy-start.26
  544.5 9.8 copy-start.3
  561.4 109.1 %copy-start.108 = (bf16[256,1024]{1,0:T(8,128)(2,1)S(1)}, bf16[256,1024]{1,0:T(8,128)(2,1)}, u32[]{:S(2)}) copy-start(bf16[256,1024]{1,0:T(8,128)(2,1)} %param.37) | copy-start | bytes 1572868
  672.6 155.7 %reduce-scatter.9.cloned.1.call-start = ((), (), s32[]{:S(2)}) async-start(), calls=%async_computation.9 | async-start | bytes 2621440 | tf_op jit(solution)/shard_map/reduce_scatter | solution.py:179
  783.7 44.6 %copy-start.1 = (bf16[2,1,256,1024]{3,2,1,0:T(8,128)(2,1)S(1)}, bf16[2,1,256,1024]{3,2,1,0:T(8,128)(2,1)}, u32[]{:S(2)}) copy-start(bf16[2,1,256,1024]{3,2,1,0:T(8,128)(2,1)} %param.28) | copy-start | bytes 3145732
  785.8 91.8 %all-gather.17.cloned.1.call-start = ((), (), s32[]{:S(2)}) async-start(), calls=%async_computation.14 | async-start | bytes 2621440 | tf_op jit(solution)/shard_map/all_gather | solution.py:186
  785.8 367.8 %copy-start.125 = (f32[1024]{0:T(1024)}, f32[1024]{0:T(1024)S(1)}, u32[]{:S(2)}) copy-start(f32[1024]{0:T(1024)S(1)} %convert_element_type.391) | copy-start | bytes 12292
  785.9 44.7 %copy-start.24 = (bf16[256,1024]{1,0:T(8,128)(2,1)S(1)}, bf16[256,1024]{1,0:T(8,128)(2,1)}, u32[]{:S(2)}) copy-start(bf16[256,1024]{1,0:T(8,128)(2,1)} %reduce-scatter.13.cloned.1.call-done) | copy-start | bytes 1572868
  830.6 323.1 %copy-start.187 = (f32[256]{0:T(256)}, f32[256]{0:T(256)S(1)}, u32[]{:S(2)}) copy-start(f32[256]{0:T(256)S(1)} %add_rsqrt_fusion.2) | copy-start | bytes 3076
  832.0 91.7 %all-gather.25.cloned.1.call-start = ((), (), s32[]{:S(2)}) async-start(), calls=%async_computation.23 | async-start | bytes 2621440 | tf_op jit(solution)/shard_map/all_gather | solution.py:196
  834.3 136.2 %all-gather.13.cloned.1.call-start = ((), (), s32[]{:S(2)}) async-start(), calls=%async_computation.10 | async-start | bytes 2621440 | tf_op jit(solution)/shard_map/all_gather | solution.py:186
  835.1 181.7 %all-gather.23.cloned.1.call-start = ((), (), s32[]{:S(2)}) async-start(), calls=%async_computation.22 | async-start | bytes 2621440 | tf_op jit(solution)/shard_map/all_gather | solution.py:196
  835.8 225.7 %reduce-scatter.21.cloned.1.call-start = ((), (), s32[]{:S(2)}) async-start(), calls=%async_computation.19 | async-start | bytes 2621440 | tf_op jit(solution)/shard_map/reduce_scatter | solution.py:203
  936.1 171.5 %reduce-scatter.17.cloned.1.call-start = ((), (), s32[]{:S(2)}) async-start(), calls=%async_computation.16 | async-start | bytes 2621440 | tf_op jit(solution)/shard_map/reduce_scatter | solution.py:203
  1028.9 124.8 %reduce-scatter.15.cloned.1.call-start = ((), (), s32[]{:S(2)}) async-start(), calls=%async_computation.15 | async-start | bytes 2621440 | tf_op jit(solution)/shard_map/reduce_scatter | solution.py:191
  1033.5 169.4 %all-gather.21.cloned.1.call-start = ((), (), s32[]{:S(2)}) async-start(), calls=%async_computation.20 | async-start | bytes 2621440 | tf_op jit(solution)/shard_map/all_gather | solution.py:212
  1157.3 245.4 %all-gather.19.cloned.1.call-start = ((), (), s32[]{:S(2)}) async-start(), calls=%async_computation.17 | async-start | bytes 2621440 | tf_op jit(solution)/shard_map/all_gather | solution.py:212
  1191.8 11.0 copy-start.109
  1194.6 640.5 %all-reduce.83.cloned.1.call-start = ((), (), s32[]{:S(2)}) async-start(), calls=%async_computation.24 | async-start | bytes 12845056 | tf_op jit(solution)/shard_map/psum | solution.py:244
  1211.1 144.9 %copy-start.131 = (f32[16,64,2]{1,2,0:T(2,128)S(1)}, f32[16,64,2]{1,2,0:T(2,128)}, u32[]{:S(2)}) copy-start(f32[16,64,2]{1,2,0:T(2,128)} %copy.344) | copy-start | bytes 24580
  1211.1 144.9 %copy-start.171 = (f32[16,1,64]{2,1,0:T(1,128)S(1)}, f32[16,1,64]{2,1,0:T(1,128)}, u32[]{:S(2)}) copy-start(f32[16,1,64]{2,1,0:T(1,128)} %get-tuple-element.1223) | copy-start | bytes 12292
  1408.1 195.6 %copy-start.4 = (f32[16,2,64,256]{3,2,1,0:T(8,128)S(1)}, f32[16,2,64,256]{3,2,1,0:T(8,128)}, u32[]{:S(2)}) copy-start(f32[16,2,64,256]{3,2,1,0:T(8,128)} %copy-done.3) | copy-start | bytes 6291460
  1693.6 8.3 copy-start.164
  1693.7 8.3 copy-start.192
  1693.7 8.3 copy-start.196
  1693.7 8.3 copy-start.200
  1693.7 8.3 copy-start.204
  1693.7 8.3 copy-start.208
  1693.7 8.3 copy-start.212
  1693.7 8.3 copy-start.219
  1693.7 8.3 copy-start.222
  1693.7 8.3 copy-start.225
  1714.7 6.9 copy-start.91
  1714.7 9.2 copy-start.96
  1715.8 10.6 copy-start.98
  1717.9 10.0 copy-start.99
  1729.5 151.9 %reduce-scatter.23.cloned.1.call-start = ((), (), s32[]{:S(2)}) async-start(), calls=%async_computation.21 | async-start | bytes 2621440 | tf_op jit(solution)/shard_map/reduce_scatter | solution.py:225
  1739.4 187.4 %reduce-scatter.19.cloned.1.call-start = ((), (), s32[]{:S(2)}) async-start(), calls=%async_computation.18 | async-start | bytes 2621440 | tf_op jit(solution)/shard_map/reduce_scatter | solution.py:225
  1748.6 225.5 %reduce-scatter.11.cloned.1.call-start = ((), (), s32[]{:S(2)}) async-start(), calls=%async_computation.11 | async-start | bytes 2621440 | tf_op jit(solution)/shard_map/reduce_scatter | solution.py:191
  1755.2 8.1 copy-start.166
  1843.5 83.3 %copy-start.2 = (bf16[2,1,256,1024]{3,2,1,0:T(8,128)(2,1)S(1)}, bf16[2,1,256,1024]{3,2,1,0:T(8,128)(2,1)}, u32[]{:S(2)}) copy-start(bf16[2,1,256,1024]{3,2,1,0:T(8,128)(2,1)} %param.28) | copy-start | bytes 3145732
  1843.5 83.3 %copy-start.146 = (f32[1024]{0:T(1024)S(1)}, f32[1024]{0:T(1024)}, u32[]{:S(2)}) copy-start(f32[1024]{0:T(1024)} %copy-done.145) | copy-start | bytes 12292
  1843.5 83.3 %copy-start.216 = (f32[256]{0:T(256)S(1)}, f32[256]{0:T(256)}, u32[]{:S(2)}) copy-start(f32[256]{0:T(256)} %copy-done.215) | copy-start | bytes 3076
  1845.6 125.7 %copy-start.25 = (bf16[256,1024]{1,0:T(8,128)(2,1)S(1)}, bf16[256,1024]{1,0:T(8,128)(2,1)}, u32[]{:S(2)}) copy-start(bf16[256,1024]{1,0:T(8,128)(2,1)} %reduce-scatter.13.cloned.1.call-done) | copy-start | bytes 1572868
  1845.6 125.7 %copy-start.126 = (f32[1024]{0:T(1024)S(1)}, f32[1024]{0:T(1024)}, u32[]{:S(2)}) copy-start(f32[1024]{0:T(1024)} %copy-done.125) | copy-start | bytes 12292
  1929.3 44.8 %copy-start.23 = (bf16[256,1024]{1,0:T(8,128)(2,1)S(1)}, bf16[256,1024]{1,0:T(8,128)(2,1)}, u32[]{:S(2)}) copy-start(bf16[256,1024]{1,0:T(8,128)(2,1)} %reduce-scatter.9.cloned.1.call-done) | copy-start | bytes 1572868
  1929.3 44.8 %copy-start.188 = (f32[256]{0:T(256)S(1)}, f32[256]{0:T(256)}, u32[]{:S(2)}) copy-start(f32[256]{0:T(256)} %copy-done.187) | copy-start | bytes 3076
  (218 other events, 597.5 us)
Sparse Core Ops, SparseCore 0:
  12.7 48.0 all-gather.14
  63.0 44.6 all-gather.10
  672.7 42.4 reduce-scatter.12
  785.9 42.3 reduce-scatter.8
  832.1 45.4 all-gather.16
  879.0 44.6 all-gather.24
  925.8 44.6 all-gather.12
  972.1 44.6 all-gather.22
  1019.1 42.4 reduce-scatter.20
  1064.3 43.1 reduce-scatter.16
  1110.4 43.1 reduce-scatter.14
  1157.4 45.4 all-gather.20
  1204.5 44.8 all-gather.18
  1729.6 105.4 all-reduce.82
  1837.4 44.0 reduce-scatter.22
  1883.6 43.1 reduce-scatter.18
  1929.0 43.3 reduce-scatter.10
where the time goes:
time: 2010 us; the launch traced here: 1990 us
  waiting for transfers between devices  557 us (28%)
  matrix products  552 us (27%)
  other arithmetic  500 us (25%)
  local copies, waits for them, and re-layouts  324 us (16%)
  blocking collectives  32.5 us (2%)
    another operation x6, other arithmetic, block_prepare(): lax.linalg.triangular_solve(system, jnp.concatenate([scaled_values, scale...  320 us
    dot_general x96, matrix products, block_step(): jnp.einsum('ghdf,ghfe->ghde', state, state_mix, precision=high)  186 us
    dot_general x96, matrix products, block_step(): jnp.einsum('ghie,ghde->ghid', query_eff, state, precision=high)  136 us
    dynamic_slice x160, local copies, waits for them, and re-layouts, delta_rule(): lax.scan(block_step, state, tuple((unflatten(p) for p in prepared)))  127 us
    all_gather x2, waiting for transfers between devices, shards(): lax.all_gather(normed1.astype(jnp.bfloat16), 'tensor', axis=0, tiled=True)  84.8 us
    reduce_scatter x2, waiting for transfers between devices, shards(): lax.psum_scatter((back_project(d_query, w_query) + back_project(d_key, w_...  80.1 us
    all_gather x2, waiting for transfers between devices, shards(): lax.all_gather(normed2.astype(jnp.bfloat16), 'tensor', axis=0, tiled=True)  76.1 us
    all_gather x2, waiting for transfers between devices, shards(): full_grad = lax.all_gather(out_grad, 'tensor', axis=0, tiled=True)  75 us
  transfers between devices with their start and end apart: 17, of which 14 were waited for; matrix products, arithmetic and copies ran while one was open for 23% of the time, Pallas kernels for 0%

commit v1 on v0

v1 whole, which is shorter than its diff:
```python
import functools

import jax
import jax.numpy as jnp
from jax import lax
from jax.experimental import pallas as pl
from jax.experimental.pallas import tpu as pltpu
from jax.sharding import PartitionSpec as P

HD = 128
HALO = 16
PIECES = 8
EPS = 1e-06
F32 = jnp.float32
BF16 = jnp.bfloat16
MIB = 1 << 20


def mm(a, b, ta=False, tb=False):
    dims = (((0 if ta else 1,), (1 if tb else 0,)), ((), ()))
    return lax.dot_general(a.astype(BF16), b.astype(BF16), dims, preferred_element_type=F32)


def invert_unit(low):
    size = low.shape[0]
    row = lax.broadcasted_iota(jnp.int32, (size, size), 0)
    col = lax.broadcasted_iota(jnp.int32, (size, size), 1)
    eye = (row == col).astype(F32)
    inv = eye - jnp.where((row >> 1) == (col >> 1), low, 0.0)
    step = 1
    while (2 << step) <= size:
        pair = ((row >> (step + 1)) == (col >> (step + 1))) & ((row >> step) != (col >> step))
        part = jnp.where(pair, low, 0.0)
        inv = inv - mm(mm(inv, part), inv)
        step += 1
    return inv


def short_conv(proj, taps, keeps):
    total = taps[0:1] * proj[HALO:]
    for i in range(1, 4):
        total = total + taps[i : i + 1] * (pltpu.roll(proj, i, 0)[HALO:] * keeps[i - 1])
    return total


def silu_unit(conv):
    sig = jax.nn.sigmoid(conv)
    act = conv * sig
    scale = lax.rsqrt(jnp.sum(act * act, axis=-1, keepdims=True) + EPS)
    return act * scale, scale, sig


def silu_unit_back(grad, conv, unit, scale, sig):
    d_act = scale * (grad - unit * jnp.sum(grad * unit, axis=-1, keepdims=True))
    return d_act * sig * (1.0 + conv * (1.0 - sig))


def masks(aux, seg_row):
    n = aux.shape[0]
    row = lax.broadcasted_iota(jnp.int32, (n, n), 0)
    col = lax.broadcasted_iota(jnp.int32, (n, n), 1)
    same = aux[:, 5:6] == seg_row
    strict = jnp.where(same & (row > col), 1.0, 0.0)
    within = jnp.where(same & (row >= col), 1.0, 0.0)
    return strict, within


def head_weights(ref):
    return ref[0]


def local_kernel(x_ref, w_ref, taps_ref, aux_ref, seg_ref, beta_ref,
                 proj_ref, qk_ref, t_ref, p_ref, ub_ref, w_out_ref, m_ref, a_ref):
    weights = w_ref[0]
    taps = taps_ref[0]
    micro = x_ref.shape[0]
    tokens = aux_ref.shape[1]
    half = tokens // 2
    for m in range(micro):
        aux = aux_ref[m]
        keeps = [aux[:, i : i + 1] for i in range(3)]
        live, last = aux[:, 3:4], aux[:, 4:5]
        strict, within = masks(aux, seg_ref[m, 0:1])
        proj = jnp.dot(x_ref[m], weights, preferred_element_type=F32)
        proj_ref[0, m] = proj
        convs = [
            short_conv(proj[:, j * HD : (j + 1) * HD], taps[4 * j : 4 * j + 4], keeps)
            for j in range(3)
        ]
        query = silu_unit(convs[0])[0]
        key = silu_unit(convs[1])[0]
        value = convs[2] * jax.nn.sigmoid(convs[2])
        beta = beta_ref[0, m]
        low = beta * mm(key, key, tb=True) * strict
        scores = mm(query, key, tb=True) * within
        top = invert_unit(low[:half, :half])
        bottom = invert_unit(low[half:, half:])
        cross = -mm(mm(bottom, low[half:, :half]), top)
        inv = jnp.concatenate(
            [
                jnp.concatenate([top, jnp.zeros_like(top)], axis=1),
                jnp.concatenate([cross, bottom], axis=1),
            ],
            axis=0,
        ).astype(BF16)
        both = mm(inv, jnp.concatenate([beta * value, (beta * live) * key], axis=1))
        late = (last * key).astype(BF16)
        sums = mm(both, late, ta=True)
        row = lax.broadcasted_iota(jnp.int32, (HD, HD), 0)
        col = lax.broadcasted_iota(jnp.int32, (HD, HD), 1)
        keep_state = jnp.where(row == col, live[tokens - 1 : tokens], 0.0)
        qk_ref[0, m] = jnp.concatenate([query, key], axis=1).astype(BF16)
        t_ref[0, m] = inv
        p_ref[0, m] = scores.astype(BF16)
        ub_ref[0, m] = both[:, :HD]
        w_out_ref[0, m] = both[:, HD:].astype(BF16)
        a_ref[0, m] = sums[:HD]
        m_ref[0, m] = keep_state - sums[HD:]


def output_kernel(qk_ref, p_ref, ub_ref, w_ref, state_ref, aux_ref, mixed_ref, u_ref):
    for m in range(aux_ref.shape[0]):
        live = aux_ref[m][:, 3:4]
        state = state_ref[0, m].astype(BF16)
        update = ub_ref[0, m] - mm(w_ref[0, m], state, tb=True)
        update = update.astype(BF16)
        mixed = live * mm(qk_ref[0, m][:, :HD], state, tb=True) + mm(p_ref[0, m], update)
        mixed_ref[m] = mixed.astype(BF16)
        u_ref[0, m] = update


def back_local_kernel(dmix_ref, qk_ref, t_ref, p_ref, beta_ref, aux_ref, y_ref, b_ref):
    for m in range(aux_ref.shape[0]):
        live = aux_ref[m][:, 3:4]
        d_out = dmix_ref[m]
        y0 = mm(t_ref[0, m], mm(p_ref[0, m], d_out, ta=True), ta=True)
        y_ref[0, m] = y0
        qk = qk_ref[0, m]
        b_ref[0, m] = mm(live * d_out, qk[:, :HD], ta=True) - mm(
            (beta_ref[0, m] * live) * y0, qk[:, HD:], ta=True
        )


def back_kernel(dmix_ref, y_ref, qk_ref, t_ref, u_ref, state_ref, dstate_ref, proj_ref,
                p_ref, taps_ref, beta_ref, aux_ref, seg_ref,
                dmain_ref, tail_ref, front_ref, dbeta_ref, dtaps_ref):
    taps = taps_ref[0]
    micro, tokens = aux_ref.shape[0], aux_ref.shape[1]
    for m in range(micro):
        aux = aux_ref[m]
        keeps = [aux[:, i : i + 1] for i in range(3)]
        live, last = aux[:, 3:4], aux[:, 4:5]
        strict, within = masks(aux, seg_ref[m, 0:1])
        proj = proj_ref[0, m]
        beta = beta_ref[0, m]
        convs = [
            short_conv(proj[:, j * HD : (j + 1) * HD], taps[4 * j : 4 * j + 4], keeps)
            for j in range(3)
        ]
        query, q_scale, q_sig = silu_unit(convs[0])
        key, k_scale, k_sig = silu_unit(convs[1])
        v_sig = jax.nn.sigmoid(convs[2])
        value = convs[2] * v_sig
        q_low, k_low = qk_ref[0, m][:, :HD], qk_ref[0, m][:, HD:]
        state = state_ref[0, m].astype(BF16)
        dstate = dstate_ref[0, m].astype(BF16)
        update = u_ref[0, m]
        d_out = dmix_ref[m].astype(BF16)
        d_right = y_ref[0, m] + mm(t_ref[0, m], last * mm(k_low, dstate, tb=True), ta=True)
        d_right_low = d_right.astype(BF16)
        d_scores = (mm(d_out, update, tb=True) * within).astype(BF16)
        grad_sys = -mm(d_right_low, update, tb=True) * strict
        keys_keys = mm(k_low, k_low, tb=True)
        d_kk = (beta * grad_sys).astype(BF16)
        carried = mm(k_low, state, tb=True)
        d_carried = ((-beta * live) * d_right).astype(BF16)
        d_query = live * mm(d_out, state) + mm(d_scores, k_low)
        d_key = (
            mm(d_scores, q_low, ta=True)
            + last * mm(update, dstate)
            + mm(d_carried, state)
            + mm(d_kk, k_low)
            + mm(d_kk, k_low, ta=True)
        )
        d_beta = jnp.sum(grad_sys * keys_keys, axis=-1, keepdims=True) + jnp.sum(
            d_right * (value - live * carried), axis=-1, keepdims=True
        )
        d_value = beta * d_right
        dbeta_ref[0, m] = d_beta * beta * (1.0 - beta)
        d_convs = [
            silu_unit_back(d_query, convs[0], query, q_scale, q_sig),
            silu_unit_back(d_key, convs[1], key, k_scale, k_sig),
            d_value * v_sig * (1.0 + convs[2] * (1.0 - v_sig)),
        ]
        tap_sums = []
        for j in range(3):
            part = proj[:, j * HD : (j + 1) * HD]
            d_conv = d_convs[j]
            tap_sums.append(jnp.sum(d_conv * part[HALO:], axis=0, keepdims=True))
            zeros = jnp.zeros((HALO, HD), F32)
            d_proj = jnp.concatenate([zeros, taps[4 * j : 4 * j + 1] * d_conv], axis=0)
            for i in range(1, 4):
                kept = keeps[i - 1] * d_conv
                tap_sums.append(
                    jnp.sum(kept * pltpu.roll(part, i, 0)[HALO:], axis=0, keepdims=True)
                )
                spread = jnp.concatenate([zeros, taps[4 * j + i : 4 * j + i + 1] * kept], axis=0)
                d_proj = d_proj + pltpu.roll(spread, HALO + tokens - i, 0)
            cols = slice(j * HD, (j + 1) * HD)
            front_ref[0, m, :, cols] = d_proj[:HALO]
            tail_ref[0, m, :, cols] = d_proj[tokens:]
            dmain_ref[m, :, cols] = d_proj[HALO:].astype(BF16)
        summed = jnp.concatenate(tap_sums + [jnp.zeros((4, HD), F32)], axis=0)
        if m == 0:
            dtaps_ref[0] = summed
        else:
            dtaps_ref[0] += summed


def grad_kernel(table_ref, left_ref, right_ref, out_ref):
    rows = out_ref.shape[2]
    blocks = []
    for pos in range(out_ref.shape[0]):
        start = pl.multiple_of(table_ref[pos] * rows, rows)
        blocks.append(left_ref[pl.ds(start, rows), :])
    sums = jnp.dot(
        jnp.concatenate(blocks, axis=0), right_ref[0], preferred_element_type=F32
    ).astype(BF16)
    for pos in range(out_ref.shape[0]):
        out_ref[pos, 0] = sums[pos * rows : (pos + 1) * rows]


def place_kernel(ids_ref, *refs):
    sems, out_ref = refs[-1], refs[-2]
    own, pieces = (refs[0], refs[1:-2]) if len(refs) == PIECES + 3 else (None, refs[:-2])
    copies = []
    if own is not None:
        copies.append(pltpu.make_async_copy(own, out_ref.at[0], sems.at[PIECES]))
    for j, piece in enumerate(pieces):
        slots = piece.shape[0]
        target = out_ref.at[pl.ds(out_ref.shape[0] - slots, slots), ids_ref[j]]
        copies.append(pltpu.make_async_copy(piece, target, sems.at[j]))
    for copy in copies:
        copy.start()
    for copy in copies:
        copy.wait()


def params(mib=56):
    return pltpu.CompilerParams(
        dimension_semantics=("arbitrary",), vmem_limit_bytes=mib * MIB
    )


def cost(flops, nbytes):
    return pl.CostEstimate(flops=int(flops), bytes_accessed=int(nbytes), transcendentals=0)


def whole(shape):
    return pl.BlockSpec(shape, lambda h: (0,) * len(shape))


def per_head(*dims):
    return pl.BlockSpec((1,) + dims, lambda h: (h,) + (0,) * len(dims))


def sds(shape, dtype):
    return jax.ShapeDtypeStruct(shape, dtype)


def mixer_local(x_ext, w_heads, taps, aux, seg_row, beta):
    micro, ext, width = x_ext.shape
    tokens = ext - HALO
    heads = taps.shape[0]
    per = heads // w_heads.shape[0]
    hm = (heads, micro)
    outs = [
        sds(hm + (ext, 3 * HD), F32),
        sds(hm + (tokens, 2 * HD), BF16),
        sds(hm + (tokens, tokens), BF16),
        sds(hm + (tokens, tokens), BF16),
        sds(hm + (tokens, HD), F32),
        sds(hm + (tokens, HD), BF16),
        sds(hm + (HD, HD), F32),
        sds(hm + (HD, HD), F32),
    ]
    return pl.pallas_call(
        local_kernel,
        grid=(heads,),
        in_specs=[
            whole(x_ext.shape),
            pl.BlockSpec((1, width, 3 * HD), lambda h: (h // per, 0, h % per)),
            per_head(16, HD),
            whole(aux.shape),
            whole(seg_row.shape),
            per_head(micro, tokens, 1),
        ],
        out_specs=[per_head(*o.shape[1:]) for o in outs],
        out_shape=outs,
        compiler_params=params(),
        cost_estimate=cost(heads * micro * 1.5e9, heads * micro * 3e6),
        name="mixer_local",
    )(x_ext, w_heads, taps, aux, seg_row, beta)


def mixer_output(qk, scores, base, mix, state, aux):
    heads, micro, tokens = qk.shape[:3]
    return pl.pallas_call(
        output_kernel,
        grid=(heads,),
        in_specs=[per_head(*a.shape[1:]) for a in (qk, scores, base, mix, state)]
        + [whole(aux.shape)],
        out_specs=[
            pl.BlockSpec((micro, tokens, HD), lambda h: (0, 0, h)),
            per_head(micro, tokens, HD),
        ],
        out_shape=[
            sds((micro, tokens, heads * HD), BF16),
            sds((heads, micro, tokens, HD), BF16),
        ],
        compiler_params=params(),
        cost_estimate=cost(heads * micro * 2e8, heads * micro * 1e6),
        name="mixer_output",
    )(qk, scores, base, mix, state, aux)


def mixer_back_local(d_mixed, qk, inv, scores, beta, aux):
    heads, micro, tokens = qk.shape[:3]
    return pl.pallas_call(
        back_local_kernel,
        grid=(heads,),
        in_specs=[pl.BlockSpec((micro, tokens, HD), lambda h: (0, 0, h))]
        + [per_head(*a.shape[1:]) for a in (qk, inv, scores, beta)]
        + [whole(aux.shape)],
        out_specs=[per_head(micro, tokens, HD), per_head(micro, HD, HD)],
        out_shape=[
            sds((heads, micro, tokens, HD), F32),
            sds((heads, micro, HD, HD), F32),
        ],
        compiler_params=params(),
        cost_estimate=cost(heads * micro * 2e8, heads * micro * 1e6),
        name="mixer_back_local",
    )(d_mixed, qk, inv, scores, beta, aux)


def mixer_back(d_mixed, y0, qk, inv, update, state, d_state, proj, scores, taps, beta, aux, seg_row):
    heads, micro, tokens = qk.shape[:3]
    columns = lambda n: pl.BlockSpec((micro, tokens, n), lambda h: (0, 0, h))
    return pl.pallas_call(
        back_kernel,
        grid=(heads,),
        in_specs=[columns(HD)]
        + [
            per_head(*a.shape[1:])
            for a in (y0, qk, inv, update, state, d_state, proj, scores, taps, beta)
        ]
        + [whole(aux.shape), whole(seg_row.shape)],
        out_specs=[
            columns(3 * HD),
            per_head(micro, HALO, 3 * HD),
            per_head(micro, HALO, 3 * HD),
            per_head(micro, tokens, 1),
            per_head(16, HD),
        ],
        out_shape=[
            sds((micro, tokens, heads * 3 * HD), BF16),
            sds((heads, micro, HALO, 3 * HD), F32),
            sds((heads, micro, HALO, 3 * HD), F32),
            sds((heads, micro, tokens, 1), F32),
            sds((heads, 16, HD), F32),
        ],
        compiler_params=params(),
        cost_estimate=cost(heads * micro * 1e9, heads * micro * 3e6),
        name="mixer_back",
    )(d_mixed, y0, qk, inv, update, state, d_state, proj, scores, taps, beta, aux, seg_row)


def grad_pieces(left, right, table):
    slots, tokens, n = right.shape
    count = table.shape[0]
    rows = left.shape[0] // PIECES
    return pl.pallas_call(
        grad_kernel,
        grid_spec=pltpu.PrefetchScalarGridSpec(
            num_scalar_prefetch=1,
            grid=(slots,),
            in_specs=[
                pl.BlockSpec(left.shape, lambda s, t: (0, 0)),
                pl.BlockSpec((1, tokens, n), lambda s, t: (s, 0, 0)),
            ],
            out_specs=pl.BlockSpec((count, 1, rows, n), lambda s, t: (0, s, 0, 0)),
        ),
        out_shape=sds((count, slots, rows, n), BF16),
        compiler_params=params(),
        cost_estimate=cost(2 * count * rows * tokens * n * slots, 2 * count * slots * rows * n),
        name="grad_pieces",
    )(table, left, right)


def place(pieces, ids, own=None):
    slots, rows, n = pieces[0].shape
    anywhere = pl.BlockSpec(memory_space=pl.ANY)
    args = ([] if own is None else [own.reshape(PIECES, rows, n)]) + list(pieces)
    shape = (slots + (own is not None), PIECES, rows, n)
    return pl.pallas_call(
        place_kernel,
        grid_spec=pltpu.PrefetchScalarGridSpec(
            num_scalar_prefetch=1,
            grid=(1,),
            in_specs=[anywhere] * len(args),
            out_specs=pl.BlockSpec(shape, lambda i, t: (0, 0, 0, 0)),
            scratch_shapes=[pltpu.SemaphoreType.DMA((PIECES + 1,))],
        ),
        out_shape=sds(shape, pieces[0].dtype),
        compiler_params=params(),
        cost_estimate=cost(0, 4 * shape[0] * PIECES * rows * n),
        name="place",
    )(jnp.stack(ids), *args)


def swap(x, mask_of, size):
    return lax.ppermute(x, "dp", [(i, i ^ mask_of(i)) for i in range(size)])


def first(i):
    return 4 if i & 1 else 2


def second(i):
    return 2 if i & 1 else 4


def across(i):
    return 1


def from_ahead(x, k, size):
    return lax.ppermute(x, "tensor", [(i, (i - k) % size) for i in range(size)])


def to_ahead(x, k, size):
    return lax.ppermute(x, "tensor", [(i, (i + k) % size) for i in range(size)])


def plane_gather(own, dp):
    b = swap(own, first, dp)
    c = swap(own, second, dp)
    d = swap(b, second, dp)
    near = [own, b, c, d]
    return near + [swap(piece, across, dp) for piece in near]


def piece_ids(own):
    core = own & 1
    f = jnp.where(core == 1, 4, 2)
    s = jnp.where(core == 1, 2, 4)
    return [own, own ^ f, own ^ s, own ^ 6, own ^ 1, own ^ 1 ^ s, own ^ 1 ^ f, own ^ 7]


def gather_quarters(quarter, dp, tensor, own):
    rows = quarter.shape[0] // PIECES
    n = quarter.shape[1]
    mine = lax.dynamic_slice_in_dim(quarter, own * rows, rows, 0)
    others = jnp.stack([from_ahead(mine, k, tensor) for k in range(1, tensor)])
    full = place(plane_gather(others, dp), piece_ids(own), quarter)
    return full.reshape(tensor, PIECES * rows, n)


def add(a, b):
    return (a.astype(F32) + b.astype(F32)).astype(BF16)


def reduce_quarters(left, right, dp, tensor, own):
    ids = piece_ids(own)
    theirs = grad_pieces(left, right, jnp.stack([ids[4], ids[6], ids[5], ids[7]]))
    got = swap(theirs, across, dp)
    mine = grad_pieces(left, right, jnp.stack([ids[0], ids[2], ids[1], ids[3]]))
    total = add(mine, got)
    total = add(total[:2], swap(total[2:], first, dp))
    total = add(total[0], swap(total[1], second, dp))
    parts = [total[0]] + [to_ahead(total[k], k, tensor) for k in range(1, tensor)]
    total = sum(p.astype(F32) for p in parts).astype(BF16)
    mask = PIECES
    while mask < dp:
        total = add(total, swap(total, lambda i: mask, dp))
        mask *= 2
    rows, n = total.shape
    full = place([piece[None] for piece in plane_gather(total, dp)], ids)
    return full.reshape(PIECES * rows, n).astype(F32)


def norm_rows(rows, gain):
    rstd = lax.rsqrt(jnp.mean(rows * rows, axis=-1, keepdims=True) + EPS)
    unit = rows * rstd
    return (unit * gain, unit, rstd)


def norm_back(grad, unit, rstd, gain):
    scaled = grad * gain
    d_rows = rstd * (scaled - unit * jnp.mean(scaled * unit, axis=-1, keepdims=True))
    return (d_rows, jnp.sum(grad * unit, axis=0))


def shards(dp, tensor, layer_input, segment, d_out, norm1_gain, w_query, w_key, w_value, w_beta,
           conv_weight, w_out, norm2_gain, w_gate, w_up, w_down):
    micro, _, tokens, width = layer_input.shape
    count = micro * tokens
    local_heads = w_query.shape[1] // HD
    heads = local_heads * tensor
    hidden_part = w_gate.shape[1]
    index = lax.axis_index("dp")
    own = index % PIECES
    place = lax.axis_index("tensor")
    gain1 = norm1_gain.astype(F32)
    gain2 = norm2_gain.astype(F32)

    rows = layer_input.reshape(count, width).astype(F32)
    normed1, unit1, rstd1 = norm_rows(rows, gain1)
    normed1 = normed1.astype(BF16)
    mixer_in = normed1.reshape(micro, tokens, width)
    ahead = [(i, i + 1) for i in range(tensor - 1)]
    behind = [(i + 1, i) for i in range(tensor - 1)]
    halo = lax.ppermute(mixer_in[:, tokens - HALO :], "tensor", ahead)
    x_ext = jnp.concatenate([halo, mixer_in], axis=1)

    heads_of = lambda w: w.reshape(width, local_heads, HD)
    w_qkv = jnp.concatenate([heads_of(w_query), heads_of(w_key), heads_of(w_value)], axis=2)
    w_qkv = w_qkv.reshape(width, local_heads * 3 * HD)
    small = jnp.concatenate([w_beta.T, conv_weight.reshape(-1, width)], axis=0)
    smalls = jnp.stack([small] + [from_ahead(small, k, tensor) for k in range(1, tensor)])
    mixer_w = gather_quarters(jnp.concatenate([w_qkv, w_out.T], axis=1), dp, tensor, own)
    ffn_w = gather_quarters(jnp.concatenate([w_gate, w_up, w_down.T], axis=1), dp, tensor, own)
    w_beta_all = smalls[:, :local_heads].reshape(heads, width)
    taps = smalls[:, local_heads:].reshape(tensor, 12, local_heads, HD).astype(F32)
    taps = jnp.swapaxes(taps, 1, 2).reshape(heads, 12, HD)
    taps = jnp.pad(taps, ((0, 0), (0, 4), (0, 0)))

    seg = jnp.pad(segment[:, 0], ((0, 0), (HALO, 0)), constant_values=-1)
    seg = lax.dynamic_slice_in_dim(seg, place * tokens, HALO + tokens, 1)
    seg_own = seg[:, HALO:]
    flags = [seg[:, HALO - i : HALO - i + tokens] == seg_own for i in (1, 2, 3)]
    flags += [seg_own == seg[:, HALO - 1 : HALO], seg_own == seg_own[:, -1:]]
    flags = [f.astype(F32) for f in flags] + [seg_own.astype(F32)]
    aux = jnp.stack(flags + [jnp.zeros_like(flags[0])] * 2, axis=-1)
    seg_row = jnp.broadcast_to(seg_own.astype(F32)[:, None], (micro, 8, tokens))

    b_proj = jnp.dot(normed1, w_beta_all.T, preferred_element_type=F32)
    beta = jax.nn.sigmoid(b_proj).reshape(micro, tokens, heads)
    beta = jnp.transpose(beta, (2, 0, 1))[..., None]
    proj, qk, inv, scores, base, mix, keep, gain = mixer_local(
        x_ext, mixer_w, taps, aux, seg_row, beta
    )
    exact = functools.partial(jnp.einsum, precision=lax.Precision.HIGHEST)
    out_state = gain
    for hop in range(tensor - 1):
        state = lax.ppermute(out_state.astype(BF16), "tensor", ahead).astype(F32)
        state = jnp.roll(state, -local_heads, axis=0)
        if hop < tensor - 2:
            out_state = exact("hmdf,hmfe->hmde", state, keep) + gain
    mixed, update = mixer_output(qk, scores, base, mix, state, aux)
    mixed = mixed.reshape(count, heads * HD)
    mixed_s = mixed.reshape(count, tensor, local_heads * HD)
    w_out_all = mixer_w[:, :, local_heads * 3 * HD :]
    attn = jnp.einsum("tsc,sdc->td", mixed_s, w_out_all, preferred_element_type=F32)
    mid = rows + attn

    normed2, unit2, rstd2 = norm_rows(mid, gain2)
    normed2 = normed2.astype(BF16)
    out_grad = d_out.reshape(count, width)
    w_gu = ffn_w[:, :, : 2 * hidden_part]
    w_dn = ffn_w[:, :, 2 * hidden_part :]
    gate_up = jnp.einsum("td,sdf->stf", normed2, w_gu, preferred_element_type=F32)
    gate, up_part = gate_up[:, :, :hidden_part], gate_up[:, :, hidden_part:]
    sigma = jax.nn.sigmoid(gate)
    hidden = (gate * sigma * up_part).astype(BF16)
    result = mid + jnp.einsum("stf,sdf->td", hidden, w_dn, preferred_element_type=F32)
    output = result.astype(BF16).reshape(micro, 1, tokens, width)
    d_hidden = jnp.einsum("td,sdf->stf", out_grad, w_dn, preferred_element_type=F32)
    d_gate = (d_hidden * up_part * sigma * (1.0 + gate * (1.0 - sigma))).astype(BF16)
    d_up = (d_hidden * gate * sigma).astype(BF16)
    d_gu = jnp.concatenate([d_gate, d_up], axis=2)
    d_normed2 = jnp.einsum("stf,sdf->td", d_gu, w_gu, preferred_element_type=F32)
    reduce = functools.partial(reduce_quarters, dp=dp, tensor=tensor, own=own)
    grad_dn = reduce(out_grad.T, hidden)
    grad_gu = reduce(normed2.T, d_gu)
    d_mid, gain2_part = norm_back(d_normed2, unit2, rstd2, gain2)
    d_mid = out_grad.astype(F32) + d_mid
    d_mid_low = d_mid.astype(BF16)

    grad_out = reduce(d_mid_low.T, jnp.swapaxes(mixed_s, 0, 1))
    d_mixed = jnp.einsum("td,sdc->tsc", d_mid_low, w_out_all, preferred_element_type=F32)
    d_mixed = d_mixed.reshape(micro, tokens, heads * HD)
    y0, back_gain = mixer_back_local(d_mixed, qk, inv, scores, beta, aux)
    out_state = back_gain
    for hop in range(tensor - 1):
        d_state = lax.ppermute(out_state.astype(BF16), "tensor", behind).astype(F32)
        d_state = jnp.roll(d_state, local_heads, axis=0)
        if hop < tensor - 2:
            out_state = exact("hmde,hmfe->hmdf", d_state, keep) + back_gain
    d_qkv, tail, front, d_beta, d_taps = mixer_back(
        d_mixed, y0, qk, inv, update, state, d_state, proj, scores, taps, beta, aux, seg_row
    )
    front = jnp.roll(lax.ppermute(front, "tensor", behind), local_heads, axis=0)
    tail = jnp.transpose(tail + front, (1, 2, 0, 3)).reshape(micro, HALO, -1).astype(BF16)
    d_qkv = lax.dynamic_update_slice(d_qkv, tail, (0, tokens - HALO, 0))
    d_qkv = d_qkv.reshape(count, tensor, local_heads * 3 * HD)
    d_b = jnp.transpose(d_beta[..., 0], (1, 2, 0)).reshape(count, heads).astype(BF16)
    grad_qkv = reduce(normed1.T, jnp.swapaxes(d_qkv, 0, 1))
    w_qkv_all = mixer_w[:, :, : local_heads * 3 * HD]
    d_normed1 = jnp.einsum("tsc,sdc->td", d_qkv, w_qkv_all, preferred_element_type=F32)
    d_normed1 = d_normed1 + jnp.dot(d_b, w_beta_all, preferred_element_type=F32)
    d_in, gain1_part = norm_back(d_normed1, unit1, rstd1, gain1)
    input_grad = (d_mid + d_in).astype(BF16).reshape(micro, 1, tokens, width)

    grad_b = jnp.einsum("th,td->hd", d_b, normed1, preferred_element_type=F32)
    part = width // tensor
    d_taps = d_taps[:, :12].reshape(tensor, local_heads, 12, HD)
    d_taps = jnp.swapaxes(d_taps, 1, 2).reshape(tensor, -1)
    packed = []
    for k in range(tensor):
        at = ((place + k) % tensor) * part
        packed.append(
            jnp.concatenate(
                [
                    grad_b[k * local_heads : (k + 1) * local_heads].reshape(-1),
                    d_taps[k],
                    lax.dynamic_slice_in_dim(gain1_part, at, part),
                    lax.dynamic_slice_in_dim(gain2_part, at, part),
                ]
            )
        )
    packed = [packed[0]] + [to_ahead(packed[k], k, tensor) for k in range(1, tensor)]
    packed = sum(packed)
    mask = 1
    while mask < dp:
        packed = packed + swap(packed, lambda i: mask, dp)
        mask *= 2
    cut = local_heads * width
    grad_beta = packed[:cut].reshape(local_heads, width).T
    grad_conv = packed[cut : cut + 12 * part].reshape(3, 4, part)
    cut += 12 * part
    grad_gain1 = packed[cut : cut + part]
    grad_gain2 = packed[cut + part : cut + 2 * part]
    grad_qkv = grad_qkv.reshape(width, local_heads, 3, HD)
    grad_q, grad_k, grad_v = (grad_qkv[:, :, j].reshape(width, -1) for j in range(3))
    return (
        output,
        input_grad,
        grad_gain1,
        grad_q,
        grad_k,
        grad_v,
        grad_beta,
        grad_conv,
        grad_out.T,
        grad_gain2,
        grad_gu[:, :hidden_part],
        grad_gu[:, hidden_part:],
        grad_dn.T,
    )


def solution(mesh):
    in_specs = (
        P(None, "dp", "tensor", None),
        P(None, "dp", None),
        P(None, "dp", "tensor", None),
        P(),
        P(None, "tensor"),
        P(None, "tensor"),
        P(None, "tensor"),
        P(None, "tensor"),
        P(None, None, "tensor"),
        P("tensor", None),
        P(),
        P(None, "tensor"),
        P(None, "tensor"),
        P("tensor", None),
    )
    out_specs = (
        P(None, "dp", "tensor", None),
        P(None, "dp", "tensor", None),
        P("tensor"),
        P(None, "tensor"),
        P(None, "tensor"),
        P(None, "tensor"),
        P(None, "tensor"),
        P(None, None, "tensor"),
        P("tensor", None),
        P("tensor"),
        P(None, "tensor"),
        P(None, "tensor"),
        P("tensor", None),
    )
    body = functools.partial(shards, mesh.shape["dp"], mesh.shape["tensor"])
    return jax.shard_map(body, mesh=mesh, in_specs=in_specs, out_specs=out_specs, check_vma=False)
```

time: 2010 us -> 732 us (0.36)
  matrix products: 552 us -> 63.8 us
  waiting for transfers between devices: 557 us -> 105 us
  other arithmetic: 500 us -> 65.3 us
  Pallas kernels: 0 us -> 202 us
  local copies, waits for them, and re-layouts: 324 us -> 157 us
  starting transfers between devices: 0.87 us -> 125 us
  blocking collectives: 32.5 us -> 0 us
    dot_general x278 -> x14, matrix products: 537 us -> 63.8 us  [the longest x1 11.1 us: shards(): jnp.einsum('stf,sdf->td', d_gu, w_gu, preferred_element_type=F32)]
    another operation x8, other arithmetic: 325 us -> 5 us  [the longest x2 2.41 us: gather_quarters(): others = jnp.stack([from_ahead(mine, k, tensor) for k in range(1, tensor)])]
    all_gather x8 -> x0, waiting for transfers between devices: 244 us -> none  [the longest x2 84.8 us: shards(): lax.all_gather(normed1.astype(jnp.bfloat16), 'tensor', axis=0, tiled=True)]
    reduce_scatter x8 -> x0, waiting for transfers between devices: 239 us -> none  [the longest x2 80.1 us: shards(): lax.psum_scatter((back_project(d_query, w_query) + back_project(d_key, w_...]
    pallas_call x0 -> x18, Pallas kernels: none -> 202 us  [the longest x1 66.1 us: mixer_local(): pl.pallas_call(local_kernel, grid=(heads,), in_specs=[whole(x_ext.shape),...]
    ppermute x0 -> x89, starting transfers between devices: none -> 125 us  [the longest x57 54.1 us: swap(): return lax.ppermute(x, 'dp', [(i, i ^ mask_of(i)) for i in range(size)])]
    dynamic_slice x160 -> x3, local copies, waits for them, and re-layouts: 127 us -> 2.27 us  [the longest x1 0.94 us: gather_quarters(): mine = lax.dynamic_slice_in_dim(quarter, own * rows, rows, 0)]
    ppermute x0 -> x89, waiting for transfers between devices: none -> 105 us  [the longest x15 43.9 us: to_ahead(): return lax.ppermute(x, 'tensor', [(i, (i + k) % size) for i in range(size)])]
  transfers between devices with their start and end apart: 17 -> 89, of which waited for: 14 -> 23; matrix products, arithmetic and copies ran while one was open for 23% -> 29% of each run, Pallas kernels for 0% -> 24%
where the time goes in v1:
time: 732 us; the launch traced here: 721 us
  Pallas kernels  202 us (28%)
  local copies, waits for them, and re-layouts  157 us (21%)
  starting transfers between devices  125 us (17%)
  waiting for transfers between devices  105 us (14%)
  other arithmetic  65.3 us (9%)
  matrix products  63.8 us (9%)
    pallas_call x1, Pallas kernels, mixer_local(): pl.pallas_call(local_kernel, grid=(heads,), in_specs=[whole(x_ext.shape),...  66.1 us
    ppermute x57, starting transfers between devices, swap(): return lax.ppermute(x, 'dp', [(i, i ^ mask_of(i)) for i in range(size)])  54.1 us
    pallas_call x8, Pallas kernels, grad_pieces(): pl.pallas_call(grad_kernel, grid_spec=pltpu.PrefetchScalarGridSpec(num_sc...  52.4 us
    ppermute x15, waiting for transfers between devices, to_ahead(): return lax.ppermute(x, 'tensor', [(i, (i + k) % size) for i in range(size)])  43.9 us
    ppermute x57, waiting for transfers between devices, swap(): return lax.ppermute(x, 'dp', [(i, i ^ mask_of(i)) for i in range(size)])  34.3 us
    pallas_call x6, Pallas kernels, place(): pl.pallas_call(place_kernel, grid_spec=pltpu.PrefetchScalarGridSpec(num_s...  33.8 us
    ppermute x10, local copies, waits for them, and re-layouts, swap(): return lax.ppermute(x, 'dp', [(i, i ^ mask_of(i)) for i in range(size)])  32.3 us
    ppermute x9, starting transfers between devices, from_ahead(): return lax.ppermute(x, 'tensor', [(i, (i - k) % size) for i in range(size)])  32.2 us
  transfers between devices with their start and end apart: 89, of which 23 were waited for; matrix products, arithmetic and copies ran while one was open for 29% of the time, Pallas kernels for 24%

profile of v1, /device:TPU:1, one launch (start us, length us, event | category | flops | bytes accessed | tf_op | source)
XLA Modules:
  0.0 721.4 jit_solution(2396151416464223844)
XLA Ops:
  20.2 3.1 collective-permute-start.19
  23.3 8.2 %collective-permute-done.2 = bf16[128,1024]{1,0:T(8,128)(2,1)S(1)} collective-permute-done((bf16[128,1024]{1,0:T(8,128)(2,1)S(1)}, bf16[128,1024]{1,0:T(8,128)(2,1)S(1)}, u32[]{:S(2)}, u32[]{:S(2)}) %collective-permute-start.2) | collective-permute-done | bytes 262176 | tf_op jit(solution)/shard_map/ppermute | solution.py:438
  38.3 7.9 %collective-permute-done.4.refs_2_ = bf16[3,128,1024]{2,1,0:T(8,128)(2,1)} collective-permute-done((bf16[3,128,1024]{2,1,0:T(8,128)(2,1)}, bf16[3,128,1024]{2,1,0:T(8,128)(2,1)}, u32[]{:S(2)}, u32[]{:S(2)}) %collective-permute-start.4) | collective-permute-done | bytes 786464 | tf_op jit(solution)/shard_map/ppermute | solution.py:422
  49.7 16.1 %collective-permute-start.18 = (bf16[128,2112]{0,1:T(8,128)(2,1)}, bf16[128,2112]{0,1:T(8,128)(2,1)}, u32[]{:S(2)}, u32[]{:S(2)}) collective-permute-start(bf16[128,2112]{0,1:T(8,128)(2,1)} %constant_dynamic-slice_fusion.4), channel_id=1, source_target_pairs={{0,2},{1,3},{2,0},{3,1},{4,6},{5,7},{6,4},{7,5},{8,10},{9,11},{10,... | collective-permute-start | bytes 1622024 | tf_op jit(solution)/shard_map/ppermute | solution.py:438
  66.5 4.9 concatenate.63
  85.0 4.5 collective-permute-start
  90.8 3.7 collective-permute-start.17
  112.1 7.4 %place.6 = bf16[4,8,128,1024]{3,2,1,0:T(8,128)(2,1)} custom-call(s32[8]{0:T(128)} %stack.87.ids_ref, bf16[8,128,1024]{2,1,0:T(8,128)(2,1)} %pad_maximum_fusion.2.refs_0_, bf16[3,128,1024]{2,1,0:T(8,128)(2,1)} %pad_maximum_fusion.7.refs_1_, bf16[3,128,1024]{2,1,0:T(8,128)(2,1)} %collective-permute-done.4.refs_2_, ...), custom_call_target="tpu_custom_call" | custom-call | bytes 16777216 | tf_op jit(solution)/shard_map/place/pallas_call | solution.py:405
  120.1 66.1 %mixer_local.1 = (f32[8,2,272,384]{3,2,1,0:T(8,128)}, bf16[8,2,256,256]{3,2,1,0:T(8,128)(2,1)}, bf16[8,2,256,256]{3,2,1,0:T(8,128)(2,1)}, bf16[8,2,256,256]{3,2,...) custom-call(bf16[2,272,1024]{2,1,0:T(8,128)(2,1)} %pad_maximum_fusio, ...), custom_call_target="tpu_custom_call" | custom-call | flops 24000000000 | bytes 48000000 | tf_op jit(solution)/shard_map/mixer_local/pallas_call | solution.py:287
  187.7 3.3 collective-permute-start.14
  194.4 5.5 collective-permute-done.14
  202.0 5.1 collective-permute-start.15
  207.1 6.4 copy.440
  218.8 5.8 collective-permute-start.16
  224.6 3.6 collective-permute-start.26
  236.1 3.8 copy.447.refs_2_
  239.9 3.7 copy.448.refs_3_
  243.7 3.8 copy.450.refs_5_
  247.4 3.8 copy.449.refs_4_
  251.2 3.8 copy.451.refs_6_
  255.0 3.8 copy.452.refs_7_
  261.8 8.5 %mixer_output.1 = (bf16[2,256,1024]{2,1,0:T(8,128)(2,1)}, bf16[8,2,256,128]{3,2,1,0:T(8,128)(2,1)}) custom-call(bf16[8,2,256,256]{3,2,1,0:T(8,128)(2,1)} %get-tuple-element.30.qk_ref, bf16[8,2,256,256]{3,2,1,0:T(8,128)(2,1)} %get-tuple-element.31.p_ref, f32[8,2,256,128]{3,2,1,0:T(8,128)} %get-tuple-element.32.ub_ref, ...), custom_call_target="tpu_custom_call" | custom-call | flops 3200000000 | bytes 16000000 | tf_op jit(solution)/shard_map/mixer_output/pallas_call | solution.py:308
  275.3 4.2 multiply_reduce_fusion.3
  279.5 3.8 copy.453.refs_8_
  283.3 13.1 %place.7 = bf16[4,8,128,2112]{3,2,1,0:T(8,128)(2,1)} custom-call(s32[8]{0:T(128)} %stack.87.ids_ref, bf16[8,128,2112]{2,1,0:T(8,128)(2,1)} %bitcast.306, bf16[3,128,2112]{2,1,0:T(8,128)(2,1)} %copy-done.8, bf16[3,128,2112]{2,1,0:T(8,128)(2,1)} %copy.447.refs_2_, bf16[3,128,2112]{2,1,0:T(8,128)(2,1)} %copy.448.refs_3_, bf16[3,128,2112]{2,1,0:T(8,128)(2,1)} %copy.449.refs_4_, ...), custom_call_target="tpu_custom_call" | custom-call | bytes 34603008 | tf_op jit(solution)/shard_map/place/pallas_call | solution.py:405
  296.4 9.9 %fusion.4 = f32[4,512,1408]{2,1,0:T(8,128)S(1)} fusion(bf16[4,1024,2112]{2,1,0:T(8,128)(2,1)} %bitcast.307, f32[512,1024]{0,1:T(8,128)S(1)} %copy-done.19, f32[1024]{0:T(1024)S(1)} %convert_element_type.362, f32[512]{0:T(512)S(1)} %add_rsqrt_fusion), kind=kOutput, calls=%fused_computation.5 | convolution fusion | flops 5907152896 | bytes 25171968 | tf_op jit(solution)/shard_map/td,sdf->stf/dot_general | solution.py:572
  306.3 9.9 %fusion.11 = (bf16[4,512,704]{2,1,0:T(8,128)(2,1)}, bf16[4,512,704]{2,1,0:T(8,128)(2,1)}, bf16[4,512,704]{2,1,0:T(8,128)(2,1)}) fusion(f32[4,512,1408]{2,1,0:T(8,128)S(1)} %fusion.4, bf16[512,1024,1]{1,0,2:T(8,128)(2,1)S(1)} %bitcast.336, bf16[4,1024,2112]{2,1,0:T(8,128)(2,1)} %bitcast.308), kind=kOutput, calls=%fused_computation.12 | convolution fusion | flops 2975858688 | bytes 27525120 | tf_op jit(solution)/shard_map/td,sdf->stf/dot_general | solution.py:578
  316.2 4.7 pad_maximum_fusion.right_ref
  320.9 11.1 %fusion.2 = f32[512,1024,1]{0,1,2:T(8,128)S(1)} fusion(bf16[4,512,1408]{2,1,0:T(8,128)(2,1)S(1)} %pad_maximum_fusion.right_ref, bf16[4,1024,2112]{2,1,0:T(8,128)(2,1)} %bitcast.309), kind=kOutput, calls=%fused_computation.3 | convolution fusion | flops 5905580032 | bytes 19398656 | tf_op jit(solution)/shard_map/stf,sdf->td/dot_general | solution.py:582
  335.2 3.6 fusion.24
  341.4 3.3 reshape.240.dmix_ref
  344.7 11.1 %mixer_back_local.1 = (f32[8,2,256,128]{3,2,1,0:T(8,128)}, f32[8,2,128,128]{3,2,1,0:T(8,128)}) custom-call(f32[2,256,1024]{2,1,0:T(8,128)} %reshape.240.dmix_ref, bf16[8,2,256,256]{3,2,1,0:T(8,128)(2,1)} %get-tuple-element.30.qk_ref, bf16[8,2,256,256]{3,2,1,0:T(8,128)(2,1)} %get-tuple-element.37.t_ref, bf16[8,2,256,256]{3,2,1,0:T(8,128)(2,1)} %get-tuple-element.31.p_ref, ...), custom_call_target="tpu_custom_call" | custom-call | flops 3200000000 | bytes 16000000 | tf_op jit(solution)/shard_map/mixer_back_local/pallas_call | solution.py:329
  358.6 5.0 grad_pieces.11
  363.5 7.6 %fusion.21 = bf16[512,1024]{0,1:T(8,128)(2,1)} fusion(f32[512,1024]{0,1:T(8,128)} %get-tuple-element.227, bf16[4,512,704]{2,1,0:T(8,128)(2,1)S(1)} %copy-done.12, bf16[4,1024,2112]{2,1,0:T(8,128)(2,1)} %bitcast.310), kind=kOutput, calls=%fused_computation.41 | convolution fusion | flops 2953838592 | bytes 12320768 | tf_op jit(solution)/shard_map/stf,sdf->td/dot_general | solution.py:576
  372.8 3.1 fusion.40
  377.2 8.7 %grad_pieces.13 = bf16[4,4,128,1408]{3,2,1,0:T(8,128)(2,1)} custom-call(s32[4]{0:T(128)} %pad_add_fusion.1.table_ref, bf16[1024,512]{1,0:T(8,128)(2,1)} %get-tuple-element.182.left_ref, bf16[4,512,1408]{2,1,0:T(8,128)(2,1)} %copy-done), custom_call_target="tpu_custom_call" | custom-call | flops 2952790016 | bytes 5767168 | tf_op jit(solution)/shard_map/grad_pieces/pallas_call | solution.py:382
  388.9 6.3 grad_pieces.15
  395.2 4.6 copy.482
  399.8 5.0 grad_pieces.10
  405.4 6.3 grad_pieces.14
  417.5 8.5 %grad_pieces.12 = bf16[4,4,128,1408]{3,2,1,0:T(8,128)(2,1)} custom-call(s32[4]{0:T(128)} %pad_add_fusion.table_ref, bf16[1024,512]{1,0:T(8,128)(2,1)} %get-tuple-element.182.left_ref, bf16[4,512,1408]{2,1,0:T(8,128)(2,1)} %copy-done), custom_call_target="tpu_custom_call" | custom-call | flops 2952790016 | bytes 5767168 | tf_op jit(solution)/shard_map/grad_pieces/pallas_call | solution.py:382
  428.6 3.8 collective-permute-done.29
  433.6 30.0 %mixer_back.1 = (bf16[2,256,3072]{2,1,0:T(8,128)(2,1)}, f32[8,2,16,384]{3,2,1,0:T(8,128)}, f32[8,2,16,384]{3,2,1,0:T(8,128)}, f32[8,2,256,1]{3,2,1,0:T(8,128)}, f32[8,16,128]{2,1,0:T(8,128)}) custom-call(f32[2,256,1024]{2,1,0:T(8,128)} %reshape.240.dmix_ref, f32[8,2,256,128]{3,2,1,0:T(8,128)} %get-tuple-element.38.y_ref, ...), custom_call_target="tpu_custom_call" | custom-call | flops 16000000000 | bytes 48000000 | tf_op jit(solution)/shard_map/mixer_back/pallas_call | solution.py:349
  474.3 5.6 collective-permute-done.30
  480.7 6.9 reshape.241
  487.7 4.1 copy.546
  491.8 5.6 bitcast_add_fusion
  499.7 6.3 grad_pieces.9
  507.9 3.1 copy.483
  517.3 6.0 add_convert_fusion
  554.1 6.5 grad_pieces.8
  563.7 4.0 add_convert_fusion.2
  568.1 6.1 collective-permute-done.64
  584.2 13.4 %collective-permute-done.80 = bf16[128,704]{1,0:T(8,128)(2,1)S(1)} collective-permute-done((bf16[128,704]{1,0:T(8,128)(2,1)S(1)}, bf16[128,704]{1,0:T(8,128)(2,1)S(1)}, u32[]{:S(2)}, u32[]{:S(2)}) %collective-permute-start.80) | collective-permute-done | bytes 180256 | tf_op jit(solution)/shard_map/ppermute | solution.py:442
  602.6 5.2 collective-permute-done.65
  610.7 6.6 collective-permute-done.39
  623.3 19.2 %collective-permute-done.67 = bf16[128,1408]{1,0:T(8,128)(2,1)S(1)} collective-permute-done((bf16[128,1408]{1,0:T(8,128)(2,1)S(1)}, bf16[128,1408]{1,0:T(8,128)(2,1)S(1)}, u32[]{:S(2)}, u32[]{:S(2)}) %collective-permute-start.67) | collective-permute-done | bytes 360480 | tf_op jit(solution)/shard_map/ppermute | solution.py:442
  654.2 3.7 collective-permute-start.85
  658.9 6.3 collective-permute-done.41
  680.6 3.3 place.11
  689.7 3.3 place.8
  693.1 3.2 copy.477
  706.2 4.1 place.10
  715.2 3.4 copy.520
  (495 shorter events, 246.5 us)
Async XLA Ops:
  10.7 20.8 %collective-permute-start.2 = (bf16[128,1024]{1,0:T(8,128)(2,1)S(1)}, bf16[128,1024]{1,0:T(8,128)(2,1)S(1)}, u32[]{:S(2)}, u32[]{:S(2)}) collective-permute-start(bf16[128,1024]{1,0:T(8,128)(2,1)S(1)} %fusion.73), channel_id=1, source_target_pairs={{0,2},{1,3},{2,0},{3,1},{4,6},{5,7},{6,4},{7,5},{8,10},{9,11},{10,... | collective-permute-start | bytes 786440 | tf_op jit(solution)/shard_map/ppermute | solution.py:438
  13.0 18.5 %collective-permute-start.1 = (bf16[128,1024]{1,0:T(8,128)(2,1)S(1)}, bf16[128,1024]{1,0:T(8,128)(2,1)S(1)}, u32[]{:S(2)}, u32[]{:S(2)}) collective-permute-start(bf16[128,1024]{1,0:T(8,128)(2,1)S(1)} %fusion.73), channel_id=1, source_target_pairs={{0,3},{1,0},{2,1},{3,2},{4,7},{5,4},{6,5},{7,6},{8,11},{9,8},{10,9... | collective-permute-start | bytes 786440 | tf_op jit(solution)/shard_map/ppermute | solution.py:438
  14.1 35.6 %collective-permute-start.13 = (bf16[5,1024]{1,0:T(8,128)(2,1)S(1)}, bf16[5,1024]{1,0:T(8,128)(2,1)S(1)}, u32[]{:S(2)}, u32[]{:S(2)}) collective-permute-start(bf16[5,1024]{1,0:T(8,128)(2,1)S(1)} %get-tuple-element.207), channel_id=1, source_target_pairs={{0,1},{1,2},{2,3},{3,0},{4,5},{5,6},{6,7},{7,4},{8,9},{9,10},{10,1... | collective-permute-start | bytes 30728 | tf_op jit(solution)/shard_map/ppermute | solution.py:438
  14.6 56.7 %collective-permute-start.12 = (bf16[5,1024]{1,0:T(8,128)(2,1)S(1)}, bf16[5,1024]{1,0:T(8,128)(2,1)S(1)}, u32[]{:S(2)}, u32[]{:S(2)}) collective-permute-start(bf16[5,1024]{1,0:T(8,128)(2,1)S(1)} %get-tuple-element.207), channel_id=1, source_target_pairs={{0,2},{1,3},{2,0},{3,1},{4,6},{5,7},{6,4},{7,5},{8,10},{9,11},{10,... | collective-permute-start | bytes 30728 | tf_op jit(solution)/shard_map/ppermute | solution.py:438
  20.2 74.5 %collective-permute-start.19 = (bf16[128,2112]{0,1:T(8,128)(2,1)}, bf16[128,2112]{0,1:T(8,128)(2,1)}, u32[]{:S(2)}, u32[]{:S(2)}) collective-permute-start(bf16[128,2112]{0,1:T(8,128)(2,1)} %constant_dynamic-slice_fusion.4), channel_id=1, source_target_pairs={{0,1},{1,2},{2,3},{3,0},{4,5},{5,6},{6,7},{7,4},{8,9},{9,10},{10,1... | collective-permute-start | bytes 1622024 | tf_op jit(solution)/shard_map/ppermute | solution.py:438
  32.5 13.8 %collective-permute-start.4 = (bf16[3,128,1024]{2,1,0:T(8,128)(2,1)}, bf16[3,128,1024]{2,1,0:T(8,128)(2,1)}, u32[]{:S(2)}, u32[]{:S(2)}) collective-permute-start(bf16[3,128,1024]{2,1,0:T(8,128)(2,1)} %pad_maximum_fusion.7.refs_1_), channel_id=1, source_target_pairs={{0,8},{4,20},{8,0},{12,28},{16,24},{20,4},{24,16},{28,12},{1,9},{5... | collective-permute-start | bytes 2359304 | tf_op jit(solution)/shard_map/ppermute | solution.py:422
  37.0 59.8 %collective-permute-start.5 = (bf16[3,128,1024]{2,1,0:T(8,128)(2,1)}, bf16[3,128,1024]{2,1,0:T(8,128)(2,1)}, u32[]{:S(2)}, u32[]{:S(2)}) collective-permute-start(bf16[3,128,1024]{2,1,0:T(8,128)(2,1)} %pad_maximum_fusion.7.refs_1_), channel_id=1, source_target_pairs={{0,16},{4,12},{8,24},{12,4},{16,0},{20,28},{24,8},{28,20},{1,17},{... | collective-permute-start | bytes 2359304 | tf_op jit(solution)/shard_map/ppermute | solution.py:422
  46.2 51.0 %collective-permute-start.6 = (bf16[3,128,1024]{2,1,0:T(8,128)(2,1)}, bf16[3,128,1024]{2,1,0:T(8,128)(2,1)}, u32[]{:S(2)}, u32[]{:S(2)}) collective-permute-start(bf16[3,128,1024]{2,1,0:T(8,128)(2,1)} %collective-permute-done.4.refs_2_), channel_id=1, source_target_pairs={{0,16},{4,12},{8,24},{12,4},{16,0},{20,28},{24,8},{28,20},{1,17},{... | collective-permute-start | bytes 2359304 | tf_op jit(solution)/shard_map/ppermute | solution.py:422
  49.7 47.0 %collective-permute-start.18 = (bf16[128,2112]{0,1:T(8,128)(2,1)}, bf16[128,2112]{0,1:T(8,128)(2,1)}, u32[]{:S(2)}, u32[]{:S(2)}) collective-permute-start(bf16[128,2112]{0,1:T(8,128)(2,1)} %constant_dynamic-slice_fusion.4), channel_id=1, source_target_pairs={{0,2},{1,3},{2,0},{3,1},{4,6},{5,7},{6,4},{7,5},{8,10},{9,11},{10,... | collective-permute-start | bytes 1622024 | tf_op jit(solution)/shard_map/ppermute | solution.py:438
  71.3 13.6 %collective-permute-start.11 = (bf16[5,1024]{1,0:T(8,128)(2,1)S(1)}, bf16[5,1024]{1,0:T(8,128)(2,1)S(1)}, u32[]{:S(2)}, u32[]{:S(2)}) collective-permute-start(bf16[5,1024]{1,0:T(8,128)(2,1)S(1)} %get-tuple-element.207), channel_id=1, source_target_pairs={{0,3},{1,0},{2,1},{3,2},{4,7},{5,4},{6,5},{7,6},{8,11},{9,8},{10,9... | collective-permute-start | bytes 30728 | tf_op jit(solution)/shard_map/ppermute | solution.py:438
  90.8 14.1 %collective-permute-start.17 = (bf16[128,2112]{0,1:T(8,128)(2,1)}, bf16[128,2112]{0,1:T(8,128)(2,1)}, u32[]{:S(2)}, u32[]{:S(2)}) collective-permute-start(bf16[128,2112]{0,1:T(8,128)(2,1)} %constant_dynamic-slice_fusion.4), channel_id=1, source_target_pairs={{0,3},{1,0},{2,1},{3,2},{4,7},{5,4},{6,5},{7,6},{8,11},{9,8},{10,9... | collective-permute-start | bytes 1622024 | tf_op jit(solution)/shard_map/ppermute | solution.py:438
  94.7 17.4 %collective-permute-start.7 = (bf16[3,128,1024]{2,1,0:T(8,128)(2,1)}, bf16[3,128,1024]{2,1,0:T(8,128)(2,1)}, u32[]{:S(2)}, u32[]{:S(2)}) collective-permute-start(bf16[3,128,1024]{2,1,0:T(8,128)(2,1)} %pad_maximum_fusion.7.refs_1_), channel_id=1, source_target_pairs={{0,4},{4,0},{8,12},{12,8},{16,20},{20,16},{24,28},{28,24},{1,5},{5... | collective-permute-start | bytes 2359304 | tf_op jit(solution)/shard_map/ppermute | solution.py:422
  96.7 15.3 %collective-permute-start.8 = (bf16[3,128,1024]{2,1,0:T(8,128)(2,1)}, bf16[3,128,1024]{2,1,0:T(8,128)(2,1)}, u32[]{:S(2)}, u32[]{:S(2)}) collective-permute-start(bf16[3,128,1024]{2,1,0:T(8,128)(2,1)} %collective-permute-done.4.refs_2_), channel_id=1, source_target_pairs={{0,4},{4,0},{8,12},{12,8},{16,20},{20,16},{24,28},{28,24},{1,5},{5... | collective-permute-start | bytes 2359304 | tf_op jit(solution)/shard_map/ppermute | solution.py:422
  96.8 15.3 %collective-permute-start.9 = (bf16[3,128,1024]{2,1,0:T(8,128)(2,1)}, bf16[3,128,1024]{2,1,0:T(8,128)(2,1)}, u32[]{:S(2)}, u32[]{:S(2)}) collective-permute-start(bf16[3,128,1024]{2,1,0:T(8,128)(2,1)} %collective-permute-done.5.refs_3_), channel_id=1, source_target_pairs={{0,4},{4,0},{8,12},{12,8},{16,20},{20,16},{24,28},{28,24},{1,5},{5... | collective-permute-start | bytes 2359304 | tf_op jit(solution)/shard_map/ppermute | solution.py:422
  97.3 14.8 %collective-permute-start.10 = (bf16[3,128,1024]{2,1,0:T(8,128)(2,1)}, bf16[3,128,1024]{2,1,0:T(8,128)(2,1)}, u32[]{:S(2)}, u32[]{:S(2)}) collective-permute-start(bf16[3,128,1024]{2,1,0:T(8,128)(2,1)} %collective-permute-done.6.refs_4_), channel_id=1, source_target_pairs={{0,4},{4,0},{8,12},{12,8},{16,20},{20,16},{24,28},{28,24},{1,5},{5... | collective-permute-start | bytes 2359304 | tf_op jit(solution)/shard_map/ppermute | solution.py:422
  110.8 80.1 %collective-permute-start.20 = (bf16[3,128,2112]{1,2,0:T(8,128)(2,1)}, bf16[3,128,2112]{1,2,0:T(8,128)(2,1)}, u32[]{:S(2)}, u32[]{:S(2)}) collective-permute-start(bf16[3,128,2112]{1,2,0:T(8,128)(2,1)} %copy.444), channel_id=1, source_target_pairs={{0,8},{4,20},{8,0},{12,28},{16,24},{20,4},{24,16},{28,12},{1,9},{5... | collective-permute-start | bytes 4866056 | tf_op jit(solution)/shard_map/ppermute | solution.py:422
  112.1 81.8 %collective-permute-start.21 = (bf16[3,128,2112]{1,2,0:T(8,128)(2,1)}, bf16[3,128,2112]{1,2,0:T(8,128)(2,1)}, u32[]{:S(2)}, u32[]{:S(2)}) collective-permute-start(bf16[3,128,2112]{1,2,0:T(8,128)(2,1)} %copy.444), channel_id=1, source_target_pairs={{0,16},{4,12},{8,24},{12,4},{16,0},{20,28},{24,8},{28,20},{1,17},{... | collective-permute-start | bytes 4866056 | tf_op jit(solution)/shard_map/ppermute | solution.py:422
  187.7 12.2 %collective-permute-start.14 = (bf16[8,2,128,128]{3,2,1,0:T(8,128)(2,1)S(1)}, bf16[8,2,128,128]{3,2,1,0:T(8,128)(2,1)S(1)}, u32[]{:S(2)}, u32[]{:S(2)}) collective-permute-start(bf16[8,2,128,128]{3,2,1,0:T(8,128)(2,1)S(1)} %convert_element_type.356), channel_id=1, source_target_pairs={{0,1},{1,2},{2,3},{4,5},{5,6},{6,7},{8,9},{9,10},{10,11},{12,13},{... | collective-permute-start | bytes 1572872 | tf_op jit(solution)/shard_map/ppermute | solution.py:556
  191.0 33.7 %collective-permute-start.22 = (bf16[3,128,2112]{1,2,0:T(8,128)(2,1)}, bf16[3,128,2112]{1,2,0:T(8,128)(2,1)}, u32[]{:S(2)}, u32[]{:S(2)}) collective-permute-start(bf16[3,128,2112]{1,2,0:T(8,128)(2,1)} %collective-permute-done.20), channel_id=1, source_target_pairs={{0,16},{4,12},{8,24},{12,4},{16,0},{20,28},{24,8},{28,20},{1,17},{... | collective-permute-start | bytes 4866056 | tf_op jit(solution)/shard_map/ppermute | solution.py:422
  192.5 51.2 %collective-permute-start.23 = (bf16[3,128,2112]{1,2,0:T(8,128)(2,1)}, bf16[3,128,2112]{1,2,0:T(8,128)(2,1)}, u32[]{:S(2)}, u32[]{:S(2)}) collective-permute-start(bf16[3,128,2112]{1,2,0:T(8,128)(2,1)} %copy.444), channel_id=1, source_target_pairs={{0,4},{4,0},{8,12},{12,8},{16,20},{20,16},{24,28},{28,24},{1,5},{5... | collective-permute-start | bytes 4866056 | tf_op jit(solution)/shard_map/ppermute | solution.py:422
  193.9 57.3 %collective-permute-start.24 = (bf16[3,128,2112]{1,2,0:T(8,128)(2,1)}, bf16[3,128,2112]{1,2,0:T(8,128)(2,1)}, u32[]{:S(2)}, u32[]{:S(2)}) collective-permute-start(bf16[3,128,2112]{1,2,0:T(8,128)(2,1)} %collective-permute-done.20), channel_id=1, source_target_pairs={{0,4},{4,0},{8,12},{12,8},{16,20},{20,16},{24,28},{28,24},{1,5},{5... | collective-permute-start | bytes 4866056 | tf_op jit(solution)/shard_map/ppermute | solution.py:422
  193.9 61.1 %collective-permute-start.25 = (bf16[3,128,2112]{1,2,0:T(8,128)(2,1)}, bf16[3,128,2112]{1,2,0:T(8,128)(2,1)}, u32[]{:S(2)}, u32[]{:S(2)}) collective-permute-start(bf16[3,128,2112]{1,2,0:T(8,128)(2,1)} %collective-permute-done.21), channel_id=1, source_target_pairs={{0,4},{4,0},{8,12},{12,8},{16,20},{20,16},{24,28},{28,24},{1,5},{5... | collective-permute-start | bytes 4866056 | tf_op jit(solution)/shard_map/ppermute | solution.py:422
  202.0 12.9 %collective-permute-start.15 = (bf16[8,2,128,128]{3,2,1,0:T(8,128)(2,1)}, bf16[8,2,128,128]{3,2,1,0:T(8,128)(2,1)}, u32[]{:S(2)}, u32[]{:S(2)}) collective-permute-start(bf16[8,2,128,128]{3,2,1,0:T(8,128)(2,1)} %fusion.38), channel_id=1, source_target_pairs={{0,1},{1,2},{2,3},{4,5},{5,6},{6,7},{8,9},{9,10},{10,11},{12,13},{... | collective-permute-start | bytes 1572872 | tf_op jit(solution)/shard_map/ppermute | solution.py:556
  218.8 39.9 %collective-permute-start.16 = (bf16[8,2,128,128]{3,2,1,0:T(8,128)(2,1)}, bf16[8,2,128,128]{3,2,1,0:T(8,128)(2,1)}, u32[]{:S(2)}, u32[]{:S(2)}) collective-permute-start(bf16[8,2,128,128]{3,2,1,0:T(8,128)(2,1)} %fusion.39), channel_id=1, source_target_pairs={{0,1},{1,2},{2,3},{4,5},{5,6},{6,7},{8,9},{9,10},{10,11},{12,13},{... | collective-permute-start | bytes 1572872 | tf_op jit(solution)/shard_map/ppermute | solution.py:556
  224.6 54.9 %collective-permute-start.26 = (bf16[3,128,2112]{1,2,0:T(8,128)(2,1)}, bf16[3,128,2112]{1,2,0:T(8,128)(2,1)}, u32[]{:S(2)}, u32[]{:S(2)}) collective-permute-start(bf16[3,128,2112]{1,2,0:T(8,128)(2,1)} %collective-permute-done.22), channel_id=1, source_target_pairs={{0,4},{4,0},{8,12},{12,8},{16,20},{20,16},{24,28},{28,24},{1,5},{5... | collective-permute-start | bytes 4866056 | tf_op jit(solution)/shard_map/ppermute | solution.py:422
  357.3 15.4 %collective-permute-start.27 = (bf16[8,2,128,128]{3,2,1,0:T(8,128)(2,1)S(1)}, bf16[8,2,128,128]{3,2,1,0:T(8,128)(2,1)S(1)}, u32[]{:S(2)}, u32[]{:S(2)}) collective-permute-start(bf16[8,2,128,128]{3,2,1,0:T(8,128)(2,1)S(1)} %convert_element_type.370), channel_id=1, source_target_pairs={{1,0},{2,1},{3,2},{5,4},{6,5},{7,6},{9,8},{10,9},{11,10},{13,12},{... | collective-permute-start | bytes 1572872 | tf_op jit(solution)/shard_map/ppermute | solution.py:596
  363.5 62.5 %collective-permute-start.50 = (bf16[4,4,128,256]{3,2,1,0:T(8,128)(2,1)}, bf16[4,4,128,256]{3,2,1,0:T(8,128)(2,1)}, u32[]{:S(2)}, u32[]{:S(2)}) collective-permute-start(bf16[4,4,128,256]{3,2,1,0:T(8,128)(2,1)} %grad_pieces.11), channel_id=1, source_target_pairs={{0,4},{4,0},{8,12},{12,8},{16,20},{20,16},{24,28},{28,24},{1,5},{5... | collective-permute-start | bytes 3145736 | tf_op jit(solution)/shard_map/ppermute | solution.py:422
  375.9 35.7 %collective-permute-start.28 = (bf16[8,2,128,128]{3,2,1,0:T(8,128)(2,1)}, bf16[8,2,128,128]{3,2,1,0:T(8,128)(2,1)}, u32[]{:S(2)}, u32[]{:S(2)}) collective-permute-start(bf16[8,2,128,128]{3,2,1,0:T(8,128)(2,1)} %fusion.40), channel_id=1, source_target_pairs={{1,0},{2,1},{3,2},{5,4},{6,5},{7,6},{9,8},{10,9},{11,10},{13,12},{... | collective-permute-start | bytes 1572872 | tf_op jit(solution)/shard_map/ppermute | solution.py:596
  388.1 129.2 %collective-permute-start.63 = (bf16[4,4,128,1408]{3,2,1,0:T(8,128)(2,1)}, bf16[4,4,128,1408]{3,2,1,0:T(8,128)(2,1)}, u32[]{:S(2)}, u32[]{:S(2)}) collective-permute-start(bf16[4,4,128,1408]{3,2,1,0:T(8,128)(2,1)} %grad_pieces.13), channel_id=1, source_target_pairs={{0,4},{4,0},{8,12},{12,8},{16,20},{20,16},{24,28},{28,24},{1,5},{5... | collective-permute-start | bytes 17301512 | tf_op jit(solution)/shard_map/ppermute | solution.py:422
  399.8 108.1 %collective-permute-start.76 = (bf16[4,4,128,704]{2,3,1,0:T(8,128)(2,1)}, bf16[4,4,128,704]{2,3,1,0:T(8,128)(2,1)}, u32[]{:S(2)}, u32[]{:S(2)}) collective-permute-start(bf16[4,4,128,704]{2,3,1,0:T(8,128)(2,1)} %copy.482), channel_id=1, source_target_pairs={{0,4},{4,0},{8,12},{12,8},{16,20},{20,16},{24,28},{28,24},{1,5},{5... | collective-permute-start | bytes 8650760 | tf_op jit(solution)/shard_map/ppermute | solution.py:422
  416.1 16.4 %collective-permute-start.29 = (bf16[8,2,128,128]{3,2,1,0:T(8,128)(2,1)S(1)}, bf16[8,2,128,128]{3,2,1,0:T(8,128)(2,1)S(1)}, u32[]{:S(2)}, u32[]{:S(2)}) collective-permute-start(bf16[8,2,128,128]{3,2,1,0:T(8,128)(2,1)S(1)} %fusion.41), channel_id=1, source_target_pairs={{1,0},{2,1},{3,2},{5,4},{6,5},{7,6},{9,8},{10,9},{11,10},{13,12},{... | collective-permute-start | bytes 1572872 | tf_op jit(solution)/shard_map/ppermute | solution.py:596
  428.4 41.2 %collective-permute-start.51 = (bf16[2,4,128,256]{3,2,1,0:T(8,128)(2,1)}, bf16[2,4,128,256]{3,2,1,0:T(8,128)(2,1)}, u32[]{:S(2)}, u32[]{:S(2)}) collective-permute-start(bf16[2,4,128,256]{3,2,1,0:T(8,128)(2,1)} %slice.372), channel_id=1, source_target_pairs={{0,8},{4,20},{8,0},{12,28},{16,24},{20,4},{24,16},{28,12},{1,9},{5... | collective-permute-start | bytes 1572872 | tf_op jit(solution)/shard_map/ppermute | solution.py:422
  471.0 57.0 %collective-permute-start.52 = (bf16[4,128,256]{2,1,0:T(8,128)(2,1)S(1)}, bf16[4,128,256]{2,1,0:T(8,128)(2,1)}, u32[]{:S(2)}, u32[]{:S(2)}) collective-permute-start(bf16[4,128,256]{2,1,0:T(8,128)(2,1)S(1)} %slice_bitcast_fusion.10), channel_id=1, source_target_pairs={{0,16},{4,12},{8,24},{12,4},{16,0},{20,28},{24,8},{28,20},{1,17},{... | collective-permute-start | bytes 786440 | tf_op jit(solution)/shard_map/ppermute | solution.py:422
  506.0 57.7 %collective-permute-start.37 = (bf16[4,4,128,768]{3,2,1,0:T(8,128)(2,1)}, bf16[4,4,128,768]{3,2,1,0:T(8,128)(2,1)}, u32[]{:S(2)}, u32[]{:S(2)}) collective-permute-start(bf16[4,4,128,768]{3,2,1,0:T(8,128)(2,1)} %grad_pieces.9), channel_id=1, source_target_pairs={{0,4},{4,0},{8,12},{12,8},{16,20},{20,16},{24,28},{28,24},{1,5},{5... | collective-permute-start | bytes 9437192 | tf_op jit(solution)/shard_map/ppermute | solution.py:422
  517.1 18.5 %collective-permute-start.77 = (bf16[2,4,128,704]{2,3,1,0:T(8,128)(2,1)}, bf16[2,4,128,704]{2,3,1,0:T(8,128)(2,1)}, u32[]{:S(2)}, u32[]{:S(2)}) collective-permute-start(bf16[2,4,128,704]{2,3,1,0:T(8,128)(2,1)} %copy.484), channel_id=1, source_target_pairs={{0,8},{4,20},{8,0},{12,28},{16,24},{20,4},{24,16},{28,12},{1,9},{5... | collective-permute-start | bytes 4325384 | tf_op jit(solution)/shard_map/ppermute | solution.py:422
  526.7 47.5 %collective-permute-start.64 = (bf16[2,4,128,1408]{3,2,1,0:T(8,128)(2,1)}, bf16[2,4,128,1408]{3,2,1,0:T(8,128)(2,1)}, u32[]{:S(2)}, u32[]{:S(2)}) collective-permute-start(bf16[2,4,128,1408]{3,2,1,0:T(8,128)(2,1)} %slice.381), channel_id=1, source_target_pairs={{0,8},{4,20},{8,0},{12,28},{16,24},{20,4},{24,16},{28,12},{1,9},{5... | collective-permute-start | bytes 8650760 | tf_op jit(solution)/shard_map/ppermute | solution.py:422
  529.9 12.7 %collective-permute-start.55 = (bf16[128,256]{1,0:T(8,128)(2,1)}, bf16[128,256]{1,0:T(8,128)(2,1)S(1)}, u32[]{:S(2)}, u32[]{:S(2)}) collective-permute-start(bf16[128,256]{1,0:T(8,128)(2,1)} %get-tuple-element.194), channel_id=1, source_target_pairs={{0,3},{1,0},{2,1},{3,2},{4,7},{5,4},{6,5},{7,6},{8,11},{9,8},{10,9... | collective-permute-start | bytes 196616 | tf_op jit(solution)/shard_map/ppermute | solution.py:442
  531.3 13.8 %collective-permute-start.54 = (bf16[128,256]{1,0:T(8,128)(2,1)}, bf16[128,256]{1,0:T(8,128)(2,1)}, u32[]{:S(2)}, u32[]{:S(2)}) collective-permute-start(bf16[128,256]{1,0:T(8,128)(2,1)} %get-tuple-element.195), channel_id=1, source_target_pairs={{0,2},{1,3},{2,0},{3,1},{4,6},{5,7},{6,4},{7,5},{8,10},{9,11},{10,... | collective-permute-start | bytes 196616 | tf_op jit(solution)/shard_map/ppermute | solution.py:442
  545.1 18.3 %collective-permute-start.78 = (bf16[4,128,704]{1,2,0:T(8,128)(2,1)S(1)}, bf16[4,128,704]{1,2,0:T(8,128)(2,1)S(1)}, u32[]{:S(2)}, u32[]{:S(2)}) collective-permute-start(bf16[4,128,704]{1,2,0:T(8,128)(2,1)S(1)} %copy.486), channel_id=1, source_target_pairs={{0,16},{4,12},{8,24},{12,4},{16,0},{20,28},{24,8},{28,20},{1,17},{... | collective-permute-start | bytes 2162696 | tf_op jit(solution)/shard_map/ppermute | solution.py:422
  560.6 20.4 %collective-permute-start.35 = (f32[5632]{0:T(1024)S(1)}, f32[5632]{0:T(1024)S(1)}, u32[]{:S(2)}, u32[]{:S(2)}) collective-permute-start(f32[5632]{0:T(1024)S(1)} %add.231), channel_id=1, source_target_pairs={{0,8},{4,12},{8,0},{12,4},{16,24},{20,28},{24,16},{28,20},{1,9},{5... | collective-permute-start | bytes 67592 | tf_op jit(solution)/shard_map/ppermute | solution.py:422
  567.8 32.8 %collective-permute-start.38 = (bf16[2,4,128,768]{3,2,1,0:T(8,128)(2,1)S(1)}, bf16[2,4,128,768]{3,2,1,0:T(8,128)(2,1)S(1)}, u32[]{:S(2)}, u32[]{:S(2)}) collective-permute-start(bf16[2,4,128,768]{3,2,1,0:T(8,128)(2,1)S(1)} %slice.359), channel_id=1, source_target_pairs={{0,8},{4,20},{8,0},{12,28},{16,24},{20,4},{24,16},{28,12},{1,9},{5... | collective-permute-start | bytes 4718600 | tf_op jit(solution)/shard_map/ppermute | solution.py:422
  576.9 30.9 %collective-permute-start.65 = (bf16[4,128,1408]{2,1,0:T(8,128)(2,1)S(1)}, bf16[4,128,1408]{2,1,0:T(8,128)(2,1)S(1)}, u32[]{:S(2)}, u32[]{:S(2)}) collective-permute-start(bf16[4,128,1408]{2,1,0:T(8,128)(2,1)S(1)} %slice_bitcast_fusion), channel_id=1, source_target_pairs={{0,16},{4,12},{8,24},{12,4},{16,0},{20,28},{24,8},{28,20},{1,17},{... | collective-permute-start | bytes 4325384 | tf_op jit(solution)/shard_map/ppermute | solution.py:422
  580.0 17.6 %collective-permute-start.80 = (bf16[128,704]{1,0:T(8,128)(2,1)S(1)}, bf16[128,704]{1,0:T(8,128)(2,1)S(1)}, u32[]{:S(2)}, u32[]{:S(2)}) collective-permute-start(bf16[128,704]{1,0:T(8,128)(2,1)S(1)} %get-tuple-element.189), channel_id=1, source_target_pairs={{0,2},{1,3},{2,0},{3,1},{4,6},{5,7},{6,4},{7,5},{8,10},{9,11},{10,... | collective-permute-start | bytes 540680 | tf_op jit(solution)/shard_map/ppermute | solution.py:442
  581.0 17.6 %collective-permute-start.79 = (bf16[128,704]{1,0:T(8,128)(2,1)S(1)}, bf16[128,704]{1,0:T(8,128)(2,1)S(1)}, u32[]{:S(2)}, u32[]{:S(2)}) collective-permute-start(bf16[128,704]{1,0:T(8,128)(2,1)S(1)} %get-tuple-element.187), channel_id=1, source_target_pairs={{0,1},{1,2},{2,3},{3,0},{4,5},{5,6},{6,7},{7,4},{8,9},{9,10},{10,1... | collective-permute-start | bytes 540680 | tf_op jit(solution)/shard_map/ppermute | solution.py:442
  584.2 25.5 %collective-permute-start.56 = (bf16[128,256]{1,0:T(8,128)(2,1)S(1)}, bf16[128,256]{1,0:T(8,128)(2,1)S(1)}, u32[]{:S(2)}, u32[]{:S(2)}) collective-permute-start(bf16[128,256]{1,0:T(8,128)(2,1)S(1)} %fusion.77), channel_id=1, source_target_pairs={{0,8},{4,20},{8,0},{12,28},{16,24},{20,4},{24,16},{28,12},{1,9},{5... | collective-permute-start | bytes 196616 | tf_op jit(solution)/shard_map/ppermute | solution.py:422
  597.6 20.9 %collective-permute-start.57 = (bf16[128,256]{1,0:T(8,128)(2,1)S(1)}, bf16[128,256]{1,0:T(8,128)(2,1)S(1)}, u32[]{:S(2)}, u32[]{:S(2)}) collective-permute-start(bf16[128,256]{1,0:T(8,128)(2,1)S(1)} %fusion.77), channel_id=1, source_target_pairs={{0,16},{4,12},{8,24},{12,4},{16,0},{20,28},{24,8},{28,20},{1,17},{... | collective-permute-start | bytes 196616 | tf_op jit(solution)/shard_map/ppermute | solution.py:422
  598.6 21.4 %collective-permute-start.59 = (bf16[128,256]{1,0:T(8,128)(2,1)S(1)}, bf16[128,256]{1,0:T(8,128)(2,1)S(1)}, u32[]{:S(2)}, u32[]{:S(2)}) collective-permute-start(bf16[128,256]{1,0:T(8,128)(2,1)S(1)} %fusion.77), channel_id=1, source_target_pairs={{0,4},{4,0},{8,12},{12,8},{16,20},{20,16},{24,28},{28,24},{1,5},{5... | collective-permute-start | bytes 196616 | tf_op jit(solution)/shard_map/ppermute | solution.py:422
  601.1 16.1 %collective-permute-start.39 = (bf16[4,128,768]{2,1,0:T(8,128)(2,1)S(1)}, bf16[4,128,768]{2,1,0:T(8,128)(2,1)S(1)}, u32[]{:S(2)}, u32[]{:S(2)}) collective-permute-start(bf16[4,128,768]{2,1,0:T(8,128)(2,1)S(1)} %slice_bitcast_fusion.4), channel_id=1, source_target_pairs={{0,16},{4,12},{8,24},{12,4},{16,0},{20,28},{24,8},{28,20},{1,17},{... | collective-permute-start | bytes 2359304 | tf_op jit(solution)/shard_map/ppermute | solution.py:422
  608.3 14.9 %collective-permute-start.68 = (bf16[128,1408]{1,0:T(8,128)(2,1)S(1)}, bf16[128,1408]{1,0:T(8,128)(2,1)S(1)}, u32[]{:S(2)}, u32[]{:S(2)}) collective-permute-start(bf16[128,1408]{1,0:T(8,128)(2,1)S(1)} %get-tuple-element.185), channel_id=1, source_target_pairs={{0,3},{1,0},{2,1},{3,2},{4,7},{5,4},{6,5},{7,6},{8,11},{9,8},{10,9... | collective-permute-start | bytes 1081352 | tf_op jit(solution)/shard_map/ppermute | solution.py:442
  609.7 32.9 %collective-permute-start.67 = (bf16[128,1408]{1,0:T(8,128)(2,1)S(1)}, bf16[128,1408]{1,0:T(8,128)(2,1)S(1)}, u32[]{:S(2)}, u32[]{:S(2)}) collective-permute-start(bf16[128,1408]{1,0:T(8,128)(2,1)S(1)} %get-tuple-element.186), channel_id=1, source_target_pairs={{0,2},{1,3},{2,0},{3,1},{4,6},{5,7},{6,4},{7,5},{8,10},{9,11},{10,... | collective-permute-start | bytes 1081352 | tf_op jit(solution)/shard_map/ppermute | solution.py:442
  617.2 25.5 %collective-permute-start.66 = (bf16[128,1408]{1,0:T(8,128)(2,1)S(1)}, bf16[128,1408]{1,0:T(8,128)(2,1)S(1)}, u32[]{:S(2)}, u32[]{:S(2)}) collective-permute-start(bf16[128,1408]{1,0:T(8,128)(2,1)S(1)} %get-tuple-element.184), channel_id=1, source_target_pairs={{0,1},{1,2},{2,3},{3,0},{4,5},{5,6},{6,7},{7,4},{8,9},{9,10},{10,1... | collective-permute-start | bytes 1081352 | tf_op jit(solution)/shard_map/ppermute | solution.py:442
  622.0 27.5 %collective-permute-start.61 = (bf16[128,256]{1,0:T(8,128)(2,1)S(1)}, bf16[128,256]{1,0:T(8,128)(2,1)S(1)}, u32[]{:S(2)}, u32[]{:S(2)}) collective-permute-start(bf16[128,256]{1,0:T(8,128)(2,1)S(1)} %collective-permute-done.57), channel_id=1, source_target_pairs={{0,4},{4,0},{8,12},{12,8},{16,20},{20,16},{24,28},{28,24},{1,5},{5... | collective-permute-start | bytes 196616 | tf_op jit(solution)/shard_map/ppermute | solution.py:422
  623.1 26.6 %collective-permute-start.62 = (bf16[128,256]{1,0:T(8,128)(2,1)S(1)}, bf16[128,256]{1,0:T(8,128)(2,1)S(1)}, u32[]{:S(2)}, u32[]{:S(2)}) collective-permute-start(bf16[128,256]{1,0:T(8,128)(2,1)S(1)} %collective-permute-done.58), channel_id=1, source_target_pairs={{0,4},{4,0},{8,12},{12,8},{16,20},{20,16},{24,28},{28,24},{1,5},{5... | collective-permute-start | bytes 196616 | tf_op jit(solution)/shard_map/ppermute | solution.py:422
  623.1 26.4 %collective-permute-start.36 = (f32[5632]{0:T(1024)S(1)}, f32[5632]{0:T(1024)S(1)}, u32[]{:S(2)}, u32[]{:S(2)}) collective-permute-start(f32[5632]{0:T(1024)S(1)} %add.232), channel_id=1, source_target_pairs={{0,16},{4,20},{8,24},{12,28},{16,0},{20,4},{24,8},{28,12},{1,17},{... | collective-permute-start | bytes 67592 | tf_op jit(solution)/shard_map/ppermute | solution.py:422
  649.6 15.6 %collective-permute-start.41 = (bf16[128,768]{1,0:T(8,128)(2,1)}, bf16[128,768]{1,0:T(8,128)(2,1)S(1)}, u32[]{:S(2)}, u32[]{:S(2)}) collective-permute-start(bf16[128,768]{1,0:T(8,128)(2,1)} %get-tuple-element.192), channel_id=1, source_target_pairs={{0,2},{1,3},{2,0},{3,1},{4,6},{5,7},{6,4},{7,5},{8,10},{9,11},{10,... | collective-permute-start | bytes 589832 | tf_op jit(solution)/shard_map/ppermute | solution.py:442
  649.7 17.2 %collective-permute-start.40 = (bf16[128,768]{1,0:T(8,128)(2,1)}, bf16[128,768]{1,0:T(8,128)(2,1)S(1)}, u32[]{:S(2)}, u32[]{:S(2)}) collective-permute-start(bf16[128,768]{1,0:T(8,128)(2,1)} %get-tuple-element.190), channel_id=1, source_target_pairs={{0,1},{1,2},{2,3},{3,0},{4,5},{5,6},{6,7},{7,4},{8,9},{9,10},{10,1... | collective-permute-start | bytes 589832 | tf_op jit(solution)/shard_map/ppermute | solution.py:442
  651.8 18.5 %collective-permute-start.69 = (bf16[128,1408]{1,0:T(8,128)(2,1)S(1)}, bf16[128,1408]{1,0:T(8,128)(2,1)}, u32[]{:S(2)}, u32[]{:S(2)}) collective-permute-start(bf16[128,1408]{1,0:T(8,128)(2,1)S(1)} %fusion.63), channel_id=1, source_target_pairs={{0,8},{4,20},{8,0},{12,28},{16,24},{20,4},{24,16},{28,12},{1,9},{5... | collective-permute-start | bytes 1081352 | tf_op jit(solution)/shard_map/ppermute | solution.py:422
  654.2 12.9 %collective-permute-start.85 = (bf16[128,704]{1,0:T(8,128)(2,1)S(1)}, bf16[128,704]{1,0:T(8,128)(2,1)S(1)}, u32[]{:S(2)}, u32[]{:S(2)}) collective-permute-start(bf16[128,704]{1,0:T(8,128)(2,1)S(1)} %fusion.69), channel_id=1, source_target_pairs={{0,4},{4,0},{8,12},{12,8},{16,20},{20,16},{24,28},{28,24},{1,5},{5... | collective-permute-start | bytes 540680 | tf_op jit(solution)/shard_map/ppermute | solution.py:422
  670.2 14.9 %collective-permute-start.70 = (bf16[128,1408]{1,0:T(8,128)(2,1)S(1)}, bf16[128,1408]{1,0:T(8,128)(2,1)}, u32[]{:S(2)}, u32[]{:S(2)}) collective-permute-start(bf16[128,1408]{1,0:T(8,128)(2,1)S(1)} %fusion.63), channel_id=1, source_target_pairs={{0,16},{4,12},{8,24},{12,4},{16,0},{20,28},{24,8},{28,20},{1,17},{... | collective-permute-start | bytes 1081352 | tf_op jit(solution)/shard_map/ppermute | solution.py:422
  670.3 15.1 %collective-permute-start.71 = (bf16[128,1408]{1,0:T(8,128)(2,1)}, bf16[128,1408]{1,0:T(8,128)(2,1)}, u32[]{:S(2)}, u32[]{:S(2)}) collective-permute-start(bf16[128,1408]{1,0:T(8,128)(2,1)} %collective-permute-done.69), channel_id=1, source_target_pairs={{0,16},{4,12},{8,24},{12,4},{16,0},{20,28},{24,8},{28,20},{1,17},{... | collective-permute-start | bytes 1081352 | tf_op jit(solution)/shard_map/ppermute | solution.py:422
  684.6 21.6 %collective-permute-start.72 = (bf16[128,1408]{1,0:T(8,128)(2,1)S(1)}, bf16[128,1408]{1,0:T(8,128)(2,1)}, u32[]{:S(2)}, u32[]{:S(2)}) collective-permute-start(bf16[128,1408]{1,0:T(8,128)(2,1)S(1)} %fusion.63), channel_id=1, source_target_pairs={{0,4},{4,0},{8,12},{12,8},{16,20},{20,16},{24,28},{28,24},{1,5},{5... | collective-permute-start | bytes 1081352 | tf_op jit(solution)/shard_map/ppermute | solution.py:422
  684.9 21.3 %collective-permute-start.73 = (bf16[128,1408]{1,0:T(8,128)(2,1)}, bf16[128,1408]{1,0:T(8,128)(2,1)}, u32[]{:S(2)}, u32[]{:S(2)}) collective-permute-start(bf16[128,1408]{1,0:T(8,128)(2,1)} %collective-permute-done.69), channel_id=1, source_target_pairs={{0,4},{4,0},{8,12},{12,8},{16,20},{20,16},{24,28},{28,24},{1,5},{5... | collective-permute-start | bytes 1081352 | tf_op jit(solution)/shard_map/ppermute | solution.py:422
  685.1 21.0 %collective-permute-start.74 = (bf16[128,1408]{1,0:T(8,128)(2,1)}, bf16[128,1408]{1,0:T(8,128)(2,1)}, u32[]{:S(2)}, u32[]{:S(2)}) collective-permute-start(bf16[128,1408]{1,0:T(8,128)(2,1)} %collective-permute-done.70), channel_id=1, source_target_pairs={{0,4},{4,0},{8,12},{12,8},{16,20},{20,16},{24,28},{28,24},{1,5},{5... | collective-permute-start | bytes 1081352 | tf_op jit(solution)/shard_map/ppermute | solution.py:422
  685.6 20.6 %collective-permute-start.75 = (bf16[128,1408]{1,0:T(8,128)(2,1)}, bf16[128,1408]{1,0:T(8,128)(2,1)}, u32[]{:S(2)}, u32[]{:S(2)}) collective-permute-start(bf16[128,1408]{1,0:T(8,128)(2,1)} %collective-permute-done.71), channel_id=1, source_target_pairs={{0,4},{4,0},{8,12},{12,8},{16,20},{20,16},{24,28},{28,24},{1,5},{5... | collective-permute-start | bytes 1081352 | tf_op jit(solution)/shard_map/ppermute | solution.py:422
  (112 other events, 1680.8 us)

commit v2 on v1

v2 whole, which is shorter than its diff:
```python
import functools

import jax
import jax.numpy as jnp
from jax import lax
from jax.experimental import pallas as pl
from jax.experimental.pallas import tpu as pltpu
from jax.sharding import PartitionSpec as P

HD = 128
HALO = 16
EXTRA = 16
LANES = 16
PIECES = 8
EPS = 1e-06
F32 = jnp.float32
BF16 = jnp.bfloat16
MIB = 1 << 20


def mm(a, b, ta=False, tb=False):
    dims = (((0 if ta else 1,), (1 if tb else 0,)), ((), ()))
    return lax.dot_general(a.astype(BF16), b.astype(BF16), dims, preferred_element_type=F32)


def interleave(makers):
    running = list(makers)
    while running:
        still = []
        for g in running:
            try:
                next(g)
                still.append(g)
            except StopIteration:
                pass
        running = still


def invert_unit(lows):
    size = lows[0].shape[0]
    row = lax.broadcasted_iota(jnp.int32, (size, size), 0)
    col = lax.broadcasted_iota(jnp.int32, (size, size), 1)
    eye = (row == col).astype(F32)
    invs = [eye - jnp.where((row >> 1) == (col >> 1), low, 0.0) for low in lows]
    step = 1
    while (2 << step) <= size:
        pair = ((row >> (step + 1)) == (col >> (step + 1))) & ((row >> step) != (col >> step))
        lefts = [mm(inv, jnp.where(pair, low, 0.0)) for inv, low in zip(invs, lows)]
        yield
        invs = [inv - mm(left, inv) for inv, left in zip(invs, lefts)]
        yield
        step += 1
    return invs


def short_conv(proj, taps, keeps):
    total = taps[0:1] * proj[HALO:]
    for i in range(1, 4):
        total = total + taps[i : i + 1] * (pltpu.roll(proj, i, 0)[HALO:] * keeps[i - 1])
    return total


def silu_unit(conv):
    sig = jax.nn.sigmoid(conv)
    act = conv * sig
    scale = lax.rsqrt(jnp.sum(act * act, axis=-1, keepdims=True) + EPS)
    return act * scale, scale, sig


def silu_unit_back(grad, conv, unit, scale, sig):
    d_act = scale * (grad - unit * jnp.sum(grad * unit, axis=-1, keepdims=True))
    return d_act * sig * (1.0 + conv * (1.0 - sig))


def flags(seg):
    own = seg[HALO:]
    equal = lambda a: jnp.where(own == a, 1.0, 0.0)
    keeps = [equal(pltpu.roll(jnp.broadcast_to(seg, (seg.shape[0], HD)), i, 0)[HALO:, 0:1]) for i in (1, 2, 3)]
    return keeps, equal(seg[HALO - 1 : HALO]), equal(seg[-1:])


def masks(seg, seg_row):
    n = seg_row.shape[1]
    row = lax.broadcasted_iota(jnp.int32, (n, n), 0)
    col = lax.broadcasted_iota(jnp.int32, (n, n), 1)
    same = seg[HALO:] == seg_row
    strict = jnp.where(same & (row > col), 1.0, 0.0)
    within = jnp.where(same & (row >= col), 1.0, 0.0)
    return strict, within


def pick(values, head):
    lane = lax.broadcasted_iota(jnp.int32, values.shape, 1)
    return jnp.sum(jnp.where(lane == head, values, 0.0), axis=-1, keepdims=True)


def piece_copies(ids_ref, own_ref, piece_refs, w_ref, sems):
    slots = [[pltpu.make_async_copy(own_ref, w_ref.at[0], sems.at[0, 0])]]
    for slot in range(1, w_ref.shape[0]):
        slots.append(
            [
                pltpu.make_async_copy(
                    piece.at[slot - 1], w_ref.at[slot, ids_ref[j]], sems.at[slot, j]
                )
                for j, piece in enumerate(piece_refs)
            ]
        )
    return slots


def local_kernel(ids_ref, x_ref, halo_ref, seg_ref, seg_row_ref, own_ref, *refs):
    pieces = refs[:PIECES]
    (w_ref, beta_ref, taps_ref, beta_w_ref, proj_ref, qk_ref, t_ref, p_ref, ub_ref, w_out_ref, m_ref,
     a_ref, s_ref, sems) = refs[PIECES:]
    slot = pl.program_id(0)
    per = taps_ref.shape[0]
    micro, tokens, width = x_ref.shape
    half = tokens // 2
    rows = width // PIECES
    copies = piece_copies(ids_ref, own_ref, pieces, w_ref, sems)

    @pl.when(slot == 0)
    def _():
        for group in copies:
            for copy in group:
                copy.start()
        beta_ref[...] = jnp.zeros_like(beta_ref)

    for k, group in enumerate(copies):

        @pl.when(slot == k)
        def _():
            for copy in group:
                copy.wait()

    def extra(piece, j):
        return w_ref[slot, piece, rows:, j * HD : (j + 1) * HD]

    beta_w = jnp.concatenate(
        [jnp.concatenate([extra(p, hh) for p in range(PIECES)], axis=1) for hh in range(per)], axis=0
    )
    beta_w_ref[0] = beta_w
    for hh in range(per):
        lines = [extra(per * (r % 4) + hh, per + r // 4)[0:1].astype(F32) for r in range(12)]
        taps_ref[hh] = jnp.concatenate(lines + [jnp.zeros((4, HD), F32)], axis=0)
    lane = lax.broadcasted_iota(jnp.int32, (tokens, HD), 1)

    weights = w_ref[slot, :, :rows].reshape(width, per * 3 * HD)
    shared = []
    for m in range(micro):
        x_ext = jnp.concatenate([halo_ref[m], x_ref[m]], axis=0)
        proj = jnp.dot(x_ext, weights, preferred_element_type=F32)
        seg = seg_ref[m]
        betas = jax.nn.sigmoid(mm(x_ref[m], beta_w, tb=True))
        shared.append((proj, betas, flags(seg), masks(seg, seg_row_ref[m, 0:1])))

    def instance(hh, m):
        proj, betas, (keeps, live, last), (strict, within) = shared[m]
        proj = proj[:, hh * 3 * HD : (hh + 1) * 3 * HD]
        taps = taps_ref[hh]
        proj_ref[hh, m] = proj
        convs = [
            short_conv(proj[:, j * HD : (j + 1) * HD], taps[4 * j : 4 * j + 4], keeps)
            for j in range(3)
        ]
        query = silu_unit(convs[0])[0]
        key = silu_unit(convs[1])[0]
        value = convs[2] * jax.nn.sigmoid(convs[2])
        beta = betas[:, hh * LANES : hh * LANES + 1]
        beta_ref[m] += jnp.where(lane == (slot * per + hh) * LANES, beta, 0.0)
        qk_ref[hh, m] = jnp.concatenate([query, key], axis=1).astype(BF16)
        yield
        low = beta * mm(key, key, tb=True) * strict
        scores = mm(query, key, tb=True) * within
        p_ref[hh, m] = scores.astype(BF16)
        yield
        top, bottom = yield from invert_unit([low[:half, :half], low[half:, half:]])
        cross = mm(bottom, low[half:, :half])
        yield
        cross = -mm(cross, top)
        yield
        inv = jnp.concatenate(
            [
                jnp.concatenate([top, jnp.zeros_like(top)], axis=1),
                jnp.concatenate([cross, bottom], axis=1),
            ],
            axis=0,
        ).astype(BF16)
        t_ref[hh, m] = inv
        both = mm(inv, jnp.concatenate([beta * value, (beta * live) * key], axis=1))
        yield
        late = (last * key).astype(BF16)
        sums = mm(both, late, ta=True)
        row = lax.broadcasted_iota(jnp.int32, (HD, HD), 0)
        col = lax.broadcasted_iota(jnp.int32, (HD, HD), 1)
        keep_state = jnp.where(row == col, live[tokens - 1 : tokens], 0.0)
        ub_ref[hh, m] = both[:, :HD]
        w_out_ref[hh, m] = both[:, HD:].astype(BF16)
        a_ref[hh, m] = sums[:HD]
        s_ref[hh, m] = sums[:HD].astype(BF16)
        m_ref[hh, m] = keep_state - sums[HD:]

    interleave([instance(hh, m) for hh in range(per) for m in range(micro)])


def hop_kernel(back, state_ref, keep_ref, gain_ref, out_ref):
    for h in range(gain_ref.shape[0]):
        for m in range(gain_ref.shape[1]):
            keep = keep_ref[h, m]
            high = keep.astype(BF16)
            rest = (keep - high.astype(F32)).astype(BF16)
            state = state_ref[h, m]
            moved = mm(state, high, tb=back) + mm(state, rest, tb=back)
            out_ref[h, m] = (moved + gain_ref[h, m]).astype(BF16)


def output_kernel(qk_ref, p_ref, ub_ref, w_ref, state_ref, seg_ref, mixed_ref, u_ref):
    per, micro = ub_ref.shape[:2]

    def instance(hh, m):
        live = flags(seg_ref[m])[1]
        state = state_ref[hh, m]
        update = ub_ref[hh, m] - mm(w_ref[hh, m], state, tb=True)
        update = update.astype(BF16)
        far = live * mm(qk_ref[hh, m][:, :HD], state, tb=True)
        yield
        mixed = far + mm(p_ref[hh, m], update)
        u_ref[hh, m] = update
        yield
        mixed_ref[m, :, hh * HD : (hh + 1) * HD] = mixed.astype(BF16)

    interleave([instance(hh, m) for hh in range(per) for m in range(micro)])


def back_local_kernel(dmix_ref, qk_ref, t_ref, p_ref, beta_ref, seg_ref, y_ref, b_ref, s_ref):
    per, micro = qk_ref.shape[:2]
    slot = pl.program_id(0)

    def instance(hh, m):
        live = flags(seg_ref[m])[1]
        d_out = dmix_ref[m, :, hh * HD : (hh + 1) * HD]
        part = mm(p_ref[hh, m], d_out, ta=True)
        yield
        y0 = mm(t_ref[hh, m], part, ta=True)
        yield
        y_ref[hh, m] = y0
        qk = qk_ref[hh, m]
        beta = pick(beta_ref[m], (slot * per + hh) * LANES)
        gain = mm(live * d_out, qk[:, :HD], ta=True) - mm((beta * live) * y0, qk[:, HD:], ta=True)
        b_ref[hh, m] = gain
        s_ref[hh, m] = gain.astype(BF16)

    interleave([instance(hh, m) for hh in range(per) for m in range(micro)])


def back_kernel(dmix_ref, y_ref, qk_ref, t_ref, u_ref, state_ref, dstate_ref, proj_ref,
                taps_ref, beta_ref, seg_ref, seg_row_ref,
                dmain_ref, tail_ref, front_ref, dbeta_ref, dtaps_ref):
    per, micro = qk_ref.shape[:2]
    tokens = qk_ref.shape[2]
    slot = pl.program_id(0)
    shared = [(flags(seg_ref[m]), masks(seg_ref[m], seg_row_ref[m, 0:1])) for m in range(micro)]
    lane = lax.broadcasted_iota(jnp.int32, (tokens, HD), 1)
    tap_totals = {}

    @pl.when(slot == 0)
    def _():
        dbeta_ref[...] = jnp.zeros_like(dbeta_ref)

    def instance(hh, m):
        (keeps, live, last), (strict, within) = shared[m]
        taps = taps_ref[hh]
        head = (slot * per + hh) * LANES
        proj = proj_ref[hh, m]
        beta = pick(beta_ref[m], head)
        q_low, k_low = qk_ref[hh, m][:, :HD], qk_ref[hh, m][:, HD:]
        state = state_ref[hh, m]
        dstate = dstate_ref[hh, m]
        update = u_ref[hh, m]
        d_out = dmix_ref[m, :, hh * HD : (hh + 1) * HD].astype(BF16)
        ahead = last * mm(k_low, dstate, tb=True)
        yield
        d_right = y_ref[hh, m] + mm(t_ref[hh, m], ahead, ta=True)
        d_right_low = d_right.astype(BF16)
        yield
        d_scores = (mm(d_out, update, tb=True) * within).astype(BF16)
        yield
        grad_sys = -mm(d_right_low, update, tb=True) * strict
        keys_keys = mm(k_low, k_low, tb=True)
        d_kk = (beta * grad_sys).astype(BF16)
        d_beta = jnp.sum(grad_sys * keys_keys, axis=-1, keepdims=True)
        yield
        carried = mm(k_low, state, tb=True)
        d_carried = ((-beta * live) * d_right).astype(BF16)
        d_query = live * mm(d_out, state) + mm(d_scores, k_low)
        yield
        d_key = (
            mm(d_scores, q_low, ta=True)
            + last * mm(update, dstate)
            + mm(d_carried, state)
            + mm(d_kk, k_low)
            + mm(d_kk, k_low, ta=True)
        )
        yield
        convs = [
            short_conv(proj[:, j * HD : (j + 1) * HD], taps[4 * j : 4 * j + 4], keeps)
            for j in range(3)
        ]
        query, q_scale, q_sig = silu_unit(convs[0])
        key, k_scale, k_sig = silu_unit(convs[1])
        v_sig = jax.nn.sigmoid(convs[2])
        value = convs[2] * v_sig
        d_beta = d_beta + jnp.sum(d_right * (value - live * carried), axis=-1, keepdims=True)
        dbeta_ref[m] += jnp.where(lane == head, d_beta * beta * (1.0 - beta), 0.0)
        d_value = beta * d_right
        d_convs = [
            silu_unit_back(d_query, convs[0], query, q_scale, q_sig),
            silu_unit_back(d_key, convs[1], key, k_scale, k_sig),
            d_value * v_sig * (1.0 + convs[2] * (1.0 - v_sig)),
        ]
        yield
        tap_sums = []
        for j in range(3):
            part = proj[:, j * HD : (j + 1) * HD]
            d_conv = d_convs[j]
            tap_sums.append(jnp.sum(d_conv * part[HALO:], axis=0, keepdims=True))
            zeros = jnp.zeros((HALO, HD), F32)
            d_proj = jnp.concatenate([zeros, taps[4 * j : 4 * j + 1] * d_conv], axis=0)
            for i in range(1, 4):
                kept = keeps[i - 1] * d_conv
                tap_sums.append(
                    jnp.sum(kept * pltpu.roll(part, i, 0)[HALO:], axis=0, keepdims=True)
                )
                spread = jnp.concatenate([zeros, taps[4 * j + i : 4 * j + i + 1] * kept], axis=0)
                d_proj = d_proj + pltpu.roll(spread, HALO + tokens - i, 0)
            at = (3 * hh + j) * HD
            front_ref[m, :, at : at + HD] = d_proj[:HALO]
            tail_ref[m, :, at : at + HD] = d_proj[tokens:]
            dmain_ref[m, :, at : at + HD] = d_proj[HALO:].astype(BF16)
            yield
        tap_totals[hh, m] = jnp.concatenate(tap_sums + [jnp.zeros((4, HD), F32)], axis=0)

    interleave([instance(hh, m) for hh in range(per) for m in range(micro)])
    for hh in range(per):
        dtaps_ref[hh] = sum(tap_totals[hh, m] for m in range(micro))


def flip(v):
    return v.astype(F32).T.astype(BF16)


def pack_mixer_kernel(table_ref, q_ref, k_ref, v_ref, beta_ref, conv_ref, out_ref):
    piece = table_ref[pl.program_id(0)]
    rows, n = q_ref.shape
    per = n // HD
    parts = []
    for hh in range(per):
        parts += [r[:, hh * HD : (hh + 1) * HD] for r in (q_ref, k_ref, v_ref)]
    out_ref[0, :rows] = jnp.concatenate(parts, axis=1)
    conv = conv_ref[...].astype(F32)
    lines = [beta_ref[hh : hh + 1].astype(F32) for hh in range(per)]
    for j in range(conv.shape[0]):
        line = jnp.zeros((1, HD), F32)
        for p in range(PIECES):
            own = conv[j, p // per : p // per + 1, p % per * HD : (p % per + 1) * HD]
            line = line + jnp.where(piece == p, own, 0.0)
        lines.append(line)
    lines.append(jnp.zeros((1, 3 * n - HD * len(lines)), F32))
    line = jnp.concatenate(lines, axis=1)
    row = lax.broadcasted_iota(jnp.int32, (EXTRA, 3 * n), 0)
    out_ref[0, rows:] = jnp.where(row == 0, line, 0.0).astype(BF16)


def pack_ffn_kernel(table_ref, gate_ref, up_ref, down_ref, out_w_ref, out_ref):
    hidden, rows = gate_ref.shape
    main = hidden // HD * HD
    out_ref[0, :, :main] = flip(gate_ref[:main])
    out_ref[0, :, main : 2 * main] = flip(up_ref[:main])
    rest = jnp.concatenate([gate_ref[main:], up_ref[main:]], axis=0)
    out_ref[0, :, 2 * main : 2 * hidden] = flip(rest)
    wide = main + HD
    down = jnp.concatenate([down_ref[...].astype(F32), jnp.zeros((wide - hidden, rows), F32)], axis=0)
    out_ref[0, :, 2 * hidden : 2 * hidden + wide] = down.T.astype(BF16)
    out_ref[0, :, 2 * hidden + wide :] = flip(out_w_ref[...])


def flip_pieces(table_ref, src_ref, dst_ref):
    rows = src_ref.shape[1] // PIECES
    for pos in range(PIECES):
        start = pl.multiple_of(table_ref[pos] * rows, rows)
        dst_ref[pos * rows : (pos + 1) * rows] = flip(src_ref[:, pl.ds(start, rows)])


def ffn_kernel(hidden, ids_ref, table_ref, mixed_ref, rows_ref, dout_ref, gain_ref, own_ref, *refs):
    pieces, refs = refs[:PIECES], refs[PIECES:]
    out_ref, dmid_ref, dlow_ref, dmixed_ref, gpart_ref = refs[:5]
    (w_ref, wo_ref, x_ref, xt_ref, dt_ref, mid_ref, res_ref, dn_ref, grad_ref, sems, o_sems,
     g_sems) = refs[-12:]
    grad_refs = refs[5:-12]
    step = pl.program_id(0)
    slots = wo_ref.shape[0]
    width = rows_ref.shape[1]
    rows = width // PIECES
    main = hidden // HD * HD
    wide = main + HD
    cut = 2 * hidden + wide
    part = mixed_ref.shape[1]
    ring = w_ref.shape[0]
    order = reduce_order(slots)

    def brought(slot, target, start, size, sem):
        columns = pl.ds(start, size)
        if slot == 0:
            return [pltpu.make_async_copy(own_ref.at[:, :, columns], target, sem.at[0])]
        return [
            pltpu.make_async_copy(piece.at[slot - 1, :, columns], target.at[ids_ref[j]], sem.at[j])
            for j, piece in enumerate(pieces)
        ]

    outs = [brought(k, wo_ref.at[k], cut, part, o_sems.at[k]) for k in range(slots)]
    mains = [brought(k, w_ref.at[i % ring], 0, cut, sems.at[i % ring]) for i, k in enumerate(order)]

    def leaving(i):
        return [
            pltpu.make_async_copy(grad_ref.at[i % 2, h], grad_refs[2 * i + h], g_sems.at[i % 2, h])
            for h in range(2)
        ]

    @pl.when(step == 0)
    def _():
        for group in outs + mains[:ring]:
            for copy in group:
                copy.start()
        mid_ref[...] = rows_ref[...].astype(F32)
        dn_ref[...] = jnp.zeros_like(dn_ref)
        flip_pieces(table_ref, dout_ref, dt_ref)

    for i in range(slots):

        @pl.when(step == i)
        def _():
            for copy in outs[i]:
                copy.wait()

        @pl.when(step == slots + i)
        def _():
            for copy in mains[i]:
                copy.wait()
            if i >= 2:
                for copy in leaving(i - 2):
                    copy.wait()

    @pl.when(step < slots)
    def _():
        mid_ref[...] += mm(mixed_ref[...], wo_ref[step].reshape(width, part), tb=True)

    def norm():
        mid = mid_ref[...]
        rstd = lax.rsqrt(jnp.mean(mid * mid, axis=-1, keepdims=True) + EPS)
        return mid * rstd, rstd

    @pl.when(step == slots - 1)
    def _():
        unit, _ = norm()
        x_ref[...] = (unit * gain_ref[...]).astype(BF16)
        flip_pieces(table_ref, x_ref, xt_ref)
        res_ref[...] = mid_ref[...]

    @pl.when(step >= slots)
    def _():
        at = lax.rem(step - slots, ring)
        w_gu = w_ref[at, :, :, : 2 * hidden].reshape(width, 2 * hidden)
        w_dn = w_ref[at, :, :, 2 * hidden :].reshape(width, wide)
        both = mm(x_ref[...], w_gu)
        rest = both[:, 2 * main :]
        gate = jnp.concatenate([both[:, :main], rest], axis=1)
        up = jnp.concatenate([both[:, main : 2 * main], pltpu.roll(rest, HD // 2, 1)], axis=1)
        sig = jax.nn.sigmoid(gate)
        act = gate * sig
        hid = (act * up).astype(BF16)
        d_hid = mm(dout_ref[...], w_dn)
        d_gate = (d_hid * up * (sig * (1.0 + gate * (1.0 - sig)))).astype(BF16)
        d_up = (d_hid * act).astype(BF16)
        last = d_gate[:, main:].astype(F32) + pltpu.roll(d_up[:, main:].astype(F32), HD // 2, 1)
        d_gu = jnp.concatenate([d_gate[:, :main], d_up[:, :main], last.astype(BF16)], axis=1)
        res_ref[...] += mm(hid, w_dn, tb=True)
        dn_ref[...] += mm(d_gu, w_gu, tb=True)
        to = lax.rem(step - slots, 2)
        shape = (PIECES // 2, rows)
        for h in range(2):
            span = slice(h * width // 2, (h + 1) * width // 2)
            grad_ref[to, h, :, :, : 2 * hidden] = (
                mm(xt_ref[span], d_gu).astype(BF16).reshape(shape + (2 * hidden,))
            )
            grad_ref[to, h, :, :, 2 * hidden :] = (
                mm(dt_ref[span], hid).astype(BF16).reshape(shape + (wide,))
            )

    for i in range(slots):

        @pl.when(step == slots + i)
        def _():
            for copy in leaving(i):
                copy.start()
            if i + ring < slots:
                for copy in mains[i + ring]:
                    copy.start()

    @pl.when(step == 2 * slots - 1)
    def _():
        out_ref[...] = res_ref[...].astype(BF16)
        unit, rstd = norm()
        grad = dn_ref[...]
        gpart_ref[...] = jnp.broadcast_to(jnp.sum(grad * unit, axis=0, keepdims=True), gpart_ref.shape)
        scaled = grad * gain_ref[...]
        d_mid = dout_ref[...].astype(F32) + rstd * (
            scaled - unit * jnp.mean(scaled * unit, axis=-1, keepdims=True)
        )
        dmid_ref[...] = d_mid
        low = d_mid.astype(BF16)
        dlow_ref[...] = low
        for k in range(slots):
            dmixed_ref[:, k * part : (k + 1) * part] = mm(low, wo_ref[k].reshape(width, part))
        for i in range(max(slots - 2, 0), slots):
            for copy in leaving(i):
                copy.wait()


def grad_mixer_kernel(table_ref, x_ref, dqkv_ref, dlow_ref, mixed_ref, *refs):
    xt_ref, lt_ref, grad_ref, g_sems = refs[-4:]
    grad_refs = refs[:-4]
    step = pl.program_id(0)
    width = x_ref.shape[1]
    rows = width // PIECES
    n = dqkv_ref.shape[1]
    slots = len(grad_refs) // 2

    def leaving(i):
        return [
            pltpu.make_async_copy(grad_ref.at[i % 2, h], grad_refs[2 * i + h], g_sems.at[i % 2, h])
            for h in range(2)
        ]

    @pl.when(step == 0)
    def _():
        flip_pieces(table_ref, x_ref, xt_ref)
        flip_pieces(table_ref, dlow_ref, lt_ref)

    for i in range(2, slots):

        @pl.when(step == i)
        def _():
            for copy in leaving(i - 2):
                copy.wait()

    to = lax.rem(step, 2)
    for h in range(2):
        span = slice(h * width // 2, (h + 1) * width // 2)
        shape = (PIECES // 2, rows)
        grad_ref[to, h, :, :, :n] = mm(xt_ref[span], dqkv_ref[...]).astype(BF16).reshape(shape + (n,))
        out = mm(lt_ref[span], mixed_ref[...]).astype(BF16)
        grad_ref[to, h, :, :, n:] = out.reshape(shape + (out.shape[1],))

    for i in range(slots):

        @pl.when(step == i)
        def _():
            for copy in leaving(i):
                copy.start()
            if i == slots - 1:
                for j in range(max(slots - 2, 0), slots):
                    for copy in leaving(j):
                        copy.wait()


def bring(ids_ref, pieces, w_ref, sems):
    @pl.when(pl.program_id(0) == 0)
    def _():
        copies = [
            pltpu.make_async_copy(piece, w_ref.at[ids_ref[j]], sems.at[j])
            for j, piece in enumerate(pieces)
        ]
        for copy in copies:
            copy.start()
        for copy in copies:
            copy.wait()


def finish_ffn_kernel(hidden, ids_ref, *refs):
    gate_ref, up_ref, down_ref, w_ref, sems = refs[PIECES:]
    bring(ids_ref, refs[:PIECES], w_ref, sems)
    step = pl.program_id(0)
    main = hidden // HD * HD
    wide = main + HD
    take = lambda at, n: w_ref[step, :, at : at + n].astype(F32).T
    gate_ref[:main] = take(0, main)
    up_ref[:main] = take(main, main)
    rest = take(2 * main, HD)
    gate_ref[main:] = rest[: HD // 2]
    up_ref[main:] = rest[HD // 2 :]
    down_ref[...] = take(2 * hidden, wide)[:hidden]


def finish_mixer_kernel(ids_ref, *refs):
    outs, out_w_ref, w_ref, sems = refs[PIECES:-3], refs[-3], refs[-2], refs[-1]
    bring(ids_ref, refs[:PIECES], w_ref, sems)
    step = pl.program_id(0)
    n = outs[0].shape[1]
    for hh in range(n // HD):
        for j, out in enumerate(outs):
            at = (3 * hh + j) * HD
            out[:, hh * HD : (hh + 1) * HD] = w_ref[step, :, at : at + HD].astype(F32)
    out_w_ref[...] = w_ref[step, :, 3 * n :].astype(F32).T


def input_kernel(dqkv_ref, w_ref, db_ref, beta_w_ref, rows_ref, dmid_ref, gain_ref, out_ref, gpart_ref, acc_ref):
    step = pl.program_id(0)

    @pl.when(step == 0)
    def _():
        acc_ref[...] = mm(db_ref[...], beta_w_ref[...])

    width, n = acc_ref.shape[1], dqkv_ref.shape[1]
    weights = w_ref[0, :, : width // PIECES].reshape(width, n)
    acc_ref[...] += mm(dqkv_ref[...], weights, tb=True)

    @pl.when(step == pl.num_programs(0) - 1)
    def _():
        grad = acc_ref[...]
        rows = rows_ref[...].astype(F32)
        rstd = lax.rsqrt(jnp.mean(rows * rows, axis=-1, keepdims=True) + EPS)
        unit = rows * rstd
        gpart_ref[...] = jnp.broadcast_to(jnp.sum(grad * unit, axis=0, keepdims=True), gpart_ref.shape)
        scaled = grad * gain_ref[...]
        out_ref[...] = (
            dmid_ref[...]
            + rstd * (scaled - unit * jnp.mean(scaled * unit, axis=-1, keepdims=True))
        ).astype(BF16)


def params(mib=60):
    return pltpu.CompilerParams(
        dimension_semantics=("arbitrary",), vmem_limit_bytes=mib * MIB
    )


def cost(flops, nbytes):
    return pl.CostEstimate(flops=int(flops), bytes_accessed=int(nbytes), transcendentals=0)


ANYWHERE = pl.BlockSpec(memory_space=pl.ANY)


def whole(shape):
    return pl.BlockSpec(tuple(shape), lambda *_: (0,) * len(shape), pipeline_mode=pl.Buffered(1))


def reduce_order(slots):
    return list(range(slots - 2, 0, -1)) + [slots - 1, 0]


def lead(n, shape):
    return pl.BlockSpec((n,) + tuple(shape[1:]), lambda h, *_: (h,) + (0,) * (len(shape) - 1))


def rolled(n, shape, shift, steps):
    return pl.BlockSpec(
        (n,) + tuple(shape[1:]), lambda h, *_: ((h + shift) % steps,) + (0,) * (len(shape) - 1)
    )


def sds(shape, dtype):
    return jax.ShapeDtypeStruct(tuple(shape), dtype)


def call(kernel, grid, in_specs, out_specs, out_shape, estimate, name, scratch=(), prefetch=0):
    return pl.pallas_call(
        kernel,
        grid_spec=pltpu.PrefetchScalarGridSpec(
            num_scalar_prefetch=prefetch,
            grid=(grid,),
            in_specs=in_specs,
            out_specs=out_specs,
            scratch_shapes=list(scratch),
        ),
        out_shape=out_shape,
        compiler_params=params(),
        cost_estimate=cost(*estimate),
        name=name,
    )


def pack_mixer(table, w_query, w_key, w_value, beta_t, conv):
    width, n = w_query.shape
    rows = width // PIECES
    spec = pl.BlockSpec((rows, n), lambda i, t: (t[i], 0))
    count = table.shape[0]
    return call(
        pack_mixer_kernel, count,
        [spec] * 3 + [pl.BlockSpec((beta_t.shape[0], rows), lambda i, t: (0, t[i])), whole(conv.shape)],
        pl.BlockSpec((1, rows + EXTRA, 3 * n), lambda i, t: (i, 0, 0)),
        sds((count, rows + EXTRA, 3 * n), BF16), (0, 12 * count * rows * n), "pack_mixer", prefetch=1,
    )(table, w_query, w_key, w_value, beta_t, conv)


def pack_ffn(table, gate_t, up_t, w_down, w_out):
    hidden, width = gate_t.shape
    rows = width // PIECES
    n = 2 * hidden + hidden // HD * HD + HD + w_out.shape[0]
    count = table.shape[0]
    return call(
        pack_ffn_kernel, count,
        [pl.BlockSpec((w.shape[0], rows), lambda i, t: (0, t[i])) for w in (gate_t, up_t, w_down, w_out)],
        pl.BlockSpec((1, rows, n), lambda i, t: (i, 0, 0)),
        sds((count, rows, n), BF16), (0, 4 * count * rows * n), "pack_ffn", prefetch=1,
    )(table, gate_t, up_t, w_down, w_out)


def mixer_local(ids, x, halo, seg, seg_row, own, pieces, heads):
    micro, tokens, width = x.shape
    slots = pieces[0].shape[0] + 1
    per = heads // slots
    hm = (heads, micro)
    rows, n = own.shape[1:]
    outs = [
        sds((slots, PIECES, rows, n), BF16),
        sds((micro, tokens, HD), F32),
        sds((heads, 16, HD), F32),
        sds((slots, per * LANES, width), BF16),
        sds(hm + (HALO + tokens, 3 * HD), F32),
        sds(hm + (tokens, 2 * HD), BF16),
        sds(hm + (tokens, tokens), BF16),
        sds(hm + (tokens, tokens), BF16),
        sds(hm + (tokens, HD), F32),
        sds(hm + (tokens, HD), BF16),
        sds(hm + (HD, HD), F32),
        sds(hm + (HD, HD), F32),
        sds(hm + (HD, HD), BF16),
    ]
    return call(
        local_kernel, slots,
        [whole(x.shape), whole(halo.shape), whole(seg.shape), whole(seg_row.shape)]
        + [ANYWHERE] * (1 + PIECES),
        [whole(o.shape) for o in outs[:2]] + [lead(per, outs[2].shape), lead(1, outs[3].shape)]
        + [lead(per, o.shape) for o in outs[4:]],
        outs, (heads * micro * 1e9, heads * micro * 2e6), "mixer_local",
        [pltpu.SemaphoreType.DMA((slots, PIECES))], prefetch=1,
    )(ids, x, halo, seg, seg_row, own, *pieces)


def hop(state, keep, gain, slots, back):
    per = gain.shape[0] // slots
    shift = slots - 1 if back else 1
    return call(
        functools.partial(hop_kernel, back), slots,
        [rolled(per, state.shape, shift, slots), lead(per, keep.shape), lead(per, gain.shape)],
        lead(per, gain.shape), sds(gain.shape, BF16),
        (gain.size * 512, gain.size * 12), "hop",
    )(state, keep, gain)


def mixer_output(qk, scores, base, mix, state, seg, slots):
    heads, micro, tokens = qk.shape[:3]
    per = heads // slots
    return call(
        output_kernel, slots,
        [lead(per, a.shape) for a in (qk, scores, base, mix)]
        + [rolled(per, state.shape, 1, slots), whole(seg.shape)],
        [pl.BlockSpec((micro, tokens, per * HD), lambda h: (0, 0, h)), lead(per, base.shape)],
        [sds((micro, tokens, heads * HD), BF16), sds(base.shape, BF16)],
        (heads * micro * 5e7, heads * micro * 5e5), "mixer_output",
    )(qk, scores, base, mix, state, seg)


def mixer_back_local(d_mixed, qk, inv, scores, beta, seg, slots):
    heads, micro, tokens = qk.shape[:3]
    per = heads // slots
    outs = [sds((heads, micro, tokens, HD), F32), sds((heads, micro, HD, HD), F32)]
    outs.append(sds((heads, micro, HD, HD), BF16))
    return call(
        back_local_kernel, slots,
        [pl.BlockSpec((micro, tokens, per * HD), lambda h: (0, 0, h))]
        + [lead(per, a.shape) for a in (qk, inv, scores)]
        + [whole(beta.shape), whole(seg.shape)],
        [lead(per, o.shape) for o in outs], outs,
        (heads * micro * 5e7, heads * micro * 5e5), "mixer_back_local",
    )(d_mixed, qk, inv, scores, beta, seg)


def mixer_back(d_mixed, y0, qk, inv, update, state, d_state, proj, taps, beta, seg, seg_row, slots):
    heads, micro, tokens = qk.shape[:3]
    per = heads // slots
    columns = lambda rows, n: pl.BlockSpec((micro, rows, per * n), lambda h: (0, 0, h))
    return call(
        back_kernel, slots,
        [columns(tokens, HD)]
        + [lead(per, a.shape) for a in (y0, qk, inv, update)]
        + [rolled(per, state.shape, 1, slots), rolled(per, d_state.shape, slots - 1, slots)]
        + [lead(per, proj.shape), lead(per, taps.shape)]
        + [whole(a.shape) for a in (beta, seg, seg_row)],
        [columns(tokens, 3 * HD), columns(HALO, 3 * HD), columns(HALO, 3 * HD), whole(beta.shape),
         lead(per, taps.shape)],
        [
            sds((micro, tokens, heads * 3 * HD), BF16),
            sds((micro, HALO, heads * 3 * HD), F32),
            sds((micro, HALO, heads * 3 * HD), F32),
            sds(beta.shape, F32),
            sds(taps.shape, F32),
        ],
        (heads * micro * 5e8, heads * micro * 2e6), "mixer_back",
    )(d_mixed, y0, qk, inv, update, state, d_state, proj, taps, beta, seg, seg_row)


def grads_out(slots, rows, n):
    shape = (PIECES // 2, rows, n)
    return (
        [sds(shape, BF16)] * (2 * slots),
        [pltpu.VMEM((2, 2) + shape, BF16)],
        pltpu.SemaphoreType.DMA((2, 2)),
    )


def ffn(ids, table, mixed, rows, d_out, gain, own, pieces, hidden):
    count, width = rows.shape
    slots = pieces[0].shape[0] + 1
    wide = hidden // HD * HD + HD
    part = mixed.shape[1] // slots
    piece = width // PIECES
    full = whole((count, width))
    grads, room, g_sems = grads_out(slots, piece, 2 * hidden + wide)
    outs = [
        sds((count, width), BF16), sds((count, width), F32), sds((count, width), BF16),
        sds((count, mixed.shape[1]), F32), sds((8, width), F32),
    ]
    ring = 2
    return call(
        functools.partial(ffn_kernel, hidden), 2 * slots,
        [pl.BlockSpec((count, part), lambda s, *_: (0, jnp.minimum(s, slots - 1))),
         full, full, whole(gain.shape)] + [ANYWHERE] * (1 + PIECES),
        [full, full, full, whole((count, mixed.shape[1])), whole((8, width))] + [ANYWHERE] * len(grads),
        outs + grads, (26 * count * width * hidden * slots, 6e7), "ffn",
        [
            pltpu.VMEM((ring, PIECES, piece, 2 * hidden + wide), BF16),
            pltpu.VMEM((slots, PIECES, piece, part), BF16),
            pltpu.VMEM((count, width), BF16),
            pltpu.VMEM((width, count), BF16),
            pltpu.VMEM((width, count), BF16),
            pltpu.VMEM((count, width), F32),
            pltpu.VMEM((count, width), F32),
            pltpu.VMEM((count, width), F32),
        ]
        + room
        + [
            pltpu.SemaphoreType.DMA((ring, PIECES)),
            pltpu.SemaphoreType.DMA((slots, PIECES)),
            g_sems,
        ],
        prefetch=2,
    )(ids, table, mixed, rows, d_out, gain, own, *pieces)


def grad_mixer(table, x, d_qkv, d_low, mixed, slots):
    count, width = x.shape
    n, part = d_qkv.shape[1] // slots, mixed.shape[1] // slots
    grads, room, g_sems = grads_out(slots, width // PIECES, n + part)
    order = reduce_order(slots)

    def at(s):
        return sum(jnp.where(s == i, k, 0) for i, k in enumerate(order))

    columns = lambda size: pl.BlockSpec((count, size), lambda s, t: (0, at(s)))
    return call(
        grad_mixer_kernel, slots,
        [whole(x.shape), columns(n), whole(d_low.shape), columns(part)],
        [ANYWHERE] * len(grads), grads,
        (2 * width * count * (n + part) * slots, 2 * width * (n + part) * slots), "grad_mixer",
        [pltpu.VMEM((width, count), BF16)] * 2 + room + [g_sems], prefetch=1,
    )(table, x, d_qkv, d_low, mixed)


def finish_ffn(ids, pieces, hidden):
    rows, n = pieces[0].shape
    width = rows * PIECES
    return call(
        functools.partial(finish_ffn_kernel, hidden), PIECES, [ANYWHERE] * PIECES,
        [pl.BlockSpec((hidden, rows), lambda i, t: (0, i))] * 3,
        [sds((hidden, width), F32)] * 3,
        (0, 6 * n * width), "finish_ffn",
        [pltpu.VMEM((PIECES, rows, n), BF16), pltpu.SemaphoreType.DMA((PIECES,))], prefetch=1,
    )(ids, *pieces)


def finish_mixer(ids, pieces, n):
    rows, total = pieces[0].shape
    width = rows * PIECES
    part = total - 3 * n
    return call(
        finish_mixer_kernel, PIECES, [ANYWHERE] * PIECES,
        [pl.BlockSpec((rows, n), lambda i, t: (i, 0))] * 3 + [pl.BlockSpec((part, rows), lambda i, t: (0, i))],
        [sds((width, n), F32)] * 3 + [sds((part, width), F32)],
        (0, 6 * total * width), "finish_mixer",
        [pltpu.VMEM((PIECES, rows, total), BF16), pltpu.SemaphoreType.DMA((PIECES,))], prefetch=1,
    )(ids, *pieces)


def input_back(d_qkv, w, d_b, beta_w, rows, d_mid, gain):
    count, width = rows.shape
    slots, n = w.shape[0], w.shape[3]
    full = whole((count, width))
    return call(
        input_kernel, slots,
        [pl.BlockSpec((count, n), lambda s: (0, s)), lead(1, w.shape),
         whole(d_b.shape), whole(beta_w.shape), full, full, whole(gain.shape)],
        [full, whole((8, width))],
        [sds((count, width), BF16), sds((8, width), F32)],
        (2 * count * width * n * slots, 2 * slots * width * n), "input_back",
        [pltpu.VMEM((count, width), F32)],
    )(d_qkv, w, d_b, beta_w, rows, d_mid, gain)


def swap(x, mask_of, size):
    return lax.ppermute(x, "dp", [(i, i ^ mask_of(i)) for i in range(size)])


def first(i):
    return 4 if i & 1 else 2


def second(i):
    return 2 if i & 1 else 4


def across(i):
    return 1


def from_ahead(x, k, size):
    return lax.ppermute(x, "tensor", [(i, (i - k) % size) for i in range(size)])


def to_ahead(x, k, size):
    return lax.ppermute(x, "tensor", [(i, (i + k) % size) for i in range(size)])


def plane_gather(own, dp):
    b = swap(own, first, dp)
    c = swap(own, second, dp)
    d = swap(b, second, dp)
    near = [own, b, c, d]
    return near + [swap(piece, across, dp) for piece in near]


def piece_ids(own):
    core = own & 1
    f = jnp.where(core == 1, 4, 2)
    s = jnp.where(core == 1, 2, 4)
    return jnp.stack([own, own ^ f, own ^ s, own ^ 6, own ^ 1, own ^ 1 ^ s, own ^ 1 ^ f, own ^ 7])


def sync(*xs):
    return lax.optimization_barrier(xs)


def add(a, b):
    return (a.astype(F32) + b.astype(F32)).astype(BF16)


class Reduction:
    def __init__(self, grads, order, dp, tensor):
        self.order, self.dp, self.tensor = order, dp, tensor
        self.theirs, self.ours = list(grads[0::2]), list(grads[1::2])
        self.across_in = [swap(g, across, dp) for g in self.theirs]
        self.first_in, self.second_in, self.parts = {}, {}, {}
        self.last = None

    def tie(self, *xs):
        if self.last is None:
            self.last = self.ours[0]
            *xs, self.ours[0] = sync(*xs, self.last)
            return xs
        *xs, self.last = sync(*xs, self.last)
        return xs

    def add(self, kept, came):
        if self.last is not None:
            kept, came, _ = sync(kept, came, self.last)
        self.last = add(kept, came)
        return self.last

    def across(self, i):
        total = self.add(self.ours[i], self.across_in[i])
        self.first_in[i] = (total[:2], swap(total[2:], first, self.dp))

    def first(self, i):
        total = self.add(*self.first_in[i])
        self.second_in[i] = (total[0], swap(total[1], second, self.dp))

    def second(self, i):
        slot = self.order[i]
        total = self.add(*self.second_in[i])
        if slot and slot < self.tensor - 1:
            if slot + 1 < self.tensor - 1:
                total = self.add(total, self.parts[slot + 1])
            self.parts[slot] = to_ahead(total, 1, self.tensor)
        else:
            self.parts[slot] = to_ahead(total, slot, self.tensor) if slot else total

    def result(self):
        parts = [self.parts[0]] + [self.parts[k] for k in {1, self.tensor - 1}]
        self.last = sum(p.astype(F32) for p in parts).astype(BF16)
        return self.last


def reduce_far(total, dp):
    mask = PIECES
    while mask < dp:
        total = add(total, swap(total, lambda i: mask, dp))
        mask *= 2
    return total


def norm_rows(rows, gain):
    rstd = lax.rsqrt(jnp.mean(rows * rows, axis=-1, keepdims=True) + EPS)
    return rows * rstd * gain


def project_t(left, right):
    return jnp.einsum("th,td->hd", left, right, preferred_element_type=F32)


def shards(dp, tensor, layer_input, segment, d_out, norm1_gain, w_query, w_key, w_value, w_beta,
           conv_weight, w_out, norm2_gain, w_gate, w_up, w_down):
    micro, _, tokens, width = layer_input.shape
    count = micro * tokens
    local_heads = w_query.shape[1] // HD
    heads = local_heads * tensor
    hidden = w_gate.shape[1]
    own = lax.axis_index("dp") % PIECES
    place = lax.axis_index("tensor")
    ids = piece_ids(own)
    gain1 = norm1_gain.astype(F32)[None]
    gain2 = norm2_gain.astype(F32)[None]
    mine = own[None].astype(jnp.int32)
    every = jnp.arange(PIECES, dtype=jnp.int32)

    pack = (w_query, w_key, w_value, w_beta.T, conv_weight)
    pack_f = (w_gate.T, w_up.T, w_down, w_out)
    piece = pack_mixer(mine, *pack)[0]
    others = [from_ahead(piece, k, tensor) for k in range(1, tensor)]
    rows = layer_input.reshape(count, width)
    _, rows, mine, every = sync(piece, rows, mine, every)
    normed1 = norm_rows(rows.astype(F32), gain1).astype(BF16)
    mixer_in = normed1.reshape(micro, tokens, width)
    ahead = [(i, i + 1) for i in range(tensor - 1)]
    behind = [(i + 1, i) for i in range(tensor - 1)]
    halo = lax.ppermute(mixer_in[:, tokens - HALO :], "tensor", ahead)
    mixer_own = pack_mixer(every, *pack)
    piece = pack_ffn(mine, *pack_f)[0]

    *others, halo, mixer_own, piece, every = sync(*others, halo, mixer_own, piece, every)
    mixer_others = jnp.stack(others)
    b, c = swap(mixer_others, first, dp), swap(mixer_others, second, dp)
    ffn_others = {k: from_ahead(piece, k, tensor) for k in (1, tensor - 1)}
    ffn_own = pack_ffn(every, *pack_f)
    mixer_others, b, c, ffn_own = sync(mixer_others, b, c, ffn_own)
    d = swap(b, second, dp)
    mixer_pieces = [mixer_others, b, c] + [swap(x, across, dp) for x in (mixer_others, b, c)]
    d, *mixer_pieces = sync(d, *mixer_pieces)
    mixer_pieces = mixer_pieces[:3] + [d] + mixer_pieces[3:] + [swap(d, across, dp)]
    ffn_others[1], *mixer_pieces = sync(ffn_others[1], *mixer_pieces)
    for k in range(2, tensor - 1):
        ffn_others[k] = from_ahead(ffn_others[k - 1], 1, tensor)

    seg = jnp.pad(segment[:, 0].astype(F32), ((0, 0), (HALO, 0)), constant_values=-1)
    seg = lax.dynamic_slice_in_dim(seg, place * tokens, HALO + tokens, 1)
    seg_row = jnp.broadcast_to(seg[:, None, HALO:], (micro, 8, tokens))
    seg = seg[..., None]

    part = local_heads * HD
    (mixer_w, beta, taps, beta_w, proj, qk, inv, scores, base, mix, keep, gain, state) = mixer_local(
        ids, mixer_in, halo, seg, seg_row, mixer_own, mixer_pieces, heads
    )
    state, *others = sync(state, *(ffn_others[k] for k in range(1, tensor)))
    near = [jnp.stack(others)]
    near += [swap(near[0], first, dp), swap(near[0], second, dp)]
    state = hop(lax.ppermute(state, "tensor", ahead), keep, gain, tensor, False)
    state, *near = sync(state, *near)
    near.append(swap(near[1], second, dp))
    far = [swap(piece, across, dp) for piece in near[:3]]
    for step in range(1, tensor - 1):
        state = lax.ppermute(state, "tensor", ahead)
        if step < tensor - 2:
            state = hop(state, keep, gain, tensor, False)
    state, near[3] = sync(state, near[3])
    far.append(swap(near[3], across, dp))
    mixed, update = mixer_output(qk, scores, base, mix, state, seg, tensor)
    mixed = mixed.reshape(count, heads * HD)

    out_grad = d_out.reshape(count, width)
    table = jnp.stack([ids[i] for i in (4, 6, 5, 7, 0, 2, 1, 3)])
    output, d_mid, d_mid_low, d_mixed, gain2_part, *grads = ffn(
        ids, table, mixed, rows, out_grad, gain2, ffn_own, near + far, hidden
    )
    order = reduce_order(tensor)
    red = Reduction(grads, order, dp, tensor)

    d_mixed = d_mixed.reshape(micro, tokens, heads * HD)
    y0, back_gain, d_state = mixer_back_local(d_mixed, qk, inv, scores, beta, seg, tensor)
    (d_state,) = red.tie(d_state)
    recv = lax.ppermute(d_state, "tensor", behind)
    red.across(0)
    red.across(1)
    (recv,) = red.tie(recv)
    recv = lax.ppermute(hop(recv, keep, back_gain, tensor, True), "tensor", behind)
    red.across(2)
    red.first(0)
    red.across(3)
    (recv,) = red.tie(recv)
    recv = lax.ppermute(hop(recv, keep, back_gain, tensor, True), "tensor", behind)
    red.first(1)
    red.second(0)
    red.first(2)
    (recv,) = red.tie(recv)
    d_qkv, tail, front, d_beta, d_taps = mixer_back(
        d_mixed, y0, qk, inv, update, state, recv, proj, taps, beta, seg, seg_row, tensor
    )
    front, d_beta = red.tie(front, d_beta)
    front = lax.ppermute(front, "tensor", behind)
    red.second(1)
    red.first(3)
    red.second(2)
    (front,) = red.tie(front)
    front = jnp.roll(front, 3 * part, axis=2)
    d_qkv = lax.dynamic_update_slice(d_qkv, (tail + front).astype(BF16), (0, tokens - HALO, 0))
    d_qkv = d_qkv.reshape(count, heads * 3 * HD)
    d_b = d_beta.reshape(count, HD).astype(BF16)
    grads = grad_mixer(table, normed1, d_qkv, d_mid_low, mixed, tensor)
    mix_red = Reduction(grads, order, dp, tensor)
    mix_red.ours[0], d_qkv = sync(mix_red.ours[0], d_qkv)
    input_grad, gain1_part = input_back(
        d_qkv, mixer_w, d_b, beta_w.reshape(-1, width), rows, d_mid, gain1
    )
    (gain1_part,) = red.tie(gain1_part)
    red.second(3)
    total = reduce_far(red.result(), dp)
    total, gain1_part = sync(total, gain1_part)
    near = [total, swap(total, first, dp), swap(total, second, dp)]
    (gain1_part,) = mix_red.tie(gain1_part)
    mix_red.across(0)
    mix_red.across(1)
    mix_red.across(2)
    mix_red.across(3)
    *near, mix_red.last = sync(*near, mix_red.last)
    near.append(swap(near[1], second, dp))
    far = [swap(piece, across, dp) for piece in near[:3]]
    mix_red.first(0)
    mix_red.first(1)
    mix_red.first(2)
    mix_red.first(3)
    near[3], mix_red.last = sync(near[3], mix_red.last)
    far.append(swap(near[3], across, dp))
    mix_red.second(0)
    mix_red.second(1)
    mix_red.second(2)
    mix_red.second(3)
    *pieces, mix_red.last = sync(*near, *far, mix_red.last)
    grad_gate, grad_up, grad_down = finish_ffn(ids, pieces, hidden)
    total = reduce_far(mix_red.result(), dp)
    grad_q, grad_k, grad_v, grad_out = finish_mixer(ids, plane_gather(total, dp), part)

    grad_b = project_t(d_b, normed1)[::LANES]
    span = width // tensor
    d_taps = d_taps[:, :12].reshape(tensor, local_heads, 12, HD)
    d_taps = jnp.swapaxes(d_taps, 1, 2).reshape(tensor, -1)
    packed = []
    for k in range(tensor):
        at = ((place + k) % tensor) * span
        packed.append(
            jnp.concatenate(
                [
                    grad_b[k * local_heads : (k + 1) * local_heads].reshape(-1),
                    d_taps[k],
                    lax.dynamic_slice_in_dim(gain1_part[0], at, span),
                    lax.dynamic_slice_in_dim(gain2_part[0], at, span),
                ]
            )
        )
    packed = sum([packed[0]] + [to_ahead(packed[k], k, tensor) for k in range(1, tensor)])
    mask = 1
    while mask < dp:
        packed = packed + swap(packed, lambda i: mask, dp)
        mask *= 2
    cut = local_heads * width
    grad_beta = packed[:cut].reshape(local_heads, width).T
    grad_conv = packed[cut : cut + 12 * span].reshape(3, 4, span)
    cut += 12 * span
    grad_gain1 = packed[cut : cut + span]
    grad_gain2 = packed[cut + span : cut + 2 * span]
    return (
        output.reshape(micro, 1, tokens, width),
        input_grad.reshape(micro, 1, tokens, width),
        grad_gain1,
        grad_q,
        grad_k,
        grad_v,
        grad_beta,
        grad_conv,
        grad_out,
        grad_gain2,
        grad_gate.T,
        grad_up.T,
        grad_down,
    )


def solution(mesh):
    in_specs = (
        P(None, "dp", "tensor", None),
        P(None, "dp", None),
        P(None, "dp", "tensor", None),
        P(),
        P(None, "tensor"),
        P(None, "tensor"),
        P(None, "tensor"),
        P(None, "tensor"),
        P(None, None, "tensor"),
        P("tensor", None),
        P(),
        P(None, "tensor"),
        P(None, "tensor"),
        P("tensor", None),
    )
    out_specs = (
        P(None, "dp", "tensor", None),
        P(None, "dp", "tensor", None),
        P("tensor"),
        P(None, "tensor"),
        P(None, "tensor"),
        P(None, "tensor"),
        P(None, "tensor"),
        P(None, None, "tensor"),
        P("tensor", None),
        P("tensor"),
        P(None, "tensor"),
        P(None, "tensor"),
        P("tensor", None),
    )
    body = functools.partial(shards, mesh.shape["dp"], mesh.shape["tensor"])
    return jax.shard_map(body, mesh=mesh, in_specs=in_specs, out_specs=out_specs, check_vma=False)
```

time: 732 us -> 500 us (0.68)
  local copies, waits for them, and re-layouts: 157 us -> 23 us
  matrix products: 63.8 us -> 0.32 us
  other arithmetic: 65.3 us -> 26.1 us
  waiting for transfers between devices: 105 us -> 143 us
  Pallas kernels: 202 us -> 182 us
  starting transfers between devices: 125 us -> 115 us
    dot_general x14 -> x1, matrix products: 63.8 us -> 0.32 us  [project_t(): return jnp.einsum('th,td->hd', left, right, preferred_element_type=F32)]
    ppermute x57 -> x55, waiting for transfers between devices: 34.3 us -> 94.5 us  [swap(): return lax.ppermute(x, 'dp', [(i, i ^ mask_of(i)) for i in range(size)])]
    ppermute x13 -> x0, local copies, waits for them, and re-layouts: 37.8 us -> none  [the longest x10 32.3 us: swap(): return lax.ppermute(x, 'dp', [(i, i ^ mask_of(i)) for i in range(size)])]
    ppermute x15 -> x9, waiting for transfers between devices: 43.9 us -> 7.34 us  [to_ahead(): return lax.ppermute(x, 'tensor', [(i, (i + k) % size) for i in range(size)])]
    ppermute x9 -> x6, starting transfers between devices: 32.2 us -> 9 us  [from_ahead(): return lax.ppermute(x, 'tensor', [(i, (i - k) % size) for i in range(size)])]
    unnamed x193 -> x100, local copies, waits for them, and re-layouts: 26.8 us -> 5.82 us
    reshape x9 -> x1, local copies, waits for them, and re-layouts: 20.4 us -> 0.61 us  [shards(): grad_conv = packed[cut:cut + 12 * span].reshape(3, 4, span)]
    pallas_call x18 -> x17, Pallas kernels: 202 us -> 182 us  [the longest x1 45.1 us: ffn(): call(functools.partial(ffn_kernel, hidden), 2 * slots, [pl.BlockSpec((cou...]
  transfers between devices with their start and end apart: 89 -> 78, of which waited for: 23 -> 29; matrix products, arithmetic and copies ran while one was open for 29% -> 9% of each run, Pallas kernels for 24% -> 26%
where the time goes in v2:
time: 500 us; the launch traced here: 491 us
  Pallas kernels  182 us (36%)
  waiting for transfers between devices  143 us (29%)
  starting transfers between devices  115 us (23%)
  other arithmetic  26.1 us (5%)
  local copies, waits for them, and re-layouts  23 us (5%)
    ppermute x55, waiting for transfers between devices, swap(): return lax.ppermute(x, 'dp', [(i, i ^ mask_of(i)) for i in range(size)])  94.5 us
    ppermute x55, starting transfers between devices, swap(): return lax.ppermute(x, 'dp', [(i, i ^ mask_of(i)) for i in range(size)])  67.1 us
    pallas_call x1, Pallas kernels, ffn(): call(functools.partial(ffn_kernel, hidden), 2 * slots, [pl.BlockSpec((cou...  45.1 us
    pallas_call x1, Pallas kernels, mixer_back(): call(back_kernel, slots, [columns(tokens, HD)] + [lead(per, a.shape) for...  26.3 us
    pallas_call x1, Pallas kernels, mixer_local(): call(local_kernel, slots, [whole(x.shape), whole(halo.shape), whole(seg.s...  26 us
    convert_element_type x24, other arithmetic, add(): return (a.astype(F32) + b.astype(F32)).astype(BF16)  21.3 us
    ppermute x9, starting transfers between devices, to_ahead(): return lax.ppermute(x, 'tensor', [(i, (i + k) % size) for i in range(size)])  16.5 us
    pallas_call x4, Pallas kernels, hop(): call(functools.partial(hop_kernel, back), slots, [rolled(per, state.shape...  16.2 us
  transfers between devices with their start and end apart: 78, of which 29 were waited for; matrix products, arithmetic and copies ran while one was open for 9% of the time, Pallas kernels for 26%

profile of v2, /device:TPU:1, one launch (start us, length us, event | category | flops | bytes accessed | tf_op | source)
XLA Modules:
  0.0 491.1 jit_solution(9503602968626806875)
XLA Ops:
  2.4 4.2 collective-permute-start
  8.2 4.1 collective-permute-start.3
  12.3 6.2 %pack_mixer.3.own_ref = bf16[8,144,768]{2,1,0:T(8,128)(2,1)} custom-call(s32[8]{0:T(128)} %iota.3.table_ref, bf16[1024,256]{1,0:T(8,128)(2,1)} %q_ref.3, bf16[1024,256]{1,0:T(8,128)(2,1)} %k_ref.3, bf16[1024,256]{1,0:T(8,128)(2,1)} %v_ref.3, bf16[2,1024]{1,0:T(2,128)(2,1)} %bitcast.156, bf16[3,4,256]{2,1,0:T(4,128)(2,1)} %conv_ref.3), custom_call_target="tpu_custom_call" | custom-call | bytes 3145728 | tf_op jit(solution)/shard_map/pack_mixer/pallas_call | solution.py:698
  18.5 2.2 pack_ffn.2
  21.9 3.1 collective-permute-done.1
  27.6 8.6 %pack_ffn.3.own_ref = bf16[8,128,2432]{2,1,0:T(8,128)(2,1)} custom-call(s32[8]{0:T(128)} %iota.3.table_ref, bf16[704,1024]{1,0:T(8,128)(2,1)} %bitcast.119, bf16[704,1024]{1,0:T(8,128)(2,1)} %bitcast.121, bf16[704,1024]{1,0:T(8,128)(2,1)} %down_ref.3, bf16[256,1024]{1,0:T(8,128)(2,1)} %out_w_ref.3), custom_call_target="tpu_custom_call" | custom-call | bytes 9961472 | tf_op jit(solution)/shard_map/pack_ffn/pallas_call | solution.py:711
  36.3 2.3 collective-permute-done.5.refs_1_
  38.5 4.1 collective-permute-done.6.refs_2_
  45.5 8.2 %collective-permute-done.7.refs_3_ = bf16[3,144,768]{2,1,0:T(8,128)(2,1)} collective-permute-done((bf16[3,144,768]{2,1,0:T(8,128)(2,1)S(1)}, bf16[3,144,768]{2,1,0:T(8,128)(2,1)}, u32[]{:S(2)}, u32[]{:S(2)}) %collective-permute-start.7) | collective-permute-done | bytes 663584 | tf_op jit(solution)/shard_map/ppermute | solution.py:922
  57.1 1.8 collective-permute-start.13
  58.9 11.7 %collective-permute-done.4 = bf16[128,2432]{1,0:T(8,128)(2,1)S(1)} collective-permute-done((bf16[128,2432]{1,0:T(8,128)(2,1)S(1)}, bf16[128,2432]{1,0:T(8,128)(2,1)S(1)}, u32[]{:S(2)}, u32[]{:S(2)}) %collective-permute-start.4) | collective-permute-done | bytes 622624 | tf_op jit(solution)/shard_map/ppermute | solution.py:938
  70.6 2.0 collective-permute-start.12
  73.3 26.0 %mixer_local.1 = (bf16[4,8,144,768]{3,2,1,0:T(8,128)(2,1)}, f32[2,256,128]{2,1,0:T(8,128)}, f32[8,16,128]{2,1,0:T(8,128)}, bf16[4,32,1024]{2,1,0:T(8,128)(2,1)},...) custom-call(s32[8]{0:T(128)} %stack.62.ids_ref, ...), custom_call_target="tpu_custom_call" | custom-call | flops 16000000000 | bytes 32000000 | tf_op jit(solution)/shard_map/mixer_local/pallas_call | solution.py:740
  103.1 3.2 collective-permute-start.14
  106.2 9.2 %collective-permute-done.14.state_ref = bf16[8,2,128,128]{3,2,1,0:T(8,128)(2,1)S(1)} collective-permute-done((bf16[8,2,128,128]{3,2,1,0:T(8,128)(2,1)S(1)}, bf16[8,2,128,128]{3,2,1,0:T(8,128)(2,1)S(1)}, u32[]{:S(2)}, u32[]{:S(2)}) %collective-permute-start.14) | collective-permute-done | bytes 524320 | tf_op jit(solution)/shard_map/ppermute | solution.py:1086
  116.2 4.0 hop.4
  120.2 18.7 %collective-permute-done.15.refs_1_ = bf16[3,128,2432]{2,1,0:T(8,128)(2,1)} collective-permute-done((bf16[3,128,2432]{2,1,0:T(8,128)(2,1)S(1)}, bf16[3,128,2432]{2,1,0:T(8,128)(2,1)}, u32[]{:S(2)}, u32[]{:S(2)}) %collective-permute-start.15) | collective-permute-done | bytes 1867808 | tf_op jit(solution)/shard_map/ppermute | solution.py:922
  138.9 1.9 collective-permute-done.16.refs_2_
  142.0 5.7 %collective-permute-start.17 = (bf16[8,2,128,128]{3,2,1,0:T(8,128)(2,1)}, bf16[8,2,128,128]{3,2,1,0:T(8,128)(2,1)S(1)}, u32[]{:S(2)}, u32[]{:S(2)}) collective-permute-start(bf16[8,2,128,128]{3,2,1,0:T(8,128)(2,1)} %hop.4), channel_id=1, source_target_pairs={{0,1},{1,2},{2,3},{4,5},{5,6},{6,7},{8,9},{9,10},{10,11},{12,13},{... | collective-permute-start | bytes 1572872 | tf_op jit(solution)/shard_map/ppermute | solution.py:1091
  147.7 9.4 %collective-permute-done.17.state_ref = bf16[8,2,128,128]{3,2,1,0:T(8,128)(2,1)S(1)} collective-permute-done((bf16[8,2,128,128]{3,2,1,0:T(8,128)(2,1)}, bf16[8,2,128,128]{3,2,1,0:T(8,128)(2,1)S(1)}, u32[]{:S(2)}, u32[]{:S(2)}) %collective-permute-start.17) | collective-permute-done | bytes 524320 | tf_op jit(solution)/shard_map/ppermute | solution.py:1091
  157.9 4.0 hop.5
  161.9 4.3 collective-permute-start.18
  166.2 3.2 collective-permute-start.21
  169.9 4.7 collective-permute-done.18.state_ref
  174.6 3.8 collective-permute-start.23
  179.7 6.1 %mixer_output.1 = (bf16[2,256,1024]{2,1,0:T(8,128)(2,1)}, bf16[8,2,256,128]{3,2,1,0:T(8,128)(2,1)}) custom-call(bf16[8,2,256,256]{3,2,1,0:T(8,128)(2,1)} %get-tuple-element.212.qk_ref, bf16[8,2,256,256]{3,2,1,0:T(8,128)(2,1)} %get-tuple-element.213.p_ref, f32[8,2,256,128]{3,2,1,0:T(8,128)} %get-tuple-element.214.ub_ref, ...), custom_call_target="tpu_custom_call" | custom-call | flops 800000000 | bytes 8000000 | tf_op jit(solution)/shard_map/mixer_output/pallas_call | solution.py:765
  185.8 45.1 %ffn.1 = (bf16[512,1024]{1,0:T(8,128)(2,1)}, f32[512,1024]{1,0:T(8,128)}, bf16[512,1024]{1,0:T(8,128)(2,1)}, f32[512,1024]{1,0:T(8,128)}, f32[8,1024]{1,0:T(8,12...) custom-call(s32[8]{0:T(128)} %stack.62.ids_ref, ...), custom_call_target="tpu_custom_call" | custom-call | flops 38386270208 | bytes 60000000 | tf_op jit(solution)/shard_map/ffn/pallas_call | solution.py:836
  231.5 9.3 %mixer_back_local.1 = (f32[8,2,256,128]{3,2,1,0:T(8,128)}, f32[8,2,128,128]{3,2,1,0:T(8,128)}, bf16[8,2,128,128]{3,2,1,0:T(8,128)(2,1)}) custom-call(f32[2,256,1024]{2,1,0:T(8,128)} %bitcast.126, bf16[8,2,256,256]{3,2,1,0:T(8,128)(2,1)} %get-tuple-element.212.qk_ref, bf16[8,2,256,256]{3,2,1,0:T(8,128)(2,1)} %get-tuple-element.234.t_ref, ...), custom_call_target="tpu_custom_call" | custom-call | flops 800000000 | bytes 8000000 | tf_op jit(solution)/shard_map/mixer_back_local/pallas_call | solution.py:780
  244.0 2.3 add_convert_fusion.3
  246.3 2.1 add_convert_fusion.2
  249.6 4.5 collective-permute-start.34
  258.4 4.1 hop.6
  263.8 3.8 collective-permute-done.34
  270.0 14.8 %collective-permute-done.29 = bf16[2,128,2176]{2,1,0:T(8,128)(2,1)} collective-permute-done((bf16[2,128,2176]{2,1,0:T(8,128)(2,1)}, bf16[2,128,2176]{2,1,0:T(8,128)(2,1)}, u32[]{:S(2)}, u32[]{:S(2)}) %collective-permute-start.29) | collective-permute-done | bytes 1114144 | tf_op jit(solution)/shard_map/ppermute | solution.py:922
  287.4 2.1 add_convert_fusion
  291.9 4.1 hop.7
  297.4 5.1 %collective-permute-done.33 = bf16[128,2176]{1,0:T(8,128)(2,1)} collective-permute-done((bf16[128,2176]{1,0:T(8,128)(2,1)}, bf16[128,2176]{1,0:T(8,128)(2,1)}, u32[]{:S(2)}, u32[]{:S(2)}) %collective-permute-start.33) | collective-permute-done | bytes 557088 | tf_op jit(solution)/shard_map/ppermute | solution.py:922
  302.4 2.0 add_convert_fusion.17
  304.4 2.8 collective-permute-start.39
  311.1 26.3 %mixer_back.1 = (bf16[2,256,3072]{2,1,0:T(8,128)(2,1)}, f32[2,16,3072]{2,1,0:T(8,128)}, f32[2,16,3072]{2,1,0:T(8,128)}, f32[2,256,128]{2,1,0:T(8,128)}, f32[8,16,128]{2,1,0:T(8,128)}) custom-call(f32[2,256,1024]{2,1,0:T(8,128)} %bitcast.127, f32[8,2,256,128]{3,2,1,0:T(8,128)} %get-tuple-element.236.y_ref, ...), custom_call_target="tpu_custom_call" | custom-call | flops 8000000000 | bytes 32000000 | tf_op jit(solution)/shard_map/mixer_back/pallas_call | solution.py:794
  343.0 2.1 collective-permute-start.41
  347.9 2.1 collective-permute-start.42
  354.0 10.6 %grad_mixer.1 = (bf16[4,128,1024]{2,1,0:T(8,128)(2,1)}, bf16[4,128,1024]{2,1,0:T(8,128)(2,1)}, bf16[4,128,1024]{2,1,0:T(8,128)(2,1)}, bf16[4,128,1024]{2,1,0:T(8...) custom-call(s32[8]{0:T(128)} %stack.63.table_ref, ...), custom_call_target="tpu_custom_call" | custom-call | flops 4294967296 | bytes 8388608 | tf_op jit(solution)/shard_map/grad_mixer/pallas_call | solution.py:872
  364.6 10.1 %input_back.1 = (bf16[512,1024]{1,0:T(8,128)(2,1)}, f32[8,1024]{1,0:T(8,128)}) custom-call(bf16[512,3072]{1,0:T(8,128)(2,1)} %bitcast.125, bf16[4,8,144,768]{3,2,1,0:T(8,128)(2,1)} %get-tuple-element.288.w_ref, bf16[512,128]{1,0:T(8,128)(2,1)} %bitcast.129, bf16[128,1024]{1,0:T(8,128)(2,1)} %bitcast.135, bf16[512,1024]{1,0:T(8,128)(2,1)} %bitcast.115, ...), custom_call_target="tpu_custom_call" | custom-call | flops 3221225472 | bytes 6291456 | tf_op jit(solution)/shard_map/input_back/pallas_call | solution.py:910
  374.8 11.6 %collective-permute-start.52 = (bf16[4,128,1024]{2,1,0:T(8,128)(2,1)}, bf16[4,128,1024]{2,1,0:T(8,128)(2,1)S(1)}, u32[]{:S(2)}, u32[]{:S(2)}) collective-permute-start(bf16[4,128,1024]{2,1,0:T(8,128)(2,1)} %get-tuple-element.308), channel_id=1, source_target_pairs={{0,4},{4,0},{8,12},{12,8},{16,20},{20,16},{24,28},{28,24},{1,5},{5... | collective-permute-start | bytes 3145736 | tf_op jit(solution)/shard_map/ppermute | solution.py:922
  387.3 1.8 collective-permute-start.71
  390.0 3.0 collective-permute-start.72
  393.4 1.8 collective-permute-start.43
  401.1 5.0 %collective-permute-done.72.refs_2_ = bf16[128,2176]{1,0:T(8,128)(2,1)S(1)} collective-permute-done((bf16[128,2176]{1,0:T(8,128)(2,1)S(1)}, bf16[128,2176]{1,0:T(8,128)(2,1)S(1)}, u32[]{:S(2)}, u32[]{:S(2)}) %collective-permute-start.72) | collective-permute-done | bytes 557088 | tf_op jit(solution)/shard_map/ppermute | solution.py:922
  406.2 1.8 collective-permute-done.56
  409.6 3.9 collective-permute-done.55
  415.3 3.9 collective-permute-done.54
  419.4 5.4 %collective-permute-done.53 = bf16[2,128,1024]{2,1,0:T(8,128)(2,1)S(1)} collective-permute-done((bf16[2,128,1024]{2,1,0:T(8,128)(2,1)S(1)}, bf16[2,128,1024]{2,1,0:T(8,128)(2,1)S(1)}, u32[]{:S(2)}, u32[]{:S(2)}) %collective-permute-start.53) | collective-permute-done | bytes 524320 | tf_op jit(solution)/shard_map/ppermute | solution.py:922
  424.8 2.9 collective-permute-start.60
  427.9 3.8 collective-permute-done.60
  431.8 2.6 collective-permute-start.61
  436.1 3.8 collective-permute-done.61
  441.6 2.6 collective-permute-start.62
  445.0 3.8 collective-permute-start.46
  452.5 3.6 collective-permute-done.63
  459.7 4.5 collective-permute-done.48
  466.9 3.3 collective-permute-done.65.refs_2_
  475.9 7.8 %finish_ffn.1 = (f32[704,1024]{1,0:T(8,128)}, f32[704,1024]{1,0:T(8,128)}, f32[704,1024]{1,0:T(8,128)}) custom-call(s32[8]{0:T(128)} %stack.62.ids_ref, bf16[128,2176]{1,0:T(8,128)(2,1)} %copy-done.3, bf16[128,2176]{1,0:T(8,128)(2,1)} %copy-done.19, bf16[128,2176]{1,0:T(8,128)(2,1)} %copy-done.20, bf16[128,2176]{1,0:T(8,128)(2,1)} %copy-done.21, ...), custom_call_target="tpu_custom_call" | custom-call | bytes 13369344 | tf_op jit(solution)/shard_map/finish_ffn/pallas_call | solution.py:884
  485.3 5.7 %finish_mixer.1 = (f32[1024,256]{1,0:T(8,128)}, f32[1024,256]{1,0:T(8,128)}, f32[1024,256]{1,0:T(8,128)}, f32[256,1024]{1,0:T(8,128)}) custom-call(s32[8]{0:T(128)} %stack.62.ids_ref, bf16[128,1024]{1,0:T(8,128)(2,1)} %copy-done.15, bf16[128,1024]{1,0:T(8,128)(2,1)} %copy-done.29, bf16[128,1024]{1,0:T(8,128)(2,1)} %collective-permute-done.65.refs_2_, ...), custom_call_target="tpu_custom_call" | custom-call | bytes 6291456 | tf_op jit(solution)/shard_map/finish_mixer/pallas_call | solution.py:897
  (290 shorter events, 90.5 us)
Async XLA Ops:
  2.4 19.5 %collective-permute-start = (bf16[144,768]{1,0:T(8,128)(2,1)}, bf16[144,768]{1,0:T(8,128)(2,1)S(1)}, u32[]{:S(2)}, u32[]{:S(2)}) collective-permute-start(bf16[144,768]{1,0:T(8,128)(2,1)} %bitcast.136), channel_id=1, source_target_pairs={{0,3},{1,0},{2,1},{3,2},{4,7},{5,4},{6,5},{7,6},{8,11},{9,8},{10,9... | collective-permute-start | bytes 663560 | tf_op jit(solution)/shard_map/ppermute | solution.py:938
  6.6 18.4 %collective-permute-start.1 = (bf16[144,768]{1,0:T(8,128)(2,1)}, bf16[144,768]{1,0:T(8,128)(2,1)S(1)}, u32[]{:S(2)}, u32[]{:S(2)}) collective-permute-start(bf16[144,768]{1,0:T(8,128)(2,1)} %bitcast.137), channel_id=1, source_target_pairs={{0,2},{1,3},{2,0},{3,1},{4,6},{5,7},{6,4},{7,5},{8,10},{9,11},{10,... | collective-permute-start | bytes 663560 | tf_op jit(solution)/shard_map/ppermute | solution.py:938
  6.6 18.4 %collective-permute-start.2 = (bf16[144,768]{1,0:T(8,128)(2,1)}, bf16[144,768]{1,0:T(8,128)(2,1)S(1)}, u32[]{:S(2)}, u32[]{:S(2)}) collective-permute-start(bf16[144,768]{1,0:T(8,128)(2,1)} %bitcast.138), channel_id=1, source_target_pairs={{0,1},{1,2},{2,3},{3,0},{4,5},{5,6},{6,7},{7,4},{8,9},{9,10},{10,1... | collective-permute-start | bytes 663560 | tf_op jit(solution)/shard_map/ppermute | solution.py:938
  8.2 13.7 %collective-permute-start.3 = (bf16[2,16,1024]{2,1,0:T(8,128)(2,1)S(1)}, bf16[2,16,1024]{2,1,0:T(8,128)(2,1)S(1)}, u32[]{:S(2)}, u32[]{:S(2)}) collective-permute-start(bf16[2,16,1024]{2,1,0:T(8,128)(2,1)S(1)} %slice.220), channel_id=1, source_target_pairs={{0,1},{1,2},{2,3},{4,5},{5,6},{6,7},{8,9},{9,10},{10,11},{12,13},{... | collective-permute-start | bytes 196616 | tf_op jit(solution)/shard_map/ppermute | solution.py:1056
  25.1 13.4 %collective-permute-start.5 = (bf16[3,144,768]{2,1,0:T(8,128)(2,1)S(1)}, bf16[3,144,768]{2,1,0:T(8,128)(2,1)S(1)}, u32[]{:S(2)}, u32[]{:S(2)}) collective-permute-start(bf16[3,144,768]{2,1,0:T(8,128)(2,1)S(1)} %pad_maximum_fusion.1.refs_0_), channel_id=1, source_target_pairs={{0,8},{4,20},{8,0},{12,28},{16,24},{20,4},{24,16},{28,12},{1,9},{5... | collective-permute-start | bytes 1990664 | tf_op jit(solution)/shard_map/ppermute | solution.py:922
  26.4 16.2 %collective-permute-start.6 = (bf16[3,144,768]{2,1,0:T(8,128)(2,1)S(1)}, bf16[3,144,768]{2,1,0:T(8,128)(2,1)S(1)}, u32[]{:S(2)}, u32[]{:S(2)}) collective-permute-start(bf16[3,144,768]{2,1,0:T(8,128)(2,1)S(1)} %pad_maximum_fusion.1.refs_0_), channel_id=1, source_target_pairs={{0,16},{4,12},{8,24},{12,4},{16,0},{20,28},{24,8},{28,20},{1,17},{... | collective-permute-start | bytes 1990664 | tf_op jit(solution)/shard_map/ppermute | solution.py:922
  43.8 9.9 %collective-permute-start.7 = (bf16[3,144,768]{2,1,0:T(8,128)(2,1)S(1)}, bf16[3,144,768]{2,1,0:T(8,128)(2,1)}, u32[]{:S(2)}, u32[]{:S(2)}) collective-permute-start(bf16[3,144,768]{2,1,0:T(8,128)(2,1)S(1)} %collective-permute-done.5.refs_1_), channel_id=1, source_target_pairs={{0,16},{4,12},{8,24},{12,4},{16,0},{20,28},{24,8},{28,20},{1,17},{... | collective-permute-start | bytes 1990664 | tf_op jit(solution)/shard_map/ppermute | solution.py:922
  53.8 16.9 %collective-permute-start.11 = (bf16[3,144,768]{2,1,0:T(8,128)(2,1)}, bf16[3,144,768]{2,1,0:T(8,128)(2,1)}, u32[]{:S(2)}, u32[]{:S(2)}) collective-permute-start(bf16[3,144,768]{2,1,0:T(8,128)(2,1)} %collective-permute-done.7.refs_3_), channel_id=1, source_target_pairs={{0,4},{4,0},{8,12},{12,8},{16,20},{20,16},{24,28},{28,24},{1,5},{5... | collective-permute-start | bytes 1990664 | tf_op jit(solution)/shard_map/ppermute | solution.py:922
  54.8 15.8 %collective-permute-start.4 = (bf16[128,2432]{1,0:T(8,128)(2,1)S(1)}, bf16[128,2432]{1,0:T(8,128)(2,1)S(1)}, u32[]{:S(2)}, u32[]{:S(2)}) collective-permute-start(bf16[128,2432]{1,0:T(8,128)(2,1)S(1)} %bitcast.133), channel_id=1, source_target_pairs={{0,3},{1,0},{2,1},{3,2},{4,7},{5,4},{6,5},{7,6},{8,11},{9,8},{10,9... | collective-permute-start | bytes 1867784 | tf_op jit(solution)/shard_map/ppermute | solution.py:938
  57.1 42.2 %collective-permute-start.13 = (bf16[128,2432]{1,0:T(8,128)(2,1)S(1)}, bf16[128,2432]{1,0:T(8,128)(2,1)S(1)}, u32[]{:S(2)}, u32[]{:S(2)}) collective-permute-start(bf16[128,2432]{1,0:T(8,128)(2,1)S(1)} %bitcast.134), channel_id=1, source_target_pairs={{0,1},{1,2},{2,3},{3,0},{4,5},{5,6},{6,7},{7,4},{8,9},{9,10},{10,1... | collective-permute-start | bytes 1867784 | tf_op jit(solution)/shard_map/ppermute | solution.py:938
  70.6 28.7 %collective-permute-start.12 = (bf16[128,2432]{1,0:T(8,128)(2,1)S(1)}, bf16[128,2432]{1,0:T(8,128)(2,1)S(1)}, u32[]{:S(2)}, u32[]{:S(2)}) collective-permute-start(bf16[128,2432]{1,0:T(8,128)(2,1)S(1)} %collective-permute-done.4), channel_id=1, source_target_pairs={{0,3},{1,0},{2,1},{3,2},{4,7},{5,4},{6,5},{7,6},{8,11},{9,8},{10,9... | collective-permute-start | bytes 1867784 | tf_op jit(solution)/shard_map/ppermute | solution.py:938
  101.6 37.3 %collective-permute-start.15 = (bf16[3,128,2432]{2,1,0:T(8,128)(2,1)S(1)}, bf16[3,128,2432]{2,1,0:T(8,128)(2,1)}, u32[]{:S(2)}, u32[]{:S(2)}) collective-permute-start(bf16[3,128,2432]{2,1,0:T(8,128)(2,1)S(1)} %pad_maximum_fusion.refs_0_), channel_id=1, source_target_pairs={{0,8},{4,20},{8,0},{12,28},{16,24},{20,4},{24,16},{28,12},{1,9},{5... | collective-permute-start | bytes 5603336 | tf_op jit(solution)/shard_map/ppermute | solution.py:922
  101.8 39.0 %collective-permute-start.16 = (bf16[3,128,2432]{2,1,0:T(8,128)(2,1)S(1)}, bf16[3,128,2432]{2,1,0:T(8,128)(2,1)}, u32[]{:S(2)}, u32[]{:S(2)}) collective-permute-start(bf16[3,128,2432]{2,1,0:T(8,128)(2,1)S(1)} %pad_maximum_fusion.refs_0_), channel_id=1, source_target_pairs={{0,16},{4,12},{8,24},{12,4},{16,0},{20,28},{24,8},{28,20},{1,17},{... | collective-permute-start | bytes 5603336 | tf_op jit(solution)/shard_map/ppermute | solution.py:922
  103.1 12.4 %collective-permute-start.14 = (bf16[8,2,128,128]{3,2,1,0:T(8,128)(2,1)S(1)}, bf16[8,2,128,128]{3,2,1,0:T(8,128)(2,1)S(1)}, u32[]{:S(2)}, u32[]{:S(2)}) collective-permute-start(bf16[8,2,128,128]{3,2,1,0:T(8,128)(2,1)S(1)} %copy-done.45), channel_id=1, source_target_pairs={{0,1},{1,2},{2,3},{4,5},{5,6},{6,7},{8,9},{9,10},{10,11},{12,13},{... | collective-permute-start | bytes 1572872 | tf_op jit(solution)/shard_map/ppermute | solution.py:1086
  140.8 33.8 %collective-permute-start.19 = (bf16[3,128,2432]{2,1,0:T(8,128)(2,1)}, bf16[3,128,2432]{2,1,0:T(8,128)(2,1)}, u32[]{:S(2)}, u32[]{:S(2)}) collective-permute-start(bf16[3,128,2432]{2,1,0:T(8,128)(2,1)} %collective-permute-done.15.refs_1_), channel_id=1, source_target_pairs={{0,16},{4,12},{8,24},{12,4},{16,0},{20,28},{24,8},{28,20},{1,17},{... | collective-permute-start | bytes 5603336 | tf_op jit(solution)/shard_map/ppermute | solution.py:922
  142.0 15.1 %collective-permute-start.17 = (bf16[8,2,128,128]{3,2,1,0:T(8,128)(2,1)}, bf16[8,2,128,128]{3,2,1,0:T(8,128)(2,1)S(1)}, u32[]{:S(2)}, u32[]{:S(2)}) collective-permute-start(bf16[8,2,128,128]{3,2,1,0:T(8,128)(2,1)} %hop.4), channel_id=1, source_target_pairs={{0,1},{1,2},{2,3},{4,5},{5,6},{6,7},{8,9},{9,10},{10,11},{12,13},{... | collective-permute-start | bytes 1572872 | tf_op jit(solution)/shard_map/ppermute | solution.py:1091
  161.9 12.7 %collective-permute-start.18 = (bf16[8,2,128,128]{3,2,1,0:T(8,128)(2,1)}, bf16[8,2,128,128]{3,2,1,0:T(8,128)(2,1)S(1)}, u32[]{:S(2)}, u32[]{:S(2)}) collective-permute-start(bf16[8,2,128,128]{3,2,1,0:T(8,128)(2,1)} %hop.5), channel_id=1, source_target_pairs={{0,1},{1,2},{2,3},{4,5},{5,6},{6,7},{8,9},{9,10},{10,11},{12,13},{... | collective-permute-start | bytes 1572872 | tf_op jit(solution)/shard_map/ppermute | solution.py:1091
  166.2 19.6 %collective-permute-start.21 = (bf16[3,128,2432]{2,1,0:T(8,128)(2,1)}, bf16[3,128,2432]{2,1,0:T(8,128)(2,1)}, u32[]{:S(2)}, u32[]{:S(2)}) collective-permute-start(bf16[3,128,2432]{2,1,0:T(8,128)(2,1)} %collective-permute-done.15.refs_1_), channel_id=1, source_target_pairs={{0,4},{4,0},{8,12},{12,8},{16,20},{20,16},{24,28},{28,24},{1,5},{5... | collective-permute-start | bytes 5603336 | tf_op jit(solution)/shard_map/ppermute | solution.py:922
  169.4 16.3 %collective-permute-start.20 = (bf16[3,128,2432]{2,1,0:T(8,128)(2,1)S(1)}, bf16[3,128,2432]{2,1,0:T(8,128)(2,1)}, u32[]{:S(2)}, u32[]{:S(2)}) collective-permute-start(bf16[3,128,2432]{2,1,0:T(8,128)(2,1)S(1)} %pad_maximum_fusion.refs_0_), channel_id=1, source_target_pairs={{0,4},{4,0},{8,12},{12,8},{16,20},{20,16},{24,28},{28,24},{1,5},{5... | collective-permute-start | bytes 5603336 | tf_op jit(solution)/shard_map/ppermute | solution.py:922
  169.5 16.3 %collective-permute-start.22 = (bf16[3,128,2432]{2,1,0:T(8,128)(2,1)}, bf16[3,128,2432]{2,1,0:T(8,128)(2,1)}, u32[]{:S(2)}, u32[]{:S(2)}) collective-permute-start(bf16[3,128,2432]{2,1,0:T(8,128)(2,1)} %collective-permute-done.16.refs_2_), channel_id=1, source_target_pairs={{0,4},{4,0},{8,12},{12,8},{16,20},{20,16},{24,28},{28,24},{1,5},{5... | collective-permute-start | bytes 5603336 | tf_op jit(solution)/shard_map/ppermute | solution.py:922
  174.6 11.2 %collective-permute-start.23 = (bf16[3,128,2432]{2,1,0:T(8,128)(2,1)}, bf16[3,128,2432]{2,1,0:T(8,128)(2,1)}, u32[]{:S(2)}, u32[]{:S(2)}) collective-permute-start(bf16[3,128,2432]{2,1,0:T(8,128)(2,1)} %collective-permute-done.19.refs_3_), channel_id=1, source_target_pairs={{0,4},{4,0},{8,12},{12,8},{16,20},{20,16},{24,28},{28,24},{1,5},{5... | collective-permute-start | bytes 5603336 | tf_op jit(solution)/shard_map/ppermute | solution.py:922
  230.9 13.0 %collective-permute-start.26 = (bf16[4,128,2176]{2,1,0:T(8,128)(2,1)}, bf16[4,128,2176]{2,1,0:T(8,128)(2,1)}, u32[]{:S(2)}, u32[]{:S(2)}) collective-permute-start(bf16[4,128,2176]{2,1,0:T(8,128)(2,1)} %get-tuple-element.244), channel_id=1, source_target_pairs={{0,4},{4,0},{8,12},{12,8},{16,20},{20,16},{24,28},{28,24},{1,5},{5... | collective-permute-start | bytes 6684680 | tf_op jit(solution)/shard_map/ppermute | solution.py:922
  231.1 15.1 %collective-permute-start.25 = (bf16[4,128,2176]{2,1,0:T(8,128)(2,1)}, bf16[4,128,2176]{2,1,0:T(8,128)(2,1)}, u32[]{:S(2)}, u32[]{:S(2)}) collective-permute-start(bf16[4,128,2176]{2,1,0:T(8,128)(2,1)} %get-tuple-element.242), channel_id=1, source_target_pairs={{0,4},{4,0},{8,12},{12,8},{16,20},{20,16},{24,28},{28,24},{1,5},{5... | collective-permute-start | bytes 6684680 | tf_op jit(solution)/shard_map/ppermute | solution.py:922
  240.8 14.5 %collective-permute-start.30 = (bf16[4,128,2176]{2,1,0:T(8,128)(2,1)}, bf16[4,128,2176]{2,1,0:T(8,128)(2,1)S(1)}, u32[]{:S(2)}, u32[]{:S(2)}) collective-permute-start(bf16[4,128,2176]{2,1,0:T(8,128)(2,1)} %get-tuple-element.254), channel_id=1, source_target_pairs={{0,4},{4,0},{8,12},{12,8},{16,20},{20,16},{24,28},{28,24},{1,5},{5... | collective-permute-start | bytes 6684680 | tf_op jit(solution)/shard_map/ppermute | solution.py:922
  240.9 46.5 %collective-permute-start.28 = (bf16[4,128,2176]{2,1,0:T(8,128)(2,1)}, bf16[4,128,2176]{2,1,0:T(8,128)(2,1)}, u32[]{:S(2)}, u32[]{:S(2)}) collective-permute-start(bf16[4,128,2176]{2,1,0:T(8,128)(2,1)} %get-tuple-element.252), channel_id=1, source_target_pairs={{0,4},{4,0},{8,12},{12,8},{16,20},{20,16},{24,28},{28,24},{1,5},{5... | collective-permute-start | bytes 6684680 | tf_op jit(solution)/shard_map/ppermute | solution.py:922
  241.3 17.1 %collective-permute-start.24 = (bf16[8,2,128,128]{3,2,1,0:T(8,128)(2,1)}, bf16[8,2,128,128]{3,2,1,0:T(8,128)(2,1)}, u32[]{:S(2)}, u32[]{:S(2)}) collective-permute-start(bf16[8,2,128,128]{3,2,1,0:T(8,128)(2,1)} %get-tuple-element.240), channel_id=1, source_target_pairs={{1,0},{2,1},{3,2},{5,4},{6,5},{7,6},{9,8},{10,9},{11,10},{13,12},{... | collective-permute-start | bytes 1572872 | tf_op jit(solution)/shard_map/ppermute | solution.py:1110
  249.6 18.0 %collective-permute-start.34 = (bf16[2,128,2176]{2,1,0:T(8,128)(2,1)}, bf16[2,128,2176]{2,1,0:T(8,128)(2,1)}, u32[]{:S(2)}, u32[]{:S(2)}) collective-permute-start(bf16[2,128,2176]{2,1,0:T(8,128)(2,1)} %get-tuple-element.385), channel_id=1, source_target_pairs={{0,8},{4,20},{8,0},{12,28},{16,24},{20,4},{24,16},{28,12},{1,9},{5... | collective-permute-start | bytes 3342344 | tf_op jit(solution)/shard_map/ppermute | solution.py:922
  255.3 29.6 %collective-permute-start.29 = (bf16[2,128,2176]{2,1,0:T(8,128)(2,1)}, bf16[2,128,2176]{2,1,0:T(8,128)(2,1)}, u32[]{:S(2)}, u32[]{:S(2)}) collective-permute-start(bf16[2,128,2176]{2,1,0:T(8,128)(2,1)} %get-tuple-element.389), channel_id=1, source_target_pairs={{0,8},{4,20},{8,0},{12,28},{16,24},{20,4},{24,16},{28,12},{1,9},{5... | collective-permute-start | bytes 3342344 | tf_op jit(solution)/shard_map/ppermute | solution.py:922
  257.0 50.2 %collective-permute-start.32 = (bf16[2,128,2176]{2,1,0:T(8,128)(2,1)}, bf16[2,128,2176]{2,1,0:T(8,128)(2,1)}, u32[]{:S(2)}, u32[]{:S(2)}) collective-permute-start(bf16[2,128,2176]{2,1,0:T(8,128)(2,1)} %get-tuple-element.387), channel_id=1, source_target_pairs={{0,8},{4,20},{8,0},{12,28},{16,24},{20,4},{24,16},{28,12},{1,9},{5... | collective-permute-start | bytes 3342344 | tf_op jit(solution)/shard_map/ppermute | solution.py:922
  262.6 29.4 %collective-permute-start.27 = (bf16[8,2,128,128]{3,2,1,0:T(8,128)(2,1)}, bf16[8,2,128,128]{3,2,1,0:T(8,128)(2,1)}, u32[]{:S(2)}, u32[]{:S(2)}) collective-permute-start(bf16[8,2,128,128]{3,2,1,0:T(8,128)(2,1)} %hop.6), channel_id=1, source_target_pairs={{1,0},{2,1},{3,2},{5,4},{6,5},{7,6},{9,8},{10,9},{11,10},{13,12},{... | collective-permute-start | bytes 1572872 | tf_op jit(solution)/shard_map/ppermute | solution.py:1114
  270.0 27.3 %collective-permute-start.38 = (bf16[128,2176]{1,0:T(8,128)(2,1)}, bf16[128,2176]{1,0:T(8,128)(2,1)S(1)}, u32[]{:S(2)}, u32[]{:S(2)}) collective-permute-start(bf16[128,2176]{1,0:T(8,128)(2,1)} %get-tuple-element.393), channel_id=1, source_target_pairs={{0,16},{4,12},{8,24},{12,4},{16,0},{20,28},{24,8},{28,20},{1,17},{... | collective-permute-start | bytes 1671176 | tf_op jit(solution)/shard_map/ppermute | solution.py:922
  287.4 15.0 %collective-permute-start.33 = (bf16[128,2176]{1,0:T(8,128)(2,1)}, bf16[128,2176]{1,0:T(8,128)(2,1)}, u32[]{:S(2)}, u32[]{:S(2)}) collective-permute-start(bf16[128,2176]{1,0:T(8,128)(2,1)} %get-tuple-element.397), channel_id=1, source_target_pairs={{0,16},{4,12},{8,24},{12,4},{16,0},{20,28},{24,8},{28,20},{1,17},{... | collective-permute-start | bytes 1671176 | tf_op jit(solution)/shard_map/ppermute | solution.py:922
  290.7 54.4 %collective-permute-start.37 = (bf16[2,128,2176]{2,1,0:T(8,128)(2,1)}, bf16[2,128,2176]{2,1,0:T(8,128)(2,1)}, u32[]{:S(2)}, u32[]{:S(2)}) collective-permute-start(bf16[2,128,2176]{2,1,0:T(8,128)(2,1)} %get-tuple-element.383), channel_id=1, source_target_pairs={{0,8},{4,20},{8,0},{12,28},{16,24},{20,4},{24,16},{28,12},{1,9},{5... | collective-permute-start | bytes 3342344 | tf_op jit(solution)/shard_map/ppermute | solution.py:922
  296.1 15.0 %collective-permute-start.31 = (bf16[8,2,128,128]{3,2,1,0:T(8,128)(2,1)}, bf16[8,2,128,128]{3,2,1,0:T(8,128)(2,1)}, u32[]{:S(2)}, u32[]{:S(2)}) collective-permute-start(bf16[8,2,128,128]{3,2,1,0:T(8,128)(2,1)} %hop.7), channel_id=1, source_target_pairs={{1,0},{2,1},{3,2},{5,4},{6,5},{7,6},{9,8},{10,9},{11,10},{13,12},{... | collective-permute-start | bytes 1572872 | tf_op jit(solution)/shard_map/ppermute | solution.py:1119
  304.4 36.9 %collective-permute-start.39 = (bf16[128,2176]{1,0:T(8,128)(2,1)}, bf16[128,2176]{1,0:T(8,128)(2,1)}, u32[]{:S(2)}, u32[]{:S(2)}) collective-permute-start(bf16[128,2176]{1,0:T(8,128)(2,1)} %add_convert_fusion.17), channel_id=1, source_target_pairs={{0,1},{1,2},{2,3},{3,0},{4,5},{5,6},{6,7},{7,4},{8,9},{9,10},{10,1... | collective-permute-start | bytes 1671176 | tf_op jit(solution)/shard_map/ppermute | solution.py:942
  309.6 37.1 %collective-permute-start.36 = (bf16[128,2176]{1,0:T(8,128)(2,1)}, bf16[128,2176]{1,0:T(8,128)(2,1)}, u32[]{:S(2)}, u32[]{:S(2)}) collective-permute-start(bf16[128,2176]{1,0:T(8,128)(2,1)} %get-tuple-element.395), channel_id=1, source_target_pairs={{0,16},{4,12},{8,24},{12,4},{16,0},{20,28},{24,8},{28,20},{1,17},{... | collective-permute-start | bytes 1671176 | tf_op jit(solution)/shard_map/ppermute | solution.py:922
  337.4 12.7 %collective-permute-start.35 = (f32[2,16,3072]{2,1,0:T(8,128)}, f32[2,16,3072]{2,1,0:T(8,128)}, u32[]{:S(2)}, u32[]{:S(2)}) collective-permute-start(f32[2,16,3072]{2,1,0:T(8,128)} %get-tuple-element.275), channel_id=1, source_target_pairs={{1,0},{2,1},{3,2},{5,4},{6,5},{7,6},{9,8},{10,9},{11,10},{13,12},{... | collective-permute-start | bytes 1179656 | tf_op jit(solution)/shard_map/ppermute | solution.py:1128
  343.0 44.0 %collective-permute-start.41 = (bf16[128,2176]{1,0:T(8,128)(2,1)S(1)}, bf16[128,2176]{1,0:T(8,128)(2,1)S(1)}, u32[]{:S(2)}, u32[]{:S(2)}) collective-permute-start(bf16[128,2176]{1,0:T(8,128)(2,1)S(1)} %add_convert_fusion.15), channel_id=1, source_target_pairs={{0,1},{1,2},{2,3},{3,0},{4,5},{5,6},{6,7},{7,4},{8,9},{9,10},{10,1... | collective-permute-start | bytes 1671176 | tf_op jit(solution)/shard_map/ppermute | solution.py:942
  347.9 39.0 %collective-permute-start.42 = (bf16[128,2176]{1,0:T(8,128)(2,1)S(1)}, bf16[128,2176]{1,0:T(8,128)(2,1)S(1)}, u32[]{:S(2)}, u32[]{:S(2)}) collective-permute-start(bf16[128,2176]{1,0:T(8,128)(2,1)S(1)} %add_convert_fusion.14), channel_id=1, source_target_pairs={{0,3},{1,0},{2,1},{3,2},{4,7},{5,4},{6,5},{7,6},{8,11},{9,8},{10,9... | collective-permute-start | bytes 1671176 | tf_op jit(solution)/shard_map/ppermute | solution.py:942
  352.1 34.4 %collective-permute-start.40 = (bf16[128,2176]{1,0:T(8,128)(2,1)S(1)}, bf16[128,2176]{1,0:T(8,128)(2,1)S(1)}, u32[]{:S(2)}, u32[]{:S(2)}) collective-permute-start(bf16[128,2176]{1,0:T(8,128)(2,1)S(1)} %get-tuple-element.391), channel_id=1, source_target_pairs={{0,16},{4,12},{8,24},{12,4},{16,0},{20,28},{24,8},{28,20},{1,17},{... | collective-permute-start | bytes 1671176 | tf_op jit(solution)/shard_map/ppermute | solution.py:922
  374.8 15.1 %collective-permute-start.52 = (bf16[4,128,1024]{2,1,0:T(8,128)(2,1)}, bf16[4,128,1024]{2,1,0:T(8,128)(2,1)S(1)}, u32[]{:S(2)}, u32[]{:S(2)}) collective-permute-start(bf16[4,128,1024]{2,1,0:T(8,128)(2,1)} %get-tuple-element.308), channel_id=1, source_target_pairs={{0,4},{4,0},{8,12},{12,8},{16,20},{20,16},{24,28},{28,24},{1,5},{5... | collective-permute-start | bytes 3145736 | tf_op jit(solution)/shard_map/ppermute | solution.py:922
  386.5 9.1 %collective-permute-start.50 = (bf16[4,128,1024]{2,1,0:T(8,128)(2,1)}, bf16[4,128,1024]{2,1,0:T(8,128)(2,1)S(1)}, u32[]{:S(2)}, u32[]{:S(2)}) collective-permute-start(bf16[4,128,1024]{2,1,0:T(8,128)(2,1)} %get-tuple-element.304), channel_id=1, source_target_pairs={{0,4},{4,0},{8,12},{12,8},{16,20},{20,16},{24,28},{28,24},{1,5},{5... | collective-permute-start | bytes 3145736 | tf_op jit(solution)/shard_map/ppermute | solution.py:922
  386.9 10.3 %collective-permute-start.49 = (bf16[4,128,1024]{2,1,0:T(8,128)(2,1)}, bf16[4,128,1024]{2,1,0:T(8,128)(2,1)S(1)}, u32[]{:S(2)}, u32[]{:S(2)}) collective-permute-start(bf16[4,128,1024]{2,1,0:T(8,128)(2,1)} %get-tuple-element.302), channel_id=1, source_target_pairs={{0,4},{4,0},{8,12},{12,8},{16,20},{20,16},{24,28},{28,24},{1,5},{5... | collective-permute-start | bytes 3145736 | tf_op jit(solution)/shard_map/ppermute | solution.py:922
  387.3 12.1 %collective-permute-start.71 = (bf16[128,2176]{1,0:T(8,128)(2,1)S(1)}, bf16[128,2176]{1,0:T(8,128)(2,1)S(1)}, u32[]{:S(2)}, u32[]{:S(2)}) collective-permute-start(bf16[128,2176]{1,0:T(8,128)(2,1)S(1)} %add_convert_fusion.12.refs_0_), channel_id=1, source_target_pairs={{0,8},{4,20},{8,0},{12,28},{16,24},{20,4},{24,16},{28,12},{1,9},{5... | collective-permute-start | bytes 1671176 | tf_op jit(solution)/shard_map/ppermute | solution.py:922
  390.0 16.2 %collective-permute-start.72 = (bf16[128,2176]{1,0:T(8,128)(2,1)S(1)}, bf16[128,2176]{1,0:T(8,128)(2,1)S(1)}, u32[]{:S(2)}, u32[]{:S(2)}) collective-permute-start(bf16[128,2176]{1,0:T(8,128)(2,1)S(1)} %add_convert_fusion.12.refs_0_), channel_id=1, source_target_pairs={{0,16},{4,12},{8,24},{12,4},{16,0},{20,28},{24,8},{28,20},{1,17},{... | collective-permute-start | bytes 1671176 | tf_op jit(solution)/shard_map/ppermute | solution.py:922
  393.4 48.3 %collective-permute-start.43 = (f32[5632]{0:T(1024)S(1)}, f32[5632]{0:T(1024)S(1)}, u32[]{:S(2)}, u32[]{:S(2)}) collective-permute-start(f32[5632]{0:T(1024)S(1)} %pad_maximum_fusion.2), channel_id=1, source_target_pairs={{0,1},{1,2},{2,3},{3,0},{4,5},{5,6},{6,7},{7,4},{8,9},{9,10},{10,1... | collective-permute-start | bytes 67592 | tf_op jit(solution)/shard_map/ppermute | solution.py:942
  397.3 10.7 %collective-permute-start.56 = (bf16[2,128,1024]{2,1,0:T(8,128)(2,1)S(1)}, bf16[2,128,1024]{2,1,0:T(8,128)(2,1)S(1)}, u32[]{:S(2)}, u32[]{:S(2)}) collective-permute-start(bf16[2,128,1024]{2,1,0:T(8,128)(2,1)S(1)} %get-tuple-element.401), channel_id=1, source_target_pairs={{0,8},{4,20},{8,0},{12,28},{16,24},{20,4},{24,16},{28,12},{1,9},{5... | collective-permute-start | bytes 1572872 | tf_op jit(solution)/shard_map/ppermute | solution.py:922
  398.2 15.4 %collective-permute-start.55 = (bf16[2,128,1024]{2,1,0:T(8,128)(2,1)S(1)}, bf16[2,128,1024]{2,1,0:T(8,128)(2,1)S(1)}, u32[]{:S(2)}, u32[]{:S(2)}) collective-permute-start(bf16[2,128,1024]{2,1,0:T(8,128)(2,1)S(1)} %get-tuple-element.403), channel_id=1, source_target_pairs={{0,8},{4,20},{8,0},{12,28},{16,24},{20,4},{24,16},{28,12},{1,9},{5... | collective-permute-start | bytes 1572872 | tf_op jit(solution)/shard_map/ppermute | solution.py:922
  399.4 44.8 %collective-permute-start.44 = (f32[5632]{0:T(1024)S(1)}, f32[5632]{0:T(1024)S(1)}, u32[]{:S(2)}, u32[]{:S(2)}) collective-permute-start(f32[5632]{0:T(1024)S(1)} %pad_maximum_fusion.3), channel_id=1, source_target_pairs={{0,2},{1,3},{2,0},{3,1},{4,6},{5,7},{6,4},{7,5},{8,10},{9,11},{10,... | collective-permute-start | bytes 67592 | tf_op jit(solution)/shard_map/ppermute | solution.py:942
  406.2 38.8 %collective-permute-start.45 = (f32[5632]{0:T(1024)S(1)}, f32[5632]{0:T(1024)S(1)}, u32[]{:S(2)}, u32[]{:S(2)}) collective-permute-start(f32[5632]{0:T(1024)S(1)} %pad_maximum_fusion.4), channel_id=1, source_target_pairs={{0,3},{1,0},{2,1},{3,2},{4,7},{5,4},{6,5},{7,6},{8,11},{9,8},{10,9... | collective-permute-start | bytes 67592 | tf_op jit(solution)/shard_map/ppermute | solution.py:942
  407.9 11.2 %collective-permute-start.54 = (bf16[2,128,1024]{2,1,0:T(8,128)(2,1)S(1)}, bf16[2,128,1024]{2,1,0:T(8,128)(2,1)S(1)}, u32[]{:S(2)}, u32[]{:S(2)}) collective-permute-start(bf16[2,128,1024]{2,1,0:T(8,128)(2,1)S(1)} %get-tuple-element.405), channel_id=1, source_target_pairs={{0,8},{4,20},{8,0},{12,28},{16,24},{20,4},{24,16},{28,12},{1,9},{5... | collective-permute-start | bytes 1572872 | tf_op jit(solution)/shard_map/ppermute | solution.py:922
  413.5 11.2 %collective-permute-start.53 = (bf16[2,128,1024]{2,1,0:T(8,128)(2,1)S(1)}, bf16[2,128,1024]{2,1,0:T(8,128)(2,1)S(1)}, u32[]{:S(2)}, u32[]{:S(2)}) collective-permute-start(bf16[2,128,1024]{2,1,0:T(8,128)(2,1)S(1)} %get-tuple-element.399), channel_id=1, source_target_pairs={{0,8},{4,20},{8,0},{12,28},{16,24},{20,4},{24,16},{28,12},{1,9},{5... | collective-permute-start | bytes 1572872 | tf_op jit(solution)/shard_map/ppermute | solution.py:922
  439.9 19.7 %collective-permute-start.73 = (bf16[128,2176]{1,0:T(8,128)(2,1)S(1)}, bf16[128,2176]{1,0:T(8,128)(2,1)S(1)}, u32[]{:S(2)}, u32[]{:S(2)}) collective-permute-start(bf16[128,2176]{1,0:T(8,128)(2,1)S(1)} %collective-permute-done.71.refs_1_), channel_id=1, source_target_pairs={{0,16},{4,12},{8,24},{12,4},{16,0},{20,28},{24,8},{28,20},{1,17},{... | collective-permute-start | bytes 1671176 | tf_op jit(solution)/shard_map/ppermute | solution.py:922
  441.1 10.2 %collective-permute-start.57 = (bf16[128,1024]{1,0:T(8,128)(2,1)S(1)}, bf16[128,1024]{1,0:T(8,128)(2,1)S(1)}, u32[]{:S(2)}, u32[]{:S(2)}) collective-permute-start(bf16[128,1024]{1,0:T(8,128)(2,1)S(1)} %get-tuple-element.407), channel_id=1, source_target_pairs={{0,16},{4,12},{8,24},{12,4},{16,0},{20,28},{24,8},{28,20},{1,17},{... | collective-permute-start | bytes 786440 | tf_op jit(solution)/shard_map/ppermute | solution.py:922
  441.6 16.2 %collective-permute-start.62 = (bf16[128,1024]{1,0:T(8,128)(2,1)S(1)}, bf16[128,1024]{1,0:T(8,128)(2,1)S(1)}, u32[]{:S(2)}, u32[]{:S(2)}) collective-permute-start(bf16[128,1024]{1,0:T(8,128)(2,1)S(1)} %add_convert_fusion.25), channel_id=1, source_target_pairs={{0,1},{1,2},{2,3},{3,0},{4,5},{5,6},{6,7},{7,4},{8,9},{9,10},{10,1... | collective-permute-start | bytes 786440 | tf_op jit(solution)/shard_map/ppermute | solution.py:942
  444.3 11.8 %collective-permute-start.63 = (bf16[128,1024]{1,0:T(8,128)(2,1)S(1)}, bf16[128,1024]{1,0:T(8,128)(2,1)S(1)}, u32[]{:S(2)}, u32[]{:S(2)}) collective-permute-start(bf16[128,1024]{1,0:T(8,128)(2,1)S(1)} %add_convert_fusion.24), channel_id=1, source_target_pairs={{0,3},{1,0},{2,1},{3,2},{4,7},{5,4},{6,5},{7,6},{8,11},{9,8},{10,9... | collective-permute-start | bytes 786440 | tf_op jit(solution)/shard_map/ppermute | solution.py:942
  449.7 14.9 %collective-permute-start.74 = (bf16[128,2176]{1,0:T(8,128)(2,1)S(1)}, bf16[128,2176]{1,0:T(8,128)(2,1)S(1)}, u32[]{:S(2)}, u32[]{:S(2)}) collective-permute-start(bf16[128,2176]{1,0:T(8,128)(2,1)S(1)} %add_convert_fusion.12.refs_0_), channel_id=1, source_target_pairs={{0,4},{4,0},{8,12},{12,8},{16,20},{20,16},{24,28},{28,24},{1,5},{5... | collective-permute-start | bytes 1671176 | tf_op jit(solution)/shard_map/ppermute | solution.py:922
  456.1 9.9 %collective-permute-start.75 = (bf16[128,2176]{1,0:T(8,128)(2,1)S(1)}, bf16[128,2176]{1,0:T(8,128)(2,1)S(1)}, u32[]{:S(2)}, u32[]{:S(2)}) collective-permute-start(bf16[128,2176]{1,0:T(8,128)(2,1)S(1)} %collective-permute-done.71.refs_1_), channel_id=1, source_target_pairs={{0,4},{4,0},{8,12},{12,8},{16,20},{20,16},{24,28},{28,24},{1,5},{5... | collective-permute-start | bytes 1671176 | tf_op jit(solution)/shard_map/ppermute | solution.py:922
  457.8 8.9 %collective-permute-start.76 = (bf16[128,2176]{1,0:T(8,128)(2,1)S(1)}, bf16[128,2176]{1,0:T(8,128)(2,1)S(1)}, u32[]{:S(2)}, u32[]{:S(2)}) collective-permute-start(bf16[128,2176]{1,0:T(8,128)(2,1)S(1)} %collective-permute-done.72.refs_2_), channel_id=1, source_target_pairs={{0,4},{4,0},{8,12},{12,8},{16,20},{20,16},{24,28},{28,24},{1,5},{5... | collective-permute-start | bytes 1671176 | tf_op jit(solution)/shard_map/ppermute | solution.py:922
  464.2 11.6 %collective-permute-start.77 = (bf16[128,2176]{1,0:T(8,128)(2,1)S(1)}, bf16[128,2176]{1,0:T(8,128)(2,1)}, u32[]{:S(2)}, u32[]{:S(2)}) collective-permute-start(bf16[128,2176]{1,0:T(8,128)(2,1)S(1)} %collective-permute-done.73.refs_3_), channel_id=1, source_target_pairs={{0,4},{4,0},{8,12},{12,8},{16,20},{20,16},{24,28},{28,24},{1,5},{5... | collective-permute-start | bytes 1671176 | tf_op jit(solution)/shard_map/ppermute | solution.py:922
  466.0 17.7 %collective-permute-start.67 = (bf16[128,1024]{1,0:T(8,128)(2,1)S(1)}, bf16[128,1024]{1,0:T(8,128)(2,1)S(1)}, u32[]{:S(2)}, u32[]{:S(2)}) collective-permute-start(bf16[128,1024]{1,0:T(8,128)(2,1)S(1)} %add_convert_fusion.22), channel_id=1, source_target_pairs={{0,4},{4,0},{8,12},{12,8},{16,20},{20,16},{24,28},{28,24},{1,5},{5... | collective-permute-start | bytes 786440 | tf_op jit(solution)/shard_map/ppermute | solution.py:922
  466.8 16.9 %collective-permute-start.68 = (bf16[128,1024]{1,0:T(8,128)(2,1)S(1)}, bf16[128,1024]{1,0:T(8,128)(2,1)S(1)}, u32[]{:S(2)}, u32[]{:S(2)}) collective-permute-start(bf16[128,1024]{1,0:T(8,128)(2,1)S(1)} %collective-permute-done.64.refs_1_), channel_id=1, source_target_pairs={{0,4},{4,0},{8,12},{12,8},{16,20},{20,16},{24,28},{28,24},{1,5},{5... | collective-permute-start | bytes 786440 | tf_op jit(solution)/shard_map/ppermute | solution.py:922
  470.2 13.5 %collective-permute-start.69 = (bf16[128,1024]{1,0:T(8,128)(2,1)}, bf16[128,1024]{1,0:T(8,128)(2,1)S(1)}, u32[]{:S(2)}, u32[]{:S(2)}) collective-permute-start(bf16[128,1024]{1,0:T(8,128)(2,1)} %collective-permute-done.65.refs_2_), channel_id=1, source_target_pairs={{0,4},{4,0},{8,12},{12,8},{16,20},{20,16},{24,28},{28,24},{1,5},{5... | collective-permute-start | bytes 786440 | tf_op jit(solution)/shard_map/ppermute | solution.py:922
  473.0 10.8 %collective-permute-start.70 = (bf16[128,1024]{1,0:T(8,128)(2,1)}, bf16[128,1024]{1,0:T(8,128)(2,1)S(1)}, u32[]{:S(2)}, u32[]{:S(2)}) collective-permute-start(bf16[128,1024]{1,0:T(8,128)(2,1)} %collective-permute-done.66.refs_3_), channel_id=1, source_target_pairs={{0,4},{4,0},{8,12},{12,8},{16,20},{20,16},{24,28},{28,24},{1,5},{5... | collective-permute-start | bytes 786440 | tf_op jit(solution)/shard_map/ppermute | solution.py:922
  (61 other events, 748.4 us)

commit v3 on v2

--- a/solution.py
+++ b/solution.py
@@ -198,7 +198,7 @@
         w_out_ref[hh, m] = both[:, HD:].astype(BF16)
         a_ref[hh, m] = sums[:HD]
         s_ref[hh, m] = sums[:HD].astype(BF16)
-        m_ref[hh, m] = keep_state - sums[HD:]
+        m_ref[hh, m] = (keep_state - sums[HD:]).astype(BF16)
 
     interleave([instance(hh, m) for hh in range(per) for m in range(micro)])
 
@@ -206,11 +206,7 @@
 def hop_kernel(back, state_ref, keep_ref, gain_ref, out_ref):
     for h in range(gain_ref.shape[0]):
         for m in range(gain_ref.shape[1]):
-            keep = keep_ref[h, m]
-            high = keep.astype(BF16)
-            rest = (keep - high.astype(F32)).astype(BF16)
-            state = state_ref[h, m]
-            moved = mm(state, high, tb=back) + mm(state, rest, tb=back)
+            moved = mm(state_ref[h, m], keep_ref[h, m], tb=back)
             out_ref[h, m] = (moved + gain_ref[h, m]).astype(BF16)
 
 
@@ -255,7 +251,7 @@
 
 def back_kernel(dmix_ref, y_ref, qk_ref, t_ref, u_ref, state_ref, dstate_ref, proj_ref,
                 taps_ref, beta_ref, seg_ref, seg_row_ref,
-                dmain_ref, tail_ref, front_ref, dbeta_ref, dtaps_ref):
+                dmain_ref, dbeta_ref, dtaps_ref):
     per, micro = qk_ref.shape[:2]
     tokens = qk_ref.shape[2]
     slot = pl.program_id(0)
@@ -334,9 +330,7 @@
                 spread = jnp.concatenate([zeros, taps[4 * j + i : 4 * j + i + 1] * kept], axis=0)
                 d_proj = d_proj + pltpu.roll(spread, HALO + tokens - i, 0)
             at = (3 * hh + j) * HD
-            front_ref[m, :, at : at + HD] = d_proj[:HALO]
-            tail_ref[m, :, at : at + HD] = d_proj[tokens:]
-            dmain_ref[m, :, at : at + HD] = d_proj[HALO:].astype(BF16)
+            dmain_ref[m, :, at : at + HD] = d_proj.astype(BF16)
             yield
         tap_totals[hh, m] = jnp.concatenate(tap_sums + [jnp.zeros((4, HD), F32)], axis=0)
 
@@ -422,7 +416,9 @@
 
     def leaving(i):
         return [
-            pltpu.make_async_copy(grad_ref.at[i % 2, h], grad_refs[2 * i + h], g_sems.at[i % 2, h])
+            pltpu.make_async_copy(
+                grad_ref.at[i % 2, h], grad_refs[i // 2 * 2 + h].at[:, i % 2], g_sems.at[i % 2, h]
+            )
             for h in range(2)
         ]
 
@@ -526,25 +522,22 @@
                 copy.wait()
 
 
-def grad_mixer_kernel(table_ref, x_ref, dqkv_ref, dlow_ref, mixed_ref, *refs):
-    xt_ref, lt_ref, grad_ref, g_sems = refs[-4:]
-    grad_refs = refs[:-4]
+def grad_mixer_kernel(xt_ref, dqkv_ref, lt_ref, mixed_ref, *refs):
+    grad_ref, g_sems = refs[-2:]
+    grad_refs = refs[:-2]
     step = pl.program_id(0)
-    width = x_ref.shape[1]
+    width = xt_ref.shape[0]
     rows = width // PIECES
     n = dqkv_ref.shape[1]
-    slots = len(grad_refs) // 2
+    slots = pl.num_programs(0)
 
     def leaving(i):
         return [
-            pltpu.make_async_copy(grad_ref.at[i % 2, h], grad_refs[2 * i + h], g_sems.at[i % 2, h])
+            pltpu.make_async_copy(
+                grad_ref.at[i % 2, h], grad_refs[i // 2 * 2 + h].at[:, i % 2], g_sems.at[i % 2, h]
+            )
             for h in range(2)
         ]
-
-    @pl.when(step == 0)
-    def _():
-        flip_pieces(table_ref, x_ref, xt_ref)
-        flip_pieces(table_ref, dlow_ref, lt_ref)
 
     for i in range(2, slots):
 
@@ -613,29 +606,41 @@
     out_w_ref[...] = w_ref[step, :, 3 * n :].astype(F32).T
 
 
-def input_kernel(dqkv_ref, w_ref, db_ref, beta_w_ref, rows_ref, dmid_ref, gain_ref, out_ref, gpart_ref, acc_ref):
+def input_kernel(dqkv_ref, w_ref, db_ref, beta_w_ref, front_ref, out_ref):
     step = pl.program_id(0)
-
-    @pl.when(step == 0)
-    def _():
-        acc_ref[...] = mm(db_ref[...], beta_w_ref[...])
-
-    width, n = acc_ref.shape[1], dqkv_ref.shape[1]
+    width, n = out_ref.shape[2], dqkv_ref.shape[2]
     weights = w_ref[0, :, : width // PIECES].reshape(width, n)
-    acc_ref[...] += mm(dqkv_ref[...], weights, tb=True)
-
-    @pl.when(step == pl.num_programs(0) - 1)
-    def _():
-        grad = acc_ref[...]
-        rows = rows_ref[...].astype(F32)
+    for m in range(out_ref.shape[0]):
+        grad = mm(dqkv_ref[m], weights, tb=True)
+        more = mm(db_ref[m], beta_w_ref[0])
+
+        @pl.when(step == 0)
+        def _():
+            front_ref[m] = grad[:HALO]
+            out_ref[m] = grad[HALO:] + more
+
+        @pl.when(step > 0)
+        def _():
+            front_ref[m] += grad[:HALO]
+            out_ref[m] += grad[HALO:] + more
+
+
+def norm_kernel(grad_ref, front_ref, rows_ref, dmid_ref, gain_ref, out_ref, gpart_ref):
+    tokens = grad_ref.shape[1]
+    cut = tokens - HALO
+    total = jnp.zeros((1, grad_ref.shape[2]), F32)
+    for m in range(grad_ref.shape[0]):
+        grad = jnp.concatenate([grad_ref[m, :cut], grad_ref[m, cut:] + front_ref[m]], axis=0)
+        rows = rows_ref[m * tokens : (m + 1) * tokens].astype(F32)
         rstd = lax.rsqrt(jnp.mean(rows * rows, axis=-1, keepdims=True) + EPS)
         unit = rows * rstd
-        gpart_ref[...] = jnp.broadcast_to(jnp.sum(grad * unit, axis=0, keepdims=True), gpart_ref.shape)
+        total = total + jnp.sum(grad * unit, axis=0, keepdims=True)
         scaled = grad * gain_ref[...]
-        out_ref[...] = (
-            dmid_ref[...]
+        out_ref[m * tokens : (m + 1) * tokens] = (
+            dmid_ref[m * tokens : (m + 1) * tokens]
             + rstd * (scaled - unit * jnp.mean(scaled * unit, axis=-1, keepdims=True))
         ).astype(BF16)
+    gpart_ref[...] = jnp.broadcast_to(total, gpart_ref.shape)
 
 
 def params(mib=60):
@@ -673,7 +678,7 @@
     return jax.ShapeDtypeStruct(tuple(shape), dtype)
 
 
-def call(kernel, grid, in_specs, out_specs, out_shape, estimate, name, scratch=(), prefetch=0):
+def call(kernel, grid, in_specs, out_specs, out_shape, estimate, name, scratch=(), prefetch=0, mib=60):
     return pl.pallas_call(
         kernel,
         grid_spec=pltpu.PrefetchScalarGridSpec(
@@ -684,7 +689,7 @@
             scratch_shapes=list(scratch),
         ),
         out_shape=out_shape,
-        compiler_params=params(),
+        compiler_params=params(mib),
         cost_estimate=cost(*estimate),
         name=name,
     )
@@ -733,7 +738,7 @@
         sds(hm + (tokens, tokens), BF16),
         sds(hm + (tokens, HD), F32),
         sds(hm + (tokens, HD), BF16),
-        sds(hm + (HD, HD), F32),
+        sds(hm + (HD, HD), BF16),
         sds(hm + (HD, HD), F32),
         sds(hm + (HD, HD), BF16),
     ]
@@ -755,7 +760,7 @@
         functools.partial(hop_kernel, back), slots,
         [rolled(per, state.shape, shift, slots), lead(per, keep.shape), lead(per, gain.shape)],
         lead(per, gain.shape), sds(gain.shape, BF16),
-        (gain.size * 512, gain.size * 12), "hop",
+        (gain.size * 512, gain.size * 12), "hop", mib=12,
     )(state, keep, gain)
 
 
@@ -798,12 +803,9 @@
         + [rolled(per, state.shape, 1, slots), rolled(per, d_state.shape, slots - 1, slots)]
         + [lead(per, proj.shape), lead(per, taps.shape)]
         + [whole(a.shape) for a in (beta, seg, seg_row)],
-        [columns(tokens, 3 * HD), columns(HALO, 3 * HD), columns(HALO, 3 * HD), whole(beta.shape),
-         lead(per, taps.shape)],
+        [columns(HALO + tokens, 3 * HD), whole(beta.shape), lead(per, taps.shape)],
         [
-            sds((micro, tokens, heads * 3 * HD), BF16),
-            sds((micro, HALO, heads * 3 * HD), F32),
-            sds((micro, HALO, heads * 3 * HD), F32),
+            sds((micro, HALO + tokens, heads * 3 * HD), BF16),
             sds(beta.shape, F32),
             sds(taps.shape, F32),
         ],
@@ -814,7 +816,7 @@
 def grads_out(slots, rows, n):
     shape = (PIECES // 2, rows, n)
     return (
-        [sds(shape, BF16)] * (2 * slots),
+        [sds((PIECES // 2, 2, rows, n), BF16)] * slots,
         [pltpu.VMEM((2, 2) + shape, BF16)],
         pltpu.SemaphoreType.DMA((2, 2)),
     )
@@ -859,8 +861,8 @@
     )(ids, table, mixed, rows, d_out, gain, own, *pieces)
 
 
-def grad_mixer(table, x, d_qkv, d_low, mixed, slots):
-    count, width = x.shape
+def grad_mixer(xt, d_qkv, lt, mixed, slots):
+    width = xt.shape[0]
     n, part = d_qkv.shape[1] // slots, mixed.shape[1] // slots
     grads, room, g_sems = grads_out(slots, width // PIECES, n + part)
     order = reduce_order(slots)
@@ -868,14 +870,14 @@
     def at(s):
         return sum(jnp.where(s == i, k, 0) for i, k in enumerate(order))
 
-    columns = lambda size: pl.BlockSpec((count, size), lambda s, t: (0, at(s)))
+    columns = lambda a, size: pl.BlockSpec((a.shape[0], size), lambda s: (0, at(s)))
     return call(
         grad_mixer_kernel, slots,
-        [whole(x.shape), columns(n), whole(d_low.shape), columns(part)],
+        [whole(xt.shape), columns(d_qkv, n), whole(lt.shape), columns(mixed, part)],
         [ANYWHERE] * len(grads), grads,
-        (2 * width * count * (n + part) * slots, 2 * width * (n + part) * slots), "grad_mixer",
-        [pltpu.VMEM((width, count), BF16)] * 2 + room + [g_sems], prefetch=1,
-    )(table, x, d_qkv, d_low, mixed)
+        (2 * width * mixed.shape[0] * (n + part) * slots, 2 * width * (n + part) * slots), "grad_mixer",
+        room + [g_sems],
+    )(xt, d_qkv, lt, mixed)
 
 
 def finish_ffn(ids, pieces, hidden):
@@ -890,6 +892,19 @@
     )(ids, *pieces)
 
 
+def flip_kernel(table_ref, x_ref, y_ref, xt_ref, yt_ref):
+    flip_pieces(table_ref, x_ref, xt_ref)
+    flip_pieces(table_ref, y_ref, yt_ref)
+
+
+def flipped(table, x, y):
+    outs = [sds(a.shape[::-1], BF16) for a in (x, y)]
+    return call(
+        flip_kernel, 1, [whole(x.shape), whole(y.shape)], [whole(o.shape) for o in outs], outs,
+        (0, 8 * x.size), "flip", prefetch=1,
+    )(table, x, y)
+
+
 def finish_mixer(ids, pieces, n):
     rows, total = pieces[0].shape
     width = rows * PIECES
@@ -903,19 +918,27 @@
     )(ids, *pieces)
 
 
-def input_back(d_qkv, w, d_b, beta_w, rows, d_mid, gain):
-    count, width = rows.shape
-    slots, n = w.shape[0], w.shape[3]
-    full = whole((count, width))
+def input_back(d_qkv, w, d_b, beta_w):
+    micro, ext, _ = d_qkv.shape
+    slots, _, _, n = w.shape
+    width = beta_w.shape[2]
+    outs = [sds((micro, HALO, width), F32), sds((micro, ext - HALO, width), F32)]
+    lanes = beta_w.shape[1]
     return call(
         input_kernel, slots,
-        [pl.BlockSpec((count, n), lambda s: (0, s)), lead(1, w.shape),
-         whole(d_b.shape), whole(beta_w.shape), full, full, whole(gain.shape)],
-        [full, whole((8, width))],
-        [sds((count, width), BF16), sds((8, width), F32)],
-        (2 * count * width * n * slots, 2 * slots * width * n), "input_back",
-        [pltpu.VMEM((count, width), F32)],
-    )(d_qkv, w, d_b, beta_w, rows, d_mid, gain)
+        [pl.BlockSpec((micro, ext, n), lambda s: (0, 0, s)), lead(1, w.shape),
+         whole(d_b.shape[:2] + (HD,)), lead(1, (slots, HD, width))],
+        [whole(o.shape) for o in outs], outs,
+        (2 * micro * ext * width * n * slots, 2 * slots * width * n), "input_back",
+    )(d_qkv, w, d_b, jnp.stack([jnp.pad(beta_w[k], ((k * lanes, HD - (k + 1) * lanes), (0, 0))) for k in range(slots)]))
+
+
+def input_norm(grad, front, rows, d_mid, gain):
+    outs = [sds(rows.shape, BF16), sds((8, rows.shape[1]), F32)]
+    return call(
+        norm_kernel, 1, [whole(a.shape) for a in (grad, front, rows, d_mid, gain)],
+        [whole(o.shape) for o in outs], outs, (0, 12 * rows.size), "input_norm",
+    )(grad, front, rows, d_mid, gain)
 
 
 def swap(x, mask_of, size):
@@ -965,50 +988,85 @@
     return (a.astype(F32) + b.astype(F32)).astype(BF16)
 
 
+class Pending:
+    def __init__(self):
+        self.kept = {}
+
+    def tie(self, *xs):
+        keys = list(self.kept)
+        values = sync(*xs, *(self.kept[k] for k in keys))
+        self.kept = dict(zip(keys, values[len(xs) :]))
+        return values[0] if len(xs) == 1 else values[: len(xs)]
+
+    def tie_all(self, *trees):
+        leaves, shape = jax.tree.flatten(trees)
+        return jax.tree.unflatten(shape, self.tie(*leaves))
+
+
+class Gather:
+    def __init__(self, own, dp):
+        self.dp, self.step = dp, 0
+        self.pieces = [own, swap(own, first, dp), swap(own, second, dp), swap(own, across, dp)]
+
+    def round(self):
+        if self.step == 0:
+            own, b, c, far = self.pieces
+            both = swap(jnp.stack([b, c]), across, self.dp)
+            self.pieces = [own, b, c, far, swap(b, second, self.dp), both]
+        else:
+            self.pieces.append(swap(self.pieces[4], across, self.dp))
+        self.step += 1
+
+    def ordered(self):
+        own, b, c, far, d, both, far_d = self.pieces
+        return [own, b, c, d, far, both[0], both[1], far_d]
+
+
 class Reduction:
-    def __init__(self, grads, order, dp, tensor):
+    def __init__(self, pending, name, grads, order, dp, tensor):
+        self.pending, self.name = pending, name
         self.order, self.dp, self.tensor = order, dp, tensor
-        self.theirs, self.ours = list(grads[0::2]), list(grads[1::2])
-        self.across_in = [swap(g, across, dp) for g in self.theirs]
-        self.first_in, self.second_in, self.parts = {}, {}, {}
-        self.last = None
-
-    def tie(self, *xs):
-        if self.last is None:
-            self.last = self.ours[0]
-            *xs, self.ours[0] = sync(*xs, self.last)
-            return xs
-        *xs, self.last = sync(*xs, self.last)
-        return xs
-
-    def add(self, kept, came):
-        if self.last is not None:
-            kept, came, _ = sync(kept, came, self.last)
-        self.last = add(kept, came)
-        return self.last
+        self.came, self.parts = {}, {}
+        for i in range(len(order) // 2):
+            self.came["one", i] = swap(grads[2 * i], across, dp)
+            pending.kept[name, "one", i] = grads[2 * i + 1]
+
+    def add(self, step, i):
+        came = self.pending.tie(self.came.pop((step, i)))
+        return add(self.pending.kept.pop((self.name, step, i)), came)
 
     def across(self, i):
-        total = self.add(self.ours[i], self.across_in[i])
-        self.first_in[i] = (total[:2], swap(total[2:], first, self.dp))
+        total = self.add("one", i)
+        self.pending.kept[self.name, "two", i] = total[:2]
+        self.came["two", i] = swap(total[2:], first, self.dp)
 
     def first(self, i):
-        total = self.add(*self.first_in[i])
-        self.second_in[i] = (total[0], swap(total[1], second, self.dp))
+        total = self.add("two", i)
+        self.pending.kept[self.name, "three", i] = total[0]
+        self.came["three", i] = swap(total[1], second, self.dp)
 
     def second(self, i):
-        slot = self.order[i]
-        total = self.add(*self.second_in[i])
-        if slot and slot < self.tensor - 1:
-            if slot + 1 < self.tensor - 1:
-                total = self.add(total, self.parts[slot + 1])
-            self.parts[slot] = to_ahead(total, 1, self.tensor)
-        else:
-            self.parts[slot] = to_ahead(total, slot, self.tensor) if slot else total
+        total = self.add("three", i)
+        for slot, part in zip(self.order[2 * i : 2 * i + 2], (total[0], total[1])):
+            self.pending.kept[self.name, "part", slot] = part
+        if i == 0:
+            slot = self.order[0]
+            self.parts[slot] = to_ahead(self.pending.kept.pop((self.name, "part", slot)), 1, self.tensor)
+
+    def along(self):
+        slot = self.order[-2]
+        self.parts[slot] = to_ahead(self.pending.kept.pop((self.name, "part", slot)), slot, self.tensor)
+        for slot in self.order[1:-2]:
+            part = add(
+                self.pending.kept.pop((self.name, "part", slot)),
+                self.pending.tie(self.parts.pop(slot + 1)),
+            )
+            self.parts[slot] = to_ahead(part, 1, self.tensor)
 
     def result(self):
-        parts = [self.parts[0]] + [self.parts[k] for k in {1, self.tensor - 1}]
-        self.last = sum(p.astype(F32) for p in parts).astype(BF16)
-        return self.last
+        parts = [self.pending.kept.pop((self.name, "part", 0))]
+        parts += [self.parts[k] for k in sorted({1, self.tensor - 1})]
+        return sum(p.astype(F32) for p in parts).astype(BF16)
 
 
 def reduce_far(total, dp):
@@ -1060,16 +1118,15 @@
     *others, halo, mixer_own, piece, every = sync(*others, halo, mixer_own, piece, every)
     mixer_others = jnp.stack(others)
     b, c = swap(mixer_others, first, dp), swap(mixer_others, second, dp)
-    ffn_others = {k: from_ahead(piece, k, tensor) for k in (1, tensor - 1)}
+    ffn_all = lax.all_gather(piece, "tensor")
     ffn_own = pack_ffn(every, *pack_f)
     mixer_others, b, c, ffn_own = sync(mixer_others, b, c, ffn_own)
     d = swap(b, second, dp)
     mixer_pieces = [mixer_others, b, c] + [swap(x, across, dp) for x in (mixer_others, b, c)]
     d, *mixer_pieces = sync(d, *mixer_pieces)
     mixer_pieces = mixer_pieces[:3] + [d] + mixer_pieces[3:] + [swap(d, across, dp)]
-    ffn_others[1], *mixer_pieces = sync(ffn_others[1], *mixer_pieces)
-    for k in range(2, tensor - 1):
-        ffn_others[k] = from_ahead(ffn_others[k - 1], 1, tensor)
+
+    x_ext = jnp.concatenate([halo, mixer_in], axis=1)
 
     seg = jnp.pad(segment[:, 0].astype(F32), ((0, 0), (HALO, 0)), constant_values=-1)
     seg = lax.dynamic_slice_in_dim(seg, place * tokens, HALO + tokens, 1)
@@ -1080,18 +1137,21 @@
     (mixer_w, beta, taps, beta_w, proj, qk, inv, scores, base, mix, keep, gain, state) = mixer_local(
         ids, mixer_in, halo, seg, seg_row, mixer_own, mixer_pieces, heads
     )
-    state, *others = sync(state, *(ffn_others[k] for k in range(1, tensor)))
-    near = [jnp.stack(others)]
-    near += [swap(near[0], first, dp), swap(near[0], second, dp)]
-    state = hop(lax.ppermute(state, "tensor", ahead), keep, gain, tensor, False)
-    state, *near = sync(state, *near)
+    state, ffn_all = sync(state, ffn_all)
+    others = jnp.stack(
+        [lax.dynamic_index_in_dim(ffn_all, (place + k) % tensor, 0, False) for k in range(1, tensor)]
+    )
+    recv = lax.ppermute(state, "tensor", ahead)
+    near = [others, swap(others, first, dp), swap(others, second, dp)]
+    far = [swap(others, across, dp)]
+    recv = lax.ppermute(hop(recv, keep, gain, tensor, False), "tensor", ahead)
+    recv = hop(recv, keep, gain, tensor, False)
+    near[0], recv = sync(near[0], recv)
+    recv = lax.ppermute(recv, "tensor", ahead)
+    near[:3] = sync(*near)
     near.append(swap(near[1], second, dp))
-    far = [swap(piece, across, dp) for piece in near[:3]]
-    for step in range(1, tensor - 1):
-        state = lax.ppermute(state, "tensor", ahead)
-        if step < tensor - 2:
-            state = hop(state, keep, gain, tensor, False)
-    state, near[3] = sync(state, near[3])
+    far += [swap(near[1], across, dp), swap(near[2], across, dp)]
+    state, near[3] = sync(recv, near[3])
     far.append(swap(near[3], across, dp))
     mixed, update = mixer_output(qk, scores, base, mix, state, seg, tensor)
     mixed = mixed.reshape(count, heads * HD)
@@ -1102,100 +1162,89 @@
         ids, table, mixed, rows, out_grad, gain2, ffn_own, near + far, hidden
     )
     order = reduce_order(tensor)
-    red = Reduction(grads, order, dp, tensor)
+    pending = Pending()
+    red = Reduction(pending, "f", grads, order, dp, tensor)
 
     d_mixed = d_mixed.reshape(micro, tokens, heads * HD)
     y0, back_gain, d_state = mixer_back_local(d_mixed, qk, inv, scores, beta, seg, tensor)
-    (d_state,) = red.tie(d_state)
     recv = lax.ppermute(d_state, "tensor", behind)
+    pending.tie(d_state)
     red.across(0)
+    recv = lax.ppermute(hop(pending.tie(recv), keep, back_gain, tensor, True), "tensor", behind)
     red.across(1)
-    (recv,) = red.tie(recv)
-    recv = lax.ppermute(hop(recv, keep, back_gain, tensor, True), "tensor", behind)
-    red.across(2)
+    xt, lt = flipped(table, *pending.tie(x_ext.reshape(-1, width), d_mid_low))
+    pending.kept["xt"] = xt
+    recv = lax.ppermute(hop(pending.tie(recv), keep, back_gain, tensor, True), "tensor", behind)
     red.first(0)
-    red.across(3)
-    (recv,) = red.tie(recv)
-    recv = lax.ppermute(hop(recv, keep, back_gain, tensor, True), "tensor", behind)
+    d_qkv, d_beta, d_taps = mixer_back(
+        d_mixed, y0, qk, inv, update, state, pending.tie(recv), proj, taps, beta, seg, seg_row, tensor
+    )
+    d_beta = pending.tie(d_beta)
+    grads = grad_mixer(
+        pending.kept.pop("xt"), d_qkv.reshape(-1, heads * 3 * HD), lt, mixed, tensor
+    )
+    mix = Reduction(pending, "m", grads, order, dp, tensor)
+    red.second(0)
     red.first(1)
-    red.second(0)
-    red.first(2)
-    (recv,) = red.tie(recv)
-    d_qkv, tail, front, d_beta, d_taps = mixer_back(
-        d_mixed, y0, qk, inv, update, state, recv, proj, taps, beta, seg, seg_row, tensor
-    )
-    front, d_beta = red.tie(front, d_beta)
+    mix.across(0)
+    mix.across(1)
+    d_qkv, d_beta, d_taps, gain2_part = pending.tie(d_qkv, d_beta, d_taps, gain2_part)
+    d_b = d_beta.astype(BF16)
+    front, d_normed1 = input_back(d_qkv, mixer_w, d_b, beta_w)
     front = lax.ppermute(front, "tensor", behind)
+    d_normed1 = pending.tie(d_normed1)
     red.second(1)
-    red.first(3)
-    red.second(2)
-    (front,) = red.tie(front)
-    front = jnp.roll(front, 3 * part, axis=2)
-    d_qkv = lax.dynamic_update_slice(d_qkv, (tail + front).astype(BF16), (0, tokens - HALO, 0))
-    d_qkv = d_qkv.reshape(count, heads * 3 * HD)
-    d_b = d_beta.reshape(count, HD).astype(BF16)
-    grads = grad_mixer(table, normed1, d_qkv, d_mid_low, mixed, tensor)
-    mix_red = Reduction(grads, order, dp, tensor)
-    mix_red.ours[0], d_qkv = sync(mix_red.ours[0], d_qkv)
-    input_grad, gain1_part = input_back(
-        d_qkv, mixer_w, d_b, beta_w.reshape(-1, width), rows, d_mid, gain1
-    )
-    (gain1_part,) = red.tie(gain1_part)
-    red.second(3)
-    total = reduce_far(red.result(), dp)
-    total, gain1_part = sync(total, gain1_part)
-    near = [total, swap(total, first, dp), swap(total, second, dp)]
-    (gain1_part,) = mix_red.tie(gain1_part)
-    mix_red.across(0)
-    mix_red.across(1)
-    mix_red.across(2)
-    mix_red.across(3)
-    *near, mix_red.last = sync(*near, mix_red.last)
-    near.append(swap(near[1], second, dp))
-    far = [swap(piece, across, dp) for piece in near[:3]]
-    mix_red.first(0)
-    mix_red.first(1)
-    mix_red.first(2)
-    mix_red.first(3)
-    near[3], mix_red.last = sync(near[3], mix_red.last)
-    far.append(swap(near[3], across, dp))
-    mix_red.second(0)
-    mix_red.second(1)
-    mix_red.second(2)
-    mix_red.second(3)
-    *pieces, mix_red.last = sync(*near, *far, mix_red.last)
-    grad_gate, grad_up, grad_down = finish_ffn(ids, pieces, hidden)
-    total = reduce_far(mix_red.result(), dp)
-    grad_q, grad_k, grad_v, grad_out = finish_mixer(ids, plane_gather(total, dp), part)
-
-    grad_b = project_t(d_b, normed1)[::LANES]
+    red.along()
+    mix.first(0)
+    mix.first(1)
+    total = pending.tie(reduce_far(red.result(), dp))
+    gather = Gather(total, dp)
+    mix.second(0)
+    mix.second(1)
+    mix.along()
+    d_normed1, front = pending.tie(d_normed1, front)
+    input_grad, gain1_part = input_norm(d_normed1, front, rows, d_mid, gain1)
+    gain1_part = pending.tie(gain1_part)
+
     span = width // tensor
+    grad_b = project_t(d_b.reshape(count, HD), normed1)[::LANES].reshape(tensor, -1)
     d_taps = d_taps[:, :12].reshape(tensor, local_heads, 12, HD)
     d_taps = jnp.swapaxes(d_taps, 1, 2).reshape(tensor, -1)
-    packed = []
-    for k in range(tensor):
-        at = ((place + k) % tensor) * span
-        packed.append(
-            jnp.concatenate(
-                [
-                    grad_b[k * local_heads : (k + 1) * local_heads].reshape(-1),
-                    d_taps[k],
-                    lax.dynamic_slice_in_dim(gain1_part[0], at, span),
-                    lax.dynamic_slice_in_dim(gain2_part[0], at, span),
-                ]
-            )
-        )
-    packed = sum([packed[0]] + [to_ahead(packed[k], k, tensor) for k in range(1, tensor)])
-    mask = 1
+    gains = jnp.concatenate([g[0].reshape(tensor, span) for g in (gain1_part, gain2_part)], axis=1)
+    gains = lax.dynamic_slice_in_dim(jnp.concatenate([gains, gains]), place, tensor, 0)
+    small = jnp.concatenate([grad_b, d_taps, gains], axis=1)
+    small_in = swap(small, across, dp)
+
+    gather.pieces, small_in, small = pending.tie_all(gather.pieces, small_in, small)
+    gather.round()
+    small = small + small_in
+    total = reduce_far(mix.result(), dp)
+    mixer_gather = Gather(total, dp)
+    small_in = swap(small, lambda i: 2, dp)
+    gather.pieces, small_in, small = pending.tie_all(gather.pieces, small_in, small)
+    gather.round()
+    small = small + small_in
+    mixer_gather.pieces, small = pending.tie_all(mixer_gather.pieces, small)
+    mixer_gather.round()
+    small_in = swap(small, lambda i: 4, dp)
+    gather.pieces, small_in, small = pending.tie_all(gather.pieces, small_in, small)
+    small = small + small_in
+    mask = PIECES
     while mask < dp:
-        packed = packed + swap(packed, lambda i: mask, dp)
+        small = small + swap(small, lambda i: mask, dp)
         mask *= 2
+    small_in = [to_ahead(small[k], k, tensor) for k in range(1, tensor)]
+    gather.pieces, mixer_gather.pieces = pending.tie_all(gather.pieces, mixer_gather.pieces)
+    mixer_gather.round()
+    grad_gate, grad_up, grad_down = finish_ffn(ids, gather.ordered(), hidden)
+    small = sum(small_in, small[0])
+    grad_q, grad_k, grad_v, grad_out = finish_mixer(ids, mixer_gather.ordered(), part)
     cut = local_heads * width
-    grad_beta = packed[:cut].reshape(local_heads, width).T
-    grad_conv = packed[cut : cut + 12 * span].reshape(3, 4, span)
+    grad_beta = small[:cut].reshape(local_heads, width).T
+    grad_conv = small[cut : cut + 12 * span].reshape(3, 4, span)
     cut += 12 * span
-    grad_gain1 = packed[cut : cut + span]
-    grad_gain2 = packed[cut + span : cut + 2 * span]
+    grad_gain1 = small[cut : cut + span]
+    grad_gain2 = small[cut + span :]
     return (
         output.reshape(micro, 1, tokens, width),
         input_grad.reshape(micro, 1, tokens, width),

time: 500 us -> 473 us (0.946)
  starting transfers between devices: 115 us -> 83 us
  between operations: 1.86 us -> 15.3 us
  waiting for transfers between devices: 143 us -> 132 us
    ppermute x55 -> x41, waiting for transfers between devices: 94.5 us -> 61.8 us  [swap(): return lax.ppermute(x, 'dp', [(i, i ^ mask_of(i)) for i in range(size)])]
    ppermute x55 -> x41, starting transfers between devices: 67.1 us -> 45.8 us  [swap(): return lax.ppermute(x, 'dp', [(i, i ^ mask_of(i)) for i in range(size)])]
    ppermute x5, waiting for transfers between devices: 24.8 us -> 43.2 us  [the longest x2 14.8 us: shards(): lax.ppermute(hop(pending.tie(recv), keep, back_gain, tensor, True), 'tens...]
    pallas_call x4, Pallas kernels: 16.2 us -> 3.27 us  [hop(): call(functools.partial(hop_kernel, back), slots, [rolled(per, state.shape...]
    ppermute x6 -> x3, waiting for transfers between devices: 14.9 us -> 3.1 us  [from_ahead(): return lax.ppermute(x, 'tensor', [(i, (i - k) % size) for i in range(size)])]
    ppermute x9, waiting for transfers between devices: 7.34 us -> 17.4 us  [to_ahead(): return lax.ppermute(x, 'tensor', [(i, (i + k) % size) for i in range(size)])]
    pallas_call x2 -> x4, Pallas kernels: 20.8 us -> 30.6 us  [the longest x1 11.4 us: input_back(): call(input_kernel, slots, [pl.BlockSpec((micro, ext, n), lambda s: (0, 0,...]
    ppermute x9, starting transfers between devices: 16.5 us -> 10.1 us  [to_ahead(): return lax.ppermute(x, 'tensor', [(i, (i + k) % size) for i in range(size)])]
  transfers between devices with their start and end apart: 78 -> 62, of which waited for: 29 -> 26; matrix products, arithmetic and copies ran while one was open for 9% -> 11% of each run, Pallas kernels for 26% -> 27%
where the time goes in v3:
time: 473 us; the launch traced here: 464 us
  Pallas kernels  179 us (38%)
  waiting for transfers between devices  132 us (28%)
  starting transfers between devices  83 us (18%)
  other arithmetic  28.5 us (6%)
  local copies, waits for them, and re-layouts  24.8 us (5%)
  between operations  15.3 us (3%)
    ppermute x41, waiting for transfers between devices, swap(): return lax.ppermute(x, 'dp', [(i, i ^ mask_of(i)) for i in range(size)])  61.8 us
    ppermute x41, starting transfers between devices, swap(): return lax.ppermute(x, 'dp', [(i, i ^ mask_of(i)) for i in range(size)])  45.8 us
    pallas_call x1, Pallas kernels, ffn(): call(functools.partial(ffn_kernel, hidden), 2 * slots, [pl.BlockSpec((cou...  45.3 us
    pallas_call x1, Pallas kernels, mixer_back(): call(back_kernel, slots, [columns(tokens, HD)] + [lead(per, a.shape) for...  26.6 us
    pallas_call x1, Pallas kernels, mixer_local(): call(local_kernel, slots, [whole(x.shape), whole(halo.shape), whole(seg.s...  26 us
    convert_element_type x14, other arithmetic, add(): return (a.astype(F32) + b.astype(F32)).astype(BF16)  22.8 us
    ppermute x9, waiting for transfers between devices, to_ahead(): return lax.ppermute(x, 'tensor', [(i, (i + k) % size) for i in range(size)])  17.4 us
    ppermute x2, waiting for transfers between devices, shards(): lax.ppermute(hop(pending.tie(recv), keep, back_gain, tensor, True), 'tens...  14.8 us
  transfers between devices with their start and end apart: 62, of which 26 were waited for; matrix products, arithmetic and copies ran while one was open for 11% of the time, Pallas kernels for 27%

profile of v3, /device:TPU:1, one launch (start us, length us, event | category | flops | bytes accessed | tf_op | source)
XLA Modules:
  0.0 464.4 jit_solution(5413601683965700424)
XLA Ops:
  7.2 1.7 pack_mixer.2
  9.0 4.2 collective-permute-start
  15.4 4.1 collective-permute-start.3
  19.5 6.2 %pack_mixer.3.own_ref = bf16[8,144,768]{2,1,0:T(8,128)(2,1)} custom-call(s32[8]{0:T(128)} %iota.3.table_ref, bf16[1024,256]{1,0:T(8,128)(2,1)} %q_ref.3, bf16[1024,256]{1,0:T(8,128)(2,1)} %k_ref.3, bf16[1024,256]{1,0:T(8,128)(2,1)} %v_ref.3, bf16[2,1024]{1,0:T(2,128)(2,1)} %bitcast.143, bf16[3,4,256]{2,1,0:T(4,128)(2,1)} %conv_ref.3), custom_call_target="tpu_custom_call" | custom-call | bytes 3145728 | tf_op jit(solution)/shard_map/pack_mixer/pallas_call | solution.py:703
  25.7 2.2 pack_ffn.2
  28.5 3.1 collective-permute-done.1
  34.2 8.8 %pack_ffn.3.own_ref = bf16[8,128,2432]{2,1,0:T(8,128)(2,1)} custom-call(s32[8]{0:T(128)} %iota.3.table_ref, bf16[704,1024]{1,0:T(8,128)(2,1)} %bitcast.116, bf16[704,1024]{1,0:T(8,128)(2,1)} %bitcast.118, bf16[704,1024]{1,0:T(8,128)(2,1)} %down_ref.3, bf16[256,1024]{1,0:T(8,128)(2,1)} %out_w_ref.3), custom_call_target="tpu_custom_call" | custom-call | bytes 9961472 | tf_op jit(solution)/shard_map/pack_ffn/pallas_call | solution.py:716
  43.0 2.2 collective-permute-done.4.refs_1_
  45.1 4.2 collective-permute-done.5.refs_2_
  51.4 7.8 %collective-permute-done.6.refs_3_ = bf16[3,144,768]{2,1,0:T(8,128)(2,1)S(1)} collective-permute-done((bf16[3,144,768]{2,1,0:T(8,128)(2,1)S(1)}, bf16[3,144,768]{2,1,0:T(8,128)(2,1)S(1)}, u32[]{:S(2)}, u32[]{:S(2)}) %collective-permute-start.6) | collective-permute-done | bytes 663584 | tf_op jit(solution)/shard_map/ppermute | solution.py:945
  60.1 1.8 collective-permute-start.10
  64.5 26.0 %mixer_local.1 = (bf16[4,8,144,768]{3,2,1,0:T(8,128)(2,1)}, f32[2,256,128]{2,1,0:T(8,128)}, f32[8,16,128]{2,1,0:T(8,128)}, bf16[4,32,1024]{2,1,0:T(8,128)(2,1)},...) custom-call(s32[8]{0:T(128)} %stack.89.ids_ref, ...), custom_call_target="tpu_custom_call" | custom-call | flops 16000000000 | bytes 32000000 | tf_op jit(solution)/shard_map/mixer_local/pallas_call | solution.py:745
  90.5 1.6 constant_dynamic-slice_fusion.2
  93.9 4.3 collective-permute-start.11
  98.2 10.2 %collective-permute-done.11.state_ref = bf16[8,2,128,128]{3,2,1,0:T(8,128)(2,1)S(1)} collective-permute-done((bf16[8,2,128,128]{3,2,1,0:T(8,128)(2,1)S(1)}, bf16[8,2,128,128]{3,2,1,0:T(8,128)(2,1)S(1)}, u32[]{:S(2)}, u32[]{:S(2)}) %collective-permute-start.11) | collective-permute-done | bytes 524320 | tf_op jit(solution)/shard_map/ppermute | solution.py:1144
  109.2 4.3 collective-permute-start.12
  113.5 9.4 %collective-permute-done.12.state_ref = bf16[8,2,128,128]{3,2,1,0:T(8,128)(2,1)S(1)} collective-permute-done((bf16[8,2,128,128]{3,2,1,0:T(8,128)(2,1)S(1)}, bf16[8,2,128,128]{3,2,1,0:T(8,128)(2,1)S(1)}, u32[]{:S(2)}, u32[]{:S(2)}) %collective-permute-start.12) | collective-permute-done | bytes 524320 | tf_op jit(solution)/shard_map/ppermute | solution.py:1147
  123.7 9.2 %collective-permute-done.14.refs_1_ = bf16[3,128,2432]{2,1,0:T(8,128)(2,1)} collective-permute-done((bf16[3,128,2432]{2,1,0:T(8,128)(2,1)S(1)}, bf16[3,128,2432]{2,1,0:T(8,128)(2,1)}, u32[]{:S(2)}, u32[]{:S(2)}) %collective-permute-start.14) | collective-permute-done | bytes 1867808 | tf_op jit(solution)/shard_map/ppermute | solution.py:945
  132.9 2.1 collective-permute-done.15.refs_2_
  136.2 4.8 %collective-permute-start.13 = (bf16[8,2,128,128]{3,2,1,0:T(8,128)(2,1)S(1)}, bf16[8,2,128,128]{3,2,1,0:T(8,128)(2,1)S(1)}, u32[]{:S(2)}, u32[]{:S(2)}) collective-permute-start(bf16[8,2,128,128]{3,2,1,0:T(8,128)(2,1)S(1)} %hop.5), channel_id=1, source_target_pairs={{0,1},{1,2},{2,3},{4,5},{5,6},{6,7},{8,9},{9,10},{10,11},{12,13},{... | collective-permute-start | bytes 1572872 | tf_op jit(solution)/shard_map/ppermute | solution.py:1150
  142.3 8.8 %collective-permute-done.13.state_ref = bf16[8,2,128,128]{3,2,1,0:T(8,128)(2,1)S(1)} collective-permute-done((bf16[8,2,128,128]{3,2,1,0:T(8,128)(2,1)S(1)}, bf16[8,2,128,128]{3,2,1,0:T(8,128)(2,1)S(1)}, u32[]{:S(2)}, u32[]{:S(2)}) %collective-permute-start.13) | collective-permute-done | bytes 524320 | tf_op jit(solution)/shard_map/ppermute | solution.py:1150
  151.2 6.8 %collective-permute-done.16.refs_3_ = bf16[3,128,2432]{2,1,0:T(8,128)(2,1)} collective-permute-done((bf16[3,128,2432]{2,1,0:T(8,128)(2,1)}, bf16[3,128,2432]{2,1,0:T(8,128)(2,1)}, u32[]{:S(2)}, u32[]{:S(2)}) %collective-permute-start.16) | collective-permute-done | bytes 1867808 | tf_op jit(solution)/shard_map/ppermute | solution.py:945
  158.0 1.8 collective-permute-start.20
  161.0 6.1 %mixer_output.1 = (bf16[2,256,1024]{2,1,0:T(8,128)(2,1)}, bf16[8,2,256,128]{3,2,1,0:T(8,128)(2,1)}) custom-call(bf16[8,2,256,256]{3,2,1,0:T(8,128)(2,1)} %get-tuple-element.248.qk_ref, bf16[8,2,256,256]{3,2,1,0:T(8,128)(2,1)} %get-tuple-element.249.p_ref, f32[8,2,256,128]{3,2,1,0:T(8,128)} %get-tuple-element.250.ub_ref, ...), custom_call_target="tpu_custom_call" | custom-call | flops 800000000 | bytes 8000000 | tf_op jit(solution)/shard_map/mixer_output/pallas_call | solution.py:770
  167.2 45.3 %ffn.1 = (bf16[512,1024]{1,0:T(8,128)(2,1)}, f32[512,1024]{1,0:T(8,128)}, bf16[512,1024]{1,0:T(8,128)(2,1)}, f32[512,1024]{1,0:T(8,128)}, f32[8,1024]{1,0:T(8,12...) custom-call(s32[8]{0:T(128)} %stack.89.ids_ref, ...), custom_call_target="tpu_custom_call" | custom-call | flops 38386270208 | bytes 60000000 | tf_op jit(solution)/shard_map/ffn/pallas_call | solution.py:838
  214.2 8.9 %mixer_back_local.1 = (f32[8,2,256,128]{3,2,1,0:T(8,128)}, f32[8,2,128,128]{3,2,1,0:T(8,128)}, bf16[8,2,128,128]{3,2,1,0:T(8,128)(2,1)}) custom-call(f32[2,256,1024]{2,1,0:T(8,128)} %bitcast.125, bf16[8,2,256,256]{3,2,1,0:T(8,128)(2,1)} %get-tuple-element.248.qk_ref, bf16[8,2,256,256]{3,2,1,0:T(8,128)(2,1)} %get-tuple-element.269.t_ref, ...), custom_call_target="tpu_custom_call" | custom-call | flops 800000000 | bytes 8000000 | tf_op jit(solution)/shard_map/mixer_back_local/pallas_call | solution.py:785
  224.4 4.9 %add_convert_fusion.1 = bf16[4,2,128,2176]{3,2,1,0:T(8,128)(2,1)S(1)} fusion(bf16[4,2,128,2176]{3,2,1,0:T(8,128)(2,1)} %collective-permute-done.22, bf16[4,2,128,2176]{3,2,1,0:T(8,128)(2,1)} %get-tuple-element.280), kind=kLoop, calls=%fused_computation.1 | loop fusion | flops 8912896 | bytes 13369344 | tf_op jit(solution)/shard_map/convert_element_type | solution.py:988
  229.3 2.5 fusion.8
  233.5 6.4 %collective-permute-done.21.state_ref = bf16[8,2,128,128]{3,2,1,0:T(8,128)(2,1)S(1)} collective-permute-done((bf16[8,2,128,128]{3,2,1,0:T(8,128)(2,1)}, bf16[8,2,128,128]{3,2,1,0:T(8,128)(2,1)S(1)}, u32[]{:S(2)}, u32[]{:S(2)}) %collective-permute-start.21) | collective-permute-done | bytes 524320 | tf_op jit(solution)/shard_map/ppermute | solution.py:1170
  242.1 3.4 add_convert_fusion
  245.5 2.4 fusion.7
  248.5 4.2 flip.1
  252.7 4.0 collective-permute-done.23.state_ref
  258.9 2.1 add_convert_fusion.3
  261.3 10.8 %collective-permute-done.25.dstate_ref = bf16[8,2,128,128]{3,2,1,0:T(8,128)(2,1)S(1)} collective-permute-done((bf16[8,2,128,128]{3,2,1,0:T(8,128)(2,1)S(1)}, bf16[8,2,128,128]{3,2,1,0:T(8,128)(2,1)S(1)}, u32[]{:S(2)}, u32[]{:S(2)}) %collective-permute-start.25) | collective-permute-done | bytes 524320 | tf_op jit(solution)/shard_map/ppermute | solution.py:1177
  273.3 26.6 %mixer_back.1 = (bf16[2,272,3072]{2,1,0:T(8,128)(2,1)}, f32[2,256,128]{2,1,0:T(8,128)}, f32[8,16,128]{2,1,0:T(8,128)}) custom-call(f32[2,256,1024]{2,1,0:T(8,128)} %bitcast.126, f32[8,2,256,128]{3,2,1,0:T(8,128)} %get-tuple-element.271.y_ref, bf16[8,2,256,256]{3,2,1,0:T(8,128)(2,1)} %get-tuple-element.248.qk_ref, ...), custom_call_target="tpu_custom_call" | custom-call | flops 8000000000 | bytes 32000000 | tf_op jit(solution)/shard_map/mixer_back/pallas_call | solution.py:799
  299.9 10.4 %grad_mixer.1 = (bf16[4,2,128,1024]{3,2,1,0:T(8,128)(2,1)}, bf16[4,2,128,1024]{3,2,1,0:T(8,128)(2,1)}, bf16[4,2,128,1024]{3,2,1,0:T(8,128)(2,1)}, bf16[4,2,128,1024]{3,2,1,0:T(8,128)(2,1)}) custom-call(bf16[1024,544]{1,0:T(8,128)(2,1)} %get-tuple-element.315.xt_ref, bf16[544,3072]{1,0:T(8,128)(2,1)} %bitcast.152, ...), custom_call_target="tpu_custom_call" | custom-call | flops 4294967296 | bytes 8388608 | tf_op jit(solution)/shard_map/grad_mixer/pallas_call | solution.py:874
  310.4 1.5 collective-permute-start.27
  311.9 1.7 add_convert_fusion.7
  315.8 2.1 add_convert_fusion.2
  321.4 1.5 fusion.10
  326.7 11.4 %input_back.1 = (f32[2,16,1024]{2,1,0:T(8,128)}, f32[2,256,1024]{2,1,0:T(8,128)}) custom-call(bf16[2,272,3072]{2,1,0:T(8,128)(2,1)} %get-tuple-element.343.dqkv_ref, bf16[4,8,144,768]{3,2,1,0:T(8,128)(2,1)} %get-tuple-element.344.w_ref, bf16[2,256,128]{2,1,0:T(8,128)(2,1)} %convert_element_type.205.db_ref, bf16[4,128,1024]{2,1,0:T(8,128)(2,1)} %pad_maximum_fusion.3.beta_w_ref), custom_call_target="tpu_custom_call" | custom-call | flops 3422552064 | bytes 6291456 | tf_op jit(solution)/shard_map/input_back/pallas_call | solution.py:927
  344.0 1.6 add_convert_fusion.6
  345.7 3.2 collective-permute-start.38
  350.2 3.5 collective-permute-done.32
  353.7 1.6 add_convert_fusion.9
  356.3 13.2 %collective-permute-done.36 = bf16[2,2,128,1024]{3,2,1,0:T(8,128)(2,1)} collective-permute-done((bf16[2,2,128,1024]{3,2,1,0:T(8,128)(2,1)}, bf16[2,2,128,1024]{3,2,1,0:T(8,128)(2,1)}, u32[]{:S(2)}, u32[]{:S(2)}) %collective-permute-start.36) | collective-permute-done | bytes 1048608 | tf_op jit(solution)/shard_map/ppermute | solution.py:945
  369.5 1.6 add_convert_fusion.8
  374.9 3.0 collective-permute-start.43
  378.1 2.2 collective-permute-done.40
  380.3 1.8 collective-permute-start.39
  382.4 5.4 %collective-permute-done.39 = bf16[128,1024]{1,0:T(8,128)(2,1)S(1)} collective-permute-done((bf16[128,1024]{1,0:T(8,128)(2,1)S(1)}, bf16[128,1024]{1,0:T(8,128)(2,1)S(1)}, u32[]{:S(2)}, u32[]{:S(2)}) %collective-permute-start.39) | collective-permute-done | bytes 262176 | tf_op jit(solution)/shard_map/ppermute | solution.py:965
  387.8 4.5 input_norm.1
  393.2 8.8 %collective-permute-start.44 = (f32[4,5632]{1,0:T(4,128)S(1)}, f32[4,5632]{1,0:T(4,128)S(1)}, u32[]{:S(2)}, u32[]{:S(2)}) collective-permute-start(f32[4,5632]{1,0:T(4,128)S(1)} %pad_maximum_fusion.6), channel_id=1, source_target_pairs={{0,4},{4,0},{8,12},{12,8},{16,20},{20,16},{24,28},{28,24},{1,5},{5... | collective-permute-start | bytes 270344 | tf_op jit(solution)/shard_map/ppermute | solution.py:945
  403.4 1.7 collective-permute-start.50
  406.9 4.3 collective-permute-done.50
  411.2 6.5 %collective-permute-done.49 = bf16[128,1024]{1,0:T(8,128)(2,1)S(1)} collective-permute-done((bf16[128,1024]{1,0:T(8,128)(2,1)S(1)}, bf16[128,1024]{1,0:T(8,128)(2,1)S(1)}, u32[]{:S(2)}, u32[]{:S(2)}) %collective-permute-start.49) | collective-permute-done | bytes 262176 | tf_op jit(solution)/shard_map/ppermute | solution.py:965
  419.7 1.5 collective-permute-start.53
  421.3 2.3 collective-permute-done.51.refs_1_
  423.6 3.2 collective-permute-done.52.refs_2_
  429.1 4.1 collective-permute-done.54
  436.5 3.6 collective-permute-start.60
  441.2 7.8 %finish_ffn.1 = (f32[704,1024]{1,0:T(8,128)}, f32[704,1024]{1,0:T(8,128)}, f32[704,1024]{1,0:T(8,128)}) custom-call(s32[8]{0:T(128)} %stack.89.ids_ref, bf16[128,2176]{1,0:T(8,128)(2,1)} %copy-done.9, bf16[128,2176]{1,0:T(8,128)(2,1)} %copy-done.10, bf16[128,2176]{1,0:T(8,128)(2,1)} %copy-done.11, bf16[128,2176]{1,0:T(8,128)(2,1)} %copy-done.21, ...), custom_call_target="tpu_custom_call" | custom-call | bytes 13369344 | tf_op jit(solution)/shard_map/finish_ffn/pallas_call | solution.py:886
  451.6 5.7 %finish_mixer.1 = (f32[1024,256]{1,0:T(8,128)}, f32[1024,256]{1,0:T(8,128)}, f32[1024,256]{1,0:T(8,128)}, f32[256,1024]{1,0:T(8,128)}) custom-call(s32[8]{0:T(128)} %stack.89.ids_ref, bf16[128,1024]{1,0:T(8,128)(2,1)} %copy-done.16, bf16[128,1024]{1,0:T(8,128)(2,1)} %copy-done.17, bf16[128,1024]{1,0:T(8,128)(2,1)} %copy-done.18, ...), custom_call_target="tpu_custom_call" | custom-call | bytes 6291456 | tf_op jit(solution)/shard_map/finish_mixer/pallas_call | solution.py:912
  (250 shorter events, 66.3 us)
Async XLA Ops:
  7.2 83.3 %all-gather.3.cloned.1.call-start = ((), (), s32[]{:S(2)}) async-start(), calls=%async_computation | async-start | bytes 3112960 | tf_op jit(solution)/shard_map/all_gather | solution.py:1121
  9.0 19.5 %collective-permute-start = (bf16[144,768]{1,0:T(8,128)(2,1)}, bf16[144,768]{1,0:T(8,128)(2,1)S(1)}, u32[]{:S(2)}, u32[]{:S(2)}) collective-permute-start(bf16[144,768]{1,0:T(8,128)(2,1)} %bitcast.131), channel_id=1, source_target_pairs={{0,3},{1,0},{2,1},{3,2},{4,7},{5,4},{6,5},{7,6},{8,11},{9,8},{10,9... | collective-permute-start | bytes 663560 | tf_op jit(solution)/shard_map/ppermute | solution.py:961
  13.1 18.4 %collective-permute-start.1 = (bf16[144,768]{1,0:T(8,128)(2,1)}, bf16[144,768]{1,0:T(8,128)(2,1)S(1)}, u32[]{:S(2)}, u32[]{:S(2)}) collective-permute-start(bf16[144,768]{1,0:T(8,128)(2,1)} %bitcast.132), channel_id=1, source_target_pairs={{0,2},{1,3},{2,0},{3,1},{4,6},{5,7},{6,4},{7,5},{8,10},{9,11},{10,... | collective-permute-start | bytes 663560 | tf_op jit(solution)/shard_map/ppermute | solution.py:961
  13.1 18.4 %collective-permute-start.2 = (bf16[144,768]{1,0:T(8,128)(2,1)}, bf16[144,768]{1,0:T(8,128)(2,1)S(1)}, u32[]{:S(2)}, u32[]{:S(2)}) collective-permute-start(bf16[144,768]{1,0:T(8,128)(2,1)} %bitcast.133), channel_id=1, source_target_pairs={{0,1},{1,2},{2,3},{3,0},{4,5},{5,6},{6,7},{7,4},{8,9},{9,10},{10,1... | collective-permute-start | bytes 663560 | tf_op jit(solution)/shard_map/ppermute | solution.py:961
  15.4 13.0 %collective-permute-start.3 = (bf16[2,16,1024]{2,1,0:T(8,128)(2,1)S(1)}, bf16[2,16,1024]{2,1,0:T(8,128)(2,1)S(1)}, u32[]{:S(2)}, u32[]{:S(2)}) collective-permute-start(bf16[2,16,1024]{2,1,0:T(8,128)(2,1)S(1)} %slice.184), channel_id=1, source_target_pairs={{0,1},{1,2},{2,3},{4,5},{5,6},{6,7},{8,9},{9,10},{10,11},{12,13},{... | collective-permute-start | bytes 196616 | tf_op jit(solution)/shard_map/ppermute | solution.py:1114
  31.7 13.4 %collective-permute-start.4 = (bf16[3,144,768]{2,1,0:T(8,128)(2,1)S(1)}, bf16[3,144,768]{2,1,0:T(8,128)(2,1)S(1)}, u32[]{:S(2)}, u32[]{:S(2)}) collective-permute-start(bf16[3,144,768]{2,1,0:T(8,128)(2,1)S(1)} %pad_maximum_fusion.4.refs_0_), channel_id=1, source_target_pairs={{0,8},{4,20},{8,0},{12,28},{16,24},{20,4},{24,16},{28,12},{1,9},{5... | collective-permute-start | bytes 1990664 | tf_op jit(solution)/shard_map/ppermute | solution.py:945
  33.0 16.3 %collective-permute-start.5 = (bf16[3,144,768]{2,1,0:T(8,128)(2,1)S(1)}, bf16[3,144,768]{2,1,0:T(8,128)(2,1)S(1)}, u32[]{:S(2)}, u32[]{:S(2)}) collective-permute-start(bf16[3,144,768]{2,1,0:T(8,128)(2,1)S(1)} %pad_maximum_fusion.4.refs_0_), channel_id=1, source_target_pairs={{0,16},{4,12},{8,24},{12,4},{16,0},{20,28},{24,8},{28,20},{1,17},{... | collective-permute-start | bytes 1990664 | tf_op jit(solution)/shard_map/ppermute | solution.py:945
  49.3 9.9 %collective-permute-start.6 = (bf16[3,144,768]{2,1,0:T(8,128)(2,1)S(1)}, bf16[3,144,768]{2,1,0:T(8,128)(2,1)S(1)}, u32[]{:S(2)}, u32[]{:S(2)}) collective-permute-start(bf16[3,144,768]{2,1,0:T(8,128)(2,1)S(1)} %collective-permute-done.4.refs_1_), channel_id=1, source_target_pairs={{0,16},{4,12},{8,24},{12,4},{16,0},{20,28},{24,8},{28,20},{1,17},{... | collective-permute-start | bytes 1990664 | tf_op jit(solution)/shard_map/ppermute | solution.py:945
  50.5 8.7 %collective-permute-start.8 = (bf16[3,144,768]{2,1,0:T(8,128)(2,1)S(1)}, bf16[3,144,768]{2,1,0:T(8,128)(2,1)S(1)}, u32[]{:S(2)}, u32[]{:S(2)}) collective-permute-start(bf16[3,144,768]{2,1,0:T(8,128)(2,1)S(1)} %collective-permute-done.4.refs_1_), channel_id=1, source_target_pairs={{0,4},{4,0},{8,12},{12,8},{16,20},{20,16},{24,28},{28,24},{1,5},{5... | collective-permute-start | bytes 1990664 | tf_op jit(solution)/shard_map/ppermute | solution.py:945
  50.9 8.3 %collective-permute-start.7 = (bf16[3,144,768]{2,1,0:T(8,128)(2,1)S(1)}, bf16[3,144,768]{2,1,0:T(8,128)(2,1)S(1)}, u32[]{:S(2)}, u32[]{:S(2)}) collective-permute-start(bf16[3,144,768]{2,1,0:T(8,128)(2,1)S(1)} %pad_maximum_fusion.4.refs_0_), channel_id=1, source_target_pairs={{0,4},{4,0},{8,12},{12,8},{16,20},{20,16},{24,28},{28,24},{1,5},{5... | collective-permute-start | bytes 1990664 | tf_op jit(solution)/shard_map/ppermute | solution.py:945
  51.0 8.2 %collective-permute-start.9 = (bf16[3,144,768]{2,1,0:T(8,128)(2,1)S(1)}, bf16[3,144,768]{2,1,0:T(8,128)(2,1)S(1)}, u32[]{:S(2)}, u32[]{:S(2)}) collective-permute-start(bf16[3,144,768]{2,1,0:T(8,128)(2,1)S(1)} %collective-permute-done.5.refs_2_), channel_id=1, source_target_pairs={{0,4},{4,0},{8,12},{12,8},{16,20},{20,16},{24,28},{28,24},{1,5},{5... | collective-permute-start | bytes 1990664 | tf_op jit(solution)/shard_map/ppermute | solution.py:945
  60.1 3.7 collective-permute-start.10
  92.4 48.6 %copy-start.15 = (bf16[3,128,2432]{2,1,0:T(8,128)(2,1)}, bf16[3,128,2432]{2,1,0:T(8,128)(2,1)S(1)}, u32[]{:S(2)}) copy-start(bf16[3,128,2432]{2,1,0:T(8,128)(2,1)S(1)} %pad_maximum_fusion.refs_0_) | copy-start | bytes 5603332
  92.4 40.5 %collective-permute-start.14 = (bf16[3,128,2432]{2,1,0:T(8,128)(2,1)S(1)}, bf16[3,128,2432]{2,1,0:T(8,128)(2,1)}, u32[]{:S(2)}, u32[]{:S(2)}) collective-permute-start(bf16[3,128,2432]{2,1,0:T(8,128)(2,1)S(1)} %pad_maximum_fusion.refs_0_), channel_id=1, source_target_pairs={{0,8},{4,20},{8,0},{12,28},{16,24},{20,4},{24,16},{28,12},{1,9},{5... | collective-permute-start | bytes 5603336 | tf_op jit(solution)/shard_map/ppermute | solution.py:945
  92.7 42.3 %collective-permute-start.15 = (bf16[3,128,2432]{2,1,0:T(8,128)(2,1)S(1)}, bf16[3,128,2432]{2,1,0:T(8,128)(2,1)}, u32[]{:S(2)}, u32[]{:S(2)}) collective-permute-start(bf16[3,128,2432]{2,1,0:T(8,128)(2,1)S(1)} %pad_maximum_fusion.refs_0_), channel_id=1, source_target_pairs={{0,16},{4,12},{8,24},{12,4},{16,0},{20,28},{24,8},{28,20},{1,17},{... | collective-permute-start | bytes 5603336 | tf_op jit(solution)/shard_map/ppermute | solution.py:945
  93.9 14.5 %collective-permute-start.11 = (bf16[8,2,128,128]{3,2,1,0:T(8,128)(2,1)S(1)}, bf16[8,2,128,128]{3,2,1,0:T(8,128)(2,1)S(1)}, u32[]{:S(2)}, u32[]{:S(2)}) collective-permute-start(bf16[8,2,128,128]{3,2,1,0:T(8,128)(2,1)S(1)} %copy-done.42), channel_id=1, source_target_pairs={{0,1},{1,2},{2,3},{4,5},{5,6},{6,7},{8,9},{9,10},{10,11},{12,13},{... | collective-permute-start | bytes 1572872 | tf_op jit(solution)/shard_map/ppermute | solution.py:1144
  108.4 52.0 %copy-start.35 = (bf16[1024]{0:T(1024)(128)(2,1)S(1)}, bf16[1024]{0:T(1024)(128)(2,1)}, u32[]{:S(2)}) copy-start(bf16[1024]{0:T(1024)(128)(2,1)} %param.24) | copy-start | bytes 6148
  109.2 13.7 %collective-permute-start.12 = (bf16[8,2,128,128]{3,2,1,0:T(8,128)(2,1)S(1)}, bf16[8,2,128,128]{3,2,1,0:T(8,128)(2,1)S(1)}, u32[]{:S(2)}, u32[]{:S(2)}) collective-permute-start(bf16[8,2,128,128]{3,2,1,0:T(8,128)(2,1)S(1)} %hop.4), channel_id=1, source_target_pairs={{0,1},{1,2},{2,3},{4,5},{5,6},{6,7},{8,9},{9,10},{10,11},{12,13},{... | collective-permute-start | bytes 1572872 | tf_op jit(solution)/shard_map/ppermute | solution.py:1147
  135.0 23.0 %collective-permute-start.16 = (bf16[3,128,2432]{2,1,0:T(8,128)(2,1)}, bf16[3,128,2432]{2,1,0:T(8,128)(2,1)}, u32[]{:S(2)}, u32[]{:S(2)}) collective-permute-start(bf16[3,128,2432]{2,1,0:T(8,128)(2,1)} %collective-permute-done.14.refs_1_), channel_id=1, source_target_pairs={{0,16},{4,12},{8,24},{12,4},{16,0},{20,28},{24,8},{28,20},{1,17},{... | collective-permute-start | bytes 5603336 | tf_op jit(solution)/shard_map/ppermute | solution.py:945
  136.2 15.0 %collective-permute-start.13 = (bf16[8,2,128,128]{3,2,1,0:T(8,128)(2,1)S(1)}, bf16[8,2,128,128]{3,2,1,0:T(8,128)(2,1)S(1)}, u32[]{:S(2)}, u32[]{:S(2)}) collective-permute-start(bf16[8,2,128,128]{3,2,1,0:T(8,128)(2,1)S(1)} %hop.5), channel_id=1, source_target_pairs={{0,1},{1,2},{2,3},{4,5},{5,6},{6,7},{8,9},{9,10},{10,11},{12,13},{... | collective-permute-start | bytes 1572872 | tf_op jit(solution)/shard_map/ppermute | solution.py:1150
  140.9 26.2 %collective-permute-start.17 = (bf16[3,128,2432]{2,1,0:T(8,128)(2,1)S(1)}, bf16[3,128,2432]{2,1,0:T(8,128)(2,1)}, u32[]{:S(2)}, u32[]{:S(2)}) collective-permute-start(bf16[3,128,2432]{2,1,0:T(8,128)(2,1)S(1)} %pad_maximum_fusion.refs_0_), channel_id=1, source_target_pairs={{0,4},{4,0},{8,12},{12,8},{16,20},{20,16},{24,28},{28,24},{1,5},{5... | collective-permute-start | bytes 5603336 | tf_op jit(solution)/shard_map/ppermute | solution.py:945
  141.8 25.3 %collective-permute-start.18 = (bf16[3,128,2432]{2,1,0:T(8,128)(2,1)}, bf16[3,128,2432]{2,1,0:T(8,128)(2,1)}, u32[]{:S(2)}, u32[]{:S(2)}) collective-permute-start(bf16[3,128,2432]{2,1,0:T(8,128)(2,1)} %collective-permute-done.14.refs_1_), channel_id=1, source_target_pairs={{0,4},{4,0},{8,12},{12,8},{16,20},{20,16},{24,28},{28,24},{1,5},{5... | collective-permute-start | bytes 5603336 | tf_op jit(solution)/shard_map/ppermute | solution.py:945
  141.9 25.2 %collective-permute-start.19 = (bf16[3,128,2432]{2,1,0:T(8,128)(2,1)}, bf16[3,128,2432]{2,1,0:T(8,128)(2,1)}, u32[]{:S(2)}, u32[]{:S(2)}) collective-permute-start(bf16[3,128,2432]{2,1,0:T(8,128)(2,1)} %collective-permute-done.15.refs_2_), channel_id=1, source_target_pairs={{0,4},{4,0},{8,12},{12,8},{16,20},{20,16},{24,28},{28,24},{1,5},{5... | collective-permute-start | bytes 5603336 | tf_op jit(solution)/shard_map/ppermute | solution.py:945
  158.0 9.1 %collective-permute-start.20 = (bf16[3,128,2432]{2,1,0:T(8,128)(2,1)}, bf16[3,128,2432]{2,1,0:T(8,128)(2,1)}, u32[]{:S(2)}, u32[]{:S(2)}) collective-permute-start(bf16[3,128,2432]{2,1,0:T(8,128)(2,1)} %collective-permute-done.16.refs_3_), channel_id=1, source_target_pairs={{0,4},{4,0},{8,12},{12,8},{16,20},{20,16},{24,28},{28,24},{1,5},{5... | collective-permute-start | bytes 5603336 | tf_op jit(solution)/shard_map/ppermute | solution.py:945
  212.4 11.9 %collective-permute-start.22 = (bf16[4,2,128,2176]{3,2,1,0:T(8,128)(2,1)}, bf16[4,2,128,2176]{3,2,1,0:T(8,128)(2,1)}, u32[]{:S(2)}, u32[]{:S(2)}) collective-permute-start(bf16[4,2,128,2176]{3,2,1,0:T(8,128)(2,1)} %get-tuple-element.274), channel_id=1, source_target_pairs={{0,4},{4,0},{8,12},{12,8},{16,20},{20,16},{24,28},{28,24},{1,5},{5... | collective-permute-start | bytes 13369352 | tf_op jit(solution)/shard_map/ppermute | solution.py:945
  212.5 29.5 %collective-permute-start.24 = (bf16[4,2,128,2176]{3,2,1,0:T(8,128)(2,1)}, bf16[4,2,128,2176]{3,2,1,0:T(8,128)(2,1)}, u32[]{:S(2)}, u32[]{:S(2)}) collective-permute-start(bf16[4,2,128,2176]{3,2,1,0:T(8,128)(2,1)} %get-tuple-element.285), channel_id=1, source_target_pairs={{0,4},{4,0},{8,12},{12,8},{16,20},{20,16},{24,28},{28,24},{1,5},{5... | collective-permute-start | bytes 13369352 | tf_op jit(solution)/shard_map/ppermute | solution.py:945
  223.1 16.8 %collective-permute-start.21 = (bf16[8,2,128,128]{3,2,1,0:T(8,128)(2,1)}, bf16[8,2,128,128]{3,2,1,0:T(8,128)(2,1)S(1)}, u32[]{:S(2)}, u32[]{:S(2)}) collective-permute-start(bf16[8,2,128,128]{3,2,1,0:T(8,128)(2,1)} %get-tuple-element.273), channel_id=1, source_target_pairs={{1,0},{2,1},{3,2},{5,4},{6,5},{7,6},{9,8},{10,9},{11,10},{13,12},{... | collective-permute-start | bytes 1572872 | tf_op jit(solution)/shard_map/ppermute | solution.py:1170
  231.8 27.1 %collective-permute-start.26 = (bf16[2,2,128,2176]{3,2,1,0:T(8,128)(2,1)}, bf16[2,2,128,2176]{3,2,1,0:T(8,128)(2,1)}, u32[]{:S(2)}, u32[]{:S(2)}) collective-permute-start(bf16[2,2,128,2176]{3,2,1,0:T(8,128)(2,1)} %get-tuple-element.477), channel_id=1, source_target_pairs={{0,8},{4,20},{8,0},{12,28},{16,24},{20,4},{24,16},{28,12},{1,9},{5... | collective-permute-start | bytes 6684680 | tf_op jit(solution)/shard_map/ppermute | solution.py:945
  240.7 16.0 %collective-permute-start.23 = (bf16[8,2,128,128]{3,2,1,0:T(8,128)(2,1)S(1)}, bf16[8,2,128,128]{3,2,1,0:T(8,128)(2,1)S(1)}, u32[]{:S(2)}, u32[]{:S(2)}) collective-permute-start(bf16[8,2,128,128]{3,2,1,0:T(8,128)(2,1)S(1)} %hop.6), channel_id=1, source_target_pairs={{1,0},{2,1},{3,2},{5,4},{6,5},{7,6},{9,8},{10,9},{11,10},{13,12},{... | collective-permute-start | bytes 1572872 | tf_op jit(solution)/shard_map/ppermute | solution.py:1173
  248.0 66.7 %collective-permute-start.29 = (bf16[2,2,128,2176]{3,2,1,0:T(8,128)(2,1)}, bf16[2,2,128,2176]{3,2,1,0:T(8,128)(2,1)}, u32[]{:S(2)}, u32[]{:S(2)}) collective-permute-start(bf16[2,2,128,2176]{3,2,1,0:T(8,128)(2,1)} %get-tuple-element.475), channel_id=1, source_target_pairs={{0,8},{4,20},{8,0},{12,28},{16,24},{20,4},{24,16},{28,12},{1,9},{5... | collective-permute-start | bytes 6684680 | tf_op jit(solution)/shard_map/ppermute | solution.py:945
  257.6 14.4 %collective-permute-start.25 = (bf16[8,2,128,128]{3,2,1,0:T(8,128)(2,1)S(1)}, bf16[8,2,128,128]{3,2,1,0:T(8,128)(2,1)S(1)}, u32[]{:S(2)}, u32[]{:S(2)}) collective-permute-start(bf16[8,2,128,128]{3,2,1,0:T(8,128)(2,1)S(1)} %hop.7), channel_id=1, source_target_pairs={{1,0},{2,1},{3,2},{5,4},{6,5},{7,6},{9,8},{10,9},{11,10},{13,12},{... | collective-permute-start | bytes 1572872 | tf_op jit(solution)/shard_map/ppermute | solution.py:1177
  272.0 39.9 %collective-permute-start.30 = (bf16[2,128,2176]{2,1,0:T(8,128)(2,1)S(1)}, bf16[2,128,2176]{2,1,0:T(8,128)(2,1)}, u32[]{:S(2)}, u32[]{:S(2)}) collective-permute-start(bf16[2,128,2176]{2,1,0:T(8,128)(2,1)S(1)} %get-tuple-element.484), channel_id=1, source_target_pairs={{0,16},{4,12},{8,24},{12,4},{16,0},{20,28},{24,8},{28,20},{1,17},{... | collective-permute-start | bytes 3342344 | tf_op jit(solution)/shard_map/ppermute | solution.py:945
  310.4 12.5 %collective-permute-start.27 = (bf16[4,2,128,1024]{3,2,1,0:T(8,128)(2,1)}, bf16[4,2,128,1024]{3,2,1,0:T(8,128)(2,1)S(1)}, u32[]{:S(2)}, u32[]{:S(2)}) collective-permute-start(bf16[4,2,128,1024]{3,2,1,0:T(8,128)(2,1)} %get-tuple-element.317), channel_id=1, source_target_pairs={{0,4},{4,0},{8,12},{12,8},{16,20},{20,16},{24,28},{28,24},{1,5},{5... | collective-permute-start | bytes 6291464 | tf_op jit(solution)/shard_map/ppermute | solution.py:945
  311.8 8.5 %collective-permute-start.28 = (bf16[4,2,128,1024]{3,2,1,0:T(8,128)(2,1)}, bf16[4,2,128,1024]{3,2,1,0:T(8,128)(2,1)S(1)}, u32[]{:S(2)}, u32[]{:S(2)}) collective-permute-start(bf16[4,2,128,1024]{3,2,1,0:T(8,128)(2,1)} %get-tuple-element.318), channel_id=1, source_target_pairs={{0,4},{4,0},{8,12},{12,8},{16,20},{20,16},{24,28},{28,24},{1,5},{5... | collective-permute-start | bytes 6291464 | tf_op jit(solution)/shard_map/ppermute | solution.py:945
  314.6 31.0 %collective-permute-start.33 = (bf16[128,2176]{1,0:T(8,128)(2,1)}, bf16[128,2176]{1,0:T(8,128)(2,1)}, u32[]{:S(2)}, u32[]{:S(2)}) collective-permute-start(bf16[128,2176]{1,0:T(8,128)(2,1)} %get-tuple-element.494), channel_id=1, source_target_pairs={{0,1},{1,2},{2,3},{3,0},{4,5},{5,6},{6,7},{7,4},{8,9},{9,10},{10,1... | collective-permute-start | bytes 1671176 | tf_op jit(solution)/shard_map/ppermute | solution.py:965
  319.1 24.9 %collective-permute-start.34 = (bf16[2,128,2176]{2,1,0:T(8,128)(2,1)}, bf16[2,128,2176]{2,1,0:T(8,128)(2,1)}, u32[]{:S(2)}, u32[]{:S(2)}) collective-permute-start(bf16[2,128,2176]{2,1,0:T(8,128)(2,1)} %get-tuple-element.482), channel_id=1, source_target_pairs={{0,16},{4,12},{8,24},{12,4},{16,0},{20,28},{24,8},{28,20},{1,17},{... | collective-permute-start | bytes 3342344 | tf_op jit(solution)/shard_map/ppermute | solution.py:945
  338.1 49.7 %collective-permute-start.31 = (f32[2,16,1024]{2,1,0:T(8,128)}, f32[2,16,1024]{2,1,0:T(8,128)}, u32[]{:S(2)}, u32[]{:S(2)}) collective-permute-start(f32[2,16,1024]{2,1,0:T(8,128)} %get-tuple-element.353), channel_id=1, source_target_pairs={{1,0},{2,1},{3,2},{5,4},{6,5},{7,6},{9,8},{10,9},{11,10},{13,12},{... | collective-permute-start | bytes 393224 | tf_op jit(solution)/shard_map/ppermute | solution.py:1194
  339.4 14.3 %collective-permute-start.32 = (bf16[2,2,128,1024]{3,2,1,0:T(8,128)(2,1)}, bf16[2,2,128,1024]{3,2,1,0:T(8,128)(2,1)}, u32[]{:S(2)}, u32[]{:S(2)}) collective-permute-start(bf16[2,2,128,1024]{3,2,1,0:T(8,128)(2,1)} %get-tuple-element.488), channel_id=1, source_target_pairs={{0,8},{4,20},{8,0},{12,28},{16,24},{20,4},{24,16},{28,12},{1,9},{5... | collective-permute-start | bytes 3145736 | tf_op jit(solution)/shard_map/ppermute | solution.py:945
  340.4 29.1 %collective-permute-start.36 = (bf16[2,2,128,1024]{3,2,1,0:T(8,128)(2,1)}, bf16[2,2,128,1024]{3,2,1,0:T(8,128)(2,1)}, u32[]{:S(2)}, u32[]{:S(2)}) collective-permute-start(bf16[2,2,128,1024]{3,2,1,0:T(8,128)(2,1)} %get-tuple-element.486), channel_id=1, source_target_pairs={{0,8},{4,20},{8,0},{12,28},{16,24},{20,4},{24,16},{28,12},{1,9},{5... | collective-permute-start | bytes 3145736 | tf_op jit(solution)/shard_map/ppermute | solution.py:945
  345.7 25.9 %collective-permute-start.38 = (bf16[128,2176]{1,0:T(8,128)(2,1)S(1)}, bf16[128,2176]{1,0:T(8,128)(2,1)S(1)}, u32[]{:S(2)}, u32[]{:S(2)}) collective-permute-start(bf16[128,2176]{1,0:T(8,128)(2,1)S(1)} %get-tuple-element.492), channel_id=1, source_target_pairs={{0,3},{1,0},{2,1},{3,2},{4,7},{5,4},{6,5},{7,6},{8,11},{9,8},{10,9... | collective-permute-start | bytes 1671176 | tf_op jit(solution)/shard_map/ppermute | solution.py:965
  350.1 22.7 %collective-permute-start.37 = (bf16[128,2176]{1,0:T(8,128)(2,1)S(1)}, bf16[128,2176]{1,0:T(8,128)(2,1)S(1)}, u32[]{:S(2)}, u32[]{:S(2)}) collective-permute-start(bf16[128,2176]{1,0:T(8,128)(2,1)S(1)} %add_convert_fusion.11), channel_id=1, source_target_pairs={{0,1},{1,2},{2,3},{3,0},{4,5},{5,6},{6,7},{7,4},{8,9},{9,10},{10,1... | collective-permute-start | bytes 1671176 | tf_op jit(solution)/shard_map/ppermute | solution.py:965
  355.4 19.5 %collective-permute-start.35 = (bf16[2,128,1024]{2,1,0:T(8,128)(2,1)S(1)}, bf16[2,128,1024]{2,1,0:T(8,128)(2,1)S(1)}, u32[]{:S(2)}, u32[]{:S(2)}) collective-permute-start(bf16[2,128,1024]{2,1,0:T(8,128)(2,1)S(1)} %get-tuple-element.499), channel_id=1, source_target_pairs={{0,16},{4,12},{8,24},{12,4},{16,0},{20,28},{24,8},{28,20},{1,17},{... | collective-permute-start | bytes 1572872 | tf_op jit(solution)/shard_map/ppermute | solution.py:945
  371.2 9.1 %collective-permute-start.40 = (bf16[2,128,1024]{2,1,0:T(8,128)(2,1)S(1)}, bf16[2,128,1024]{2,1,0:T(8,128)(2,1)S(1)}, u32[]{:S(2)}, u32[]{:S(2)}) collective-permute-start(bf16[2,128,1024]{2,1,0:T(8,128)(2,1)S(1)} %get-tuple-element.496), channel_id=1, source_target_pairs={{0,16},{4,12},{8,24},{12,4},{16,0},{20,28},{24,8},{28,20},{1,17},{... | collective-permute-start | bytes 1572872 | tf_op jit(solution)/shard_map/ppermute | solution.py:945
  373.0 28.9 %collective-permute-start.41 = (bf16[128,2176]{1,0:T(8,128)(2,1)S(1)}, bf16[128,2176]{1,0:T(8,128)(2,1)S(1)}, u32[]{:S(2)}, u32[]{:S(2)}) collective-permute-start(bf16[128,2176]{1,0:T(8,128)(2,1)S(1)} %add_convert_fusion.10.refs_0_), channel_id=1, source_target_pairs={{0,8},{4,20},{8,0},{12,28},{16,24},{20,4},{24,16},{28,12},{1,9},{5... | collective-permute-start | bytes 1671176 | tf_op jit(solution)/shard_map/ppermute | solution.py:945
  374.5 27.5 %collective-permute-start.42 = (bf16[128,2176]{1,0:T(8,128)(2,1)S(1)}, bf16[128,2176]{1,0:T(8,128)(2,1)S(1)}, u32[]{:S(2)}, u32[]{:S(2)}) collective-permute-start(bf16[128,2176]{1,0:T(8,128)(2,1)S(1)} %add_convert_fusion.10.refs_0_), channel_id=1, source_target_pairs={{0,16},{4,12},{8,24},{12,4},{16,0},{20,28},{24,8},{28,20},{1,17},{... | collective-permute-start | bytes 1671176 | tf_op jit(solution)/shard_map/ppermute | solution.py:945
  374.9 27.1 %collective-permute-start.43 = (bf16[128,2176]{1,0:T(8,128)(2,1)S(1)}, bf16[128,2176]{1,0:T(8,128)(2,1)S(1)}, u32[]{:S(2)}, u32[]{:S(2)}) collective-permute-start(bf16[128,2176]{1,0:T(8,128)(2,1)S(1)} %add_convert_fusion.10.refs_0_), channel_id=1, source_target_pairs={{0,4},{4,0},{8,12},{12,8},{16,20},{20,16},{24,28},{28,24},{1,5},{5... | collective-permute-start | bytes 1671176 | tf_op jit(solution)/shard_map/ppermute | solution.py:945
  380.3 7.4 %collective-permute-start.39 = (bf16[128,1024]{1,0:T(8,128)(2,1)S(1)}, bf16[128,1024]{1,0:T(8,128)(2,1)S(1)}, u32[]{:S(2)}, u32[]{:S(2)}) collective-permute-start(bf16[128,1024]{1,0:T(8,128)(2,1)S(1)} %get-tuple-element.505), channel_id=1, source_target_pairs={{0,1},{1,2},{2,3},{3,0},{4,5},{5,6},{6,7},{7,4},{8,9},{9,10},{10,1... | collective-permute-start | bytes 786440 | tf_op jit(solution)/shard_map/ppermute | solution.py:965
  393.2 9.7 %collective-permute-start.44 = (f32[4,5632]{1,0:T(4,128)S(1)}, f32[4,5632]{1,0:T(4,128)S(1)}, u32[]{:S(2)}, u32[]{:S(2)}) collective-permute-start(f32[4,5632]{1,0:T(4,128)S(1)} %pad_maximum_fusion.6), channel_id=1, source_target_pairs={{0,4},{4,0},{8,12},{12,8},{16,20},{20,16},{24,28},{28,24},{1,5},{5... | collective-permute-start | bytes 270344 | tf_op jit(solution)/shard_map/ppermute | solution.py:945
  403.0 18.2 %collective-permute-start.46 = (bf16[2,128,2176]{2,1,0:T(8,128)(2,1)S(1)}, bf16[2,128,2176]{2,1,0:T(8,128)(2,1)S(1)}, u32[]{:S(2)}, u32[]{:S(2)}) collective-permute-start(bf16[2,128,2176]{2,1,0:T(8,128)(2,1)S(1)} %pad_maximum_fusion.2), channel_id=1, source_target_pairs={{0,4},{4,0},{8,12},{12,8},{16,20},{20,16},{24,28},{28,24},{1,5},{5... | collective-permute-start | bytes 3342344 | tf_op jit(solution)/shard_map/ppermute | solution.py:945
  403.4 7.8 %collective-permute-start.50 = (bf16[128,1024]{1,0:T(8,128)(2,1)S(1)}, bf16[128,1024]{1,0:T(8,128)(2,1)S(1)}, u32[]{:S(2)}, u32[]{:S(2)}) collective-permute-start(bf16[128,1024]{1,0:T(8,128)(2,1)S(1)} %get-tuple-element.502), channel_id=1, source_target_pairs={{0,3},{1,0},{2,1},{3,2},{4,7},{5,4},{6,5},{7,6},{8,11},{9,8},{10,9... | collective-permute-start | bytes 786440 | tf_op jit(solution)/shard_map/ppermute | solution.py:965
  405.2 12.4 %collective-permute-start.49 = (bf16[128,1024]{1,0:T(8,128)(2,1)S(1)}, bf16[128,1024]{1,0:T(8,128)(2,1)S(1)}, u32[]{:S(2)}, u32[]{:S(2)}) collective-permute-start(bf16[128,1024]{1,0:T(8,128)(2,1)S(1)} %add_convert_fusion.15), channel_id=1, source_target_pairs={{0,1},{1,2},{2,3},{3,0},{4,5},{5,6},{6,7},{7,4},{8,9},{9,10},{10,1... | collective-permute-start | bytes 786440 | tf_op jit(solution)/shard_map/ppermute | solution.py:965
  405.3 15.9 %collective-permute-start.45 = (bf16[128,2176]{1,0:T(8,128)(2,1)S(1)}, bf16[128,2176]{1,0:T(8,128)(2,1)S(1)}, u32[]{:S(2)}, u32[]{:S(2)}) collective-permute-start(bf16[128,2176]{1,0:T(8,128)(2,1)S(1)} %collective-permute-done.41.refs_1_), channel_id=1, source_target_pairs={{0,16},{4,12},{8,24},{12,4},{16,0},{20,28},{24,8},{28,20},{1,17},{... | collective-permute-start | bytes 1671176 | tf_op jit(solution)/shard_map/ppermute | solution.py:945
  406.5 13.2 %collective-permute-start.47 = (f32[4,5632]{1,0:T(4,128)S(1)}, f32[4,5632]{1,0:T(4,128)S(1)}, u32[]{:S(2)}, u32[]{:S(2)}) collective-permute-start(f32[4,5632]{1,0:T(4,128)S(1)} %add.160), channel_id=1, source_target_pairs={{0,8},{4,12},{8,0},{12,4},{16,24},{20,28},{24,16},{28,20},{1,9},{5... | collective-permute-start | bytes 270344 | tf_op jit(solution)/shard_map/ppermute | solution.py:945
  417.8 5.8 %collective-permute-start.51 = (bf16[128,1024]{1,0:T(8,128)(2,1)S(1)}, bf16[128,1024]{1,0:T(8,128)(2,1)S(1)}, u32[]{:S(2)}, u32[]{:S(2)}) collective-permute-start(bf16[128,1024]{1,0:T(8,128)(2,1)S(1)} %add_convert_fusion.14.refs_0_), channel_id=1, source_target_pairs={{0,8},{4,20},{8,0},{12,28},{16,24},{20,4},{24,16},{28,12},{1,9},{5... | collective-permute-start | bytes 786440 | tf_op jit(solution)/shard_map/ppermute | solution.py:945
  418.9 7.9 %collective-permute-start.52 = (bf16[128,1024]{1,0:T(8,128)(2,1)S(1)}, bf16[128,1024]{1,0:T(8,128)(2,1)S(1)}, u32[]{:S(2)}, u32[]{:S(2)}) collective-permute-start(bf16[128,1024]{1,0:T(8,128)(2,1)S(1)} %add_convert_fusion.14.refs_0_), channel_id=1, source_target_pairs={{0,16},{4,12},{8,24},{12,4},{16,0},{20,28},{24,8},{28,20},{1,17},{... | collective-permute-start | bytes 786440 | tf_op jit(solution)/shard_map/ppermute | solution.py:945
  419.7 7.1 %collective-permute-start.53 = (bf16[128,1024]{1,0:T(8,128)(2,1)S(1)}, bf16[128,1024]{1,0:T(8,128)(2,1)S(1)}, u32[]{:S(2)}, u32[]{:S(2)}) collective-permute-start(bf16[128,1024]{1,0:T(8,128)(2,1)S(1)} %add_convert_fusion.14.refs_0_), channel_id=1, source_target_pairs={{0,4},{4,0},{8,12},{12,8},{16,20},{20,16},{24,28},{28,24},{1,5},{5... | collective-permute-start | bytes 786440 | tf_op jit(solution)/shard_map/ppermute | solution.py:945
  421.2 12.0 %collective-permute-start.48 = (bf16[128,2176]{1,0:T(8,128)(2,1)S(1)}, bf16[128,2176]{1,0:T(8,128)(2,1)S(1)}, u32[]{:S(2)}, u32[]{:S(2)}) collective-permute-start(bf16[128,2176]{1,0:T(8,128)(2,1)S(1)} %collective-permute-done.45.refs_3_), channel_id=1, source_target_pairs={{0,4},{4,0},{8,12},{12,8},{16,20},{20,16},{24,28},{28,24},{1,5},{5... | collective-permute-start | bytes 1671176 | tf_op jit(solution)/shard_map/ppermute | solution.py:945
  426.9 8.7 %collective-permute-start.59 = (bf16[2,128,1024]{2,1,0:T(8,128)(2,1)S(1)}, bf16[2,128,1024]{2,1,0:T(8,128)(2,1)S(1)}, u32[]{:S(2)}, u32[]{:S(2)}) collective-permute-start(bf16[2,128,1024]{2,1,0:T(8,128)(2,1)S(1)} %pad_maximum_fusion.5), channel_id=1, source_target_pairs={{0,4},{4,0},{8,12},{12,8},{16,20},{20,16},{24,28},{28,24},{1,5},{5... | collective-permute-start | bytes 1572872 | tf_op jit(solution)/shard_map/ppermute | solution.py:945
  427.7 7.8 %collective-permute-start.58 = (bf16[128,1024]{1,0:T(8,128)(2,1)S(1)}, bf16[128,1024]{1,0:T(8,128)(2,1)S(1)}, u32[]{:S(2)}, u32[]{:S(2)}) collective-permute-start(bf16[128,1024]{1,0:T(8,128)(2,1)S(1)} %collective-permute-done.51.refs_1_), channel_id=1, source_target_pairs={{0,16},{4,12},{8,24},{12,4},{16,0},{20,28},{24,8},{28,20},{1,17},{... | collective-permute-start | bytes 786440 | tf_op jit(solution)/shard_map/ppermute | solution.py:945
  428.5 4.6 collective-permute-start.54
  433.5 15.6 %collective-permute-start.57 = (f32[5632]{0:T(1024)S(1)}, f32[5632]{0:T(1024)S(1)}, u32[]{:S(2)}, u32[]{:S(2)}) collective-permute-start(f32[5632]{0:T(1024)S(1)} %get-tuple-element.472), channel_id=1, source_target_pairs={{0,3},{1,0},{2,1},{3,2},{4,7},{5,4},{6,5},{7,6},{8,11},{9,8},{10,9... | collective-permute-start | bytes 67592 | tf_op jit(solution)/shard_map/ppermute | solution.py:965
  434.6 14.4 %collective-permute-start.56 = (f32[5632]{0:T(1024)S(1)}, f32[5632]{0:T(1024)S(1)}, u32[]{:S(2)}, u32[]{:S(2)}) collective-permute-start(f32[5632]{0:T(1024)S(1)} %get-tuple-element.473), channel_id=1, source_target_pairs={{0,2},{1,3},{2,0},{3,1},{4,6},{5,7},{6,4},{7,5},{8,10},{9,11},{10,... | collective-permute-start | bytes 67592 | tf_op jit(solution)/shard_map/ppermute | solution.py:965
  435.6 13.5 %collective-permute-start.55 = (f32[5632]{0:T(1024)S(1)}, f32[5632]{0:T(1024)S(1)}, u32[]{:S(2)}, u32[]{:S(2)}) collective-permute-start(f32[5632]{0:T(1024)S(1)} %get-tuple-element.471), channel_id=1, source_target_pairs={{0,1},{1,2},{2,3},{3,0},{4,5},{5,6},{6,7},{7,4},{8,9},{9,10},{10,1... | collective-permute-start | bytes 67592 | tf_op jit(solution)/shard_map/ppermute | solution.py:965
  436.5 14.4 %collective-permute-start.60 = (bf16[128,1024]{1,0:T(8,128)(2,1)S(1)}, bf16[128,1024]{1,0:T(8,128)(2,1)S(1)}, u32[]{:S(2)}, u32[]{:S(2)}) collective-permute-start(bf16[128,1024]{1,0:T(8,128)(2,1)S(1)} %collective-permute-done.58.refs_3_), channel_id=1, source_target_pairs={{0,4},{4,0},{8,12},{12,8},{16,20},{20,16},{24,28},{28,24},{1,5},{5... | collective-permute-start | bytes 786440 | tf_op jit(solution)/shard_map/ppermute | solution.py:945
  (44 other events, 551.5 us)
Sparse Core Ops, SparseCore 0:
  31.7 55.3 all-gather.2

commit v4 on v3

--- a/solution.py
+++ b/solution.py
@@ -365,17 +365,16 @@
     out_ref[0, rows:] = jnp.where(row == 0, line, 0.0).astype(BF16)
 
 
-def pack_ffn_kernel(table_ref, gate_ref, up_ref, down_ref, out_w_ref, out_ref):
+def pack_ffn_kernel(table_ref, gate_ref, up_ref, down_ref, out_w_ref, gu_ref, do_ref):
     hidden, rows = gate_ref.shape
     main = hidden // HD * HD
-    out_ref[0, :, :main] = flip(gate_ref[:main])
-    out_ref[0, :, main : 2 * main] = flip(up_ref[:main])
-    rest = jnp.concatenate([gate_ref[main:], up_ref[main:]], axis=0)
-    out_ref[0, :, 2 * main : 2 * hidden] = flip(rest)
+    gu_ref[0, :, :main] = flip(gate_ref[:main])
+    gu_ref[0, :, main : 2 * main] = flip(up_ref[:main])
+    gu_ref[0, :, 2 * main :] = flip(jnp.concatenate([gate_ref[main:], up_ref[main:]], axis=0))
     wide = main + HD
     down = jnp.concatenate([down_ref[...].astype(F32), jnp.zeros((wide - hidden, rows), F32)], axis=0)
-    out_ref[0, :, 2 * hidden : 2 * hidden + wide] = down.T.astype(BF16)
-    out_ref[0, :, 2 * hidden + wide :] = flip(out_w_ref[...])
+    do_ref[0, :, :wide] = down.T.astype(BF16)
+    do_ref[0, :, wide:] = flip(out_w_ref[...])
 
 
 def flip_pieces(table_ref, src_ref, dst_ref):
@@ -385,8 +384,13 @@
         dst_ref[pos * rows : (pos + 1) * rows] = flip(src_ref[:, pl.ds(start, rows)])
 
 
-def ffn_kernel(hidden, ids_ref, table_ref, mixed_ref, rows_ref, dout_ref, gain_ref, own_ref, *refs):
-    pieces, refs = refs[:PIECES], refs[PIECES:]
+def ordered(pieces):
+    own, b, c, far, d, both, far_d = pieces
+    return [own, b, c, d, far, both.at[0], both.at[1], far_d]
+
+
+def ffn_kernel(hidden, ids_ref, table_ref, mixed_ref, rows_ref, dout_ref, gain_ref, *refs):
+    owns, groups, refs = refs[:2], [ordered(refs[2:9]), ordered(refs[9:16])], refs[16:]
     out_ref, dmid_ref, dlow_ref, dmixed_ref, gpart_ref = refs[:5]
     (w_ref, wo_ref, x_ref, xt_ref, dt_ref, mid_ref, res_ref, dn_ref, grad_ref, sems, o_sems,
      g_sems) = refs[-12:]
@@ -402,17 +406,21 @@
     ring = w_ref.shape[0]
     order = reduce_order(slots)
 
-    def brought(slot, target, start, size, sem):
-        columns = pl.ds(start, size)
+    def brought(slot, group, at, target, start, size, sem):
+        to = lambda ref: ref.at[:, pl.ds(start, size)]
         if slot == 0:
-            return [pltpu.make_async_copy(own_ref.at[:, :, columns], target, sem.at[0])]
+            return [pltpu.make_async_copy(owns[group].at[:, :, pl.ds(at, size)], target.at[:, :, pl.ds(start, size)], sem.at[0])]
         return [
-            pltpu.make_async_copy(piece.at[slot - 1, :, columns], target.at[ids_ref[j]], sem.at[j])
-            for j, piece in enumerate(pieces)
+            pltpu.make_async_copy(piece.at[slot - 1, :, pl.ds(at, size)], to(target.at[ids_ref[j]]), sem.at[j])
+            for j, piece in enumerate(groups[group])
         ]
 
-    outs = [brought(k, wo_ref.at[k], cut, part, o_sems.at[k]) for k in range(slots)]
-    mains = [brought(k, w_ref.at[i % ring], 0, cut, sems.at[i % ring]) for i, k in enumerate(order)]
+    outs = [brought(k, 1, wide, wo_ref.at[k], 0, part, o_sems.at[k]) for k in range(slots)]
+    mains = [
+        brought(k, 0, 0, w_ref.at[i % ring], 0, 2 * hidden, sems.at[0, i % ring])
+        + brought(k, 1, 0, w_ref.at[i % ring], 2 * hidden, wide, sems.at[1, i % ring])
+        for i, k in enumerate(order)
+    ]
 
     def leaving(i):
         return [
@@ -711,13 +719,13 @@
 def pack_ffn(table, gate_t, up_t, w_down, w_out):
     hidden, width = gate_t.shape
     rows = width // PIECES
-    n = 2 * hidden + hidden // HD * HD + HD + w_out.shape[0]
+    n = hidden // HD * HD + HD + w_out.shape[0]
     count = table.shape[0]
     return call(
         pack_ffn_kernel, count,
         [pl.BlockSpec((w.shape[0], rows), lambda i, t: (0, t[i])) for w in (gate_t, up_t, w_down, w_out)],
-        pl.BlockSpec((1, rows, n), lambda i, t: (i, 0, 0)),
-        sds((count, rows, n), BF16), (0, 4 * count * rows * n), "pack_ffn", prefetch=1,
+        [pl.BlockSpec((1, rows, m), lambda i, t: (i, 0, 0)) for m in (2 * hidden, n)],
+        [sds((count, rows, m), BF16) for m in (2 * hidden, n)], (0, 0), "pack_ffn", prefetch=1,
     )(table, gate_t, up_t, w_down, w_out)
 
 
@@ -825,6 +833,7 @@
 def ffn(ids, table, mixed, rows, d_out, gain, own, pieces, hidden):
     count, width = rows.shape
     slots = pieces[0].shape[0] + 1
+    assert len(pieces) == 14
     wide = hidden // HD * HD + HD
     part = mixed.shape[1] // slots
     piece = width // PIECES
@@ -838,7 +847,7 @@
     return call(
         functools.partial(ffn_kernel, hidden), 2 * slots,
         [pl.BlockSpec((count, part), lambda s, *_: (0, jnp.minimum(s, slots - 1))),
-         full, full, whole(gain.shape)] + [ANYWHERE] * (1 + PIECES),
+         full, full, whole(gain.shape)] + [ANYWHERE] * 16,
         [full, full, full, whole((count, mixed.shape[1])), whole((8, width))] + [ANYWHERE] * len(grads),
         outs + grads, (26 * count * width * hidden * slots, 6e7), "ffn",
         [
@@ -853,12 +862,12 @@
         ]
         + room
         + [
-            pltpu.SemaphoreType.DMA((ring, PIECES)),
+            pltpu.SemaphoreType.DMA((2, ring, PIECES)),
             pltpu.SemaphoreType.DMA((slots, PIECES)),
             g_sems,
         ],
         prefetch=2,
-    )(ids, table, mixed, rows, d_out, gain, own, *pieces)
+    )(ids, table, mixed, rows, d_out, gain, *own, *pieces)
 
 
 def grad_mixer(xt, d_qkv, lt, mixed, slots):
@@ -1113,18 +1122,28 @@
     behind = [(i + 1, i) for i in range(tensor - 1)]
     halo = lax.ppermute(mixer_in[:, tokens - HALO :], "tensor", ahead)
     mixer_own = pack_mixer(every, *pack)
-    piece = pack_ffn(mine, *pack_f)[0]
-
-    *others, halo, mixer_own, piece, every = sync(*others, halo, mixer_own, piece, every)
+    piece, piece2 = (a[0] for a in pack_ffn(mine, *pack_f))
+
+    *others, halo, mixer_own, piece, piece2, every = sync(
+        *others, halo, mixer_own, piece, piece2, every
+    )
     mixer_others = jnp.stack(others)
     b, c = swap(mixer_others, first, dp), swap(mixer_others, second, dp)
-    ffn_all = lax.all_gather(piece, "tensor")
+    ffn_all = [lax.all_gather(p, "tensor") for p in (piece, piece2)]
     ffn_own = pack_ffn(every, *pack_f)
-    mixer_others, b, c, ffn_own = sync(mixer_others, b, c, ffn_own)
+    mixer_others, b, c, *ffn_own = sync(mixer_others, b, c, *ffn_own)
     d = swap(b, second, dp)
     mixer_pieces = [mixer_others, b, c] + [swap(x, across, dp) for x in (mixer_others, b, c)]
-    d, *mixer_pieces = sync(d, *mixer_pieces)
+    ffn_all[0], d, *mixer_pieces = sync(ffn_all[0], d, *mixer_pieces)
     mixer_pieces = mixer_pieces[:3] + [d] + mixer_pieces[3:] + [swap(d, across, dp)]
+
+    def others_of(array):
+        return jnp.stack(
+            [lax.dynamic_index_in_dim(array, (place + k) % tensor, 0, False) for k in range(1, tensor)]
+        )
+
+    gates = Gather(others_of(ffn_all[0]), dp)
+
 
     x_ext = jnp.concatenate([halo, mixer_in], axis=1)
 
@@ -1137,29 +1156,25 @@
     (mixer_w, beta, taps, beta_w, proj, qk, inv, scores, base, mix, keep, gain, state) = mixer_local(
         ids, mixer_in, halo, seg, seg_row, mixer_own, mixer_pieces, heads
     )
-    state, ffn_all = sync(state, ffn_all)
-    others = jnp.stack(
-        [lax.dynamic_index_in_dim(ffn_all, (place + k) % tensor, 0, False) for k in range(1, tensor)]
-    )
+    tie = Pending().tie_all
+    state, ffn_all[1], gates.pieces = tie(state, ffn_all[1], gates.pieces)
     recv = lax.ppermute(state, "tensor", ahead)
-    near = [others, swap(others, first, dp), swap(others, second, dp)]
-    far = [swap(others, across, dp)]
+    gates.round()
+    downs = Gather(others_of(ffn_all[1]), dp)
     recv = lax.ppermute(hop(recv, keep, gain, tensor, False), "tensor", ahead)
-    recv = hop(recv, keep, gain, tensor, False)
-    near[0], recv = sync(near[0], recv)
-    recv = lax.ppermute(recv, "tensor", ahead)
-    near[:3] = sync(*near)
-    near.append(swap(near[1], second, dp))
-    far += [swap(near[1], across, dp), swap(near[2], across, dp)]
-    state, near[3] = sync(recv, near[3])
-    far.append(swap(near[3], across, dp))
+    recv, gates.pieces = tie(recv, gates.pieces)
+    recv = lax.ppermute(hop(recv, keep, gain, tensor, False), "tensor", ahead)
+    gates.round()
+    downs.round()
+    state, gates.pieces, downs.pieces = tie(recv, gates.pieces, downs.pieces)
+    downs.round()
     mixed, update = mixer_output(qk, scores, base, mix, state, seg, tensor)
     mixed = mixed.reshape(count, heads * HD)
 
     out_grad = d_out.reshape(count, width)
     table = jnp.stack([ids[i] for i in (4, 6, 5, 7, 0, 2, 1, 3)])
     output, d_mid, d_mid_low, d_mixed, gain2_part, *grads = ffn(
-        ids, table, mixed, rows, out_grad, gain2, ffn_own, near + far, hidden
+        ids, table, mixed, rows, out_grad, gain2, ffn_own, gates.pieces + downs.pieces, hidden
     )
     order = reduce_order(tensor)
     pending = Pending()

time: 473 us -> 468 us (0.989)
  waiting for transfers between devices: 132 us -> 123 us
    all_gather x1 -> x2, waiting for transfers between devices: 0.02 us -> 9.45 us  [shards(): ffn_all = [lax.all_gather(p, 'tensor') for p in (piece, piece2)]]
    ppermute x1 -> x0, waiting for transfers between devices: 8.81 us -> none  [shards(): recv = lax.ppermute(recv, 'tensor', ahead)]
    ppermute x41 -> x46, waiting for transfers between devices: 61.8 us -> 56.1 us  [swap(): return lax.ppermute(x, 'dp', [(i, i ^ mask_of(i)) for i in range(size)])]
    ppermute x1 -> x0, starting transfers between devices: 4.76 us -> none  [shards(): recv = lax.ppermute(recv, 'tensor', ahead)]
    ppermute x41 -> x46, starting transfers between devices: 45.8 us -> 50.1 us  [swap(): return lax.ppermute(x, 'dp', [(i, i ^ mask_of(i)) for i in range(size)])]
    ppermute x1 -> x2, waiting for transfers between devices: 9.43 us -> 10.1 us  [shards(): recv = lax.ppermute(hop(recv, keep, gain, tensor, False), 'tensor', ahead)]
  transfers between devices with their start and end apart: 62 -> 68, of which waited for: 26 -> 27; matrix products, arithmetic and copies ran while one was open for 11% -> 11% of each run, Pallas kernels for 27% -> 27%
where the time goes in v4:
time: 468 us; the launch traced here: 459 us
  Pallas kernels  179 us (38%)
  waiting for transfers between devices  123 us (26%)
  starting transfers between devices  83.8 us (18%)
  other arithmetic  30.3 us (6%)
  local copies, waits for them, and re-layouts  26.5 us (6%)
  between operations  15.7 us (3%)
    ppermute x46, waiting for transfers between devices, swap(): return lax.ppermute(x, 'dp', [(i, i ^ mask_of(i)) for i in range(size)])  56.1 us
    ppermute x46, starting transfers between devices, swap(): return lax.ppermute(x, 'dp', [(i, i ^ mask_of(i)) for i in range(size)])  50.1 us
    pallas_call x1, Pallas kernels, ffn(): call(functools.partial(ffn_kernel, hidden), 2 * slots, [pl.BlockSpec((cou...  45.6 us
    pallas_call x1, Pallas kernels, mixer_back(): call(back_kernel, slots, [columns(tokens, HD)] + [lead(per, a.shape) for...  26.7 us
    pallas_call x1, Pallas kernels, mixer_local(): call(local_kernel, slots, [whole(x.shape), whole(halo.shape), whole(seg.s...  26 us
    convert_element_type x14, other arithmetic, add(): return (a.astype(F32) + b.astype(F32)).astype(BF16)  22.8 us
    ppermute x9, waiting for transfers between devices, to_ahead(): return lax.ppermute(x, 'tensor', [(i, (i + k) % size) for i in range(size)])  16.8 us
    ppermute x2, waiting for transfers between devices, shards(): lax.ppermute(hop(pending.tie(recv), keep, back_gain, tensor, True), 'tens...  11.7 us
  transfers between devices with their start and end apart: 68, of which 27 were waited for; matrix products, arithmetic and copies ran while one was open for 11% of the time, Pallas kernels for 27%

profile of v4, /device:TPU:1, one launch (start us, length us, event | category | flops | bytes accessed | tf_op | source)
XLA Modules:
  0.0 459.1 jit_solution(11295763077268194301)
XLA Ops:
  7.2 1.7 pack_mixer.2
  9.0 4.2 collective-permute-start
  15.4 4.1 collective-permute-start.3
  19.5 6.2 %pack_mixer.3.own_ref = bf16[8,144,768]{2,1,0:T(8,128)(2,1)} custom-call(s32[8]{0:T(128)} %iota.3.table_ref, bf16[1024,256]{1,0:T(8,128)(2,1)} %q_ref.3, bf16[1024,256]{1,0:T(8,128)(2,1)} %k_ref.3, bf16[1024,256]{1,0:T(8,128)(2,1)} %v_ref.3, bf16[2,1024]{1,0:T(2,128)(2,1)} %bitcast.154, bf16[3,4,256]{2,1,0:T(4,128)(2,1)} %conv_ref.3), custom_call_target="tpu_custom_call" | custom-call | bytes 3145728 | tf_op jit(solution)/shard_map/pack_mixer/pallas_call | solution.py:711
  25.7 2.1 pack_ffn.2
  28.5 3.1 collective-permute-done.1
  34.2 8.4 %pack_ffn.3 = (bf16[8,128,1408]{2,1,0:T(8,128)(2,1)}, bf16[8,128,1024]{2,1,0:T(8,128)(2,1)}) custom-call(s32[8]{0:T(128)} %iota.3.table_ref, bf16[704,1024]{1,0:T(8,128)(2,1)} %bitcast.122, bf16[704,1024]{1,0:T(8,128)(2,1)} %bitcast.124, bf16[704,1024]{1,0:T(8,128)(2,1)} %down_ref.3, bf16[256,1024]{1,0:T(8,128)(2,1)} %out_w_ref.3), custom_call_target="tpu_custom_call" | custom-call | tf_op jit(solution)/shard_map/pack_ffn/pallas_call | solution.py:724
  42.7 2.5 collective-permute-done.4.refs_1_
  45.2 4.2 collective-permute-done.5.refs_2_
  51.5 7.8 %collective-permute-done.6.refs_3_ = bf16[3,144,768]{2,1,0:T(8,128)(2,1)} collective-permute-done((bf16[3,144,768]{2,1,0:T(8,128)(2,1)S(1)}, bf16[3,144,768]{2,1,0:T(8,128)(2,1)}, u32[]{:S(2)}, u32[]{:S(2)}) %collective-permute-start.6) | collective-permute-done | bytes 663584 | tf_op jit(solution)/shard_map/ppermute | solution.py:954
  59.3 9.4 %all-gather.5.cloned.1.call-done = bf16[512,1408]{1,0:T(8,128)(2,1)} async-done(((bf16[128,1408]{1,0:T(8,128)(2,1)}), bf16[512,1408]{1,0:T(8,128)(2,1)}) %all-gather.5.cloned.1.call-update) | async-done | bytes 1441808 | tf_op jit(solution)/shard_map/all_gather | solution.py:1132
  68.7 1.4 collective-permute-start.10
  77.0 26.0 %mixer_local.1 = (bf16[4,8,144,768]{3,2,1,0:T(8,128)(2,1)}, f32[2,256,128]{2,1,0:T(8,128)}, f32[8,16,128]{2,1,0:T(8,128)}, bf16[4,32,1024]{2,1,0:T(8,128)(2,1)},...) custom-call(s32[8]{0:T(128)} %stack.113.ids_ref, ...), custom_call_target="tpu_custom_call" | custom-call | flops 16000000000 | bytes 32000000 | tf_op jit(solution)/shard_map/mixer_local/pallas_call | solution.py:753
  104.0 1.6 pad_maximum_fusion
  106.6 2.3 collective-permute-start.14
  110.1 9.1 %collective-permute-done.14.state_ref = bf16[8,2,128,128]{3,2,1,0:T(8,128)(2,1)S(1)} collective-permute-done((bf16[8,2,128,128]{3,2,1,0:T(8,128)(2,1)S(1)}, bf16[8,2,128,128]{3,2,1,0:T(8,128)(2,1)S(1)}, u32[]{:S(2)}, u32[]{:S(2)}) %collective-permute-start.14) | collective-permute-done | bytes 524320 | tf_op jit(solution)/shard_map/ppermute | solution.py:1161
  119.9 4.1 collective-permute-start.15
  125.5 1.6 collective-permute-start.24
  127.1 6.4 %collective-permute-done.15.state_ref = bf16[8,2,128,128]{3,2,1,0:T(8,128)(2,1)S(1)} collective-permute-done((bf16[8,2,128,128]{3,2,1,0:T(8,128)(2,1)S(1)}, bf16[8,2,128,128]{3,2,1,0:T(8,128)(2,1)S(1)}, u32[]{:S(2)}, u32[]{:S(2)}) %collective-permute-start.15) | collective-permute-done | bytes 524320 | tf_op jit(solution)/shard_map/ppermute | solution.py:1164
  133.4 3.7 collective-permute-done.16.refs_6_
  138.8 3.8 collective-permute-start.18
  142.7 6.3 %collective-permute-done.23.refs_13_ = bf16[3,128,1024]{2,1,0:T(8,128)(2,1)} collective-permute-done((bf16[3,128,1024]{2,1,0:T(8,128)(2,1)S(1)}, bf16[3,128,1024]{2,1,0:T(8,128)(2,1)}, u32[]{:S(2)}, u32[]{:S(2)}) %collective-permute-start.23) | collective-permute-done | bytes 786464 | tf_op jit(solution)/shard_map/ppermute | solution.py:954
  149.0 3.7 collective-permute-done.18.state_ref
  153.7 1.6 collective-permute-start.25
  156.5 6.1 %mixer_output.1 = (bf16[2,256,1024]{2,1,0:T(8,128)(2,1)}, bf16[8,2,256,128]{3,2,1,0:T(8,128)(2,1)}) custom-call(bf16[8,2,256,256]{3,2,1,0:T(8,128)(2,1)} %get-tuple-element.278.qk_ref, bf16[8,2,256,256]{3,2,1,0:T(8,128)(2,1)} %get-tuple-element.279.p_ref, f32[8,2,256,128]{3,2,1,0:T(8,128)} %get-tuple-element.280.ub_ref, ...), custom_call_target="tpu_custom_call" | custom-call | flops 800000000 | bytes 8000000 | tf_op jit(solution)/shard_map/mixer_output/pallas_call | solution.py:778
  162.7 45.6 %ffn.1 = (bf16[512,1024]{1,0:T(8,128)(2,1)}, f32[512,1024]{1,0:T(8,128)}, bf16[512,1024]{1,0:T(8,128)(2,1)}, f32[512,1024]{1,0:T(8,128)}, f32[8,1024]{1,0:T(8,12...) custom-call(s32[8]{0:T(128)} %stack.113.ids_ref, ...), custom_call_target="tpu_custom_call" | custom-call | flops 38386270208 | bytes 60000000 | tf_op jit(solution)/shard_map/ffn/pallas_call | solution.py:847
  210.1 8.9 %mixer_back_local.1 = (f32[8,2,256,128]{3,2,1,0:T(8,128)}, f32[8,2,128,128]{3,2,1,0:T(8,128)}, bf16[8,2,128,128]{3,2,1,0:T(8,128)(2,1)}) custom-call(f32[2,256,1024]{2,1,0:T(8,128)} %bitcast.130, bf16[8,2,256,256]{3,2,1,0:T(8,128)(2,1)} %get-tuple-element.278.qk_ref, bf16[8,2,256,256]{3,2,1,0:T(8,128)(2,1)} %get-tuple-element.319.t_ref, ...), custom_call_target="tpu_custom_call" | custom-call | flops 800000000 | bytes 8000000 | tf_op jit(solution)/shard_map/mixer_back_local/pallas_call | solution.py:793
  220.3 4.9 %add_convert_fusion.1 = bf16[4,2,128,2176]{3,2,1,0:T(8,128)(2,1)S(1)} fusion(bf16[4,2,128,2176]{3,2,1,0:T(8,128)(2,1)} %collective-permute-done.27, bf16[4,2,128,2176]{3,2,1,0:T(8,128)(2,1)} %get-tuple-element.330), kind=kLoop, calls=%fused_computation.1 | loop fusion | flops 8912896 | bytes 13369344 | tf_op jit(solution)/shard_map/convert_element_type | solution.py:997
  225.2 2.5 fusion.8
  230.1 5.5 %collective-permute-done.26.state_ref = bf16[8,2,128,128]{3,2,1,0:T(8,128)(2,1)S(1)} collective-permute-done((bf16[8,2,128,128]{3,2,1,0:T(8,128)(2,1)}, bf16[8,2,128,128]{3,2,1,0:T(8,128)(2,1)S(1)}, u32[]{:S(2)}, u32[]{:S(2)}) %collective-permute-start.26) | collective-permute-done | bytes 524320 | tf_op jit(solution)/shard_map/ppermute | solution.py:1185
  237.9 3.4 add_convert_fusion
  241.3 2.4 fusion.7
  245.0 4.2 flip.1
  249.2 2.3 collective-permute-done.28.state_ref
  254.6 2.1 add_convert_fusion.3
  257.0 9.5 %collective-permute-done.30.dstate_ref = bf16[8,2,128,128]{3,2,1,0:T(8,128)(2,1)S(1)} collective-permute-done((bf16[8,2,128,128]{3,2,1,0:T(8,128)(2,1)S(1)}, bf16[8,2,128,128]{3,2,1,0:T(8,128)(2,1)S(1)}, u32[]{:S(2)}, u32[]{:S(2)}) %collective-permute-start.30) | collective-permute-done | bytes 524320 | tf_op jit(solution)/shard_map/ppermute | solution.py:1192
  267.2 26.7 %mixer_back.1 = (bf16[2,272,3072]{2,1,0:T(8,128)(2,1)}, f32[2,256,128]{2,1,0:T(8,128)}, f32[8,16,128]{2,1,0:T(8,128)}) custom-call(f32[2,256,1024]{2,1,0:T(8,128)} %bitcast.131, f32[8,2,256,128]{3,2,1,0:T(8,128)} %get-tuple-element.321.y_ref, bf16[8,2,256,256]{3,2,1,0:T(8,128)(2,1)} %get-tuple-element.278.qk_ref, ...), custom_call_target="tpu_custom_call" | custom-call | flops 8000000000 | bytes 32000000 | tf_op jit(solution)/shard_map/mixer_back/pallas_call | solution.py:807
  294.0 10.4 %grad_mixer.1 = (bf16[4,2,128,1024]{3,2,1,0:T(8,128)(2,1)}, bf16[4,2,128,1024]{3,2,1,0:T(8,128)(2,1)}, bf16[4,2,128,1024]{3,2,1,0:T(8,128)(2,1)}, bf16[4,2,128,1024]{3,2,1,0:T(8,128)(2,1)}) custom-call(bf16[1024,544]{1,0:T(8,128)(2,1)} %get-tuple-element.365.xt_ref, bf16[544,3072]{1,0:T(8,128)(2,1)} %bitcast.163, ...), custom_call_target="tpu_custom_call" | custom-call | flops 4294967296 | bytes 8388608 | tf_op jit(solution)/shard_map/grad_mixer/pallas_call | solution.py:883
  304.4 2.9 collective-permute-start.32
  307.4 1.7 add_convert_fusion.7
  311.1 2.1 add_convert_fusion.2
  316.3 1.5 fusion.10
  321.6 11.3 %input_back.1 = (f32[2,16,1024]{2,1,0:T(8,128)}, f32[2,256,1024]{2,1,0:T(8,128)}) custom-call(bf16[2,272,3072]{2,1,0:T(8,128)(2,1)} %get-tuple-element.393.dqkv_ref, bf16[4,8,144,768]{3,2,1,0:T(8,128)(2,1)} %get-tuple-element.394.w_ref, bf16[2,256,128]{2,1,0:T(8,128)(2,1)} %convert_element_type.205.db_ref, bf16[4,128,1024]{2,1,0:T(8,128)(2,1)} %pad_maximum_fusion.5.beta_w_ref), custom_call_target="tpu_custom_call" | custom-call | flops 3422552064 | bytes 6291456 | tf_op jit(solution)/shard_map/input_back/pallas_call | solution.py:936
  338.9 1.6 add_convert_fusion.6
  340.6 3.2 collective-permute-start.43
  345.1 3.5 collective-permute-done.37
  348.6 1.6 add_convert_fusion.9
  351.0 13.3 %collective-permute-done.41 = bf16[2,2,128,1024]{3,2,1,0:T(8,128)(2,1)} collective-permute-done((bf16[2,2,128,1024]{3,2,1,0:T(8,128)(2,1)}, bf16[2,2,128,1024]{3,2,1,0:T(8,128)(2,1)}, u32[]{:S(2)}, u32[]{:S(2)}) %collective-permute-start.41) | collective-permute-done | bytes 1048608 | tf_op jit(solution)/shard_map/ppermute | solution.py:954
  364.4 1.6 add_convert_fusion.8
  369.1 3.1 collective-permute-start.48
  372.4 2.8 collective-permute-done.45
  376.9 5.5 %collective-permute-done.44 = bf16[128,1024]{1,0:T(8,128)(2,1)S(1)} collective-permute-done((bf16[128,1024]{1,0:T(8,128)(2,1)S(1)}, bf16[128,1024]{1,0:T(8,128)(2,1)S(1)}, u32[]{:S(2)}, u32[]{:S(2)}) %collective-permute-start.44) | collective-permute-done | bytes 262176 | tf_op jit(solution)/shard_map/ppermute | solution.py:974
  382.4 4.5 input_norm.1
  387.8 9.0 %collective-permute-start.49 = (f32[4,5632]{1,0:T(4,128)S(1)}, f32[4,5632]{1,0:T(4,128)S(1)}, u32[]{:S(2)}, u32[]{:S(2)}) collective-permute-start(f32[4,5632]{1,0:T(4,128)S(1)} %pad_maximum_fusion.9), channel_id=1, source_target_pairs={{0,4},{4,0},{8,12},{12,8},{16,20},{20,16},{24,28},{28,24},{1,5},{5... | collective-permute-start | bytes 270344 | tf_op jit(solution)/shard_map/ppermute | solution.py:954
  398.2 1.7 collective-permute-start.55
  401.8 4.3 collective-permute-done.55
  406.0 6.6 %collective-permute-done.54 = bf16[128,1024]{1,0:T(8,128)(2,1)S(1)} collective-permute-done((bf16[128,1024]{1,0:T(8,128)(2,1)S(1)}, bf16[128,1024]{1,0:T(8,128)(2,1)S(1)}, u32[]{:S(2)}, u32[]{:S(2)}) %collective-permute-start.54) | collective-permute-done | bytes 262176 | tf_op jit(solution)/shard_map/ppermute | solution.py:974
  413.9 1.5 collective-permute-start.58
  415.6 3.2 collective-permute-done.56.refs_1_
  418.7 2.0 collective-permute-done.57.refs_2_
  423.8 3.7 collective-permute-done.59
  430.6 4.0 collective-permute-start.65
  435.7 7.8 %finish_ffn.1 = (f32[704,1024]{1,0:T(8,128)}, f32[704,1024]{1,0:T(8,128)}, f32[704,1024]{1,0:T(8,128)}) custom-call(s32[8]{0:T(128)} %stack.113.ids_ref, bf16[128,2176]{1,0:T(8,128)(2,1)} %copy-done.9, bf16[128,2176]{1,0:T(8,128)(2,1)} %copy-done.10, bf16[128,2176]{1,0:T(8,128)(2,1)} %copy-done.11, bf16[128,2176]{1,0:T(8,128)(2,1)} %copy-done.27, ...), custom_call_target="tpu_custom_call" | custom-call | bytes 13369344 | tf_op jit(solution)/shard_map/finish_ffn/pallas_call | solution.py:895
  446.1 5.7 %finish_mixer.1 = (f32[1024,256]{1,0:T(8,128)}, f32[1024,256]{1,0:T(8,128)}, f32[1024,256]{1,0:T(8,128)}, f32[256,1024]{1,0:T(8,128)}) custom-call(s32[8]{0:T(128)} %stack.113.ids_ref, bf16[128,1024]{1,0:T(8,128)(2,1)} %copy-done.18, bf16[128,1024]{1,0:T(8,128)(2,1)} %copy-done.19, bf16[128,1024]{1,0:T(8,128)(2,1)} %copy-done.20, ...), custom_call_target="tpu_custom_call" | custom-call | bytes 6291456 | tf_op jit(solution)/shard_map/finish_mixer/pallas_call | solution.py:921
  (287 shorter events, 73.7 us)
Async XLA Ops:
  7.2 61.5 %all-gather.5.cloned.1.call-start = ((), (), s32[]{:S(2)}) async-start(), calls=%async_computation | async-start | bytes 1802240 | tf_op jit(solution)/shard_map/all_gather | solution.py:1132
  9.0 19.5 %collective-permute-start = (bf16[144,768]{1,0:T(8,128)(2,1)}, bf16[144,768]{1,0:T(8,128)(2,1)S(1)}, u32[]{:S(2)}, u32[]{:S(2)}) collective-permute-start(bf16[144,768]{1,0:T(8,128)(2,1)} %bitcast.142), channel_id=1, source_target_pairs={{0,3},{1,0},{2,1},{3,2},{4,7},{5,4},{6,5},{7,6},{8,11},{9,8},{10,9... | collective-permute-start | bytes 663560 | tf_op jit(solution)/shard_map/ppermute | solution.py:970
  13.1 18.4 %collective-permute-start.1 = (bf16[144,768]{1,0:T(8,128)(2,1)}, bf16[144,768]{1,0:T(8,128)(2,1)S(1)}, u32[]{:S(2)}, u32[]{:S(2)}) collective-permute-start(bf16[144,768]{1,0:T(8,128)(2,1)} %bitcast.143), channel_id=1, source_target_pairs={{0,2},{1,3},{2,0},{3,1},{4,6},{5,7},{6,4},{7,5},{8,10},{9,11},{10,... | collective-permute-start | bytes 663560 | tf_op jit(solution)/shard_map/ppermute | solution.py:970
  13.1 18.4 %collective-permute-start.2 = (bf16[144,768]{1,0:T(8,128)(2,1)}, bf16[144,768]{1,0:T(8,128)(2,1)S(1)}, u32[]{:S(2)}, u32[]{:S(2)}) collective-permute-start(bf16[144,768]{1,0:T(8,128)(2,1)} %bitcast.144), channel_id=1, source_target_pairs={{0,1},{1,2},{2,3},{3,0},{4,5},{5,6},{6,7},{7,4},{8,9},{9,10},{10,1... | collective-permute-start | bytes 663560 | tf_op jit(solution)/shard_map/ppermute | solution.py:970
  15.4 13.0 %collective-permute-start.3 = (bf16[2,16,1024]{2,1,0:T(8,128)(2,1)S(1)}, bf16[2,16,1024]{2,1,0:T(8,128)(2,1)S(1)}, u32[]{:S(2)}, u32[]{:S(2)}) collective-permute-start(bf16[2,16,1024]{2,1,0:T(8,128)(2,1)S(1)} %slice.184), channel_id=1, source_target_pairs={{0,1},{1,2},{2,3},{4,5},{5,6},{6,7},{8,9},{9,10},{10,11},{12,13},{... | collective-permute-start | bytes 196616 | tf_op jit(solution)/shard_map/ppermute | solution.py:1123
  31.6 71.5 %all-gather.7.cloned.1.call-start = ((), (), s32[]{:S(2)}) async-start(), calls=%async_computation.1 | async-start | bytes 1310720 | tf_op jit(solution)/shard_map/all_gather | solution.py:1132
  31.7 13.4 %collective-permute-start.4 = (bf16[3,144,768]{2,1,0:T(8,128)(2,1)S(1)}, bf16[3,144,768]{2,1,0:T(8,128)(2,1)S(1)}, u32[]{:S(2)}, u32[]{:S(2)}) collective-permute-start(bf16[3,144,768]{2,1,0:T(8,128)(2,1)S(1)} %pad_maximum_fusion.7.refs_0_), channel_id=1, source_target_pairs={{0,8},{4,20},{8,0},{12,28},{16,24},{20,4},{24,16},{28,12},{1,9},{5... | collective-permute-start | bytes 1990664 | tf_op jit(solution)/shard_map/ppermute | solution.py:954
  33.0 16.3 %collective-permute-start.5 = (bf16[3,144,768]{2,1,0:T(8,128)(2,1)S(1)}, bf16[3,144,768]{2,1,0:T(8,128)(2,1)S(1)}, u32[]{:S(2)}, u32[]{:S(2)}) collective-permute-start(bf16[3,144,768]{2,1,0:T(8,128)(2,1)S(1)} %pad_maximum_fusion.7.refs_0_), channel_id=1, source_target_pairs={{0,16},{4,12},{8,24},{12,4},{16,0},{20,28},{24,8},{28,20},{1,17},{... | collective-permute-start | bytes 1990664 | tf_op jit(solution)/shard_map/ppermute | solution.py:954
  49.3 9.9 %collective-permute-start.6 = (bf16[3,144,768]{2,1,0:T(8,128)(2,1)S(1)}, bf16[3,144,768]{2,1,0:T(8,128)(2,1)}, u32[]{:S(2)}, u32[]{:S(2)}) collective-permute-start(bf16[3,144,768]{2,1,0:T(8,128)(2,1)S(1)} %collective-permute-done.4.refs_1_), channel_id=1, source_target_pairs={{0,16},{4,12},{8,24},{12,4},{16,0},{20,28},{24,8},{28,20},{1,17},{... | collective-permute-start | bytes 1990664 | tf_op jit(solution)/shard_map/ppermute | solution.py:954
  50.6 8.7 %collective-permute-start.8 = (bf16[3,144,768]{2,1,0:T(8,128)(2,1)S(1)}, bf16[3,144,768]{2,1,0:T(8,128)(2,1)S(1)}, u32[]{:S(2)}, u32[]{:S(2)}) collective-permute-start(bf16[3,144,768]{2,1,0:T(8,128)(2,1)S(1)} %collective-permute-done.4.refs_1_), channel_id=1, source_target_pairs={{0,4},{4,0},{8,12},{12,8},{16,20},{20,16},{24,28},{28,24},{1,5},{5... | collective-permute-start | bytes 1990664 | tf_op jit(solution)/shard_map/ppermute | solution.py:954
  50.9 8.3 %collective-permute-start.7 = (bf16[3,144,768]{2,1,0:T(8,128)(2,1)S(1)}, bf16[3,144,768]{2,1,0:T(8,128)(2,1)S(1)}, u32[]{:S(2)}, u32[]{:S(2)}) collective-permute-start(bf16[3,144,768]{2,1,0:T(8,128)(2,1)S(1)} %pad_maximum_fusion.7.refs_0_), channel_id=1, source_target_pairs={{0,4},{4,0},{8,12},{12,8},{16,20},{20,16},{24,28},{28,24},{1,5},{5... | collective-permute-start | bytes 1990664 | tf_op jit(solution)/shard_map/ppermute | solution.py:954
  51.1 8.2 %collective-permute-start.9 = (bf16[3,144,768]{2,1,0:T(8,128)(2,1)S(1)}, bf16[3,144,768]{2,1,0:T(8,128)(2,1)}, u32[]{:S(2)}, u32[]{:S(2)}) collective-permute-start(bf16[3,144,768]{2,1,0:T(8,128)(2,1)S(1)} %collective-permute-done.5.refs_2_), channel_id=1, source_target_pairs={{0,4},{4,0},{8,12},{12,8},{16,20},{20,16},{24,28},{28,24},{1,5},{5... | collective-permute-start | bytes 1990664 | tf_op jit(solution)/shard_map/ppermute | solution.py:954
  68.7 7.6 %collective-permute-start.10 = (bf16[3,144,768]{2,1,0:T(8,128)(2,1)}, bf16[3,144,768]{2,1,0:T(8,128)(2,1)}, u32[]{:S(2)}, u32[]{:S(2)}) collective-permute-start(bf16[3,144,768]{2,1,0:T(8,128)(2,1)} %collective-permute-done.6.refs_3_), channel_id=1, source_target_pairs={{0,4},{4,0},{8,12},{12,8},{16,20},{20,16},{24,28},{28,24},{1,5},{5... | collective-permute-start | bytes 1990664 | tf_op jit(solution)/shard_map/ppermute | solution.py:954
  73.3 29.7 %collective-permute-start.11 = (bf16[3,128,1408]{2,1,0:T(8,128)(2,1)S(1)}, bf16[3,128,1408]{2,1,0:T(8,128)(2,1)S(1)}, u32[]{:S(2)}, u32[]{:S(2)}) collective-permute-start(bf16[3,128,1408]{2,1,0:T(8,128)(2,1)S(1)} %pad_maximum_fusion.4.refs_2_), channel_id=1, source_target_pairs={{0,8},{4,20},{8,0},{12,28},{16,24},{20,4},{24,16},{28,12},{1,9},{5... | collective-permute-start | bytes 3244040 | tf_op jit(solution)/shard_map/ppermute | solution.py:954
  74.6 28.5 %collective-permute-start.12 = (bf16[3,128,1408]{2,1,0:T(8,128)(2,1)S(1)}, bf16[3,128,1408]{2,1,0:T(8,128)(2,1)}, u32[]{:S(2)}, u32[]{:S(2)}) collective-permute-start(bf16[3,128,1408]{2,1,0:T(8,128)(2,1)S(1)} %pad_maximum_fusion.4.refs_2_), channel_id=1, source_target_pairs={{0,16},{4,12},{8,24},{12,4},{16,0},{20,28},{24,8},{28,20},{1,17},{... | collective-permute-start | bytes 3244040 | tf_op jit(solution)/shard_map/ppermute | solution.py:954
  75.8 27.3 %collective-permute-start.13 = (bf16[3,128,1408]{2,1,0:T(8,128)(2,1)S(1)}, bf16[3,128,1408]{2,1,0:T(8,128)(2,1)S(1)}, u32[]{:S(2)}, u32[]{:S(2)}) collective-permute-start(bf16[3,128,1408]{2,1,0:T(8,128)(2,1)S(1)} %pad_maximum_fusion.4.refs_2_), channel_id=1, source_target_pairs={{0,4},{4,0},{8,12},{12,8},{16,20},{20,16},{24,28},{28,24},{1,5},{5... | collective-permute-start | bytes 3244040 | tf_op jit(solution)/shard_map/ppermute | solution.py:954
  105.7 31.5 %collective-permute-start.17 = (bf16[2,3,128,1408]{3,2,1,0:T(8,128)(2,1)S(1)}, bf16[2,3,128,1408]{3,2,1,0:T(8,128)(2,1)S(1)}, u32[]{:S(2)}, u32[]{:S(2)}) collective-permute-start(bf16[2,3,128,1408]{3,2,1,0:T(8,128)(2,1)S(1)} %pad_maximum_fusion), channel_id=1, source_target_pairs={{0,4},{4,0},{8,12},{12,8},{16,20},{20,16},{24,28},{28,24},{1,5},{5... | collective-permute-start | bytes 6488072 | tf_op jit(solution)/shard_map/ppermute | solution.py:954
  105.9 18.2 %collective-permute-start.20 = (bf16[3,128,1024]{2,1,0:T(8,128)(2,1)S(1)}, bf16[3,128,1024]{2,1,0:T(8,128)(2,1)S(1)}, u32[]{:S(2)}, u32[]{:S(2)}) collective-permute-start(bf16[3,128,1024]{2,1,0:T(8,128)(2,1)S(1)} %pad_maximum_fusion.6.refs_9_), channel_id=1, source_target_pairs={{0,8},{4,20},{8,0},{12,28},{16,24},{20,4},{24,16},{28,12},{1,9},{5... | collective-permute-start | bytes 2359304 | tf_op jit(solution)/shard_map/ppermute | solution.py:954
  106.3 19.0 %collective-permute-start.21 = (bf16[3,128,1024]{2,1,0:T(8,128)(2,1)S(1)}, bf16[3,128,1024]{2,1,0:T(8,128)(2,1)S(1)}, u32[]{:S(2)}, u32[]{:S(2)}) collective-permute-start(bf16[3,128,1024]{2,1,0:T(8,128)(2,1)S(1)} %pad_maximum_fusion.6.refs_9_), channel_id=1, source_target_pairs={{0,16},{4,12},{8,24},{12,4},{16,0},{20,28},{24,8},{28,20},{1,17},{... | collective-permute-start | bytes 2359304 | tf_op jit(solution)/shard_map/ppermute | solution.py:954
  106.6 12.6 %collective-permute-start.14 = (bf16[8,2,128,128]{3,2,1,0:T(8,128)(2,1)S(1)}, bf16[8,2,128,128]{3,2,1,0:T(8,128)(2,1)S(1)}, u32[]{:S(2)}, u32[]{:S(2)}) collective-permute-start(bf16[8,2,128,128]{3,2,1,0:T(8,128)(2,1)S(1)} %copy-done.52), channel_id=1, source_target_pairs={{0,1},{1,2},{2,3},{4,5},{5,6},{6,7},{8,9},{9,10},{10,11},{12,13},{... | collective-permute-start | bytes 1572872 | tf_op jit(solution)/shard_map/ppermute | solution.py:1161
  108.9 28.3 %collective-permute-start.16 = (bf16[3,128,1408]{2,1,0:T(8,128)(2,1)S(1)}, bf16[3,128,1408]{2,1,0:T(8,128)(2,1)S(1)}, u32[]{:S(2)}, u32[]{:S(2)}) collective-permute-start(bf16[3,128,1408]{2,1,0:T(8,128)(2,1)S(1)} %copy-done.17), channel_id=1, source_target_pairs={{0,16},{4,12},{8,24},{12,4},{16,0},{20,28},{24,8},{28,20},{1,17},{... | collective-permute-start | bytes 3244040 | tf_op jit(solution)/shard_map/ppermute | solution.py:954
  119.9 13.5 %collective-permute-start.15 = (bf16[8,2,128,128]{3,2,1,0:T(8,128)(2,1)S(1)}, bf16[8,2,128,128]{3,2,1,0:T(8,128)(2,1)S(1)}, u32[]{:S(2)}, u32[]{:S(2)}) collective-permute-start(bf16[8,2,128,128]{3,2,1,0:T(8,128)(2,1)S(1)} %hop.4), channel_id=1, source_target_pairs={{0,1},{1,2},{2,3},{4,5},{5,6},{6,7},{8,9},{9,10},{10,11},{12,13},{... | collective-permute-start | bytes 1572872 | tf_op jit(solution)/shard_map/ppermute | solution.py:1164
  125.5 23.5 %collective-permute-start.24 = (bf16[2,3,128,1024]{3,2,1,0:T(8,128)(2,1)S(1)}, bf16[2,3,128,1024]{3,2,1,0:T(8,128)(2,1)S(1)}, u32[]{:S(2)}, u32[]{:S(2)}) collective-permute-start(bf16[2,3,128,1024]{3,2,1,0:T(8,128)(2,1)S(1)} %pad_maximum_fusion.1), channel_id=1, source_target_pairs={{0,4},{4,0},{8,12},{12,8},{16,20},{20,16},{24,28},{28,24},{1,5},{5... | collective-permute-start | bytes 4718600 | tf_op jit(solution)/shard_map/ppermute | solution.py:954
  137.2 15.5 %collective-permute-start.19 = (bf16[3,128,1408]{2,1,0:T(8,128)(2,1)S(1)}, bf16[3,128,1408]{2,1,0:T(8,128)(2,1)S(1)}, u32[]{:S(2)}, u32[]{:S(2)}) collective-permute-start(bf16[3,128,1408]{2,1,0:T(8,128)(2,1)S(1)} %collective-permute-done.16.refs_6_), channel_id=1, source_target_pairs={{0,4},{4,0},{8,12},{12,8},{16,20},{20,16},{24,28},{28,24},{1,5},{5... | collective-permute-start | bytes 3244040 | tf_op jit(solution)/shard_map/ppermute | solution.py:954
  137.7 11.2 %collective-permute-start.23 = (bf16[3,128,1024]{2,1,0:T(8,128)(2,1)S(1)}, bf16[3,128,1024]{2,1,0:T(8,128)(2,1)}, u32[]{:S(2)}, u32[]{:S(2)}) collective-permute-start(bf16[3,128,1024]{2,1,0:T(8,128)(2,1)S(1)} %collective-permute-done.20.refs_10_), channel_id=1, source_target_pairs={{0,16},{4,12},{8,24},{12,4},{16,0},{20,28},{24,8},{28,20},{1,17},{... | collective-permute-start | bytes 2359304 | tf_op jit(solution)/shard_map/ppermute | solution.py:954
  138.8 13.9 %collective-permute-start.18 = (bf16[8,2,128,128]{3,2,1,0:T(8,128)(2,1)S(1)}, bf16[8,2,128,128]{3,2,1,0:T(8,128)(2,1)S(1)}, u32[]{:S(2)}, u32[]{:S(2)}) collective-permute-start(bf16[8,2,128,128]{3,2,1,0:T(8,128)(2,1)S(1)} %hop.5), channel_id=1, source_target_pairs={{0,1},{1,2},{2,3},{4,5},{5,6},{6,7},{8,9},{9,10},{10,11},{12,13},{... | collective-permute-start | bytes 1572872 | tf_op jit(solution)/shard_map/ppermute | solution.py:1166
  153.7 8.9 %collective-permute-start.25 = (bf16[3,128,1024]{2,1,0:T(8,128)(2,1)}, bf16[3,128,1024]{2,1,0:T(8,128)(2,1)}, u32[]{:S(2)}, u32[]{:S(2)}) collective-permute-start(bf16[3,128,1024]{2,1,0:T(8,128)(2,1)} %collective-permute-done.23.refs_13_), channel_id=1, source_target_pairs={{0,4},{4,0},{8,12},{12,8},{16,20},{20,16},{24,28},{28,24},{1,5},{5... | collective-permute-start | bytes 2359304 | tf_op jit(solution)/shard_map/ppermute | solution.py:954
  208.4 11.9 %collective-permute-start.27 = (bf16[4,2,128,2176]{3,2,1,0:T(8,128)(2,1)}, bf16[4,2,128,2176]{3,2,1,0:T(8,128)(2,1)}, u32[]{:S(2)}, u32[]{:S(2)}) collective-permute-start(bf16[4,2,128,2176]{3,2,1,0:T(8,128)(2,1)} %get-tuple-element.324), channel_id=1, source_target_pairs={{0,4},{4,0},{8,12},{12,8},{16,20},{20,16},{24,28},{28,24},{1,5},{5... | collective-permute-start | bytes 13369352 | tf_op jit(solution)/shard_map/ppermute | solution.py:954
  208.4 29.4 %collective-permute-start.29 = (bf16[4,2,128,2176]{3,2,1,0:T(8,128)(2,1)}, bf16[4,2,128,2176]{3,2,1,0:T(8,128)(2,1)}, u32[]{:S(2)}, u32[]{:S(2)}) collective-permute-start(bf16[4,2,128,2176]{3,2,1,0:T(8,128)(2,1)} %get-tuple-element.335), channel_id=1, source_target_pairs={{0,4},{4,0},{8,12},{12,8},{16,20},{20,16},{24,28},{28,24},{1,5},{5... | collective-permute-start | bytes 13369352 | tf_op jit(solution)/shard_map/ppermute | solution.py:954
  219.0 16.6 %collective-permute-start.26 = (bf16[8,2,128,128]{3,2,1,0:T(8,128)(2,1)}, bf16[8,2,128,128]{3,2,1,0:T(8,128)(2,1)S(1)}, u32[]{:S(2)}, u32[]{:S(2)}) collective-permute-start(bf16[8,2,128,128]{3,2,1,0:T(8,128)(2,1)} %get-tuple-element.323), channel_id=1, source_target_pairs={{1,0},{2,1},{3,2},{5,4},{6,5},{7,6},{9,8},{10,9},{11,10},{13,12},{... | collective-permute-start | bytes 1572872 | tf_op jit(solution)/shard_map/ppermute | solution.py:1185
  227.7 26.9 %collective-permute-start.31 = (bf16[2,2,128,2176]{3,2,1,0:T(8,128)(2,1)}, bf16[2,2,128,2176]{3,2,1,0:T(8,128)(2,1)}, u32[]{:S(2)}, u32[]{:S(2)}) collective-permute-start(bf16[2,2,128,2176]{3,2,1,0:T(8,128)(2,1)} %get-tuple-element.527), channel_id=1, source_target_pairs={{0,8},{4,20},{8,0},{12,28},{16,24},{20,4},{24,16},{28,12},{1,9},{5... | collective-permute-start | bytes 6684680 | tf_op jit(solution)/shard_map/ppermute | solution.py:954
  236.5 14.9 %collective-permute-start.28 = (bf16[8,2,128,128]{3,2,1,0:T(8,128)(2,1)S(1)}, bf16[8,2,128,128]{3,2,1,0:T(8,128)(2,1)S(1)}, u32[]{:S(2)}, u32[]{:S(2)}) collective-permute-start(bf16[8,2,128,128]{3,2,1,0:T(8,128)(2,1)S(1)} %hop.6), channel_id=1, source_target_pairs={{1,0},{2,1},{3,2},{5,4},{6,5},{7,6},{9,8},{10,9},{11,10},{13,12},{... | collective-permute-start | bytes 1572872 | tf_op jit(solution)/shard_map/ppermute | solution.py:1188
  243.8 66.3 %collective-permute-start.34 = (bf16[2,2,128,2176]{3,2,1,0:T(8,128)(2,1)}, bf16[2,2,128,2176]{3,2,1,0:T(8,128)(2,1)}, u32[]{:S(2)}, u32[]{:S(2)}) collective-permute-start(bf16[2,2,128,2176]{3,2,1,0:T(8,128)(2,1)} %get-tuple-element.525), channel_id=1, source_target_pairs={{0,8},{4,20},{8,0},{12,28},{16,24},{20,4},{24,16},{28,12},{1,9},{5... | collective-permute-start | bytes 6684680 | tf_op jit(solution)/shard_map/ppermute | solution.py:954
  252.3 14.1 %collective-permute-start.30 = (bf16[8,2,128,128]{3,2,1,0:T(8,128)(2,1)S(1)}, bf16[8,2,128,128]{3,2,1,0:T(8,128)(2,1)S(1)}, u32[]{:S(2)}, u32[]{:S(2)}) collective-permute-start(bf16[8,2,128,128]{3,2,1,0:T(8,128)(2,1)S(1)} %hop.7), channel_id=1, source_target_pairs={{1,0},{2,1},{3,2},{5,4},{6,5},{7,6},{9,8},{10,9},{11,10},{13,12},{... | collective-permute-start | bytes 1572872 | tf_op jit(solution)/shard_map/ppermute | solution.py:1192
  266.5 40.9 %collective-permute-start.35 = (bf16[2,128,2176]{2,1,0:T(8,128)(2,1)S(1)}, bf16[2,128,2176]{2,1,0:T(8,128)(2,1)}, u32[]{:S(2)}, u32[]{:S(2)}) collective-permute-start(bf16[2,128,2176]{2,1,0:T(8,128)(2,1)S(1)} %get-tuple-element.531), channel_id=1, source_target_pairs={{0,16},{4,12},{8,24},{12,4},{16,0},{20,28},{24,8},{28,20},{1,17},{... | collective-permute-start | bytes 3342344 | tf_op jit(solution)/shard_map/ppermute | solution.py:954
  304.4 13.5 %collective-permute-start.32 = (bf16[4,2,128,1024]{3,2,1,0:T(8,128)(2,1)}, bf16[4,2,128,1024]{3,2,1,0:T(8,128)(2,1)S(1)}, u32[]{:S(2)}, u32[]{:S(2)}) collective-permute-start(bf16[4,2,128,1024]{3,2,1,0:T(8,128)(2,1)} %get-tuple-element.367), channel_id=1, source_target_pairs={{0,4},{4,0},{8,12},{12,8},{16,20},{20,16},{24,28},{28,24},{1,5},{5... | collective-permute-start | bytes 6291464 | tf_op jit(solution)/shard_map/ppermute | solution.py:954
  307.3 7.4 %collective-permute-start.33 = (bf16[4,2,128,1024]{3,2,1,0:T(8,128)(2,1)}, bf16[4,2,128,1024]{3,2,1,0:T(8,128)(2,1)S(1)}, u32[]{:S(2)}, u32[]{:S(2)}) collective-permute-start(bf16[4,2,128,1024]{3,2,1,0:T(8,128)(2,1)} %get-tuple-element.368), channel_id=1, source_target_pairs={{0,4},{4,0},{8,12},{12,8},{16,20},{20,16},{24,28},{28,24},{1,5},{5... | collective-permute-start | bytes 6291464 | tf_op jit(solution)/shard_map/ppermute | solution.py:954
  310.1 30.5 %collective-permute-start.38 = (bf16[128,2176]{1,0:T(8,128)(2,1)}, bf16[128,2176]{1,0:T(8,128)(2,1)}, u32[]{:S(2)}, u32[]{:S(2)}) collective-permute-start(bf16[128,2176]{1,0:T(8,128)(2,1)} %get-tuple-element.544), channel_id=1, source_target_pairs={{0,1},{1,2},{2,3},{3,0},{4,5},{5,6},{6,7},{7,4},{8,9},{9,10},{10,1... | collective-permute-start | bytes 1671176 | tf_op jit(solution)/shard_map/ppermute | solution.py:974
  314.5 24.5 %collective-permute-start.39 = (bf16[2,128,2176]{2,1,0:T(8,128)(2,1)}, bf16[2,128,2176]{2,1,0:T(8,128)(2,1)}, u32[]{:S(2)}, u32[]{:S(2)}) collective-permute-start(bf16[2,128,2176]{2,1,0:T(8,128)(2,1)} %get-tuple-element.529), channel_id=1, source_target_pairs={{0,16},{4,12},{8,24},{12,4},{16,0},{20,28},{24,8},{28,20},{1,17},{... | collective-permute-start | bytes 3342344 | tf_op jit(solution)/shard_map/ppermute | solution.py:954
  333.0 49.4 %collective-permute-start.36 = (f32[2,16,1024]{2,1,0:T(8,128)}, f32[2,16,1024]{2,1,0:T(8,128)}, u32[]{:S(2)}, u32[]{:S(2)}) collective-permute-start(f32[2,16,1024]{2,1,0:T(8,128)} %get-tuple-element.403), channel_id=1, source_target_pairs={{1,0},{2,1},{3,2},{5,4},{6,5},{7,6},{9,8},{10,9},{11,10},{13,12},{... | collective-permute-start | bytes 393224 | tf_op jit(solution)/shard_map/ppermute | solution.py:1209
  334.3 14.3 %collective-permute-start.37 = (bf16[2,2,128,1024]{3,2,1,0:T(8,128)(2,1)}, bf16[2,2,128,1024]{3,2,1,0:T(8,128)(2,1)}, u32[]{:S(2)}, u32[]{:S(2)}) collective-permute-start(bf16[2,2,128,1024]{3,2,1,0:T(8,128)(2,1)} %get-tuple-element.535), channel_id=1, source_target_pairs={{0,8},{4,20},{8,0},{12,28},{16,24},{20,4},{24,16},{28,12},{1,9},{5... | collective-permute-start | bytes 3145736 | tf_op jit(solution)/shard_map/ppermute | solution.py:954
  334.8 29.5 %collective-permute-start.41 = (bf16[2,2,128,1024]{3,2,1,0:T(8,128)(2,1)}, bf16[2,2,128,1024]{3,2,1,0:T(8,128)(2,1)}, u32[]{:S(2)}, u32[]{:S(2)}) collective-permute-start(bf16[2,2,128,1024]{3,2,1,0:T(8,128)(2,1)} %get-tuple-element.533), channel_id=1, source_target_pairs={{0,8},{4,20},{8,0},{12,28},{16,24},{20,4},{24,16},{28,12},{1,9},{5... | collective-permute-start | bytes 3145736 | tf_op jit(solution)/shard_map/ppermute | solution.py:954
  340.6 26.6 %collective-permute-start.43 = (bf16[128,2176]{1,0:T(8,128)(2,1)S(1)}, bf16[128,2176]{1,0:T(8,128)(2,1)S(1)}, u32[]{:S(2)}, u32[]{:S(2)}) collective-permute-start(bf16[128,2176]{1,0:T(8,128)(2,1)S(1)} %get-tuple-element.542), channel_id=1, source_target_pairs={{0,3},{1,0},{2,1},{3,2},{4,7},{5,4},{6,5},{7,6},{8,11},{9,8},{10,9... | collective-permute-start | bytes 1671176 | tf_op jit(solution)/shard_map/ppermute | solution.py:974
  345.0 22.7 %collective-permute-start.42 = (bf16[128,2176]{1,0:T(8,128)(2,1)S(1)}, bf16[128,2176]{1,0:T(8,128)(2,1)S(1)}, u32[]{:S(2)}, u32[]{:S(2)}) collective-permute-start(bf16[128,2176]{1,0:T(8,128)(2,1)S(1)} %add_convert_fusion.11), channel_id=1, source_target_pairs={{0,1},{1,2},{2,3},{3,0},{4,5},{5,6},{6,7},{7,4},{8,9},{9,10},{10,1... | collective-permute-start | bytes 1671176 | tf_op jit(solution)/shard_map/ppermute | solution.py:974
  350.3 18.8 %collective-permute-start.40 = (bf16[2,128,1024]{2,1,0:T(8,128)(2,1)S(1)}, bf16[2,128,1024]{2,1,0:T(8,128)(2,1)S(1)}, u32[]{:S(2)}, u32[]{:S(2)}) collective-permute-start(bf16[2,128,1024]{2,1,0:T(8,128)(2,1)S(1)} %get-tuple-element.549), channel_id=1, source_target_pairs={{0,16},{4,12},{8,24},{12,4},{16,0},{20,28},{24,8},{28,20},{1,17},{... | collective-permute-start | bytes 1572872 | tf_op jit(solution)/shard_map/ppermute | solution.py:954
  366.1 9.2 %collective-permute-start.45 = (bf16[2,128,1024]{2,1,0:T(8,128)(2,1)S(1)}, bf16[2,128,1024]{2,1,0:T(8,128)(2,1)S(1)}, u32[]{:S(2)}, u32[]{:S(2)}) collective-permute-start(bf16[2,128,1024]{2,1,0:T(8,128)(2,1)S(1)} %get-tuple-element.546), channel_id=1, source_target_pairs={{0,16},{4,12},{8,24},{12,4},{16,0},{20,28},{24,8},{28,20},{1,17},{... | collective-permute-start | bytes 1572872 | tf_op jit(solution)/shard_map/ppermute | solution.py:954
  367.9 28.9 %collective-permute-start.46 = (bf16[128,2176]{1,0:T(8,128)(2,1)S(1)}, bf16[128,2176]{1,0:T(8,128)(2,1)S(1)}, u32[]{:S(2)}, u32[]{:S(2)}) collective-permute-start(bf16[128,2176]{1,0:T(8,128)(2,1)S(1)} %add_convert_fusion.10.refs_0_), channel_id=1, source_target_pairs={{0,8},{4,20},{8,0},{12,28},{16,24},{20,4},{24,16},{28,12},{1,9},{5... | collective-permute-start | bytes 1671176 | tf_op jit(solution)/shard_map/ppermute | solution.py:954
  368.1 28.7 %collective-permute-start.47 = (bf16[128,2176]{1,0:T(8,128)(2,1)S(1)}, bf16[128,2176]{1,0:T(8,128)(2,1)S(1)}, u32[]{:S(2)}, u32[]{:S(2)}) collective-permute-start(bf16[128,2176]{1,0:T(8,128)(2,1)S(1)} %add_convert_fusion.10.refs_0_), channel_id=1, source_target_pairs={{0,16},{4,12},{8,24},{12,4},{16,0},{20,28},{24,8},{28,20},{1,17},{... | collective-permute-start | bytes 1671176 | tf_op jit(solution)/shard_map/ppermute | solution.py:954
  369.1 27.7 %collective-permute-start.48 = (bf16[128,2176]{1,0:T(8,128)(2,1)S(1)}, bf16[128,2176]{1,0:T(8,128)(2,1)S(1)}, u32[]{:S(2)}, u32[]{:S(2)}) collective-permute-start(bf16[128,2176]{1,0:T(8,128)(2,1)S(1)} %add_convert_fusion.10.refs_0_), channel_id=1, source_target_pairs={{0,4},{4,0},{8,12},{12,8},{16,20},{20,16},{24,28},{28,24},{1,5},{5... | collective-permute-start | bytes 1671176 | tf_op jit(solution)/shard_map/ppermute | solution.py:954
  375.3 7.2 %collective-permute-start.44 = (bf16[128,1024]{1,0:T(8,128)(2,1)S(1)}, bf16[128,1024]{1,0:T(8,128)(2,1)S(1)}, u32[]{:S(2)}, u32[]{:S(2)}) collective-permute-start(bf16[128,1024]{1,0:T(8,128)(2,1)S(1)} %get-tuple-element.558), channel_id=1, source_target_pairs={{0,1},{1,2},{2,3},{3,0},{4,5},{5,6},{6,7},{7,4},{8,9},{9,10},{10,1... | collective-permute-start | bytes 786440 | tf_op jit(solution)/shard_map/ppermute | solution.py:974
  387.8 9.9 %collective-permute-start.49 = (f32[4,5632]{1,0:T(4,128)S(1)}, f32[4,5632]{1,0:T(4,128)S(1)}, u32[]{:S(2)}, u32[]{:S(2)}) collective-permute-start(f32[4,5632]{1,0:T(4,128)S(1)} %pad_maximum_fusion.9), channel_id=1, source_target_pairs={{0,4},{4,0},{8,12},{12,8},{16,20},{20,16},{24,28},{28,24},{1,5},{5... | collective-permute-start | bytes 270344 | tf_op jit(solution)/shard_map/ppermute | solution.py:954
  397.8 17.6 %collective-permute-start.51 = (bf16[2,128,2176]{2,1,0:T(8,128)(2,1)S(1)}, bf16[2,128,2176]{2,1,0:T(8,128)(2,1)S(1)}, u32[]{:S(2)}, u32[]{:S(2)}) collective-permute-start(bf16[2,128,2176]{2,1,0:T(8,128)(2,1)S(1)} %pad_maximum_fusion.3), channel_id=1, source_target_pairs={{0,4},{4,0},{8,12},{12,8},{16,20},{20,16},{24,28},{28,24},{1,5},{5... | collective-permute-start | bytes 3342344 | tf_op jit(solution)/shard_map/ppermute | solution.py:954
  398.2 7.8 %collective-permute-start.55 = (bf16[128,1024]{1,0:T(8,128)(2,1)S(1)}, bf16[128,1024]{1,0:T(8,128)(2,1)S(1)}, u32[]{:S(2)}, u32[]{:S(2)}) collective-permute-start(bf16[128,1024]{1,0:T(8,128)(2,1)S(1)} %get-tuple-element.555), channel_id=1, source_target_pairs={{0,3},{1,0},{2,1},{3,2},{4,7},{5,4},{6,5},{7,6},{8,11},{9,8},{10,9... | collective-permute-start | bytes 786440 | tf_op jit(solution)/shard_map/ppermute | solution.py:974
  400.1 12.5 %collective-permute-start.54 = (bf16[128,1024]{1,0:T(8,128)(2,1)S(1)}, bf16[128,1024]{1,0:T(8,128)(2,1)S(1)}, u32[]{:S(2)}, u32[]{:S(2)}) collective-permute-start(bf16[128,1024]{1,0:T(8,128)(2,1)S(1)} %add_convert_fusion.15), channel_id=1, source_target_pairs={{0,1},{1,2},{2,3},{3,0},{4,5},{5,6},{6,7},{7,4},{8,9},{9,10},{10,1... | collective-permute-start | bytes 786440 | tf_op jit(solution)/shard_map/ppermute | solution.py:974
  400.1 15.3 %collective-permute-start.50 = (bf16[128,2176]{1,0:T(8,128)(2,1)S(1)}, bf16[128,2176]{1,0:T(8,128)(2,1)S(1)}, u32[]{:S(2)}, u32[]{:S(2)}) collective-permute-start(bf16[128,2176]{1,0:T(8,128)(2,1)S(1)} %collective-permute-done.46.refs_1_), channel_id=1, source_target_pairs={{0,16},{4,12},{8,24},{12,4},{16,0},{20,28},{24,8},{28,20},{1,17},{... | collective-permute-start | bytes 1671176 | tf_op jit(solution)/shard_map/ppermute | solution.py:954
  400.4 13.5 %collective-permute-start.52 = (f32[4,5632]{1,0:T(4,128)S(1)}, f32[4,5632]{1,0:T(4,128)S(1)}, u32[]{:S(2)}, u32[]{:S(2)}) collective-permute-start(f32[4,5632]{1,0:T(4,128)S(1)} %add.170), channel_id=1, source_target_pairs={{0,8},{4,12},{8,0},{12,4},{16,24},{20,28},{24,16},{28,20},{1,9},{5... | collective-permute-start | bytes 270344 | tf_op jit(solution)/shard_map/ppermute | solution.py:954
  413.3 7.4 %collective-permute-start.57 = (bf16[128,1024]{1,0:T(8,128)(2,1)S(1)}, bf16[128,1024]{1,0:T(8,128)(2,1)S(1)}, u32[]{:S(2)}, u32[]{:S(2)}) collective-permute-start(bf16[128,1024]{1,0:T(8,128)(2,1)S(1)} %add_convert_fusion.14.refs_0_), channel_id=1, source_target_pairs={{0,16},{4,12},{8,24},{12,4},{16,0},{20,28},{24,8},{28,20},{1,17},{... | collective-permute-start | bytes 786440 | tf_op jit(solution)/shard_map/ppermute | solution.py:954
  415.5 12.0 %collective-permute-start.53 = (bf16[128,2176]{1,0:T(8,128)(2,1)S(1)}, bf16[128,2176]{1,0:T(8,128)(2,1)S(1)}, u32[]{:S(2)}, u32[]{:S(2)}) collective-permute-start(bf16[128,2176]{1,0:T(8,128)(2,1)S(1)} %collective-permute-done.50.refs_3_), channel_id=1, source_target_pairs={{0,4},{4,0},{8,12},{12,8},{16,20},{20,16},{24,28},{28,24},{1,5},{5... | collective-permute-start | bytes 1671176 | tf_op jit(solution)/shard_map/ppermute | solution.py:954
  420.8 8.9 %collective-permute-start.64 = (bf16[2,128,1024]{2,1,0:T(8,128)(2,1)S(1)}, bf16[2,128,1024]{2,1,0:T(8,128)(2,1)S(1)}, u32[]{:S(2)}, u32[]{:S(2)}) collective-permute-start(bf16[2,128,1024]{2,1,0:T(8,128)(2,1)S(1)} %pad_maximum_fusion.8), channel_id=1, source_target_pairs={{0,4},{4,0},{8,12},{12,8},{16,20},{20,16},{24,28},{28,24},{1,5},{5... | collective-permute-start | bytes 1572872 | tf_op jit(solution)/shard_map/ppermute | solution.py:954
  422.2 7.5 %collective-permute-start.63 = (bf16[128,1024]{1,0:T(8,128)(2,1)S(1)}, bf16[128,1024]{1,0:T(8,128)(2,1)S(1)}, u32[]{:S(2)}, u32[]{:S(2)}) collective-permute-start(bf16[128,1024]{1,0:T(8,128)(2,1)S(1)} %collective-permute-done.56.refs_1_), channel_id=1, source_target_pairs={{0,16},{4,12},{8,24},{12,4},{16,0},{20,28},{24,8},{28,20},{1,17},{... | collective-permute-start | bytes 786440 | tf_op jit(solution)/shard_map/ppermute | solution.py:954
  427.7 15.9 %collective-permute-start.62 = (f32[5632]{0:T(1024)S(1)}, f32[5632]{0:T(1024)S(1)}, u32[]{:S(2)}, u32[]{:S(2)}) collective-permute-start(f32[5632]{0:T(1024)S(1)} %get-tuple-element.522), channel_id=1, source_target_pairs={{0,3},{1,0},{2,1},{3,2},{4,7},{5,4},{6,5},{7,6},{8,11},{9,8},{10,9... | collective-permute-start | bytes 67592 | tf_op jit(solution)/shard_map/ppermute | solution.py:974
  429.0 14.5 %collective-permute-start.61 = (f32[5632]{0:T(1024)S(1)}, f32[5632]{0:T(1024)S(1)}, u32[]{:S(2)}, u32[]{:S(2)}) collective-permute-start(f32[5632]{0:T(1024)S(1)} %get-tuple-element.523), channel_id=1, source_target_pairs={{0,2},{1,3},{2,0},{3,1},{4,6},{5,7},{6,4},{7,5},{8,10},{9,11},{10,... | collective-permute-start | bytes 67592 | tf_op jit(solution)/shard_map/ppermute | solution.py:974
  429.7 13.9 %collective-permute-start.60 = (f32[5632]{0:T(1024)S(1)}, f32[5632]{0:T(1024)S(1)}, u32[]{:S(2)}, u32[]{:S(2)}) collective-permute-start(f32[5632]{0:T(1024)S(1)} %get-tuple-element.521), channel_id=1, source_target_pairs={{0,1},{1,2},{2,3},{3,0},{4,5},{5,6},{6,7},{7,4},{8,9},{9,10},{10,1... | collective-permute-start | bytes 67592 | tf_op jit(solution)/shard_map/ppermute | solution.py:974
  430.6 14.8 %collective-permute-start.65 = (bf16[128,1024]{1,0:T(8,128)(2,1)S(1)}, bf16[128,1024]{1,0:T(8,128)(2,1)S(1)}, u32[]{:S(2)}, u32[]{:S(2)}) collective-permute-start(bf16[128,1024]{1,0:T(8,128)(2,1)S(1)} %collective-permute-done.63.refs_3_), channel_id=1, source_target_pairs={{0,4},{4,0},{8,12},{12,8},{16,20},{20,16},{24,28},{28,24},{1,5},{5... | collective-permute-start | bytes 786440 | tf_op jit(solution)/shard_map/ppermute | solution.py:954
  (60 other events, 764.2 us)
Sparse Core Ops, SparseCore 0:
  31.7 36.9 all-gather.4
  72.0 26.1 all-gather.6

commit v5 on v4

--- a/solution.py
+++ b/solution.py
@@ -1208,9 +1208,9 @@
     front, d_normed1 = input_back(d_qkv, mixer_w, d_b, beta_w)
     front = lax.ppermute(front, "tensor", behind)
     d_normed1 = pending.tie(d_normed1)
+    mix.first(0)
     red.second(1)
     red.along()
-    mix.first(0)
     mix.first(1)
     total = pending.tie(reduce_far(red.result(), dp))
     gather = Gather(total, dp)
@@ -1249,9 +1249,9 @@
         small = small + swap(small, lambda i: mask, dp)
         mask *= 2
     small_in = [to_ahead(small[k], k, tensor) for k in range(1, tensor)]
-    gather.pieces, mixer_gather.pieces = pending.tie_all(gather.pieces, mixer_gather.pieces)
+    grad_gate, grad_up, grad_down = finish_ffn(ids, gather.ordered(), hidden)
+    grad_gate, mixer_gather.pieces = pending.tie_all(grad_gate, mixer_gather.pieces)
     mixer_gather.round()
-    grad_gate, grad_up, grad_down = finish_ffn(ids, gather.ordered(), hidden)
     small = sum(small_in, small[0])
     grad_q, grad_k, grad_v, grad_out = finish_mixer(ids, mixer_gather.ordered(), part)
     cut = local_heads * width

time: 468 us -> 460 us (0.983)
  starting transfers between devices: 83.8 us -> 71.8 us
    ppermute x46, starting transfers between devices: 50.1 us -> 40.8 us  [swap(): return lax.ppermute(x, 'dp', [(i, i ^ mask_of(i)) for i in range(size)])]
    ppermute x9, waiting for transfers between devices: 16.8 us -> 22 us  [to_ahead(): return lax.ppermute(x, 'tensor', [(i, (i + k) % size) for i in range(size)])]
  transfers between devices with their start and end apart: 68 -> 68, of which waited for: 27 -> 26; matrix products, arithmetic and copies ran while one was open for 11% -> 12% of each run, Pallas kernels for 27% -> 28%
where the time goes in v5:
time: 460 us; the launch traced here: 451 us
  Pallas kernels  179 us (39%)
  waiting for transfers between devices  127 us (28%)
  starting transfers between devices  71.8 us (16%)
  other arithmetic  30.6 us (7%)
  local copies, waits for them, and re-layouts  26.1 us (6%)
  between operations  15.6 us (3%)
    ppermute x46, waiting for transfers between devices, swap(): return lax.ppermute(x, 'dp', [(i, i ^ mask_of(i)) for i in range(size)])  55.2 us
    pallas_call x1, Pallas kernels, ffn(): call(functools.partial(ffn_kernel, hidden), 2 * slots, [pl.BlockSpec((cou...  45.6 us
    ppermute x46, starting transfers between devices, swap(): return lax.ppermute(x, 'dp', [(i, i ^ mask_of(i)) for i in range(size)])  40.8 us
    pallas_call x1, Pallas kernels, mixer_back(): call(back_kernel, slots, [columns(tokens, HD)] + [lead(per, a.shape) for...  26.8 us
    pallas_call x1, Pallas kernels, mixer_local(): call(local_kernel, slots, [whole(x.shape), whole(halo.shape), whole(seg.s...  26 us
    convert_element_type x14, other arithmetic, add(): return (a.astype(F32) + b.astype(F32)).astype(BF16)  23.1 us
    ppermute x9, waiting for transfers between devices, to_ahead(): return lax.ppermute(x, 'tensor', [(i, (i + k) % size) for i in range(size)])  22 us
    ppermute x2, waiting for transfers between devices, shards(): lax.ppermute(hop(pending.tie(recv), keep, back_gain, tensor, True), 'tens...  11.7 us
  transfers between devices with their start and end apart: 68, of which 26 were waited for; matrix products, arithmetic and copies ran while one was open for 12% of the time, Pallas kernels for 28%

profile of v5, /device:TPU:1, one launch (start us, length us, event | category | flops | bytes accessed | tf_op | source)
XLA Modules:
  0.0 451.3 jit_solution(8262962025576104629)
XLA Ops:
  7.2 1.7 pack_mixer.2
  9.0 4.2 collective-permute-start
  15.4 4.1 collective-permute-start.3
  19.5 6.2 %pack_mixer.3.own_ref = bf16[8,144,768]{2,1,0:T(8,128)(2,1)} custom-call(s32[8]{0:T(128)} %iota.3.table_ref, bf16[1024,256]{1,0:T(8,128)(2,1)} %q_ref.3, bf16[1024,256]{1,0:T(8,128)(2,1)} %k_ref.3, bf16[1024,256]{1,0:T(8,128)(2,1)} %v_ref.3, bf16[2,1024]{1,0:T(2,128)(2,1)} %bitcast.154, bf16[3,4,256]{2,1,0:T(4,128)(2,1)} %conv_ref.3), custom_call_target="tpu_custom_call" | custom-call | bytes 3145728 | tf_op jit(solution)/shard_map/pack_mixer/pallas_call | solution.py:711
  25.7 2.1 pack_ffn.2
  28.5 3.1 collective-permute-done.1
  34.2 8.4 %pack_ffn.3 = (bf16[8,128,1408]{2,1,0:T(8,128)(2,1)}, bf16[8,128,1024]{2,1,0:T(8,128)(2,1)}) custom-call(s32[8]{0:T(128)} %iota.3.table_ref, bf16[704,1024]{1,0:T(8,128)(2,1)} %bitcast.122, bf16[704,1024]{1,0:T(8,128)(2,1)} %bitcast.124, bf16[704,1024]{1,0:T(8,128)(2,1)} %down_ref.3, bf16[256,1024]{1,0:T(8,128)(2,1)} %out_w_ref.3), custom_call_target="tpu_custom_call" | custom-call | tf_op jit(solution)/shard_map/pack_ffn/pallas_call | solution.py:724
  42.6 2.5 collective-permute-done.4.refs_1_
  45.2 4.2 collective-permute-done.5.refs_2_
  51.5 7.8 %collective-permute-done.6.refs_3_ = bf16[3,144,768]{2,1,0:T(8,128)(2,1)} collective-permute-done((bf16[3,144,768]{2,1,0:T(8,128)(2,1)S(1)}, bf16[3,144,768]{2,1,0:T(8,128)(2,1)}, u32[]{:S(2)}, u32[]{:S(2)}) %collective-permute-start.6) | collective-permute-done | bytes 663584 | tf_op jit(solution)/shard_map/ppermute | solution.py:954
  59.3 9.4 %all-gather.5.cloned.1.call-done = bf16[512,1408]{1,0:T(8,128)(2,1)} async-done(((bf16[128,1408]{1,0:T(8,128)(2,1)}), bf16[512,1408]{1,0:T(8,128)(2,1)}) %all-gather.5.cloned.1.call-update) | async-done | bytes 1441808 | tf_op jit(solution)/shard_map/all_gather | solution.py:1132
  68.7 1.4 collective-permute-start.10
  77.0 26.0 %mixer_local.1 = (bf16[4,8,144,768]{3,2,1,0:T(8,128)(2,1)}, f32[2,256,128]{2,1,0:T(8,128)}, f32[8,16,128]{2,1,0:T(8,128)}, bf16[4,32,1024]{2,1,0:T(8,128)(2,1)},...) custom-call(s32[8]{0:T(128)} %stack.113.ids_ref, ...), custom_call_target="tpu_custom_call" | custom-call | flops 16000000000 | bytes 32000000 | tf_op jit(solution)/shard_map/mixer_local/pallas_call | solution.py:753
  104.0 1.6 pad_maximum_fusion
  106.6 2.3 collective-permute-start.14
  110.1 9.1 %collective-permute-done.14.state_ref = bf16[8,2,128,128]{3,2,1,0:T(8,128)(2,1)S(1)} collective-permute-done((bf16[8,2,128,128]{3,2,1,0:T(8,128)(2,1)S(1)}, bf16[8,2,128,128]{3,2,1,0:T(8,128)(2,1)S(1)}, u32[]{:S(2)}, u32[]{:S(2)}) %collective-permute-start.14) | collective-permute-done | bytes 524320 | tf_op jit(solution)/shard_map/ppermute | solution.py:1161
  119.9 4.1 collective-permute-start.15
  125.5 1.6 collective-permute-start.24
  127.1 6.4 %collective-permute-done.15.state_ref = bf16[8,2,128,128]{3,2,1,0:T(8,128)(2,1)S(1)} collective-permute-done((bf16[8,2,128,128]{3,2,1,0:T(8,128)(2,1)S(1)}, bf16[8,2,128,128]{3,2,1,0:T(8,128)(2,1)S(1)}, u32[]{:S(2)}, u32[]{:S(2)}) %collective-permute-start.15) | collective-permute-done | bytes 524320 | tf_op jit(solution)/shard_map/ppermute | solution.py:1164
  133.4 3.7 collective-permute-done.16.refs_6_
  138.8 3.9 collective-permute-start.18
  142.7 6.3 %collective-permute-done.23.refs_13_ = bf16[3,128,1024]{2,1,0:T(8,128)(2,1)} collective-permute-done((bf16[3,128,1024]{2,1,0:T(8,128)(2,1)S(1)}, bf16[3,128,1024]{2,1,0:T(8,128)(2,1)}, u32[]{:S(2)}, u32[]{:S(2)}) %collective-permute-start.23) | collective-permute-done | bytes 786464 | tf_op jit(solution)/shard_map/ppermute | solution.py:954
  149.0 3.7 collective-permute-done.18.state_ref
  153.8 1.6 collective-permute-start.25
  156.6 6.1 %mixer_output.1 = (bf16[2,256,1024]{2,1,0:T(8,128)(2,1)}, bf16[8,2,256,128]{3,2,1,0:T(8,128)(2,1)}) custom-call(bf16[8,2,256,256]{3,2,1,0:T(8,128)(2,1)} %get-tuple-element.273.qk_ref, bf16[8,2,256,256]{3,2,1,0:T(8,128)(2,1)} %get-tuple-element.274.p_ref, f32[8,2,256,128]{3,2,1,0:T(8,128)} %get-tuple-element.275.ub_ref, ...), custom_call_target="tpu_custom_call" | custom-call | flops 800000000 | bytes 8000000 | tf_op jit(solution)/shard_map/mixer_output/pallas_call | solution.py:778
  162.8 45.6 %ffn.1 = (bf16[512,1024]{1,0:T(8,128)(2,1)}, f32[512,1024]{1,0:T(8,128)}, bf16[512,1024]{1,0:T(8,128)(2,1)}, f32[512,1024]{1,0:T(8,128)}, f32[8,1024]{1,0:T(8,12...) custom-call(s32[8]{0:T(128)} %stack.113.ids_ref, ...), custom_call_target="tpu_custom_call" | custom-call | flops 38386270208 | bytes 60000000 | tf_op jit(solution)/shard_map/ffn/pallas_call | solution.py:847
  210.2 8.9 %mixer_back_local.1 = (f32[8,2,256,128]{3,2,1,0:T(8,128)}, f32[8,2,128,128]{3,2,1,0:T(8,128)}, bf16[8,2,128,128]{3,2,1,0:T(8,128)(2,1)}) custom-call(f32[2,256,1024]{2,1,0:T(8,128)} %bitcast.130, bf16[8,2,256,256]{3,2,1,0:T(8,128)(2,1)} %get-tuple-element.273.qk_ref, bf16[8,2,256,256]{3,2,1,0:T(8,128)(2,1)} %get-tuple-element.314.t_ref, ...), custom_call_target="tpu_custom_call" | custom-call | flops 800000000 | bytes 8000000 | tf_op jit(solution)/shard_map/mixer_back_local/pallas_call | solution.py:793
  220.4 4.9 %add_convert_fusion.1 = bf16[4,2,128,2176]{3,2,1,0:T(8,128)(2,1)S(1)} fusion(bf16[4,2,128,2176]{3,2,1,0:T(8,128)(2,1)} %collective-permute-done.27, bf16[4,2,128,2176]{3,2,1,0:T(8,128)(2,1)} %get-tuple-element.325), kind=kLoop, calls=%fused_computation.1 | loop fusion | flops 8912896 | bytes 13369344 | tf_op jit(solution)/shard_map/convert_element_type | solution.py:997
  225.3 2.5 fusion.8
  230.2 5.5 %collective-permute-done.26.state_ref = bf16[8,2,128,128]{3,2,1,0:T(8,128)(2,1)S(1)} collective-permute-done((bf16[8,2,128,128]{3,2,1,0:T(8,128)(2,1)}, bf16[8,2,128,128]{3,2,1,0:T(8,128)(2,1)S(1)}, u32[]{:S(2)}, u32[]{:S(2)}) %collective-permute-start.26) | collective-permute-done | bytes 524320 | tf_op jit(solution)/shard_map/ppermute | solution.py:1185
  238.0 3.4 add_convert_fusion
  241.4 2.4 fusion.7
  245.1 4.2 flip.1
  249.3 2.3 collective-permute-done.28.state_ref
  254.7 2.1 add_convert_fusion.3
  257.1 9.5 %collective-permute-done.30.dstate_ref = bf16[8,2,128,128]{3,2,1,0:T(8,128)(2,1)S(1)} collective-permute-done((bf16[8,2,128,128]{3,2,1,0:T(8,128)(2,1)S(1)}, bf16[8,2,128,128]{3,2,1,0:T(8,128)(2,1)S(1)}, u32[]{:S(2)}, u32[]{:S(2)}) %collective-permute-start.30) | collective-permute-done | bytes 524320 | tf_op jit(solution)/shard_map/ppermute | solution.py:1192
  267.3 26.8 %mixer_back.1 = (bf16[2,272,3072]{2,1,0:T(8,128)(2,1)}, f32[2,256,128]{2,1,0:T(8,128)}, f32[8,16,128]{2,1,0:T(8,128)}) custom-call(f32[2,256,1024]{2,1,0:T(8,128)} %bitcast.131, f32[8,2,256,128]{3,2,1,0:T(8,128)} %get-tuple-element.316.y_ref, bf16[8,2,256,256]{3,2,1,0:T(8,128)(2,1)} %get-tuple-element.273.qk_ref, ...), custom_call_target="tpu_custom_call" | custom-call | flops 8000000000 | bytes 32000000 | tf_op jit(solution)/shard_map/mixer_back/pallas_call | solution.py:807
  294.1 10.4 %grad_mixer.1 = (bf16[4,2,128,1024]{3,2,1,0:T(8,128)(2,1)}, bf16[4,2,128,1024]{3,2,1,0:T(8,128)(2,1)}, bf16[4,2,128,1024]{3,2,1,0:T(8,128)(2,1)}, bf16[4,2,128,1024]{3,2,1,0:T(8,128)(2,1)}) custom-call(bf16[1024,544]{1,0:T(8,128)(2,1)} %get-tuple-element.360.xt_ref, bf16[544,3072]{1,0:T(8,128)(2,1)} %bitcast.163, ...), custom_call_target="tpu_custom_call" | custom-call | flops 4294967296 | bytes 8388608 | tf_op jit(solution)/shard_map/grad_mixer/pallas_call | solution.py:883
  304.5 2.9 collective-permute-start.32
  307.5 1.7 add_convert_fusion.7
  310.2 2.1 add_convert_fusion.2
  315.9 1.5 fusion.10
  321.2 11.3 %input_back.1 = (f32[2,16,1024]{2,1,0:T(8,128)}, f32[2,256,1024]{2,1,0:T(8,128)}) custom-call(bf16[2,272,3072]{2,1,0:T(8,128)(2,1)} %get-tuple-element.388.dqkv_ref, bf16[4,8,144,768]{3,2,1,0:T(8,128)(2,1)} %get-tuple-element.389.w_ref, bf16[2,256,128]{2,1,0:T(8,128)(2,1)} %convert_element_type.205.db_ref, bf16[4,128,1024]{2,1,0:T(8,128)(2,1)} %pad_maximum_fusion.5.beta_w_ref), custom_call_target="tpu_custom_call" | custom-call | flops 3422552064 | bytes 6291456 | tf_op jit(solution)/shard_map/input_back/pallas_call | solution.py:936
  337.6 3.0 collective-permute-done.37
  340.7 1.9 add_convert_fusion.9
  343.0 1.6 add_convert_fusion.6
  347.5 10.0 %collective-permute-done.39 = bf16[2,2,128,1024]{3,2,1,0:T(8,128)(2,1)} collective-permute-done((bf16[2,2,128,1024]{3,2,1,0:T(8,128)(2,1)}, bf16[2,2,128,1024]{3,2,1,0:T(8,128)(2,1)}, u32[]{:S(2)}, u32[]{:S(2)}) %collective-permute-start.39) | collective-permute-done | bytes 1048608 | tf_op jit(solution)/shard_map/ppermute | solution.py:954
  357.4 1.6 add_convert_fusion.8
  359.4 11.7 %collective-permute-done.42 = bf16[128,2176]{1,0:T(8,128)(2,1)S(1)} collective-permute-done((bf16[128,2176]{1,0:T(8,128)(2,1)S(1)}, bf16[128,2176]{1,0:T(8,128)(2,1)S(1)}, u32[]{:S(2)}, u32[]{:S(2)}) %collective-permute-start.42) | collective-permute-done | bytes 557088 | tf_op jit(solution)/shard_map/ppermute | solution.py:974
  371.5 2.4 collective-permute-start.47
  373.9 1.9 collective-permute-start.48
  377.0 8.8 %collective-permute-done.44 = bf16[128,1024]{1,0:T(8,128)(2,1)S(1)} collective-permute-done((bf16[128,1024]{1,0:T(8,128)(2,1)S(1)}, bf16[128,1024]{1,0:T(8,128)(2,1)S(1)}, u32[]{:S(2)}, u32[]{:S(2)}) %collective-permute-start.44) | collective-permute-done | bytes 262176 | tf_op jit(solution)/shard_map/ppermute | solution.py:974
  385.8 4.5 %input_norm.1 = (bf16[512,1024]{1,0:T(8,128)(2,1)}, f32[8,1024]{1,0:T(8,128)}) custom-call(f32[2,256,1024]{2,1,0:T(8,128)} %get-tuple-element.429.grad_ref, f32[2,16,1024]{2,1,0:T(8,128)} %collective-permute-done.36.front_ref, bf16[512,1024]{1,0:T(8,128)(2,1)} %bitcast.118, f32[512,1024]{1,0:T(8,128)} %get-tuple-element.431.dmid_ref, f32[1,1024]{1,0:T(1,128)} %bitcast.152), custom_call_target="tpu_custom_call" | custom-call | bytes 6291456 | tf_op jit(solution)/shard_map/input_norm/pallas_call | solution.py:947
  395.2 1.5 collective-permute-start.52
  396.7 7.5 %collective-permute-done.52 = f32[4,5632]{1,0:T(4,128)S(1)} collective-permute-done((f32[4,5632]{1,0:T(4,128)S(1)}, f32[4,5632]{1,0:T(4,128)S(1)}, u32[]{:S(2)}, u32[]{:S(2)}) %collective-permute-start.52) | collective-permute-done | bytes 90144 | tf_op jit(solution)/shard_map/ppermute | solution.py:954
  404.3 1.6 collective-permute-done.54
  406.0 1.9 collective-permute-start.56
  408.0 2.3 collective-permute-start.57
  412.0 5.1 %collective-permute-done.57.refs_2_ = bf16[128,1024]{1,0:T(8,128)(2,1)S(1)} collective-permute-done((bf16[128,1024]{1,0:T(8,128)(2,1)S(1)}, bf16[128,1024]{1,0:T(8,128)(2,1)S(1)}, u32[]{:S(2)}, u32[]{:S(2)}) %collective-permute-start.57) | collective-permute-done | bytes 262176 | tf_op jit(solution)/shard_map/ppermute | solution.py:954
  417.2 1.5 collective-permute-start.63
  422.4 1.4 collective-permute-start.60
  424.9 7.8 %finish_ffn.1 = (f32[704,1024]{1,0:T(8,128)}, f32[704,1024]{1,0:T(8,128)}, f32[704,1024]{1,0:T(8,128)}) custom-call(s32[8]{0:T(128)} %stack.113.ids_ref, bf16[128,2176]{1,0:T(8,128)(2,1)} %copy-done.8, bf16[128,2176]{1,0:T(8,128)(2,1)} %copy-done.9, bf16[128,2176]{1,0:T(8,128)(2,1)} %copy-done.10, bf16[128,2176]{1,0:T(8,128)(2,1)} %copy-done.26, ...), custom_call_target="tpu_custom_call" | custom-call | bytes 13369344 | tf_op jit(solution)/shard_map/finish_ffn/pallas_call | solution.py:895
  433.7 2.1 collective-permute-start.65
  438.3 5.7 %finish_mixer.1 = (f32[1024,256]{1,0:T(8,128)}, f32[1024,256]{1,0:T(8,128)}, f32[1024,256]{1,0:T(8,128)}, f32[256,1024]{1,0:T(8,128)}) custom-call(s32[8]{0:T(128)} %stack.113.ids_ref, bf16[128,1024]{1,0:T(8,128)(2,1)} %copy-done.17, bf16[128,1024]{1,0:T(8,128)(2,1)} %copy-done.18, bf16[128,1024]{1,0:T(8,128)(2,1)} %copy-done.19, ...), custom_call_target="tpu_custom_call" | custom-call | bytes 6291456 | tf_op jit(solution)/shard_map/finish_mixer/pallas_call | solution.py:921
  (285 shorter events, 70.3 us)
Async XLA Ops:
  7.2 61.5 %all-gather.5.cloned.1.call-start = ((), (), s32[]{:S(2)}) async-start(), calls=%async_computation | async-start | bytes 1802240 | tf_op jit(solution)/shard_map/all_gather | solution.py:1132
  9.0 19.5 %collective-permute-start = (bf16[144,768]{1,0:T(8,128)(2,1)}, bf16[144,768]{1,0:T(8,128)(2,1)S(1)}, u32[]{:S(2)}, u32[]{:S(2)}) collective-permute-start(bf16[144,768]{1,0:T(8,128)(2,1)} %bitcast.142), channel_id=1, source_target_pairs={{0,3},{1,0},{2,1},{3,2},{4,7},{5,4},{6,5},{7,6},{8,11},{9,8},{10,9... | collective-permute-start | bytes 663560 | tf_op jit(solution)/shard_map/ppermute | solution.py:970
  13.1 18.4 %collective-permute-start.1 = (bf16[144,768]{1,0:T(8,128)(2,1)}, bf16[144,768]{1,0:T(8,128)(2,1)S(1)}, u32[]{:S(2)}, u32[]{:S(2)}) collective-permute-start(bf16[144,768]{1,0:T(8,128)(2,1)} %bitcast.143), channel_id=1, source_target_pairs={{0,2},{1,3},{2,0},{3,1},{4,6},{5,7},{6,4},{7,5},{8,10},{9,11},{10,... | collective-permute-start | bytes 663560 | tf_op jit(solution)/shard_map/ppermute | solution.py:970
  13.1 18.4 %collective-permute-start.2 = (bf16[144,768]{1,0:T(8,128)(2,1)}, bf16[144,768]{1,0:T(8,128)(2,1)S(1)}, u32[]{:S(2)}, u32[]{:S(2)}) collective-permute-start(bf16[144,768]{1,0:T(8,128)(2,1)} %bitcast.144), channel_id=1, source_target_pairs={{0,1},{1,2},{2,3},{3,0},{4,5},{5,6},{6,7},{7,4},{8,9},{9,10},{10,1... | collective-permute-start | bytes 663560 | tf_op jit(solution)/shard_map/ppermute | solution.py:970
  15.4 13.0 %collective-permute-start.3 = (bf16[2,16,1024]{2,1,0:T(8,128)(2,1)S(1)}, bf16[2,16,1024]{2,1,0:T(8,128)(2,1)S(1)}, u32[]{:S(2)}, u32[]{:S(2)}) collective-permute-start(bf16[2,16,1024]{2,1,0:T(8,128)(2,1)S(1)} %slice.184), channel_id=1, source_target_pairs={{0,1},{1,2},{2,3},{4,5},{5,6},{6,7},{8,9},{9,10},{10,11},{12,13},{... | collective-permute-start | bytes 196616 | tf_op jit(solution)/shard_map/ppermute | solution.py:1123
  31.6 71.5 %all-gather.7.cloned.1.call-start = ((), (), s32[]{:S(2)}) async-start(), calls=%async_computation.1 | async-start | bytes 1310720 | tf_op jit(solution)/shard_map/all_gather | solution.py:1132
  31.7 13.4 %collective-permute-start.4 = (bf16[3,144,768]{2,1,0:T(8,128)(2,1)S(1)}, bf16[3,144,768]{2,1,0:T(8,128)(2,1)S(1)}, u32[]{:S(2)}, u32[]{:S(2)}) collective-permute-start(bf16[3,144,768]{2,1,0:T(8,128)(2,1)S(1)} %pad_maximum_fusion.7.refs_0_), channel_id=1, source_target_pairs={{0,8},{4,20},{8,0},{12,28},{16,24},{20,4},{24,16},{28,12},{1,9},{5... | collective-permute-start | bytes 1990664 | tf_op jit(solution)/shard_map/ppermute | solution.py:954
  33.0 16.3 %collective-permute-start.5 = (bf16[3,144,768]{2,1,0:T(8,128)(2,1)S(1)}, bf16[3,144,768]{2,1,0:T(8,128)(2,1)S(1)}, u32[]{:S(2)}, u32[]{:S(2)}) collective-permute-start(bf16[3,144,768]{2,1,0:T(8,128)(2,1)S(1)} %pad_maximum_fusion.7.refs_0_), channel_id=1, source_target_pairs={{0,16},{4,12},{8,24},{12,4},{16,0},{20,28},{24,8},{28,20},{1,17},{... | collective-permute-start | bytes 1990664 | tf_op jit(solution)/shard_map/ppermute | solution.py:954
  49.3 9.9 %collective-permute-start.6 = (bf16[3,144,768]{2,1,0:T(8,128)(2,1)S(1)}, bf16[3,144,768]{2,1,0:T(8,128)(2,1)}, u32[]{:S(2)}, u32[]{:S(2)}) collective-permute-start(bf16[3,144,768]{2,1,0:T(8,128)(2,1)S(1)} %collective-permute-done.4.refs_1_), channel_id=1, source_target_pairs={{0,16},{4,12},{8,24},{12,4},{16,0},{20,28},{24,8},{28,20},{1,17},{... | collective-permute-start | bytes 1990664 | tf_op jit(solution)/shard_map/ppermute | solution.py:954
  50.6 8.7 %collective-permute-start.8 = (bf16[3,144,768]{2,1,0:T(8,128)(2,1)S(1)}, bf16[3,144,768]{2,1,0:T(8,128)(2,1)S(1)}, u32[]{:S(2)}, u32[]{:S(2)}) collective-permute-start(bf16[3,144,768]{2,1,0:T(8,128)(2,1)S(1)} %collective-permute-done.4.refs_1_), channel_id=1, source_target_pairs={{0,4},{4,0},{8,12},{12,8},{16,20},{20,16},{24,28},{28,24},{1,5},{5... | collective-permute-start | bytes 1990664 | tf_op jit(solution)/shard_map/ppermute | solution.py:954
  50.9 8.3 %collective-permute-start.7 = (bf16[3,144,768]{2,1,0:T(8,128)(2,1)S(1)}, bf16[3,144,768]{2,1,0:T(8,128)(2,1)S(1)}, u32[]{:S(2)}, u32[]{:S(2)}) collective-permute-start(bf16[3,144,768]{2,1,0:T(8,128)(2,1)S(1)} %pad_maximum_fusion.7.refs_0_), channel_id=1, source_target_pairs={{0,4},{4,0},{8,12},{12,8},{16,20},{20,16},{24,28},{28,24},{1,5},{5... | collective-permute-start | bytes 1990664 | tf_op jit(solution)/shard_map/ppermute | solution.py:954
  51.1 8.2 %collective-permute-start.9 = (bf16[3,144,768]{2,1,0:T(8,128)(2,1)S(1)}, bf16[3,144,768]{2,1,0:T(8,128)(2,1)}, u32[]{:S(2)}, u32[]{:S(2)}) collective-permute-start(bf16[3,144,768]{2,1,0:T(8,128)(2,1)S(1)} %collective-permute-done.5.refs_2_), channel_id=1, source_target_pairs={{0,4},{4,0},{8,12},{12,8},{16,20},{20,16},{24,28},{28,24},{1,5},{5... | collective-permute-start | bytes 1990664 | tf_op jit(solution)/shard_map/ppermute | solution.py:954
  68.7 7.6 %collective-permute-start.10 = (bf16[3,144,768]{2,1,0:T(8,128)(2,1)}, bf16[3,144,768]{2,1,0:T(8,128)(2,1)}, u32[]{:S(2)}, u32[]{:S(2)}) collective-permute-start(bf16[3,144,768]{2,1,0:T(8,128)(2,1)} %collective-permute-done.6.refs_3_), channel_id=1, source_target_pairs={{0,4},{4,0},{8,12},{12,8},{16,20},{20,16},{24,28},{28,24},{1,5},{5... | collective-permute-start | bytes 1990664 | tf_op jit(solution)/shard_map/ppermute | solution.py:954
  73.4 29.7 %collective-permute-start.11 = (bf16[3,128,1408]{2,1,0:T(8,128)(2,1)S(1)}, bf16[3,128,1408]{2,1,0:T(8,128)(2,1)S(1)}, u32[]{:S(2)}, u32[]{:S(2)}) collective-permute-start(bf16[3,128,1408]{2,1,0:T(8,128)(2,1)S(1)} %pad_maximum_fusion.4.refs_2_), channel_id=1, source_target_pairs={{0,8},{4,20},{8,0},{12,28},{16,24},{20,4},{24,16},{28,12},{1,9},{5... | collective-permute-start | bytes 3244040 | tf_op jit(solution)/shard_map/ppermute | solution.py:954
  74.6 28.4 %collective-permute-start.12 = (bf16[3,128,1408]{2,1,0:T(8,128)(2,1)S(1)}, bf16[3,128,1408]{2,1,0:T(8,128)(2,1)}, u32[]{:S(2)}, u32[]{:S(2)}) collective-permute-start(bf16[3,128,1408]{2,1,0:T(8,128)(2,1)S(1)} %pad_maximum_fusion.4.refs_2_), channel_id=1, source_target_pairs={{0,16},{4,12},{8,24},{12,4},{16,0},{20,28},{24,8},{28,20},{1,17},{... | collective-permute-start | bytes 3244040 | tf_op jit(solution)/shard_map/ppermute | solution.py:954
  75.8 27.3 %collective-permute-start.13 = (bf16[3,128,1408]{2,1,0:T(8,128)(2,1)S(1)}, bf16[3,128,1408]{2,1,0:T(8,128)(2,1)S(1)}, u32[]{:S(2)}, u32[]{:S(2)}) collective-permute-start(bf16[3,128,1408]{2,1,0:T(8,128)(2,1)S(1)} %pad_maximum_fusion.4.refs_2_), channel_id=1, source_target_pairs={{0,4},{4,0},{8,12},{12,8},{16,20},{20,16},{24,28},{28,24},{1,5},{5... | collective-permute-start | bytes 3244040 | tf_op jit(solution)/shard_map/ppermute | solution.py:954
  105.7 31.5 %collective-permute-start.17 = (bf16[2,3,128,1408]{3,2,1,0:T(8,128)(2,1)S(1)}, bf16[2,3,128,1408]{3,2,1,0:T(8,128)(2,1)S(1)}, u32[]{:S(2)}, u32[]{:S(2)}) collective-permute-start(bf16[2,3,128,1408]{3,2,1,0:T(8,128)(2,1)S(1)} %pad_maximum_fusion), channel_id=1, source_target_pairs={{0,4},{4,0},{8,12},{12,8},{16,20},{20,16},{24,28},{28,24},{1,5},{5... | collective-permute-start | bytes 6488072 | tf_op jit(solution)/shard_map/ppermute | solution.py:954
  105.9 18.2 %collective-permute-start.20 = (bf16[3,128,1024]{2,1,0:T(8,128)(2,1)S(1)}, bf16[3,128,1024]{2,1,0:T(8,128)(2,1)S(1)}, u32[]{:S(2)}, u32[]{:S(2)}) collective-permute-start(bf16[3,128,1024]{2,1,0:T(8,128)(2,1)S(1)} %pad_maximum_fusion.6.refs_9_), channel_id=1, source_target_pairs={{0,8},{4,20},{8,0},{12,28},{16,24},{20,4},{24,16},{28,12},{1,9},{5... | collective-permute-start | bytes 2359304 | tf_op jit(solution)/shard_map/ppermute | solution.py:954
  106.3 19.0 %collective-permute-start.21 = (bf16[3,128,1024]{2,1,0:T(8,128)(2,1)S(1)}, bf16[3,128,1024]{2,1,0:T(8,128)(2,1)S(1)}, u32[]{:S(2)}, u32[]{:S(2)}) collective-permute-start(bf16[3,128,1024]{2,1,0:T(8,128)(2,1)S(1)} %pad_maximum_fusion.6.refs_9_), channel_id=1, source_target_pairs={{0,16},{4,12},{8,24},{12,4},{16,0},{20,28},{24,8},{28,20},{1,17},{... | collective-permute-start | bytes 2359304 | tf_op jit(solution)/shard_map/ppermute | solution.py:954
  106.6 12.6 %collective-permute-start.14 = (bf16[8,2,128,128]{3,2,1,0:T(8,128)(2,1)S(1)}, bf16[8,2,128,128]{3,2,1,0:T(8,128)(2,1)S(1)}, u32[]{:S(2)}, u32[]{:S(2)}) collective-permute-start(bf16[8,2,128,128]{3,2,1,0:T(8,128)(2,1)S(1)} %copy-done.51), channel_id=1, source_target_pairs={{0,1},{1,2},{2,3},{4,5},{5,6},{6,7},{8,9},{9,10},{10,11},{12,13},{... | collective-permute-start | bytes 1572872 | tf_op jit(solution)/shard_map/ppermute | solution.py:1161
  108.9 28.3 %collective-permute-start.16 = (bf16[3,128,1408]{2,1,0:T(8,128)(2,1)S(1)}, bf16[3,128,1408]{2,1,0:T(8,128)(2,1)S(1)}, u32[]{:S(2)}, u32[]{:S(2)}) collective-permute-start(bf16[3,128,1408]{2,1,0:T(8,128)(2,1)S(1)} %copy-done.16), channel_id=1, source_target_pairs={{0,16},{4,12},{8,24},{12,4},{16,0},{20,28},{24,8},{28,20},{1,17},{... | collective-permute-start | bytes 3244040 | tf_op jit(solution)/shard_map/ppermute | solution.py:954
  119.9 13.5 %collective-permute-start.15 = (bf16[8,2,128,128]{3,2,1,0:T(8,128)(2,1)S(1)}, bf16[8,2,128,128]{3,2,1,0:T(8,128)(2,1)S(1)}, u32[]{:S(2)}, u32[]{:S(2)}) collective-permute-start(bf16[8,2,128,128]{3,2,1,0:T(8,128)(2,1)S(1)} %hop.4), channel_id=1, source_target_pairs={{0,1},{1,2},{2,3},{4,5},{5,6},{6,7},{8,9},{9,10},{10,11},{12,13},{... | collective-permute-start | bytes 1572872 | tf_op jit(solution)/shard_map/ppermute | solution.py:1164
  125.5 23.5 %collective-permute-start.24 = (bf16[2,3,128,1024]{3,2,1,0:T(8,128)(2,1)S(1)}, bf16[2,3,128,1024]{3,2,1,0:T(8,128)(2,1)S(1)}, u32[]{:S(2)}, u32[]{:S(2)}) collective-permute-start(bf16[2,3,128,1024]{3,2,1,0:T(8,128)(2,1)S(1)} %pad_maximum_fusion.1), channel_id=1, source_target_pairs={{0,4},{4,0},{8,12},{12,8},{16,20},{20,16},{24,28},{28,24},{1,5},{5... | collective-permute-start | bytes 4718600 | tf_op jit(solution)/shard_map/ppermute | solution.py:954
  137.2 15.6 %collective-permute-start.19 = (bf16[3,128,1408]{2,1,0:T(8,128)(2,1)S(1)}, bf16[3,128,1408]{2,1,0:T(8,128)(2,1)S(1)}, u32[]{:S(2)}, u32[]{:S(2)}) collective-permute-start(bf16[3,128,1408]{2,1,0:T(8,128)(2,1)S(1)} %collective-permute-done.16.refs_6_), channel_id=1, source_target_pairs={{0,4},{4,0},{8,12},{12,8},{16,20},{20,16},{24,28},{28,24},{1,5},{5... | collective-permute-start | bytes 3244040 | tf_op jit(solution)/shard_map/ppermute | solution.py:954
  137.7 11.2 %collective-permute-start.23 = (bf16[3,128,1024]{2,1,0:T(8,128)(2,1)S(1)}, bf16[3,128,1024]{2,1,0:T(8,128)(2,1)}, u32[]{:S(2)}, u32[]{:S(2)}) collective-permute-start(bf16[3,128,1024]{2,1,0:T(8,128)(2,1)S(1)} %collective-permute-done.20.refs_10_), channel_id=1, source_target_pairs={{0,16},{4,12},{8,24},{12,4},{16,0},{20,28},{24,8},{28,20},{1,17},{... | collective-permute-start | bytes 2359304 | tf_op jit(solution)/shard_map/ppermute | solution.py:954
  138.8 13.9 %collective-permute-start.18 = (bf16[8,2,128,128]{3,2,1,0:T(8,128)(2,1)S(1)}, bf16[8,2,128,128]{3,2,1,0:T(8,128)(2,1)S(1)}, u32[]{:S(2)}, u32[]{:S(2)}) collective-permute-start(bf16[8,2,128,128]{3,2,1,0:T(8,128)(2,1)S(1)} %hop.5), channel_id=1, source_target_pairs={{0,1},{1,2},{2,3},{4,5},{5,6},{6,7},{8,9},{9,10},{10,11},{12,13},{... | collective-permute-start | bytes 1572872 | tf_op jit(solution)/shard_map/ppermute | solution.py:1166
  153.8 9.0 %collective-permute-start.25 = (bf16[3,128,1024]{2,1,0:T(8,128)(2,1)}, bf16[3,128,1024]{2,1,0:T(8,128)(2,1)}, u32[]{:S(2)}, u32[]{:S(2)}) collective-permute-start(bf16[3,128,1024]{2,1,0:T(8,128)(2,1)} %collective-permute-done.23.refs_13_), channel_id=1, source_target_pairs={{0,4},{4,0},{8,12},{12,8},{16,20},{20,16},{24,28},{28,24},{1,5},{5... | collective-permute-start | bytes 2359304 | tf_op jit(solution)/shard_map/ppermute | solution.py:954
  208.4 11.9 %collective-permute-start.27 = (bf16[4,2,128,2176]{3,2,1,0:T(8,128)(2,1)}, bf16[4,2,128,2176]{3,2,1,0:T(8,128)(2,1)}, u32[]{:S(2)}, u32[]{:S(2)}) collective-permute-start(bf16[4,2,128,2176]{3,2,1,0:T(8,128)(2,1)} %get-tuple-element.319), channel_id=1, source_target_pairs={{0,4},{4,0},{8,12},{12,8},{16,20},{20,16},{24,28},{28,24},{1,5},{5... | collective-permute-start | bytes 13369352 | tf_op jit(solution)/shard_map/ppermute | solution.py:954
  208.5 29.4 %collective-permute-start.29 = (bf16[4,2,128,2176]{3,2,1,0:T(8,128)(2,1)}, bf16[4,2,128,2176]{3,2,1,0:T(8,128)(2,1)}, u32[]{:S(2)}, u32[]{:S(2)}) collective-permute-start(bf16[4,2,128,2176]{3,2,1,0:T(8,128)(2,1)} %get-tuple-element.330), channel_id=1, source_target_pairs={{0,4},{4,0},{8,12},{12,8},{16,20},{20,16},{24,28},{28,24},{1,5},{5... | collective-permute-start | bytes 13369352 | tf_op jit(solution)/shard_map/ppermute | solution.py:954
  219.1 16.6 %collective-permute-start.26 = (bf16[8,2,128,128]{3,2,1,0:T(8,128)(2,1)}, bf16[8,2,128,128]{3,2,1,0:T(8,128)(2,1)S(1)}, u32[]{:S(2)}, u32[]{:S(2)}) collective-permute-start(bf16[8,2,128,128]{3,2,1,0:T(8,128)(2,1)} %get-tuple-element.318), channel_id=1, source_target_pairs={{1,0},{2,1},{3,2},{5,4},{6,5},{7,6},{9,8},{10,9},{11,10},{13,12},{... | collective-permute-start | bytes 1572872 | tf_op jit(solution)/shard_map/ppermute | solution.py:1185
  227.8 26.9 %collective-permute-start.31 = (bf16[2,2,128,2176]{3,2,1,0:T(8,128)(2,1)}, bf16[2,2,128,2176]{3,2,1,0:T(8,128)(2,1)}, u32[]{:S(2)}, u32[]{:S(2)}) collective-permute-start(bf16[2,2,128,2176]{3,2,1,0:T(8,128)(2,1)} %get-tuple-element.517), channel_id=1, source_target_pairs={{0,8},{4,20},{8,0},{12,28},{16,24},{20,4},{24,16},{28,12},{1,9},{5... | collective-permute-start | bytes 6684680 | tf_op jit(solution)/shard_map/ppermute | solution.py:954
  236.6 14.9 %collective-permute-start.28 = (bf16[8,2,128,128]{3,2,1,0:T(8,128)(2,1)S(1)}, bf16[8,2,128,128]{3,2,1,0:T(8,128)(2,1)S(1)}, u32[]{:S(2)}, u32[]{:S(2)}) collective-permute-start(bf16[8,2,128,128]{3,2,1,0:T(8,128)(2,1)S(1)} %hop.6), channel_id=1, source_target_pairs={{1,0},{2,1},{3,2},{5,4},{6,5},{7,6},{9,8},{10,9},{11,10},{13,12},{... | collective-permute-start | bytes 1572872 | tf_op jit(solution)/shard_map/ppermute | solution.py:1188
  243.8 66.4 %collective-permute-start.34 = (bf16[2,2,128,2176]{3,2,1,0:T(8,128)(2,1)}, bf16[2,2,128,2176]{3,2,1,0:T(8,128)(2,1)}, u32[]{:S(2)}, u32[]{:S(2)}) collective-permute-start(bf16[2,2,128,2176]{3,2,1,0:T(8,128)(2,1)} %get-tuple-element.515), channel_id=1, source_target_pairs={{0,8},{4,20},{8,0},{12,28},{16,24},{20,4},{24,16},{28,12},{1,9},{5... | collective-permute-start | bytes 6684680 | tf_op jit(solution)/shard_map/ppermute | solution.py:954
  252.4 14.1 %collective-permute-start.30 = (bf16[8,2,128,128]{3,2,1,0:T(8,128)(2,1)S(1)}, bf16[8,2,128,128]{3,2,1,0:T(8,128)(2,1)S(1)}, u32[]{:S(2)}, u32[]{:S(2)}) collective-permute-start(bf16[8,2,128,128]{3,2,1,0:T(8,128)(2,1)S(1)} %hop.7), channel_id=1, source_target_pairs={{1,0},{2,1},{3,2},{5,4},{6,5},{7,6},{9,8},{10,9},{11,10},{13,12},{... | collective-permute-start | bytes 1572872 | tf_op jit(solution)/shard_map/ppermute | solution.py:1192
  266.5 41.0 %collective-permute-start.35 = (bf16[2,128,2176]{2,1,0:T(8,128)(2,1)S(1)}, bf16[2,128,2176]{2,1,0:T(8,128)(2,1)}, u32[]{:S(2)}, u32[]{:S(2)}) collective-permute-start(bf16[2,128,2176]{2,1,0:T(8,128)(2,1)S(1)} %get-tuple-element.521), channel_id=1, source_target_pairs={{0,16},{4,12},{8,24},{12,4},{16,0},{20,28},{24,8},{28,20},{1,17},{... | collective-permute-start | bytes 3342344 | tf_op jit(solution)/shard_map/ppermute | solution.py:954
  304.5 12.9 %collective-permute-start.32 = (bf16[4,2,128,1024]{3,2,1,0:T(8,128)(2,1)}, bf16[4,2,128,1024]{3,2,1,0:T(8,128)(2,1)S(1)}, u32[]{:S(2)}, u32[]{:S(2)}) collective-permute-start(bf16[4,2,128,1024]{3,2,1,0:T(8,128)(2,1)} %get-tuple-element.362), channel_id=1, source_target_pairs={{0,4},{4,0},{8,12},{12,8},{16,20},{20,16},{24,28},{28,24},{1,5},{5... | collective-permute-start | bytes 6291464 | tf_op jit(solution)/shard_map/ppermute | solution.py:954
  307.4 7.4 %collective-permute-start.33 = (bf16[4,2,128,1024]{3,2,1,0:T(8,128)(2,1)}, bf16[4,2,128,1024]{3,2,1,0:T(8,128)(2,1)S(1)}, u32[]{:S(2)}, u32[]{:S(2)}) collective-permute-start(bf16[4,2,128,1024]{3,2,1,0:T(8,128)(2,1)} %get-tuple-element.363), channel_id=1, source_target_pairs={{0,4},{4,0},{8,12},{12,8},{16,20},{20,16},{24,28},{28,24},{1,5},{5... | collective-permute-start | bytes 6291464 | tf_op jit(solution)/shard_map/ppermute | solution.py:954
  313.6 29.4 %collective-permute-start.41 = (bf16[2,128,2176]{2,1,0:T(8,128)(2,1)}, bf16[2,128,2176]{2,1,0:T(8,128)(2,1)}, u32[]{:S(2)}, u32[]{:S(2)}) collective-permute-start(bf16[2,128,2176]{2,1,0:T(8,128)(2,1)} %get-tuple-element.519), channel_id=1, source_target_pairs={{0,16},{4,12},{8,24},{12,4},{16,0},{20,28},{24,8},{28,20},{1,17},{... | collective-permute-start | bytes 3342344 | tf_op jit(solution)/shard_map/ppermute | solution.py:954
  313.8 32.0 %collective-permute-start.40 = (bf16[128,2176]{1,0:T(8,128)(2,1)}, bf16[128,2176]{1,0:T(8,128)(2,1)}, u32[]{:S(2)}, u32[]{:S(2)}) collective-permute-start(bf16[128,2176]{1,0:T(8,128)(2,1)} %get-tuple-element.534), channel_id=1, source_target_pairs={{0,1},{1,2},{2,3},{3,0},{4,5},{5,6},{6,7},{7,4},{8,9},{9,10},{10,1... | collective-permute-start | bytes 1671176 | tf_op jit(solution)/shard_map/ppermute | solution.py:974
  317.4 23.3 %collective-permute-start.37 = (bf16[2,2,128,1024]{3,2,1,0:T(8,128)(2,1)}, bf16[2,2,128,1024]{3,2,1,0:T(8,128)(2,1)}, u32[]{:S(2)}, u32[]{:S(2)}) collective-permute-start(bf16[2,2,128,1024]{3,2,1,0:T(8,128)(2,1)} %get-tuple-element.525), channel_id=1, source_target_pairs={{0,8},{4,20},{8,0},{12,28},{16,24},{20,4},{24,16},{28,12},{1,9},{5... | collective-permute-start | bytes 3145736 | tf_op jit(solution)/shard_map/ppermute | solution.py:954
  332.5 53.3 %collective-permute-start.36 = (f32[2,16,1024]{2,1,0:T(8,128)}, f32[2,16,1024]{2,1,0:T(8,128)}, u32[]{:S(2)}, u32[]{:S(2)}) collective-permute-start(f32[2,16,1024]{2,1,0:T(8,128)} %get-tuple-element.398), channel_id=1, source_target_pairs={{1,0},{2,1},{3,2},{5,4},{6,5},{7,6},{9,8},{10,9},{11,10},{13,12},{... | collective-permute-start | bytes 393224 | tf_op jit(solution)/shard_map/ppermute | solution.py:1209
  333.8 23.6 %collective-permute-start.39 = (bf16[2,2,128,1024]{3,2,1,0:T(8,128)(2,1)}, bf16[2,2,128,1024]{3,2,1,0:T(8,128)(2,1)}, u32[]{:S(2)}, u32[]{:S(2)}) collective-permute-start(bf16[2,2,128,1024]{3,2,1,0:T(8,128)(2,1)} %get-tuple-element.523), channel_id=1, source_target_pairs={{0,8},{4,20},{8,0},{12,28},{16,24},{20,4},{24,16},{28,12},{1,9},{5... | collective-permute-start | bytes 3145736 | tf_op jit(solution)/shard_map/ppermute | solution.py:954
  342.7 31.2 %collective-permute-start.38 = (bf16[2,128,1024]{2,1,0:T(8,128)(2,1)S(1)}, bf16[2,128,1024]{2,1,0:T(8,128)(2,1)S(1)}, u32[]{:S(2)}, u32[]{:S(2)}) collective-permute-start(bf16[2,128,1024]{2,1,0:T(8,128)(2,1)S(1)} %get-tuple-element.539), channel_id=1, source_target_pairs={{0,16},{4,12},{8,24},{12,4},{16,0},{20,28},{24,8},{28,20},{1,17},{... | collective-permute-start | bytes 1572872 | tf_op jit(solution)/shard_map/ppermute | solution.py:954
  344.6 14.8 %collective-permute-start.43 = (bf16[128,2176]{1,0:T(8,128)(2,1)S(1)}, bf16[128,2176]{1,0:T(8,128)(2,1)S(1)}, u32[]{:S(2)}, u32[]{:S(2)}) collective-permute-start(bf16[128,2176]{1,0:T(8,128)(2,1)S(1)} %get-tuple-element.533), channel_id=1, source_target_pairs={{0,3},{1,0},{2,1},{3,2},{4,7},{5,4},{6,5},{7,6},{8,11},{9,8},{10,9... | collective-permute-start | bytes 1671176 | tf_op jit(solution)/shard_map/ppermute | solution.py:974
  347.0 24.1 %collective-permute-start.42 = (bf16[128,2176]{1,0:T(8,128)(2,1)S(1)}, bf16[128,2176]{1,0:T(8,128)(2,1)S(1)}, u32[]{:S(2)}, u32[]{:S(2)}) collective-permute-start(bf16[128,2176]{1,0:T(8,128)(2,1)S(1)} %add_convert_fusion.11), channel_id=1, source_target_pairs={{0,1},{1,2},{2,3},{3,0},{4,5},{5,6},{6,7},{7,4},{8,9},{9,10},{10,1... | collective-permute-start | bytes 1671176 | tf_op jit(solution)/shard_map/ppermute | solution.py:974
  359.1 16.9 %collective-permute-start.45 = (bf16[2,128,1024]{2,1,0:T(8,128)(2,1)S(1)}, bf16[2,128,1024]{2,1,0:T(8,128)(2,1)S(1)}, u32[]{:S(2)}, u32[]{:S(2)}) collective-permute-start(bf16[2,128,1024]{2,1,0:T(8,128)(2,1)S(1)} %get-tuple-element.536), channel_id=1, source_target_pairs={{0,16},{4,12},{8,24},{12,4},{16,0},{20,28},{24,8},{28,20},{1,17},{... | collective-permute-start | bytes 1572872 | tf_op jit(solution)/shard_map/ppermute | solution.py:954
  371.3 21.7 %collective-permute-start.46 = (bf16[128,2176]{1,0:T(8,128)(2,1)S(1)}, bf16[128,2176]{1,0:T(8,128)(2,1)S(1)}, u32[]{:S(2)}, u32[]{:S(2)}) collective-permute-start(bf16[128,2176]{1,0:T(8,128)(2,1)S(1)} %add_convert_fusion.10.refs_0_), channel_id=1, source_target_pairs={{0,8},{4,20},{8,0},{12,28},{16,24},{20,4},{24,16},{28,12},{1,9},{5... | collective-permute-start | bytes 1671176 | tf_op jit(solution)/shard_map/ppermute | solution.py:954
  371.5 21.5 %collective-permute-start.47 = (bf16[128,2176]{1,0:T(8,128)(2,1)S(1)}, bf16[128,2176]{1,0:T(8,128)(2,1)S(1)}, u32[]{:S(2)}, u32[]{:S(2)}) collective-permute-start(bf16[128,2176]{1,0:T(8,128)(2,1)S(1)} %add_convert_fusion.10.refs_0_), channel_id=1, source_target_pairs={{0,16},{4,12},{8,24},{12,4},{16,0},{20,28},{24,8},{28,20},{1,17},{... | collective-permute-start | bytes 1671176 | tf_op jit(solution)/shard_map/ppermute | solution.py:954
  373.9 19.1 %collective-permute-start.48 = (bf16[128,2176]{1,0:T(8,128)(2,1)S(1)}, bf16[128,2176]{1,0:T(8,128)(2,1)S(1)}, u32[]{:S(2)}, u32[]{:S(2)}) collective-permute-start(bf16[128,2176]{1,0:T(8,128)(2,1)S(1)} %add_convert_fusion.10.refs_0_), channel_id=1, source_target_pairs={{0,4},{4,0},{8,12},{12,8},{16,20},{20,16},{24,28},{28,24},{1,5},{5... | collective-permute-start | bytes 1671176 | tf_op jit(solution)/shard_map/ppermute | solution.py:954
  376.0 9.8 %collective-permute-start.44 = (bf16[128,1024]{1,0:T(8,128)(2,1)S(1)}, bf16[128,1024]{1,0:T(8,128)(2,1)S(1)}, u32[]{:S(2)}, u32[]{:S(2)}) collective-permute-start(bf16[128,1024]{1,0:T(8,128)(2,1)S(1)} %get-tuple-element.548), channel_id=1, source_target_pairs={{0,1},{1,2},{2,3},{3,0},{4,5},{5,6},{6,7},{7,4},{8,9},{9,10},{10,1... | collective-permute-start | bytes 786440 | tf_op jit(solution)/shard_map/ppermute | solution.py:974
  393.1 11.0 %collective-permute-start.51 = (bf16[2,128,2176]{2,1,0:T(8,128)(2,1)S(1)}, bf16[2,128,2176]{2,1,0:T(8,128)(2,1)S(1)}, u32[]{:S(2)}, u32[]{:S(2)}) collective-permute-start(bf16[2,128,2176]{2,1,0:T(8,128)(2,1)S(1)} %pad_maximum_fusion.3), channel_id=1, source_target_pairs={{0,4},{4,0},{8,12},{12,8},{16,20},{20,16},{24,28},{28,24},{1,5},{5... | collective-permute-start | bytes 3342344 | tf_op jit(solution)/shard_map/ppermute | solution.py:954
  393.6 10.6 %collective-permute-start.50 = (bf16[128,2176]{1,0:T(8,128)(2,1)S(1)}, bf16[128,2176]{1,0:T(8,128)(2,1)S(1)}, u32[]{:S(2)}, u32[]{:S(2)}) collective-permute-start(bf16[128,2176]{1,0:T(8,128)(2,1)S(1)} %collective-permute-done.46.refs_1_), channel_id=1, source_target_pairs={{0,16},{4,12},{8,24},{12,4},{16,0},{20,28},{24,8},{28,20},{1,17},{... | collective-permute-start | bytes 1671176 | tf_op jit(solution)/shard_map/ppermute | solution.py:954
  393.6 10.7 %collective-permute-start.55 = (bf16[128,1024]{1,0:T(8,128)(2,1)}, bf16[128,1024]{1,0:T(8,128)(2,1)S(1)}, u32[]{:S(2)}, u32[]{:S(2)}) collective-permute-start(bf16[128,1024]{1,0:T(8,128)(2,1)} %get-tuple-element.545), channel_id=1, source_target_pairs={{0,3},{1,0},{2,1},{3,2},{4,7},{5,4},{6,5},{7,6},{8,11},{9,8},{10,9... | collective-permute-start | bytes 786440 | tf_op jit(solution)/shard_map/ppermute | solution.py:974
  393.8 12.1 %collective-permute-start.54 = (bf16[128,1024]{1,0:T(8,128)(2,1)S(1)}, bf16[128,1024]{1,0:T(8,128)(2,1)S(1)}, u32[]{:S(2)}, u32[]{:S(2)}) collective-permute-start(bf16[128,1024]{1,0:T(8,128)(2,1)S(1)} %add_convert_fusion.15), channel_id=1, source_target_pairs={{0,1},{1,2},{2,3},{3,0},{4,5},{5,6},{6,7},{7,4},{8,9},{9,10},{10,1... | collective-permute-start | bytes 786440 | tf_op jit(solution)/shard_map/ppermute | solution.py:974
  395.2 9.0 %collective-permute-start.52 = (f32[4,5632]{1,0:T(4,128)S(1)}, f32[4,5632]{1,0:T(4,128)S(1)}, u32[]{:S(2)}, u32[]{:S(2)}) collective-permute-start(f32[4,5632]{1,0:T(4,128)S(1)} %add.170), channel_id=1, source_target_pairs={{0,8},{4,12},{8,0},{12,4},{16,24},{20,28},{24,16},{28,20},{1,9},{5... | collective-permute-start | bytes 270344 | tf_op jit(solution)/shard_map/ppermute | solution.py:954
  404.2 16.8 %collective-permute-start.53 = (bf16[128,2176]{1,0:T(8,128)(2,1)S(1)}, bf16[128,2176]{1,0:T(8,128)(2,1)S(1)}, u32[]{:S(2)}, u32[]{:S(2)}) collective-permute-start(bf16[128,2176]{1,0:T(8,128)(2,1)S(1)} %collective-permute-done.50.refs_3_), channel_id=1, source_target_pairs={{0,4},{4,0},{8,12},{12,8},{16,20},{20,16},{24,28},{28,24},{1,5},{5... | collective-permute-start | bytes 1671176 | tf_op jit(solution)/shard_map/ppermute | solution.py:954
  406.0 6.0 %collective-permute-start.56 = (bf16[128,1024]{1,0:T(8,128)(2,1)S(1)}, bf16[128,1024]{1,0:T(8,128)(2,1)S(1)}, u32[]{:S(2)}, u32[]{:S(2)}) collective-permute-start(bf16[128,1024]{1,0:T(8,128)(2,1)S(1)} %add_convert_fusion.14.refs_0_), channel_id=1, source_target_pairs={{0,8},{4,20},{8,0},{12,28},{16,24},{20,4},{24,16},{28,12},{1,9},{5... | collective-permute-start | bytes 786440 | tf_op jit(solution)/shard_map/ppermute | solution.py:954
  408.0 9.2 %collective-permute-start.57 = (bf16[128,1024]{1,0:T(8,128)(2,1)S(1)}, bf16[128,1024]{1,0:T(8,128)(2,1)S(1)}, u32[]{:S(2)}, u32[]{:S(2)}) collective-permute-start(bf16[128,1024]{1,0:T(8,128)(2,1)S(1)} %add_convert_fusion.14.refs_0_), channel_id=1, source_target_pairs={{0,16},{4,12},{8,24},{12,4},{16,0},{20,28},{24,8},{28,20},{1,17},{... | collective-permute-start | bytes 786440 | tf_op jit(solution)/shard_map/ppermute | solution.py:954
  410.3 6.9 %collective-permute-start.58 = (bf16[128,1024]{1,0:T(8,128)(2,1)S(1)}, bf16[128,1024]{1,0:T(8,128)(2,1)S(1)}, u32[]{:S(2)}, u32[]{:S(2)}) collective-permute-start(bf16[128,1024]{1,0:T(8,128)(2,1)S(1)} %add_convert_fusion.14.refs_0_), channel_id=1, source_target_pairs={{0,4},{4,0},{8,12},{12,8},{16,20},{20,16},{24,28},{28,24},{1,5},{5... | collective-permute-start | bytes 786440 | tf_op jit(solution)/shard_map/ppermute | solution.py:954
  417.2 15.5 %collective-permute-start.63 = (bf16[128,1024]{1,0:T(8,128)(2,1)S(1)}, bf16[128,1024]{1,0:T(8,128)(2,1)S(1)}, u32[]{:S(2)}, u32[]{:S(2)}) collective-permute-start(bf16[128,1024]{1,0:T(8,128)(2,1)S(1)} %collective-permute-done.56.refs_1_), channel_id=1, source_target_pairs={{0,16},{4,12},{8,24},{12,4},{16,0},{20,28},{24,8},{28,20},{1,17},{... | collective-permute-start | bytes 786440 | tf_op jit(solution)/shard_map/ppermute | solution.py:954
  418.8 14.0 %collective-permute-start.64 = (bf16[2,128,1024]{2,1,0:T(8,128)(2,1)S(1)}, bf16[2,128,1024]{2,1,0:T(8,128)(2,1)S(1)}, u32[]{:S(2)}, u32[]{:S(2)}) collective-permute-start(bf16[2,128,1024]{2,1,0:T(8,128)(2,1)S(1)} %pad_maximum_fusion.8), channel_id=1, source_target_pairs={{0,4},{4,0},{8,12},{12,8},{16,20},{20,16},{24,28},{28,24},{1,5},{5... | collective-permute-start | bytes 1572872 | tf_op jit(solution)/shard_map/ppermute | solution.py:954
  421.3 14.5 %collective-permute-start.62 = (f32[5632]{0:T(1024)S(1)}, f32[5632]{0:T(1024)S(1)}, u32[]{:S(2)}, u32[]{:S(2)}) collective-permute-start(f32[5632]{0:T(1024)S(1)} %get-tuple-element.512), channel_id=1, source_target_pairs={{0,3},{1,0},{2,1},{3,2},{4,7},{5,4},{6,5},{7,6},{8,11},{9,8},{10,9... | collective-permute-start | bytes 67592 | tf_op jit(solution)/shard_map/ppermute | solution.py:974
  421.3 14.4 %collective-permute-start.61 = (f32[5632]{0:T(1024)S(1)}, f32[5632]{0:T(1024)S(1)}, u32[]{:S(2)}, u32[]{:S(2)}) collective-permute-start(f32[5632]{0:T(1024)S(1)} %get-tuple-element.513), channel_id=1, source_target_pairs={{0,2},{1,3},{2,0},{3,1},{4,6},{5,7},{6,4},{7,5},{8,10},{9,11},{10,... | collective-permute-start | bytes 67592 | tf_op jit(solution)/shard_map/ppermute | solution.py:974
  422.4 13.3 %collective-permute-start.60 = (f32[5632]{0:T(1024)S(1)}, f32[5632]{0:T(1024)S(1)}, u32[]{:S(2)}, u32[]{:S(2)}) collective-permute-start(f32[5632]{0:T(1024)S(1)} %get-tuple-element.511), channel_id=1, source_target_pairs={{0,1},{1,2},{2,3},{3,0},{4,5},{5,6},{6,7},{7,4},{8,9},{9,10},{10,1... | collective-permute-start | bytes 67592 | tf_op jit(solution)/shard_map/ppermute | solution.py:974
  (59 other events, 727.2 us)
Sparse Core Ops, SparseCore 0:
  31.7 36.9 all-gather.4
  72.0 26.1 all-gather.6
